TPU v7x, 256 devices: a whole 4x4x8 slice. The times are simulated.
256 devices in a mesh: pipe: 16 (over z, y_hi), seq: 16 (over x, y_lo, core).
Axes of the slice: x: 4, y: 4 (y_hi: 2, y_lo: 2; y = y_hi * 2 + y_lo), z: 8, core: 2. Of those that a mesh axis runs over, the one named last changes fastest.
Arguments:
- hidden_in: bfloat16 [16, 2048, 3072], P('pipe', 'seq'), may hold values from -6 to 6
- queries: bfloat16 [16, 2, 2048, 2048], P('pipe', None, 'seq'), may hold values from -40 to 40
- keys: bfloat16 [16, 2, 2048, 2048], P('pipe', None, 'seq'), may hold values from -40 to 40
- values: bfloat16 [16, 2, 2048, 2048], P('pipe', None, 'seq'), may hold values from -6 to 6
- segments: int32 [16, 2, 2048], P('pipe', None, 'seq'), may hold values from 0 to 3, never falling along the last dimension, each value on 1 to 1024 neighbouring positions
- gates: float32 [16, 2, 4, 3072], P('pipe'), may hold values from -32 to 32
- out_weight: bfloat16 [16, 2048, 3072], P('pipe', 'seq'), may hold values from -0.125 to 0.125
- upstream: bfloat16 [16, 2048, 3072], P('pipe', 'seq'), may hold values from -6 to 6
- fresh: bfloat16 [2048, 3072], P('seq'), may hold values from -6 to 6
- loss_grad: bfloat16 [2048, 3072], P('seq'), may hold values from -6 to 6
Outputs:
- next_act: bfloat16 [16, 2048, 3072], P('pipe', 'seq')
- next_grad: bfloat16 [16, 2048, 3072], P('pipe', 'seq')
- qkv_grads: bfloat16 [16, 3, 2048, 2048], P('pipe', None, 'seq')
All inputs are finite; a program needn't handle non-finite values.
Results may differ from a plain program's by a relative error of at most 0.029.
Values may be sent and summed in bfloat16 or wider, within the bound.
No kernel may reach another device: no remote copies, remote signals or barrier semaphores. Data moves between devices by JAX's collectives and lax.ppermute only.
A program may use at most 128 MiB of HBM per device.

v0:
```python
import functools

import jax
import jax.numpy as jnp
from jax import lax
from jax.experimental import pallas as pl
from jax.experimental.pallas import tpu as pltpu
from jax.sharding import PartitionSpec as P

HD = 128
SCALE = HD ** (-0.5)
EXP2 = SCALE * 1.4426950408889634
LOW = -1e30
QB = 256
KT = 512
SEG_ROWS = 16
F32 = jnp.float32
BF16 = jnp.bfloat16

XN, YN = 4, 2
CHIPS = XN * YN
SAME_CORE = [[2 * i + c for i in range(CHIPS)] for c in range(2)]
CORE = [(i, i ^ 1) for i in range(2 * CHIPS)]
YSWAP = [(i, i ^ 2) for i in range(2 * CHIPS)]
XUP = [(i, (i + 4) % 16) for i in range(2 * CHIPS)]
XDOWN = [(i, (i - 4) % 16) for i in range(2 * CHIPS)]


def params(mib):
    return pltpu.CompilerParams(vmem_limit_bytes=mib * 1024 * 1024)


def whole(count):
    return [pl.BlockSpec(memory_space=pltpu.VMEM)] * count


def anywhere(arrays):
    return [pl.BlockSpec(memory_space=pl.ANY)] * len(arrays)


def cost(microseconds):
    return pl.CostEstimate(
        flops=int(microseconds * 1e9), bytes_accessed=0, transcendentals=0
    )


def dot(a, b, dims):
    return lax.dot_general(a, b, (dims, ((), ())), preferred_element_type=F32)


def pack_kernel(seg_ref, q_ref, k_ref, v_ref, *refs):
    out_ref = refs[-1]
    rows = q_ref.shape[0]
    for h in range(out_ref.shape[0]):
        cols = slice(h * HD, (h + 1) * HD)
        out_ref[h, 0:rows, :] = q_ref[:, cols]
        out_ref[h, rows:2 * rows, :] = k_ref[:, cols]
        out_ref[h, 2 * rows:3 * rows, :] = v_ref[:, cols]
        out_ref[h, 3 * rows:, :] = jnp.broadcast_to(
            seg_ref[...].astype(F32), (SEG_ROWS, HD)
        ).astype(BF16)


def pack(queries, keys, values, segments, batch, *later):
    rows, width = queries.shape[2], queries.shape[3]
    heads = width // HD
    block = pl.BlockSpec((None, None, rows, width), lambda i: (0, batch, 0, 0))
    return pl.pallas_call(
        pack_kernel,
        grid=(1,),
        out_shape=jax.ShapeDtypeStruct((heads, 3 * rows + SEG_ROWS, HD), BF16),
        in_specs=[pl.BlockSpec((1, rows), lambda i: (0, 0)), block, block, block] + anywhere(later),
        out_specs=pl.BlockSpec((heads, 3 * rows + SEG_ROWS, HD), lambda i: (0, 0, 0)),
        compiler_params=params(24),
        cost_estimate=cost(2),
        name="pack",
    )(segments[0, batch][None], queries, keys, values, *later)


def sample_starts(in_ref, rows):
    ids = in_ref[:, 3 * rows:, :].astype(F32)
    return [
        jnp.sum(jnp.where(ids < s, 1.0, 0.0)).astype(jnp.int32) // SEG_ROWS for s in (1, 2, 3)
    ]


def sample_of(position, starts):
    return sum(jnp.where(position >= b, 1.0, 0.0) for b in starts)


def tile_range(first, last, starts, total):
    low, high = 0, total
    for b in starts:
        low = jnp.maximum(low, jnp.where(b <= first, b, 0))
        high = jnp.minimum(high, jnp.where(b > last, b, total))
    return low // KT, (high + KT - 1) // KT


def block_rows(ref, index, count, start, rows):
    per = count // rows
    return ref[pl.ds(index * per, per), start:start + rows, :].reshape(count, HD)


def fill_samples(seg_s, starts):
    total = seg_s.shape[0]
    for i in range(total // 256):
        position = i * 256 + lax.broadcasted_iota(jnp.int32, (256, HD), 0)
        seg_s[i * 256:(i + 1) * 256, :] = sample_of(position, starts)


def forward_kernel(in_ref, *refs):
    out_ref, vt_s, seg_s = refs[-3:]
    blocks, rows = in_ref.shape[0], 128
    total = blocks * rows
    starts = sample_starts(in_ref, rows)
    fill_samples(seg_s, starts)
    for i in range(blocks):
        vt_s[:, i * rows:(i + 1) * rows] = in_ref[i, 2 * rows:3 * rows, :].T

    def per_block(i, _):
        q = block_rows(in_ref, i, QB, 0, rows)
        first = i * QB
        seg_q = sample_of(first + lax.broadcasted_iota(jnp.int32, (1, QB), 1), starts)
        begin, end = tile_range(first, first + QB - 1, starts, total)

        def per_tile(t, carry):
            m, l, acc = carry
            k = block_rows(in_ref, t, KT, rows, rows)
            s = dot(k, q, ((1,), (1,)))
            seg_k = seg_s[pl.ds(pl.multiple_of(t * KT, KT), KT), :]
            s = jnp.where(jnp.concatenate([seg_k, seg_k], axis=1) == seg_q, s, LOW)
            m_new = jnp.maximum(m, jnp.max(s, axis=0, keepdims=True))
            p = jnp.exp2((s - m_new) * EXP2)
            alpha = jnp.exp2((m - m_new) * EXP2)
            l = l * alpha + jnp.sum(p, axis=0, keepdims=True)
            vt = vt_s[:, pl.ds(pl.multiple_of(t * KT, KT), KT)]
            acc = acc * alpha + dot(vt, p.astype(BF16), ((1,), (0,)))
            return m_new, l, acc

        m0 = jnp.full((1, QB), LOW, F32)
        l0 = jnp.zeros((1, QB), F32)
        m, l, acc = lax.fori_loop(begin, end, per_tile, (m0, l0, jnp.zeros((HD, QB), F32)))
        out_ref[i] = (acc / l).T.astype(BF16)
        return 0

    lax.fori_loop(0, total // QB, per_block, 0)


def attention_forward(packed, *later):
    blocks = packed.shape[0]
    total = blocks * 128
    return pl.pallas_call(
        forward_kernel,
        out_shape=jax.ShapeDtypeStruct((total // QB, QB, HD), BF16),
        in_specs=whole(1) + anywhere(later),
        out_specs=whole(1)[0],
        scratch_shapes=[pltpu.VMEM((HD, total), BF16), pltpu.VMEM((total, HD), F32)],
        compiler_params=params(24),
        cost_estimate=cost(0.2),
        name="attention_forward",
    )(packed, *later)


OFFSETS = ((0, 0), (0, 1), (3, 0), (1, 0), (3, 1), (1, 1), (2, 0), (2, 1))


def chip_at(position, offset):
    x, y = position // 4, (position // 2) % 2
    return ((x + offset[0]) % XN) * YN + (y + offset[1]) % YN


def backward_kernel(place_ref, in_ref, *refs):
    g_refs, (out_ref, g_ref, kt_s, seg_s, s_s, dp_s, dk_s, dv_s) = refs[:CHIPS], refs[-8:]
    blocks, rows = in_ref.shape[0], 128
    for offset, ref in zip(OFFSETS, g_refs):
        g_ref[chip_at(place_ref[0], (-offset[0] % XN, offset[1]))] = ref[...]
    total = blocks * rows
    starts = sample_starts(in_ref, rows)
    fill_samples(seg_s, starts)
    for i in range(blocks):
        kt_s[:, i * rows:(i + 1) * rows] = in_ref[i, rows:2 * rows, :].T
    dk_s[...] = jnp.zeros_like(dk_s)
    dv_s[...] = jnp.zeros_like(dv_s)

    def per_block(i, _):
        q = block_rows(in_ref, i, QB, 0, rows)
        g = g_ref[i]
        first = i * QB
        seg_q = sample_of(first + lax.broadcasted_iota(jnp.int32, (1, QB), 1), starts)
        begin, end = tile_range(first, first + QB - 1, starts, total)

        def scores(t, carry):
            m, l, d = carry
            here = pl.ds(pl.multiple_of(t * KT, KT), KT)
            s = dot(block_rows(in_ref, t, KT, rows, rows), q, ((1,), (1,)))
            dp = dot(block_rows(in_ref, t, KT, 2 * rows, rows), g, ((1,), (1,)))
            seg_k = seg_s[here, :]
            s = jnp.where(jnp.concatenate([seg_k, seg_k], axis=1) == seg_q, s, LOW)
            s_s[here, :] = s
            dp_s[here, :] = dp
            m_new = jnp.maximum(m, jnp.max(s, axis=0, keepdims=True))
            p = jnp.exp2((s - m_new) * EXP2)
            alpha = jnp.exp2((m - m_new) * EXP2)
            l = l * alpha + jnp.sum(p, axis=0, keepdims=True)
            d = d * alpha + jnp.sum(p * dp, axis=0, keepdims=True)
            return m_new, l, d

        zero = jnp.zeros((1, QB), F32)
        m, l, d = lax.fori_loop(begin, end, scores, (jnp.full((1, QB), LOW, F32), zero, zero))
        inverse = 1.0 / l
        delta = d * inverse

        def grads(t, acc):
            here = pl.ds(pl.multiple_of(t * KT, KT), KT)
            p = jnp.exp2((s_s[here, :] - m) * EXP2) * inverse
            ds = (p * (dp_s[here, :] - delta)).astype(BF16)
            dv_s[here, :] += dot(p.astype(BF16), g, ((1,), (0,)))
            dk_s[here, :] += dot(ds, q, ((1,), (0,)))
            return acc + dot(kt_s[:, here], ds, ((1,), (0,)))

        acc = lax.fori_loop(begin, end, grads, jnp.zeros((HD, QB), F32))
        dq = (acc * SCALE).T.astype(BF16)
        per = QB // rows
        out_ref[pl.ds(i * per, per), 0:rows, :] = dq.reshape(per, rows, HD)
        return 0

    lax.fori_loop(0, total // QB, per_block, 0)
    for i in range(blocks):
        here = slice(i * rows, (i + 1) * rows)
        out_ref[i, rows:2 * rows, :] = (dk_s[here, :] * SCALE).astype(BF16)
        out_ref[i, 2 * rows:3 * rows, :] = dv_s[here, :].astype(BF16)


def attention_backward(place, packed, grads, *later):
    blocks = packed.shape[0]
    total = blocks * 128
    return pl.pallas_call(
        backward_kernel,
        out_shape=jax.ShapeDtypeStruct((blocks, 3 * 128, HD), BF16),
        in_specs=[pl.BlockSpec(memory_space=pltpu.SMEM)] + whole(1 + CHIPS) + anywhere(later),
        out_specs=whole(1)[0],
        scratch_shapes=[
            pltpu.VMEM((total // QB, QB, HD), BF16),
            pltpu.VMEM((HD, total), BF16),
            pltpu.VMEM((total, HD), F32),
            pltpu.VMEM((total, QB), F32),
            pltpu.VMEM((total, QB), F32),
            pltpu.VMEM((total, HD), F32),
            pltpu.VMEM((total, HD), F32),
        ],
        compiler_params=params(32),
        cost_estimate=cost(30),
        name="attention_backward",
    )(place, packed, *grads, *later)


def grad_kernel(count, place_ref, own_ref, other_ref, *refs):
    pieces, outs, g_s = refs[:count], refs[-1 - count:-1], refs[-1]
    rows = own_ref.shape[0]
    core = place_ref[0] % 2
    g_s[pl.ds(pl.multiple_of(core * rows, rows), rows), :] = own_ref[...]
    g_s[pl.ds(pl.multiple_of((1 - core) * rows, rows), rows), :] = other_ref[...]
    for j in range(0, count, 2):
        w = jnp.concatenate([pieces[j][...], pieces[j + 1][...]], axis=0)
        r = dot(g_s[...], w, ((1,), (1,))).astype(BF16)
        outs[j][...] = r[:, :HD]
        outs[j + 1][...] = r[:, HD:]


def attention_grad(place, own, other, pieces, *later):
    rows, width = own.shape
    count = len(pieces)
    return pl.pallas_call(
        functools.partial(grad_kernel, count),
        out_shape=(jax.ShapeDtypeStruct((2 * rows, HD), BF16),) * count,
        in_specs=[pl.BlockSpec(memory_space=pltpu.SMEM)] + whole(2 + count) + anywhere(later),
        out_specs=tuple(whole(count)),
        scratch_shapes=[pltpu.VMEM((2 * rows, width), BF16)],
        compiler_params=params(32),
        cost_estimate=cost(0.2),
        name="attention_grad",
    )(place, own, other, *pieces, *later)


def project_kernel(place_ref, attn_ref, *refs):
    pieces, (own_ref, other_ref, a_s) = refs[:CHIPS], refs[-3:]
    rows, width = own_ref.shape
    core = place_ref[0] % 2
    for half, at in ((0, core), (1, 1 - core)):
        src = pl.ds(pl.multiple_of(at * rows, rows), rows)
        for j in range(CHIPS):
            a_s[half * rows:(half + 1) * rows, j * HD:(j + 1) * HD] = attn_ref[chip_at(place_ref[0], OFFSETS[j]), src, :]
    step = 512
    for n in range(0, width, step):
        acc = None
        for j in range(0, CHIPS, 2):
            w = jnp.concatenate([pieces[j][:, n:n + step], pieces[j + 1][:, n:n + step]], axis=0)
            r = dot(a_s[:, j * HD:(j + 2) * HD], w, ((1,), (0,)))
            acc = r if acc is None else acc + r
        own_ref[:, n:n + step] = acc[:rows]
        other_ref[:, n:n + step] = acc[rows:].astype(other_ref.dtype)


def project(place, attn, pieces, *later):
    rows, width = pieces[0].shape
    return pl.pallas_call(
        project_kernel,
        out_shape=(
            jax.ShapeDtypeStruct((rows, width), F32),
            jax.ShapeDtypeStruct((rows, width), F32),
        ),
        in_specs=[pl.BlockSpec(memory_space=pltpu.SMEM)] + whole(1 + CHIPS) + anywhere(later),
        out_specs=tuple(whole(2)),
        scratch_shapes=[pltpu.VMEM((2 * rows, CHIPS * HD), BF16)],
        compiler_params=params(32),
        cost_estimate=cost(0.2),
        name="project",
    )(place, attn, *pieces, *later)


def unpack_kernel(in_ref, out_ref):
    rows = out_ref.shape[1]
    for h in range(in_ref.shape[0]):
        for t in range(3):
            out_ref[t, :, h * HD:(h + 1) * HD] = in_ref[h, t * rows:(t + 1) * rows, :]


def unpack(received):
    heads, rows = received.shape[0], received.shape[1] // 3
    return pl.pallas_call(
        unpack_kernel,
        out_shape=jax.ShapeDtypeStruct((3, rows, heads * HD), BF16),
        in_specs=whole(1),
        out_specs=whole(1)[0],
        compiler_params=params(24),
        cost_estimate=cost(2),
        name="unpack",
    )(received)


def choose_kernel(section_ref, first_ref, second_ref, *refs):
    out_ref = refs[-1]
    out_ref[...] = jnp.where(section_ref[0] == section_ref[1], first_ref[...], second_ref[...])


def choose(sections, first, second, *later):
    return pl.pallas_call(
        choose_kernel,
        out_shape=jax.ShapeDtypeStruct(first.shape, first.dtype),
        in_specs=[pl.BlockSpec(memory_space=pltpu.SMEM)] + whole(2) + anywhere(later),
        out_specs=whole(1)[0],
        compiler_params=params(16),
        cost_estimate=cost(2),
        name="choose",
    )(sections, first, second, *later)


def rotated(array, axis, by):
    length = lax.axis_size(axis)
    return lax.ppermute(array, axis, [(i, (i + by) % length) for i in range(length)])


def per_sample(seg, table):
    onehot = (seg[:, None] == jnp.arange(table.shape[0], dtype=jnp.int32)[None, :]).astype(F32)
    return jnp.sum(onehot[:, :, None] * table[None, :, :], axis=1)


def to_chip(array, offset):
    if offset == (0, 0):
        return array
    pairs = [(i, 2 * chip_at(i, offset) + i % 2) for i in range(2 * CHIPS)]
    return lax.ppermute(array, "seq", pairs)


def exchange(array):
    return lax.all_to_all(array, "seq", 0, 0, tiled=True)


def exchange_same_core(array):
    return lax.all_to_all(array, "seq", 0, 0, tiled=True, axis_index_groups=SAME_CORE)


def body(hidden_in, queries, keys, values, segments, gates, out_weight, upstream, fresh, loss_grad):
    section = lax.axis_index("pipe")
    last_section = lax.axis_size("pipe") - 1
    place = lax.axis_index("seq")[None]

    own = out_weight[0]
    y_own = lax.ppermute(own, "seq", YSWAP)
    left = lax.ppermute(own, "seq", XUP)
    right = lax.ppermute(own, "seq", XDOWN)
    y_left = lax.ppermute(y_own, "seq", XUP)
    y_right = lax.ppermute(y_own, "seq", XDOWN)
    far = lax.ppermute(left, "seq", XUP)
    y_far = lax.ppermute(y_right, "seq", XDOWN)
    pieces = (own, y_own, left, right, y_left, y_right, far, y_far)

    local_seg = segments[0]
    g_scaled = (per_sample(local_seg[1], gates[0, 1]) * upstream[0].astype(F32)).astype(BF16)
    g_other = lax.ppermute(g_scaled, "seq", CORE)

    gate_tok = per_sample(local_seg[0], gates[0, 0])
    fwd = exchange(pack(queries, keys, values, segments, 0))
    packed = pack(queries, keys, values, segments, 1, fwd, right)
    bwd = exchange(packed)

    sections = jnp.stack([section, jnp.zeros_like(section)])
    turned = choose(sections, loss_grad, upstream[0], y_own)
    next_grad = rotated(turned, "pipe", -1)

    attn = exchange_same_core(attention_forward(fwd, packed, turned, gate_tok))
    near = attention_grad(place, g_scaled, g_other, pieces[:4])
    near = tuple(to_chip(g, o) for g, o in zip(near, OFFSETS[:4]))
    distant = attention_grad(place, g_scaled, g_other, pieces[4:], bwd, *near)
    distant = tuple(to_chip(g, o) for g, o in zip(distant, OFFSETS[4:]))
    part, part_other = project(place, attn, pieces, distant[0], next_grad)
    grads = attention_backward(place, bwd, near + distant)
    proj = part + lax.ppermute(part_other, "seq", CORE)
    section_out = (hidden_in[0].astype(F32) + gate_tok * proj).astype(BF16)
    next_act = rotated(jnp.where(section == last_section, fresh, section_out), "pipe", 1)[None]

    qkv_grads = unpack(exchange(grads))[None]
    return (next_act, next_grad[None], qkv_grads)


def solution(mesh):
    in_specs = (
        P("pipe", "seq", None),
        P("pipe", None, "seq", None),
        P("pipe", None, "seq", None),
        P("pipe", None, "seq", None),
        P("pipe", None, "seq"),
        P("pipe", None, None, None),
        P("pipe", "seq", None),
        P("pipe", "seq", None),
        P("seq", None),
        P("seq", None),
    )
    out_specs = (P("pipe", "seq", None), P("pipe", "seq", None), P("pipe", None, "seq", None))
    return jax.shard_map(body, mesh=mesh, in_specs=in_specs, out_specs=out_specs, check_vma=False)
```

profile of v0, /device:TPU:1, one launch (start us, length us, event | category | flops | bytes accessed | tf_op | source)
XLA Modules:
  0.0 228.7 jit_solution(7704061709215386416)
XLA Ops:
  6.5 7.0 %all-to-all-start = ((bf16[16,400,128]{2,1,0:T(8,128)(2,1)}), bf16[16,400,128]{2,1,0:T(8,128)(2,1)S(1)}, u32[]{:S(2)}, u32[]{:S(2)}) async-start(bf16[16,400,128]{2,1,0:T(8,128)(2,1)} %copy-done.8), calls=%async_computation | async-start | bytes 3276800 | tf_op jit(solution)/shard_map/all_to_all | solution.py:376
  13.5 1.5 collective-permute-start.1
  15.0 2.4 %collective-permute-start = (bf16[128,3072]{1,0:T(8,128)(2,1)S(1)}, bf16[128,3072]{1,0:T(8,128)(2,1)S(1)}, u32[]{:S(2)}, u32[]{:S(2)}) collective-permute-start(bf16[128,3072]{1,0:T(8,128)(2,1)S(1)} %bitcast.24), channel_id=1, source_target_pairs={{0,12},{1,13},{2,14},{3,15},{4,0},{5,1},{6,2},{7,3},{8,4},{9,5},{1... | collective-permute-start | bytes 2359304 | tf_op jit(solution)/shard_map/ppermute | solution.py:391
  17.4 1.4 slice_bitcast_fusion
  18.8 31.6 %collective-permute-done.refs_1_.refs_3_ = bf16[128,3072]{1,0:T(8,128)(2,1)S(1)} collective-permute-done((bf16[128,3072]{1,0:T(8,128)(2,1)S(1)}, bf16[128,3072]{1,0:T(8,128)(2,1)S(1)}, u32[]{:S(2)}, u32[]{:S(2)}) %collective-permute-start) | collective-permute-done | bytes 786464 | tf_op jit(solution)/shard_map/ppermute | solution.py:391
  51.4 1.7 copy-done.4
  55.5 1.4 pack.3.refs_0_
  57.0 6.5 %all-to-all-start.2 = ((bf16[16,400,128]{2,1,0:T(8,128)(2,1)}), bf16[16,400,128]{2,1,0:T(8,128)(2,1)}, u32[]{:S(2)}, u32[]{:S(2)}) async-start(bf16[16,400,128]{2,1,0:T(8,128)(2,1)} %pack.3.refs_0_), calls=%async_computation.2 | async-start | bytes 3276800 | tf_op jit(solution)/shard_map/all_to_all | solution.py:376
  64.1 2.7 %collective-permute-start.4 = (bf16[128,3072]{1,0:T(8,128)(2,1)}, bf16[128,3072]{1,0:T(8,128)(2,1)}, u32[]{:S(2)}, u32[]{:S(2)}) collective-permute-start(bf16[128,3072]{1,0:T(8,128)(2,1)} %collective-permute-done.1.refs_0_.refs_1_), channel_id=1, source_target_pairs={{0,12},{1,13},{2,14},{3,15},{4,0},{5,1},{6,2},{7,3},{8,4},{9,5},{1... | collective-permute-start | bytes 2359304 | tf_op jit(solution)/shard_map/ppermute | solution.py:393
  67.8 1.5 choose.1.refs_1_
  69.3 7.9 %collective-permute-start.12 = (bf16[128,3072]{1,0:T(8,128)(2,1)}, bf16[128,3072]{1,0:T(8,128)(2,1)}, u32[]{:S(2)}, u32[]{:S(2)}) collective-permute-start(bf16[128,3072]{1,0:T(8,128)(2,1)} %choose.1.refs_1_), channel_id=1, source_target_pairs={{0,240},{16,0},{32,16},{48,32},{64,48},{80,64},{96,80},{112,96},{1... | collective-permute-start | bytes 2359304 | tf_op jit(solution)/shard_map/ppermute | solution.py:360
  77.5 24.7 %collective-permute-done.4.refs_1_.refs_5_ = bf16[128,3072]{1,0:T(8,128)(2,1)} collective-permute-done((bf16[128,3072]{1,0:T(8,128)(2,1)}, bf16[128,3072]{1,0:T(8,128)(2,1)}, u32[]{:S(2)}, u32[]{:S(2)}) %collective-permute-start.4) | collective-permute-done | bytes 786464 | tf_op jit(solution)/shard_map/ppermute | solution.py:393
  102.2 4.4 %collective-permute-start.6 = (bf16[128,3072]{1,0:T(8,128)(2,1)}, bf16[128,3072]{1,0:T(8,128)(2,1)}, u32[]{:S(2)}, u32[]{:S(2)}) collective-permute-start(bf16[128,3072]{1,0:T(8,128)(2,1)} %collective-permute-done.4.refs_1_.refs_5_), channel_id=1, source_target_pairs={{0,12},{1,13},{2,14},{3,15},{4,0},{5,1},{6,2},{7,3},{8,4},{9,5},{1... | collective-permute-start | bytes 2359304 | tf_op jit(solution)/shard_map/ppermute | solution.py:395
  107.2 13.2 %attention_forward.1 = bf16[8,256,128]{2,1,0:T(8,128)(2,1)S(1)} custom-call(bf16[16,400,128]{2,1,0:T(8,128)(2,1)S(1)} %copy-done.1, bf16[16,400,128]{2,1,0:T(8,128)(2,1)} %pack.3.refs_0_, bf16[128,3072]{1,0:T(8,128)(2,1)} %choose.1.refs_1_, f32[128,3072]{1,0:T(8,128)S(1)} %multiply_reduce_fusion.1.refs_2_), custom_call_target="tpu_custom_call" | custom-call | flops 200000000 | tf_op jit(solution)/shard_map/attention_forward/pallas_call | solution.py:152
  121.2 4.4 %all-to-all-start.1 = ((bf16[8,256,128]{2,1,0:T(8,128)(2,1)}), bf16[8,256,128]{2,1,0:T(8,128)(2,1)}, u32[]{:S(2)}, u32[]{:S(2)}) async-start(bf16[8,256,128]{2,1,0:T(8,128)(2,1)} %copy-done.7), calls=%async_computation.1 | async-start | bytes 1048576 | tf_op jit(solution)/shard_map/all_to_all | solution.py:380
  126.7 2.6 %attention_grad.2 = (bf16[256,128]{1,0:T(8,128)(2,1)S(1)}, bf16[256,128]{1,0:T(8,128)(2,1)S(1)}, bf16[256,128]{1,0:T(8,128)(2,1)S(1)}, bf16[256,128]{1,0:T(8,128)(2,1)S(1)}) custom-call(s32[1]{0:T(128)} %bitcast.3.place_ref, bf16[128,3072]{1,0:T(8,128)(2,1)S(1)} %multiply_convert_fusion.own_ref, bf16[128,3072]{1,0:T(8,128)(2,1)} %collective-permute-done.7.other_ref, ...), custom_call_target="tpu_custom_call" | custom-call | flops 200000000 | tf_op jit(solution)/shard_map/attention_grad/pallas_call | solution.py:273
  129.3 1.5 collective-permute-start.10
  130.8 5.5 %collective-permute-done.10.refs_8_.refs_3_ = bf16[256,128]{1,0:T(8,128)(2,1)S(1)} collective-permute-done((bf16[256,128]{1,0:T(8,128)(2,1)S(1)}, bf16[256,128]{1,0:T(8,128)(2,1)S(1)}, u32[]{:S(2)}, u32[]{:S(2)}) %collective-permute-start.10) | collective-permute-done | bytes 65568 | tf_op jit(solution)/shard_map/ppermute | solution.py:372
  136.4 3.1 %collective-permute-done.8.refs_6_.refs_1_ = bf16[256,128]{1,0:T(8,128)(2,1)S(1)} collective-permute-done((bf16[256,128]{1,0:T(8,128)(2,1)S(1)}, bf16[256,128]{1,0:T(8,128)(2,1)S(1)}, u32[]{:S(2)}, u32[]{:S(2)}) %collective-permute-start.8) | collective-permute-done | bytes 65568 | tf_op jit(solution)/shard_map/ppermute | solution.py:372
  139.5 3.1 %collective-permute-done.9.refs_7_.refs_2_ = bf16[256,128]{1,0:T(8,128)(2,1)S(1)} collective-permute-done((bf16[256,128]{1,0:T(8,128)(2,1)S(1)}, bf16[256,128]{1,0:T(8,128)(2,1)S(1)}, u32[]{:S(2)}, u32[]{:S(2)}) %collective-permute-start.9) | collective-permute-done | bytes 65568 | tf_op jit(solution)/shard_map/ppermute | solution.py:372
  142.6 3.8 %attention_grad.3 = (bf16[256,128]{1,0:T(8,128)(2,1)}, bf16[256,128]{1,0:T(8,128)(2,1)}, bf16[256,128]{1,0:T(8,128)(2,1)S(1)}, bf16[256,128]{1,0:T(8,128)(2,1)S(1)}) custom-call(s32[1]{0:T(128)} %bitcast.3.place_ref, bf16[128,3072]{1,0:T(8,128)(2,1)S(1)} %multiply_convert_fusion.own_ref, bf16[128,3072]{1,0:T(8,128)(2,1)} %collective-permute-done.7.other_ref, ...), custom_call_target="tpu_custom_call" | custom-call | flops 200000000 | tf_op jit(solution)/shard_map/attention_grad/pallas_call | solution.py:273
  146.4 2.1 collective-permute-start.11
  149.6 1.8 collective-permute-start.17
  152.6 5.4 %project.1 = (f32[128,3072]{1,0:T(8,128)S(1)}, f32[128,3072]{1,0:T(8,128)}) custom-call(s32[1]{0:T(128)} %bitcast.3.place_ref, bf16[8,256,128]{2,1,0:T(8,128)(2,1)} %all-to-all-done.1.attn_ref, bf16[128,3072]{1,0:T(8,128)(2,1)S(1)} %bitcast.27, bf16[128,3072]{1,0:T(8,128)(2,1)} %collective-permute-done.1.refs_0_.refs_1_, ...), custom_call_target="tpu_custom_call" | custom-call | flops 200000000 | tf_op jit(solution)/shard_map/project/pallas_call | solution.py:306
  159.2 5.5 %collective-permute-start.13 = (f32[128,3072]{1,0:T(8,128)}, f32[128,3072]{1,0:T(8,128)}, u32[]{:S(2)}, u32[]{:S(2)}) collective-permute-start(f32[128,3072]{1,0:T(8,128)} %get-tuple-element.19), channel_id=1, source_target_pairs={{0,1},{1,0},{2,3},{3,2},{4,5},{5,4},{6,7},{7,6},{8,9},{9,8},{10,11... | collective-permute-start | bytes 4718600 | tf_op jit(solution)/shard_map/ppermute | solution.py:418
  164.7 20.6 %attention_backward.1 = bf16[16,384,128]{2,1,0:T(8,128)(2,1)S(1)} custom-call(s32[1]{0:T(128)} %bitcast.3.place_ref, bf16[16,400,128]{2,1,0:T(8,128)(2,1)} %all-to-all-done.2.refs_4_.in_ref, bf16[256,128]{1,0:T(8,128)(2,1)S(1)} %get-tuple-element.13.refs_5_.refs_0_, bf16[256,128]{1,0:T(8,128)(2,1)S(1)} %collective-permute-done.8.refs_6_.refs_1_, ...), custom_call_target="tpu_custom_call" | custom-call | flops 30000001024 | tf_op jit(solution)/shard_map/attention_backward/pallas_call | solution.py:237
  186.5 5.0 %all-to-all-start.3 = ((bf16[16,384,128]{2,1,0:T(8,128)(2,1)}), bf16[16,384,128]{2,1,0:T(8,128)(2,1)}, u32[]{:S(2)}, u32[]{:S(2)}) async-start(bf16[16,384,128]{2,1,0:T(8,128)(2,1)} %copy-done.10), calls=%async_computation.3 | async-start | bytes 3145728 | tf_op jit(solution)/shard_map/all_to_all | solution.py:376
  191.5 3.3 %fusion.1 = bf16[128,3072]{1,0:T(8,128)(2,1)} fusion(bf16[128,3072]{1,0:T(8,128)(2,1)S(1)} %copy-done.19, f32[128,3072]{1,0:T(8,128)S(1)} %multiply_reduce_fusion.1.refs_2_, f32[128,3072]{1,0:T(8,128)} %copy-done.9, f32[128,3072]{1,0:T(8,128)} %collective-permute-done.13, bf16[1,128,3072]{2,1,0:T(8,128)(2,1)S(1)} %copy-done.20, pred[]{:T(512)S(6)} %eq.41), kind=kLoop, calls=%fused_computation.5 | loop fusion | flops 2359296 | bytes 7077889 | tf_op jit(solution)/shard_map/jit(_where)/select_n | solution.py:420
  194.8 18.1 %all-to-all-done.3.in_ref = bf16[16,384,128]{2,1,0:T(8,128)(2,1)} async-done(((bf16[16,384,128]{2,1,0:T(8,128)(2,1)}), bf16[16,384,128]{2,1,0:T(8,128)(2,1)}, u32[]{:S(2)}, u32[]{:S(2)}) %all-to-all-start.3) | async-done | bytes 1572896 | tf_op jit(solution)/shard_map/all_to_all | solution.py:376
  212.9 3.0 %unpack.1 = bf16[3,128,2048]{2,1,0:T(8,128)(2,1)} custom-call(bf16[16,384,128]{2,1,0:T(8,128)(2,1)} %all-to-all-done.3.in_ref), custom_call_target="tpu_custom_call" | custom-call | flops 2000000000 | tf_op jit(solution)/shard_map/unpack/pallas_call | solution.py:330
  215.9 9.9 %collective-permute-done.14 = bf16[128,3072]{1,0:T(8,128)(2,1)S(1)} collective-permute-done((bf16[128,3072]{1,0:T(8,128)(2,1)}, bf16[128,3072]{1,0:T(8,128)(2,1)S(1)}, u32[]{:S(2)}, u32[]{:S(2)}) %collective-permute-start.14) | collective-permute-done | bytes 786464 | tf_op jit(solution)/shard_map/ppermute | solution.py:360
  226.7 2.1 copy.16
  (76 shorter events, 19.2 us)
Async XLA Ops:
  6.5 7.0 %copy-start.2 = (bf16[1,128,3072]{2,1,0:T(8,128)(2,1)S(1)}, bf16[1,128,3072]{2,1,0:T(8,128)(2,1)}, u32[]{:S(2)}) copy-start(bf16[1,128,3072]{2,1,0:T(8,128)(2,1)} %param.16) | copy-start | bytes 2359300
  6.5 44.8 %copy-start.13 = (bf16[1,2,128,2048]{3,2,1,0:T(8,128)(2,1)S(1)}, bf16[1,2,128,2048]{3,2,1,0:T(8,128)(2,1)}, u32[]{:S(2)}) copy-start(bf16[1,2,128,2048]{3,2,1,0:T(8,128)(2,1)} %q_ref.3) | copy-start | bytes 3145732
  6.5 44.8 %all-to-all-start = ((bf16[16,400,128]{2,1,0:T(8,128)(2,1)}), bf16[16,400,128]{2,1,0:T(8,128)(2,1)S(1)}, u32[]{:S(2)}, u32[]{:S(2)}) async-start(bf16[16,400,128]{2,1,0:T(8,128)(2,1)} %copy-done.8), calls=%async_computation | async-start | bytes 3276800 | tf_op jit(solution)/shard_map/all_to_all | solution.py:376
  13.5 50.6 %collective-permute-start.1 = (bf16[128,3072]{1,0:T(8,128)(2,1)S(1)}, bf16[128,3072]{1,0:T(8,128)(2,1)}, u32[]{:S(2)}, u32[]{:S(2)}) collective-permute-start(bf16[128,3072]{1,0:T(8,128)(2,1)S(1)} %bitcast.23), channel_id=1, source_target_pairs={{0,2},{1,3},{2,0},{3,1},{4,6},{5,7},{6,4},{7,5},{8,10},{9,11},{10,... | collective-permute-start | bytes 2359304 | tf_op jit(solution)/shard_map/ppermute | solution.py:389
  15.0 35.5 %collective-permute-start = (bf16[128,3072]{1,0:T(8,128)(2,1)S(1)}, bf16[128,3072]{1,0:T(8,128)(2,1)S(1)}, u32[]{:S(2)}, u32[]{:S(2)}) collective-permute-start(bf16[128,3072]{1,0:T(8,128)(2,1)S(1)} %bitcast.24), channel_id=1, source_target_pairs={{0,12},{1,13},{2,14},{3,15},{4,0},{5,1},{6,2},{7,3},{8,4},{9,5},{1... | collective-permute-start | bytes 2359304 | tf_op jit(solution)/shard_map/ppermute | solution.py:391
  17.4 59.8 %collective-permute-start.2 = (bf16[128,3072]{1,0:T(8,128)(2,1)S(1)}, bf16[128,3072]{1,0:T(8,128)(2,1)}, u32[]{:S(2)}, u32[]{:S(2)}) collective-permute-start(bf16[128,3072]{1,0:T(8,128)(2,1)S(1)} %bitcast.25), channel_id=1, source_target_pairs={{0,4},{1,5},{2,6},{3,7},{4,8},{5,9},{6,10},{7,11},{8,12},{9,13},{1... | collective-permute-start | bytes 2359304 | tf_op jit(solution)/shard_map/ppermute | solution.py:390
  51.4 5.6 %copy-start = (bf16[16,400,128]{2,1,0:T(8,128)(2,1)}, bf16[16,400,128]{2,1,0:T(8,128)(2,1)S(1)}, u32[]{:S(2)}) copy-start(bf16[16,400,128]{2,1,0:T(8,128)(2,1)S(1)} %all-to-all-done.refs_0_.in_ref) | copy-start | bytes 4915204
  51.4 1.7 copy-start.4
  57.0 6.5 %copy-start.21 = (f32[4,3072]{1,0:T(4,128)S(1)}, f32[4,3072]{1,0:T(4,128)}, u32[]{:S(2)}) copy-start(f32[4,3072]{1,0:T(4,128)} %get-tuple-element.23) | copy-start | bytes 147460
  57.0 64.2 %all-to-all-start.2 = ((bf16[16,400,128]{2,1,0:T(8,128)(2,1)}), bf16[16,400,128]{2,1,0:T(8,128)(2,1)}, u32[]{:S(2)}, u32[]{:S(2)}) async-start(bf16[16,400,128]{2,1,0:T(8,128)(2,1)} %pack.3.refs_0_), calls=%async_computation.2 | async-start | bytes 3276800 | tf_op jit(solution)/shard_map/all_to_all | solution.py:376
  63.5 3.3 %copy-start.11 = (bf16[1,128,3072]{2,1,0:T(8,128)(2,1)S(1)}, bf16[1,128,3072]{2,1,0:T(8,128)(2,1)}, u32[]{:S(2)}) copy-start(bf16[1,128,3072]{2,1,0:T(8,128)(2,1)} %param.17) | copy-start | bytes 2359300
  64.1 3.7 %copy-start.18 = (bf16[128,3072]{1,0:T(8,128)(2,1)S(1)}, bf16[128,3072]{1,0:T(8,128)(2,1)}, u32[]{:S(2)}) copy-start(bf16[128,3072]{1,0:T(8,128)(2,1)} %first_ref.1) | copy-start | bytes 2359300
  64.1 38.1 %collective-permute-start.4 = (bf16[128,3072]{1,0:T(8,128)(2,1)}, bf16[128,3072]{1,0:T(8,128)(2,1)}, u32[]{:S(2)}, u32[]{:S(2)}) collective-permute-start(bf16[128,3072]{1,0:T(8,128)(2,1)} %collective-permute-done.1.refs_0_.refs_1_), channel_id=1, source_target_pairs={{0,12},{1,13},{2,14},{3,15},{4,0},{5,1},{6,2},{7,3},{8,4},{9,5},{1... | collective-permute-start | bytes 2359304 | tf_op jit(solution)/shard_map/ppermute | solution.py:393
  67.0 58.5 %collective-permute-start.7 = (bf16[128,3072]{1,0:T(8,128)(2,1)S(1)}, bf16[128,3072]{1,0:T(8,128)(2,1)}, u32[]{:S(2)}, u32[]{:S(2)}) collective-permute-start(bf16[128,3072]{1,0:T(8,128)(2,1)S(1)} %multiply_convert_fusion.own_ref), channel_id=1, source_target_pairs={{0,1},{1,0},{2,3},{3,2},{4,5},{5,4},{6,7},{7,6},{8,9},{9,8},{10,11... | collective-permute-start | bytes 2359304 | tf_op jit(solution)/shard_map/ppermute | solution.py:400
  67.8 39.4 %copy-start.1 = (bf16[16,400,128]{2,1,0:T(8,128)(2,1)S(1)}, bf16[16,400,128]{2,1,0:T(8,128)(2,1)}, u32[]{:S(2)}) copy-start(bf16[16,400,128]{2,1,0:T(8,128)(2,1)} %copy-done) | copy-start | bytes 4915204
  69.3 82.2 %collective-permute-start.12 = (bf16[128,3072]{1,0:T(8,128)(2,1)}, bf16[128,3072]{1,0:T(8,128)(2,1)}, u32[]{:S(2)}, u32[]{:S(2)}) collective-permute-start(bf16[128,3072]{1,0:T(8,128)(2,1)} %choose.1.refs_1_), channel_id=1, source_target_pairs={{0,240},{16,0},{32,16},{48,32},{64,48},{80,64},{96,80},{112,96},{1... | collective-permute-start | bytes 2359304 | tf_op jit(solution)/shard_map/ppermute | solution.py:360
  77.2 65.4 %collective-permute-start.3 = (bf16[128,3072]{1,0:T(8,128)(2,1)}, bf16[128,3072]{1,0:T(8,128)(2,1)}, u32[]{:S(2)}, u32[]{:S(2)}) collective-permute-start(bf16[128,3072]{1,0:T(8,128)(2,1)} %collective-permute-done.1.refs_0_.refs_1_), channel_id=1, source_target_pairs={{0,4},{1,5},{2,6},{3,7},{4,8},{5,9},{6,10},{7,11},{8,12},{9,13},{1... | collective-permute-start | bytes 2359304 | tf_op jit(solution)/shard_map/ppermute | solution.py:392
  77.2 65.4 %collective-permute-start.5 = (bf16[128,3072]{1,0:T(8,128)(2,1)}, bf16[128,3072]{1,0:T(8,128)(2,1)}, u32[]{:S(2)}, u32[]{:S(2)}) collective-permute-start(bf16[128,3072]{1,0:T(8,128)(2,1)} %collective-permute-done.2.refs_2_), channel_id=1, source_target_pairs={{0,4},{1,5},{2,6},{3,7},{4,8},{5,9},{6,10},{7,11},{8,12},{9,13},{1... | collective-permute-start | bytes 2359304 | tf_op jit(solution)/shard_map/ppermute | solution.py:394
  102.2 40.4 %collective-permute-start.6 = (bf16[128,3072]{1,0:T(8,128)(2,1)}, bf16[128,3072]{1,0:T(8,128)(2,1)}, u32[]{:S(2)}, u32[]{:S(2)}) collective-permute-start(bf16[128,3072]{1,0:T(8,128)(2,1)} %collective-permute-done.4.refs_1_.refs_5_), channel_id=1, source_target_pairs={{0,12},{1,13},{2,14},{3,15},{4,0},{5,1},{6,2},{7,3},{8,4},{9,5},{1... | collective-permute-start | bytes 2359304 | tf_op jit(solution)/shard_map/ppermute | solution.py:395
  121.2 30.3 %all-to-all-start.1 = ((bf16[8,256,128]{2,1,0:T(8,128)(2,1)}), bf16[8,256,128]{2,1,0:T(8,128)(2,1)}, u32[]{:S(2)}, u32[]{:S(2)}) async-start(bf16[8,256,128]{2,1,0:T(8,128)(2,1)} %copy-done.7), calls=%async_computation.1 | async-start | bytes 1048576 | tf_op jit(solution)/shard_map/all_to_all | solution.py:380
  129.3 7.1 %collective-permute-start.10 = (bf16[256,128]{1,0:T(8,128)(2,1)S(1)}, bf16[256,128]{1,0:T(8,128)(2,1)S(1)}, u32[]{:S(2)}, u32[]{:S(2)}) collective-permute-start(bf16[256,128]{1,0:T(8,128)(2,1)S(1)} %get-tuple-element.16), channel_id=1, source_target_pairs={{0,4},{1,5},{2,6},{3,7},{4,8},{5,9},{6,10},{7,11},{8,12},{9,13},{1... | collective-permute-start | bytes 196616 | tf_op jit(solution)/shard_map/ppermute | solution.py:372
  136.4 3.1 %collective-permute-start.8 = (bf16[256,128]{1,0:T(8,128)(2,1)S(1)}, bf16[256,128]{1,0:T(8,128)(2,1)S(1)}, u32[]{:S(2)}, u32[]{:S(2)}) collective-permute-start(bf16[256,128]{1,0:T(8,128)(2,1)S(1)} %get-tuple-element.14), channel_id=1, source_target_pairs={{0,2},{1,3},{2,0},{3,1},{4,6},{5,7},{6,4},{7,5},{8,10},{9,11},{10,... | collective-permute-start | bytes 196616 | tf_op jit(solution)/shard_map/ppermute | solution.py:372
  139.5 3.1 %collective-permute-start.9 = (bf16[256,128]{1,0:T(8,128)(2,1)S(1)}, bf16[256,128]{1,0:T(8,128)(2,1)S(1)}, u32[]{:S(2)}, u32[]{:S(2)}) collective-permute-start(bf16[256,128]{1,0:T(8,128)(2,1)S(1)} %get-tuple-element.15), channel_id=1, source_target_pairs={{0,12},{1,13},{2,14},{3,15},{4,0},{5,1},{6,2},{7,3},{8,4},{9,5},{1... | collective-permute-start | bytes 196616 | tf_op jit(solution)/shard_map/ppermute | solution.py:372
  146.4 5.1 %collective-permute-start.11 = (bf16[256,128]{1,0:T(8,128)(2,1)}, bf16[256,128]{1,0:T(8,128)(2,1)S(1)}, u32[]{:S(2)}, u32[]{:S(2)}) collective-permute-start(bf16[256,128]{1,0:T(8,128)(2,1)} %get-tuple-element.17), channel_id=1, source_target_pairs={{0,14},{1,15},{2,12},{3,13},{4,2},{5,3},{6,0},{7,1},{8,6},{9,7},{1... | collective-permute-start | bytes 196616 | tf_op jit(solution)/shard_map/ppermute | solution.py:372
  148.4 16.3 %collective-permute-start.15 = (bf16[256,128]{1,0:T(8,128)(2,1)}, bf16[256,128]{1,0:T(8,128)(2,1)S(1)}, u32[]{:S(2)}, u32[]{:S(2)}) collective-permute-start(bf16[256,128]{1,0:T(8,128)(2,1)} %get-tuple-element.20), channel_id=1, source_target_pairs={{0,6},{1,7},{2,4},{3,5},{4,10},{5,11},{6,8},{7,9},{8,14},{9,15},{1... | collective-permute-start | bytes 196616 | tf_op jit(solution)/shard_map/ppermute | solution.py:372
  148.8 15.9 %collective-permute-start.16 = (bf16[256,128]{1,0:T(8,128)(2,1)S(1)}, bf16[256,128]{1,0:T(8,128)(2,1)S(1)}, u32[]{:S(2)}, u32[]{:S(2)}) collective-permute-start(bf16[256,128]{1,0:T(8,128)(2,1)S(1)} %get-tuple-element.21), channel_id=1, source_target_pairs={{0,8},{1,9},{2,10},{3,11},{4,12},{5,13},{6,14},{7,15},{8,0},{9,1},... | collective-permute-start | bytes 196616 | tf_op jit(solution)/shard_map/ppermute | solution.py:372
  149.6 15.1 %collective-permute-start.17 = (bf16[256,128]{1,0:T(8,128)(2,1)S(1)}, bf16[256,128]{1,0:T(8,128)(2,1)S(1)}, u32[]{:S(2)}, u32[]{:S(2)}) collective-permute-start(bf16[256,128]{1,0:T(8,128)(2,1)S(1)} %get-tuple-element.22), channel_id=1, source_target_pairs={{0,10},{1,11},{2,8},{3,9},{4,14},{5,15},{6,12},{7,13},{8,2},{9,3},... | collective-permute-start | bytes 196616 | tf_op jit(solution)/shard_map/ppermute | solution.py:372
  159.2 32.3 %collective-permute-start.13 = (f32[128,3072]{1,0:T(8,128)}, f32[128,3072]{1,0:T(8,128)}, u32[]{:S(2)}, u32[]{:S(2)}) collective-permute-start(f32[128,3072]{1,0:T(8,128)} %get-tuple-element.19), channel_id=1, source_target_pairs={{0,1},{1,0},{2,3},{3,2},{4,5},{5,4},{6,7},{7,6},{8,9},{9,8},{10,11... | collective-permute-start | bytes 4718600 | tf_op jit(solution)/shard_map/ppermute | solution.py:418
  186.5 5.0 %copy-start.19 = (bf16[128,3072]{1,0:T(8,128)(2,1)S(1)}, bf16[128,3072]{1,0:T(8,128)(2,1)}, u32[]{:S(2)}) copy-start(bf16[128,3072]{1,0:T(8,128)(2,1)} %param.18) | copy-start | bytes 2359300
  186.5 5.0 %copy-start.20 = (bf16[1,128,3072]{2,1,0:T(8,128)(2,1)S(1)}, bf16[1,128,3072]{2,1,0:T(8,128)(2,1)}, u32[]{:S(2)}) copy-start(bf16[1,128,3072]{2,1,0:T(8,128)(2,1)} %param.10) | copy-start | bytes 2359300
  186.5 26.4 %all-to-all-start.3 = ((bf16[16,384,128]{2,1,0:T(8,128)(2,1)}), bf16[16,384,128]{2,1,0:T(8,128)(2,1)}, u32[]{:S(2)}, u32[]{:S(2)}) async-start(bf16[16,384,128]{2,1,0:T(8,128)(2,1)} %copy-done.10), calls=%async_computation.3 | async-start | bytes 3145728 | tf_op jit(solution)/shard_map/all_to_all | solution.py:376
  194.8 31.0 %collective-permute-start.14 = (bf16[128,3072]{1,0:T(8,128)(2,1)}, bf16[128,3072]{1,0:T(8,128)(2,1)S(1)}, u32[]{:S(2)}, u32[]{:S(2)}) collective-permute-start(bf16[128,3072]{1,0:T(8,128)(2,1)} %fusion.1), channel_id=1, source_target_pairs={{0,16},{16,32},{32,48},{48,64},{64,80},{80,96},{96,112},{112,128},... | collective-permute-start | bytes 2359304 | tf_op jit(solution)/shard_map/ppermute | solution.py:360
  (12 other events, 13.6 us)
where the time goes:
time: 230 us; the launch traced here: 229 us
  waiting for transfers between devices  96.1 us (42%)
  starting transfers between devices  54.8 us (24%)
  Pallas kernels  51.8 us (23%)
  local copies, waits for them, and re-layouts  20.5 us (9%)
  other arithmetic  4.71 us (2%)
    ppermute x1, waiting for transfers between devices, body(): right = lax.ppermute(own, 'seq', XDOWN)  31.6 us
    ppermute x1, waiting for transfers between devices, body(): y_right = lax.ppermute(y_own, 'seq', XDOWN)  24.7 us
    pallas_call x1, Pallas kernels, attention_backward(): pl.pallas_call(backward_kernel, out_shape=jax.ShapeDtypeStruct((blocks, 3...  20.6 us
    all_to_all x3, starting transfers between devices, exchange(): return lax.all_to_all(array, 'seq', 0, 0, tiled=True)  18.5 us
    unnamed x46, local copies, waits for them, and re-layouts  18.3 us
    all_to_all x3, waiting for transfers between devices, exchange(): return lax.all_to_all(array, 'seq', 0, 0, tiled=True)  18.1 us
    pallas_call x1, Pallas kernels, attention_forward(): pl.pallas_call(forward_kernel, out_shape=jax.ShapeDtypeStruct((total // Q...  13.2 us
    ppermute x7, waiting for transfers between devices, to_chip(): return lax.ppermute(array, 'seq', pairs)  11.8 us
  transfers between devices with their start and end apart: 22, of which 7 were waited for; matrix products, arithmetic and copies ran while one was open for 3% of the time, Pallas kernels for 23%

commit v1 on v0

--- a/solution.py
+++ b/solution.py
@@ -38,6 +38,15 @@
     return [pl.BlockSpec(memory_space=pl.ANY)] * len(arrays)
 
 
+def in_hbm(count):
+    return [pl.BlockSpec(memory_space=pltpu.HBM)] * count
+
+
+def batch_rows(packed, batch):
+    heads, height = packed.shape[0], packed.shape[1] // 2
+    return pl.BlockSpec((heads, height, HD), lambda i: (0, batch, 0))
+
+
 def cost(microseconds):
     return pl.CostEstimate(
         flops=int(microseconds * 1e9), bytes_accessed=0, transcendentals=0
@@ -48,33 +57,69 @@
     return lax.dot_general(a, b, (dims, ((), ())), preferred_element_type=F32)
 
 
-def pack_kernel(seg_ref, q_ref, k_ref, v_ref, *refs):
-    out_ref = refs[-1]
-    rows = q_ref.shape[0]
-    for h in range(out_ref.shape[0]):
-        cols = slice(h * HD, (h + 1) * HD)
-        out_ref[h, 0:rows, :] = q_ref[:, cols]
-        out_ref[h, rows:2 * rows, :] = k_ref[:, cols]
-        out_ref[h, 2 * rows:3 * rows, :] = v_ref[:, cols]
-        out_ref[h, 3 * rows:, :] = jnp.broadcast_to(
-            seg_ref[...].astype(F32), (SEG_ROWS, HD)
-        ).astype(BF16)
-
-
-def pack(queries, keys, values, segments, batch, *later):
-    rows, width = queries.shape[2], queries.shape[3]
+def pack_kernel(seg_ref, q_ref, k_ref, v_ref, out_ref, ids_s, sems):
+    batches, rows = q_ref.shape[1], q_ref.shape[2]
+    heads = out_ref.shape[0]
+    height = 3 * rows + SEG_ROWS
+    for b in range(batches):
+        ids = jnp.broadcast_to(seg_ref[b:b + 1, :].astype(F32), (SEG_ROWS, HD)).astype(BF16)
+        for h in range(heads):
+            ids_s[b, h] = ids
+    for b in range(batches):
+        for a, ref in enumerate((q_ref, k_ref, v_ref)):
+            for h in range(heads):
+                pltpu.make_async_copy(
+                    ref.at[0, b, :, h * HD:(h + 1) * HD],
+                    out_ref.at[h, b * height + a * rows:b * height + (a + 1) * rows, :],
+                    sems.at[b * 4 + a],
+                ).start()
+        pltpu.make_async_copy(
+            ids_s.at[b],
+            out_ref.at[:, b * height + 3 * rows:(b + 1) * height, :],
+            sems.at[b * 4 + 3],
+        ).start()
+    for b in range(batches):
+        for a in range(3):
+            done = out_ref.at[:, b * height + a * rows:b * height + (a + 1) * rows, :]
+            pltpu.make_async_copy(done, done, sems.at[b * 4 + a]).wait()
+        done = out_ref.at[:, b * height + 3 * rows:(b + 1) * height, :]
+        pltpu.make_async_copy(ids_s.at[b], done, sems.at[b * 4 + 3]).wait()
+
+
+def pack(queries, keys, values, segments):
+    batches, rows, width = queries.shape[1:]
     heads = width // HD
-    block = pl.BlockSpec((None, None, rows, width), lambda i: (0, batch, 0, 0))
+    height = 3 * rows + SEG_ROWS
     return pl.pallas_call(
         pack_kernel,
-        grid=(1,),
-        out_shape=jax.ShapeDtypeStruct((heads, 3 * rows + SEG_ROWS, HD), BF16),
-        in_specs=[pl.BlockSpec((1, rows), lambda i: (0, 0)), block, block, block] + anywhere(later),
-        out_specs=pl.BlockSpec((heads, 3 * rows + SEG_ROWS, HD), lambda i: (0, 0, 0)),
-        compiler_params=params(24),
+        out_shape=jax.ShapeDtypeStruct((heads, batches * height, HD), BF16),
+        in_specs=whole(1) + in_hbm(3),
+        out_specs=in_hbm(1)[0],
+        scratch_shapes=[
+            pltpu.VMEM((batches, heads, SEG_ROWS, HD), BF16),
+            pltpu.SemaphoreType.DMA((4 * batches,)),
+        ],
+        compiler_params=params(60),
         cost_estimate=cost(2),
         name="pack",
-    )(segments[0, batch][None], queries, keys, values, *later)
+    )(segments[0], queries, keys, values)
+
+
+def follow_kernel(array_ref, *refs):
+    pass
+
+
+def follow(array, *later):
+    return pl.pallas_call(
+        follow_kernel,
+        out_shape=jax.ShapeDtypeStruct(array.shape, array.dtype),
+        in_specs=anywhere((array,) + later),
+        out_specs=pl.BlockSpec(memory_space=pl.ANY),
+        input_output_aliases={0: 0},
+        compiler_params=params(1),
+        cost_estimate=cost(0.01),
+        name="follow",
+    )(array, *later)
 
 
 def sample_starts(in_ref, rows):
@@ -152,7 +197,8 @@
     return pl.pallas_call(
         forward_kernel,
         out_shape=jax.ShapeDtypeStruct((total // QB, QB, HD), BF16),
-        in_specs=whole(1) + anywhere(later),
+        grid=(1,),
+        in_specs=[batch_rows(packed, 0)] + anywhere(later),
         out_specs=whole(1)[0],
         scratch_shapes=[pltpu.VMEM((HD, total), BF16), pltpu.VMEM((total, HD), F32)],
         compiler_params=params(24),
@@ -170,10 +216,14 @@
 
 
 def backward_kernel(place_ref, in_ref, *refs):
-    g_refs, (out_ref, g_ref, kt_s, seg_s, s_s, dp_s, dk_s, dv_s) = refs[:CHIPS], refs[-8:]
+    g_refs = refs[:CHIPS]
+    out_ref, g_ref, out_s, kt_s, seg_s, s_s, dp_s, dk_s, dv_s, in_sems, out_sem = refs[-11:]
     blocks, rows = in_ref.shape[0], 128
-    for offset, ref in zip(OFFSETS, g_refs):
-        g_ref[chip_at(place_ref[0], (-offset[0] % XN, offset[1]))] = ref[...]
+    arriving = []
+    for n, (offset, ref) in enumerate(zip(OFFSETS, g_refs)):
+        chip = chip_at(place_ref[0], (-offset[0] % XN, offset[1]))
+        arriving.append(pltpu.make_async_copy(ref, g_ref.at[chip], in_sems.at[n]))
+        arriving[-1].start()
     total = blocks * rows
     starts = sample_starts(in_ref, rows)
     fill_samples(seg_s, starts)
@@ -181,6 +231,8 @@
         kt_s[:, i * rows:(i + 1) * rows] = in_ref[i, rows:2 * rows, :].T
     dk_s[...] = jnp.zeros_like(dk_s)
     dv_s[...] = jnp.zeros_like(dv_s)
+    for copy in arriving:
+        copy.wait()
 
     def per_block(i, _):
         q = block_rows(in_ref, i, QB, 0, rows)
@@ -221,14 +273,16 @@
         acc = lax.fori_loop(begin, end, grads, jnp.zeros((HD, QB), F32))
         dq = (acc * SCALE).T.astype(BF16)
         per = QB // rows
-        out_ref[pl.ds(i * per, per), 0:rows, :] = dq.reshape(per, rows, HD)
+        out_s[pl.ds(i * per, per), 0:rows, :] = dq.reshape(per, rows, HD)
         return 0
 
     lax.fori_loop(0, total // QB, per_block, 0)
     for i in range(blocks):
         here = slice(i * rows, (i + 1) * rows)
-        out_ref[i, rows:2 * rows, :] = (dk_s[here, :] * SCALE).astype(BF16)
-        out_ref[i, 2 * rows:3 * rows, :] = dv_s[here, :].astype(BF16)
+        out_s[i, rows:2 * rows, :] = (dk_s[here, :] * SCALE).astype(BF16)
+        out_s[i, 2 * rows:3 * rows, :] = dv_s[here, :].astype(BF16)
+        pltpu.make_async_copy(out_s.at[i], out_ref.at[i], out_sem).start()
+    pltpu.make_async_copy(out_s, out_ref, out_sem).wait()
 
 
 def attention_backward(place, packed, grads, *later):
@@ -237,18 +291,24 @@
     return pl.pallas_call(
         backward_kernel,
         out_shape=jax.ShapeDtypeStruct((blocks, 3 * 128, HD), BF16),
-        in_specs=[pl.BlockSpec(memory_space=pltpu.SMEM)] + whole(1 + CHIPS) + anywhere(later),
-        out_specs=whole(1)[0],
+        grid=(1,),
+        in_specs=[pl.BlockSpec(memory_space=pltpu.SMEM), batch_rows(packed, 1)]
+        + in_hbm(CHIPS)
+        + anywhere(later),
+        out_specs=in_hbm(1)[0],
         scratch_shapes=[
             pltpu.VMEM((total // QB, QB, HD), BF16),
+            pltpu.VMEM((blocks, 3 * 128, HD), BF16),
             pltpu.VMEM((HD, total), BF16),
             pltpu.VMEM((total, HD), F32),
             pltpu.VMEM((total, QB), F32),
             pltpu.VMEM((total, QB), F32),
             pltpu.VMEM((total, HD), F32),
             pltpu.VMEM((total, HD), F32),
+            pltpu.SemaphoreType.DMA((CHIPS,)),
+            pltpu.SemaphoreType.DMA,
         ],
-        compiler_params=params(32),
+        compiler_params=params(60),
         cost_estimate=cost(30),
         name="attention_backward",
     )(place, packed, *grads, *later)
@@ -355,6 +415,22 @@
     )(sections, first, second, *later)
 
 
+def settle_kernel(in_ref, out_ref):
+    out_ref[...] = in_ref[...]
+
+
+def settle(array):
+    return pl.pallas_call(
+        settle_kernel,
+        out_shape=jax.ShapeDtypeStruct(array.shape, array.dtype),
+        in_specs=whole(1),
+        out_specs=whole(1)[0],
+        compiler_params=params(8),
+        cost_estimate=cost(0.2),
+        name="settle",
+    )(array)
+
+
 def rotated(array, axis, by):
     length = lax.axis_size(axis)
     return lax.ppermute(array, axis, [(i, (i + by) % length) for i in range(length)])
@@ -384,6 +460,8 @@
     section = lax.axis_index("pipe")
     last_section = lax.axis_size("pipe") - 1
     place = lax.axis_index("seq")[None]
+
+    packed = exchange(pack(queries, keys, values, segments))
 
     own = out_weight[0]
     y_own = lax.ppermute(own, "seq", YSWAP)
@@ -392,35 +470,37 @@
     y_left = lax.ppermute(y_own, "seq", XUP)
     y_right = lax.ppermute(y_own, "seq", XDOWN)
     far = lax.ppermute(left, "seq", XUP)
-    y_far = lax.ppermute(y_right, "seq", XDOWN)
-    pieces = (own, y_own, left, right, y_left, y_right, far, y_far)
 
     local_seg = segments[0]
+    gate_tok = per_sample(local_seg[0], gates[0, 0])
     g_scaled = (per_sample(local_seg[1], gates[0, 1]) * upstream[0].astype(F32)).astype(BF16)
     g_other = lax.ppermute(g_scaled, "seq", CORE)
-
-    gate_tok = per_sample(local_seg[0], gates[0, 0])
-    fwd = exchange(pack(queries, keys, values, segments, 0))
-    packed = pack(queries, keys, values, segments, 1, fwd, right)
-    bwd = exchange(packed)
+    near = attention_grad(place, g_scaled, g_other, (own, y_own, left, right))
+    near = tuple(to_chip(g, o) for g, o in zip(near, OFFSETS[:4]))
 
     sections = jnp.stack([section, jnp.zeros_like(section)])
     turned = choose(sections, loss_grad, upstream[0], y_own)
     next_grad = rotated(turned, "pipe", -1)
 
-    attn = exchange_same_core(attention_forward(fwd, packed, turned, gate_tok))
-    near = attention_grad(place, g_scaled, g_other, pieces[:4])
-    near = tuple(to_chip(g, o) for g, o in zip(near, OFFSETS[:4]))
-    distant = attention_grad(place, g_scaled, g_other, pieces[4:], bwd, *near)
+    heads = attention_forward(packed, turned, gate_tok)
+    attn = exchange_same_core(heads)
+
+    y_right = follow(y_right, heads, *near, y_left, far)
+    y_far = lax.ppermute(y_right, "seq", XDOWN)
+    pieces = (own, y_own, left, right, y_left, y_right, far, y_far)
+    next_grad = settle(next_grad)
+    distant = attention_grad(place, g_scaled, g_other, pieces[4:], next_grad)
     distant = tuple(to_chip(g, o) for g, o in zip(distant, OFFSETS[4:]))
-    part, part_other = project(place, attn, pieces, distant[0], next_grad)
-    grads = attention_backward(place, bwd, near + distant)
-    proj = part + lax.ppermute(part_other, "seq", CORE)
-    section_out = (hidden_in[0].astype(F32) + gate_tok * proj).astype(BF16)
-    next_act = rotated(jnp.where(section == last_section, fresh, section_out), "pipe", 1)[None]
-
-    qkv_grads = unpack(exchange(grads))[None]
-    return (next_act, next_grad[None], qkv_grads)
+    part, part_other = project(place, attn, pieces)
+    part_other = lax.ppermute(follow(part_other, *distant), "seq", CORE)
+    grads = attention_backward(place, packed, near + distant)
+
+    section_out = (hidden_in[0].astype(F32) + gate_tok * (part + part_other)).astype(BF16)
+    section_out = jnp.where(section == last_section, fresh, section_out)
+    next_act = rotated(section_out, "pipe", 1)
+
+    qkv_grads = unpack(exchange(grads))
+    return (next_act[None], next_grad[None], qkv_grads[None])
 
 
 def solution(mesh):

time: 230 us -> 313 us (1.36)
  Pallas kernels: 51.8 us -> 148 us
  local copies, waits for them, and re-layouts: 20.5 us -> 4.38 us
    pallas_call x2 -> x4, Pallas kernels: 1.72 us -> 99.2 us  [the longest x1 97.2 us: pack(): pl.pallas_call(pack_kernel, out_shape=jax.ShapeDtypeStruct((heads, batche...]
    ppermute x1, waiting for transfers between devices: 24.7 us -> 0.01 us  [body(): y_right = lax.ppermute(y_own, 'seq', XDOWN)]
    ppermute x1, waiting for transfers between devices: 31.6 us -> 47.5 us  [body(): right = lax.ppermute(own, 'seq', XDOWN)]
    unnamed x46 -> x37, local copies, waits for them, and re-layouts: 18.3 us -> 4.37 us
    ppermute x1, waiting for transfers between devices: 0.01 us -> 12.4 us  [body(): y_far = lax.ppermute(y_right, 'seq', XDOWN)]
    ppermute x7, starting transfers between devices: 6.63 us -> 14.6 us  [to_chip(): return lax.ppermute(array, 'seq', pairs)]
    all_to_all x3 -> x2, starting transfers between devices: 18.5 us -> 11.7 us  [exchange(): return lax.all_to_all(array, 'seq', 0, 0, tiled=True)]
    ppermute x7, waiting for transfers between devices: 11.8 us -> 6.32 us  [to_chip(): return lax.ppermute(array, 'seq', pairs)]
  transfers between devices with their start and end apart: 22 -> 21, of which waited for: 7 -> 5; matrix products, arithmetic and copies ran while one was open for 3% -> 2% of each run, Pallas kernels for 23% -> 47%
where the time goes in v1:
time: 313 us; the launch traced here: 311 us
  Pallas kernels  148 us (47%)
  waiting for transfers between devices  95.7 us (31%)
  starting transfers between devices  57.8 us (18%)
  other arithmetic  4.66 us (1%)
  local copies, waits for them, and re-layouts  4.38 us (1%)
    pallas_call x1, Pallas kernels, pack(): pl.pallas_call(pack_kernel, out_shape=jax.ShapeDtypeStruct((heads, batche...  97.2 us
    ppermute x1, waiting for transfers between devices, body(): right = lax.ppermute(own, 'seq', XDOWN)  47.5 us
    pallas_call x1, Pallas kernels, attention_backward(): pl.pallas_call(backward_kernel, out_shape=jax.ShapeDtypeStruct((blocks, 3...  20.8 us
    all_to_all x2, waiting for transfers between devices, exchange(): return lax.all_to_all(array, 'seq', 0, 0, tiled=True)  18.1 us
    ppermute x7, starting transfers between devices, to_chip(): return lax.ppermute(array, 'seq', pairs)  14.6 us
    ppermute x1, waiting for transfers between devices, body(): y_far = lax.ppermute(y_right, 'seq', XDOWN)  12.4 us
    all_to_all x2, starting transfers between devices, exchange(): return lax.all_to_all(array, 'seq', 0, 0, tiled=True)  11.7 us
    ppermute x2, waiting for transfers between devices, rotated(): lax.ppermute(array, axis, [(i, (i + by) % length) for i in range(length)])  11.3 us
  transfers between devices with their start and end apart: 21, of which 5 were waited for; matrix products, arithmetic and copies ran while one was open for 2% of the time, Pallas kernels for 47%

profile of v1, /device:TPU:1, one launch (start us, length us, event | category | flops | bytes accessed | tf_op | source)
XLA Modules:
  0.0 311.1 jit_solution(8681945584709136623)
XLA Ops:
  0.6 2.2 collective-permute-start
  2.8 1.2 collective-permute-start.1
  4.1 97.2 %pack.1 = bf16[16,800,128]{2,1,0:T(8,128)(2,1)} custom-call(s32[2,128]{1,0:T(2,128)} %bitcast.23, bf16[1,2,128,2048]{3,2,1,0:T(8,128)(2,1)} %q_ref.1, bf16[1,2,128,2048]{3,2,1,0:T(8,128)(2,1)} %k_ref.1, bf16[1,2,128,2048]{3,2,1,0:T(8,128)(2,1)} %v_ref.1), custom_call_target="tpu_custom_call" | custom-call | flops 2000000000 | tf_op jit(solution)/shard_map/pack/pallas_call | solution.py:93
  101.2 6.0 %all-to-all-start = ((bf16[16,800,128]{2,1,0:T(8,128)(2,1)}), bf16[16,800,128]{2,1,0:T(8,128)(2,1)}, u32[]{:S(2)}, u32[]{:S(2)}) async-start(bf16[16,800,128]{2,1,0:T(8,128)(2,1)} %pack.1), calls=%async_computation | async-start | bytes 6553600 | tf_op jit(solution)/shard_map/all_to_all | solution.py:452
  108.8 2.8 collective-permute-start.2
  111.6 2.7 collective-permute-start.4
  114.9 47.5 %collective-permute-done.2.refs_3_ = bf16[128,3072]{1,0:T(8,128)(2,1)} collective-permute-done((bf16[128,3072]{1,0:T(8,128)(2,1)}, bf16[128,3072]{1,0:T(8,128)(2,1)}, u32[]{:S(2)}, u32[]{:S(2)}) %collective-permute-start.2) | collective-permute-done | bytes 786464 | tf_op jit(solution)/shard_map/ppermute | solution.py:469
  162.4 3.2 %attention_grad.2 = (bf16[256,128]{1,0:T(8,128)(2,1)S(1)}, bf16[256,128]{1,0:T(8,128)(2,1)S(1)}, bf16[256,128]{1,0:T(8,128)(2,1)S(1)}, bf16[256,128]{1,0:T(8,128)(2,1)S(1)}) custom-call(s32[1]{0:T(128)} %bitcast.3.place_ref, bf16[128,3072]{1,0:T(8,128)(2,1)S(1)} %multiply_convert_fusion.own_ref, bf16[128,3072]{1,0:T(8,128)(2,1)} %collective-permute-done.5.other_ref, ...), custom_call_target="tpu_custom_call" | custom-call | flops 200000000 | tf_op jit(solution)/shard_map/attention_grad/pallas_call | solution.py:333
  165.7 2.3 collective-permute-start.6
  168.0 4.8 %collective-permute-start.7 = (bf16[256,128]{1,0:T(8,128)(2,1)S(1)}, bf16[256,128]{1,0:T(8,128)(2,1)S(1)}, u32[]{:S(2)}, u32[]{:S(2)}) collective-permute-start(bf16[256,128]{1,0:T(8,128)(2,1)S(1)} %get-tuple-element.15), channel_id=1, source_target_pairs={{0,12},{1,13},{2,14},{3,15},{4,0},{5,1},{6,2},{7,3},{8,4},{9,5},{1... | collective-permute-start | bytes 196616 | tf_op jit(solution)/shard_map/ppermute | solution.py:448
  172.9 1.5 choose.1.refs_0_
  174.4 6.3 %collective-permute-done.7.refs_3_.refs_2_ = bf16[256,128]{1,0:T(8,128)(2,1)S(1)} collective-permute-done((bf16[256,128]{1,0:T(8,128)(2,1)S(1)}, bf16[256,128]{1,0:T(8,128)(2,1)S(1)}, u32[]{:S(2)}, u32[]{:S(2)}) %collective-permute-start.7) | collective-permute-done | bytes 65568 | tf_op jit(solution)/shard_map/ppermute | solution.py:448
  180.7 7.5 %collective-permute-start.11 = (bf16[128,3072]{1,0:T(8,128)(2,1)}, bf16[128,3072]{1,0:T(8,128)(2,1)}, u32[]{:S(2)}, u32[]{:S(2)}) collective-permute-start(bf16[128,3072]{1,0:T(8,128)(2,1)} %choose.1.refs_0_), channel_id=1, source_target_pairs={{0,240},{16,0},{32,16},{48,32},{64,48},{80,64},{96,80},{112,96},{1... | collective-permute-start | bytes 2359304 | tf_op jit(solution)/shard_map/ppermute | solution.py:436
  188.2 11.3 %attention_forward.1.refs_0_ = bf16[8,256,128]{2,1,0:T(8,128)(2,1)S(1)} custom-call(bf16[16,800,128]{2,1,0:T(8,128)(2,1)} %all-to-all-done.in_ref, bf16[128,3072]{1,0:T(8,128)(2,1)} %choose.1.refs_0_, f32[128,3072]{1,0:T(8,128)S(1)} %multiply_reduce_fusion.1.refs_1_), custom_call_target="tpu_custom_call" | custom-call | flops 200000000 | tf_op jit(solution)/shard_map/attention_forward/pallas_call | solution.py:197
  200.3 6.3 %collective-permute-start.10 = (bf16[128,3072]{1,0:T(8,128)(2,1)}, bf16[128,3072]{1,0:T(8,128)(2,1)}, u32[]{:S(2)}, u32[]{:S(2)}) collective-permute-start(bf16[128,3072]{1,0:T(8,128)(2,1)} %follow.2.refs_5_.refs_1_), channel_id=1, source_target_pairs={{0,12},{1,13},{2,14},{3,15},{4,0},{5,1},{6,2},{7,3},{8,4},{9,5},{1... | collective-permute-start | bytes 2359304 | tf_op jit(solution)/shard_map/ppermute | solution.py:489
  206.6 4.1 %all-to-all-start.1 = ((bf16[8,256,128]{2,1,0:T(8,128)(2,1)}), bf16[8,256,128]{2,1,0:T(8,128)(2,1)}, u32[]{:S(2)}, u32[]{:S(2)}) async-start(bf16[8,256,128]{2,1,0:T(8,128)(2,1)} %copy-done), calls=%async_computation.1 | async-start | bytes 1048576 | tf_op jit(solution)/shard_map/all_to_all | solution.py:456
  210.8 2.1 settle.1.refs_4_
  212.8 12.4 %collective-permute-done.10.refs_7_.refs_3_ = bf16[128,3072]{1,0:T(8,128)(2,1)} collective-permute-done((bf16[128,3072]{1,0:T(8,128)(2,1)}, bf16[128,3072]{1,0:T(8,128)(2,1)}, u32[]{:S(2)}, u32[]{:S(2)}) %collective-permute-start.10) | collective-permute-done | bytes 786464 | tf_op jit(solution)/shard_map/ppermute | solution.py:489
  225.3 1.1 copy-done.1
  226.4 2.9 attention_grad.3
  229.4 2.4 collective-permute-start.13
  231.7 1.5 collective-permute-start.14
  233.2 3.6 %collective-permute-start.15 = (bf16[256,128]{1,0:T(8,128)(2,1)S(1)}, bf16[256,128]{1,0:T(8,128)(2,1)S(1)}, u32[]{:S(2)}, u32[]{:S(2)}) collective-permute-start(bf16[256,128]{1,0:T(8,128)(2,1)S(1)} %get-tuple-element.22), channel_id=1, source_target_pairs={{0,10},{1,11},{2,8},{3,9},{4,14},{5,15},{6,12},{7,13},{8,2},{9,3},... | collective-permute-start | bytes 196616 | tf_op jit(solution)/shard_map/ppermute | solution.py:448
  236.8 5.7 %project.1 = (f32[128,3072]{1,0:T(8,128)S(1)}, f32[128,3072]{1,0:T(8,128)}) custom-call(s32[1]{0:T(128)} %bitcast.3.place_ref, bf16[8,256,128]{2,1,0:T(8,128)(2,1)} %all-to-all-done.1.attn_ref, bf16[128,3072]{1,0:T(8,128)(2,1)} %bitcast.7.refs_0_, bf16[128,3072]{1,0:T(8,128)(2,1)} %collective-permute-done.refs_0_.refs_1_, ...), custom_call_target="tpu_custom_call" | custom-call | flops 200000000 | tf_op jit(solution)/shard_map/project/pallas_call | solution.py:366
  242.5 1.1 copy-done.2
  243.6 4.4 %collective-permute-start.16 = (f32[128,3072]{1,0:T(8,128)}, f32[128,3072]{1,0:T(8,128)}, u32[]{:S(2)}, u32[]{:S(2)}) collective-permute-start(f32[128,3072]{1,0:T(8,128)} %follow.3), channel_id=1, source_target_pairs={{0,1},{1,0},{2,3},{3,2},{4,5},{5,4},{6,7},{7,6},{8,9},{9,8},{10,11... | collective-permute-start | bytes 4718600 | tf_op jit(solution)/shard_map/ppermute | solution.py:495
  248.0 20.8 %attention_backward.1 = bf16[16,384,128]{2,1,0:T(8,128)(2,1)} custom-call(s32[1]{0:T(128)} %bitcast.3.place_ref, bf16[16,800,128]{2,1,0:T(8,128)(2,1)} %all-to-all-done.in_ref, bf16[256,128]{1,0:T(8,128)(2,1)} %copy-done.5, bf16[256,128]{1,0:T(8,128)(2,1)} %copy-done.6, bf16[256,128]{1,0:T(8,128)(2,1)} %copy-done.7, bf16[256,128]{1,0:T(8,128)(2,1)} %copy-done.8, ...), custom_call_target="tpu_custom_call" | custom-call | flops 30000001024 | tf_op jit(solution)/shard_map/attention_backward/pallas_call | solution.py:291
  268.8 5.7 %all-to-all-start.2 = ((bf16[16,384,128]{2,1,0:T(8,128)(2,1)}), bf16[16,384,128]{2,1,0:T(8,128)(2,1)}, u32[]{:S(2)}, u32[]{:S(2)}) async-start(bf16[16,384,128]{2,1,0:T(8,128)(2,1)} %attention_backward.1), calls=%async_computation.2 | async-start | bytes 3145728 | tf_op jit(solution)/shard_map/all_to_all | solution.py:452
  274.5 3.3 %fusion.1 = bf16[128,3072]{1,0:T(8,128)(2,1)} fusion(bf16[128,3072]{1,0:T(8,128)(2,1)S(1)} %copy-done.14, f32[128,3072]{1,0:T(8,128)S(1)} %multiply_reduce_fusion.1.refs_1_, f32[128,3072]{1,0:T(8,128)} %copy-done.2, f32[128,3072]{1,0:T(8,128)} %collective-permute-done.16, bf16[1,128,3072]{2,1,0:T(8,128)(2,1)S(1)} %copy-done.15, pred[]{:T(512)S(6)} %eq.41), kind=kLoop, calls=%fused_computation.5 | loop fusion | flops 2359296 | bytes 7077889 | tf_op jit(solution)/shard_map/jit(_where)/select_n | solution.py:499
  277.9 18.1 %all-to-all-done.2.in_ref = bf16[16,384,128]{2,1,0:T(8,128)(2,1)} async-done(((bf16[16,384,128]{2,1,0:T(8,128)(2,1)}), bf16[16,384,128]{2,1,0:T(8,128)(2,1)}, u32[]{:S(2)}, u32[]{:S(2)}) %all-to-all-start.2) | async-done | bytes 1572896 | tf_op jit(solution)/shard_map/all_to_all | solution.py:452
  295.9 3.0 unpack.1
  298.9 11.3 %collective-permute-done.17 = bf16[128,3072]{1,0:T(8,128)(2,1)S(1)} collective-permute-done((bf16[128,3072]{1,0:T(8,128)(2,1)}, bf16[128,3072]{1,0:T(8,128)(2,1)S(1)}, u32[]{:S(2)}, u32[]{:S(2)}) %collective-permute-start.17) | collective-permute-done | bytes 786464 | tf_op jit(solution)/shard_map/ppermute | solution.py:436
  (67 shorter events, 4.0 us)
Async XLA Ops:
  0.6 111.0 %collective-permute-start = (bf16[128,3072]{1,0:T(8,128)(2,1)}, bf16[128,3072]{1,0:T(8,128)(2,1)}, u32[]{:S(2)}, u32[]{:S(2)}) collective-permute-start(bf16[128,3072]{1,0:T(8,128)(2,1)} %bitcast.7.refs_0_), channel_id=1, source_target_pairs={{0,2},{1,3},{2,0},{3,1},{4,6},{5,7},{6,4},{7,5},{8,10},{9,11},{10,... | collective-permute-start | bytes 2359304 | tf_op jit(solution)/shard_map/ppermute | solution.py:467
  2.8 111.5 %collective-permute-start.1 = (bf16[128,3072]{1,0:T(8,128)(2,1)}, bf16[128,3072]{1,0:T(8,128)(2,1)}, u32[]{:S(2)}, u32[]{:S(2)}) collective-permute-start(bf16[128,3072]{1,0:T(8,128)(2,1)} %bitcast.7.refs_0_), channel_id=1, source_target_pairs={{0,4},{1,5},{2,6},{3,7},{4,8},{5,9},{6,10},{7,11},{8,12},{9,13},{1... | collective-permute-start | bytes 2359304 | tf_op jit(solution)/shard_map/ppermute | solution.py:468
  101.2 6.1 %copy-start.17 = (s32[1,2,128]{2,1,0:T(2,128)S(1)}, s32[1,2,128]{2,1,0:T(2,128)}, u32[]{:S(2)}) copy-start(s32[1,2,128]{2,1,0:T(2,128)} %param.14) | copy-start | bytes 3076
  101.2 6.1 %copy-start.16 = (f32[1,2,4,3072]{3,2,1,0:T(4,128)S(1)}, f32[1,2,4,3072]{3,2,1,0:T(4,128)}, u32[]{:S(2)}) copy-start(f32[1,2,4,3072]{3,2,1,0:T(4,128)} %param.15) | copy-start | bytes 294916
  101.2 87.0 %all-to-all-start = ((bf16[16,800,128]{2,1,0:T(8,128)(2,1)}), bf16[16,800,128]{2,1,0:T(8,128)(2,1)}, u32[]{:S(2)}, u32[]{:S(2)}) async-start(bf16[16,800,128]{2,1,0:T(8,128)(2,1)} %pack.1), calls=%async_computation | async-start | bytes 6553600 | tf_op jit(solution)/shard_map/all_to_all | solution.py:452
  108.6 6.3 %collective-permute-start.5 = (bf16[128,3072]{1,0:T(8,128)(2,1)S(1)}, bf16[128,3072]{1,0:T(8,128)(2,1)}, u32[]{:S(2)}, u32[]{:S(2)}) collective-permute-start(bf16[128,3072]{1,0:T(8,128)(2,1)S(1)} %multiply_convert_fusion.own_ref), channel_id=1, source_target_pairs={{0,1},{1,0},{2,3},{3,2},{4,5},{5,4},{6,7},{7,6},{8,9},{9,8},{10,11... | collective-permute-start | bytes 2359304 | tf_op jit(solution)/shard_map/ppermute | solution.py:477
  108.8 53.6 %collective-permute-start.2 = (bf16[128,3072]{1,0:T(8,128)(2,1)}, bf16[128,3072]{1,0:T(8,128)(2,1)}, u32[]{:S(2)}, u32[]{:S(2)}) collective-permute-start(bf16[128,3072]{1,0:T(8,128)(2,1)} %bitcast.7.refs_0_), channel_id=1, source_target_pairs={{0,12},{1,13},{2,14},{3,15},{4,0},{5,1},{6,2},{7,3},{8,4},{9,5},{1... | collective-permute-start | bytes 2359304 | tf_op jit(solution)/shard_map/ppermute | solution.py:469
  111.6 87.9 %collective-permute-start.3 = (bf16[128,3072]{1,0:T(8,128)(2,1)}, bf16[128,3072]{1,0:T(8,128)(2,1)S(1)}, u32[]{:S(2)}, u32[]{:S(2)}) collective-permute-start(bf16[128,3072]{1,0:T(8,128)(2,1)} %collective-permute-done.refs_0_.refs_1_), channel_id=1, source_target_pairs={{0,4},{1,5},{2,6},{3,7},{4,8},{5,9},{6,10},{7,11},{8,12},{9,13},{1... | collective-permute-start | bytes 2359304 | tf_op jit(solution)/shard_map/ppermute | solution.py:470
  111.6 87.9 %collective-permute-start.4 = (bf16[128,3072]{1,0:T(8,128)(2,1)}, bf16[128,3072]{1,0:T(8,128)(2,1)}, u32[]{:S(2)}, u32[]{:S(2)}) collective-permute-start(bf16[128,3072]{1,0:T(8,128)(2,1)} %collective-permute-done.refs_0_.refs_1_), channel_id=1, source_target_pairs={{0,12},{1,13},{2,14},{3,15},{4,0},{5,1},{6,2},{7,3},{8,4},{9,5},{1... | collective-permute-start | bytes 2359304 | tf_op jit(solution)/shard_map/ppermute | solution.py:471
  114.3 85.3 %collective-permute-start.9 = (bf16[128,3072]{1,0:T(8,128)(2,1)}, bf16[128,3072]{1,0:T(8,128)(2,1)}, u32[]{:S(2)}, u32[]{:S(2)}) collective-permute-start(bf16[128,3072]{1,0:T(8,128)(2,1)} %collective-permute-done.1.refs_2_), channel_id=1, source_target_pairs={{0,4},{1,5},{2,6},{3,7},{4,8},{5,9},{6,10},{7,11},{8,12},{9,13},{1... | collective-permute-start | bytes 2359304 | tf_op jit(solution)/shard_map/ppermute | solution.py:472
  162.4 10.4 %copy-start.4 = (bf16[1,128,3072]{2,1,0:T(8,128)(2,1)S(1)}, bf16[1,128,3072]{2,1,0:T(8,128)(2,1)}, u32[]{:S(2)}) copy-start(bf16[1,128,3072]{2,1,0:T(8,128)(2,1)} %param.17) | copy-start | bytes 2359300
  162.4 10.4 %copy-start.13 = (bf16[128,3072]{1,0:T(8,128)(2,1)S(1)}, bf16[128,3072]{1,0:T(8,128)(2,1)}, u32[]{:S(2)}) copy-start(bf16[128,3072]{1,0:T(8,128)(2,1)} %first_ref.1) | copy-start | bytes 2359300
  165.7 33.9 %copy-start.5 = (bf16[256,128]{1,0:T(8,128)(2,1)}, bf16[256,128]{1,0:T(8,128)(2,1)S(1)}, u32[]{:S(2)}) copy-start(bf16[256,128]{1,0:T(8,128)(2,1)S(1)} %get-tuple-element.13.refs_1_.refs_0_) | copy-start | bytes 196612
  165.7 7.2 %collective-permute-start.6 = (bf16[256,128]{1,0:T(8,128)(2,1)S(1)}, bf16[256,128]{1,0:T(8,128)(2,1)S(1)}, u32[]{:S(2)}, u32[]{:S(2)}) collective-permute-start(bf16[256,128]{1,0:T(8,128)(2,1)S(1)} %get-tuple-element.14), channel_id=1, source_target_pairs={{0,2},{1,3},{2,0},{3,1},{4,6},{5,7},{6,4},{7,5},{8,10},{9,11},{10,... | collective-permute-start | bytes 196616 | tf_op jit(solution)/shard_map/ppermute | solution.py:448
  168.0 12.7 %collective-permute-start.7 = (bf16[256,128]{1,0:T(8,128)(2,1)S(1)}, bf16[256,128]{1,0:T(8,128)(2,1)S(1)}, u32[]{:S(2)}, u32[]{:S(2)}) collective-permute-start(bf16[256,128]{1,0:T(8,128)(2,1)S(1)} %get-tuple-element.15), channel_id=1, source_target_pairs={{0,12},{1,13},{2,14},{3,15},{4,0},{5,1},{6,2},{7,3},{8,4},{9,5},{1... | collective-permute-start | bytes 196616 | tf_op jit(solution)/shard_map/ppermute | solution.py:448
  172.9 26.7 %copy-start.6 = (bf16[256,128]{1,0:T(8,128)(2,1)}, bf16[256,128]{1,0:T(8,128)(2,1)S(1)}, u32[]{:S(2)}) copy-start(bf16[256,128]{1,0:T(8,128)(2,1)S(1)} %collective-permute-done.6.refs_2_.refs_1_) | copy-start | bytes 196612
  172.9 26.7 %collective-permute-start.8 = (bf16[256,128]{1,0:T(8,128)(2,1)S(1)}, bf16[256,128]{1,0:T(8,128)(2,1)S(1)}, u32[]{:S(2)}, u32[]{:S(2)}) collective-permute-start(bf16[256,128]{1,0:T(8,128)(2,1)S(1)} %get-tuple-element.16), channel_id=1, source_target_pairs={{0,4},{1,5},{2,6},{3,7},{4,8},{5,9},{6,10},{7,11},{8,12},{9,13},{1... | collective-permute-start | bytes 196616 | tf_op jit(solution)/shard_map/ppermute | solution.py:448
  180.7 18.9 %copy-start.7 = (bf16[256,128]{1,0:T(8,128)(2,1)}, bf16[256,128]{1,0:T(8,128)(2,1)S(1)}, u32[]{:S(2)}) copy-start(bf16[256,128]{1,0:T(8,128)(2,1)S(1)} %collective-permute-done.7.refs_3_.refs_2_) | copy-start | bytes 196612
  180.7 30.1 %collective-permute-start.11 = (bf16[128,3072]{1,0:T(8,128)(2,1)}, bf16[128,3072]{1,0:T(8,128)(2,1)}, u32[]{:S(2)}, u32[]{:S(2)}) collective-permute-start(bf16[128,3072]{1,0:T(8,128)(2,1)} %choose.1.refs_0_), channel_id=1, source_target_pairs={{0,240},{16,0},{32,16},{48,32},{64,48},{80,64},{96,80},{112,96},{1... | collective-permute-start | bytes 2359304 | tf_op jit(solution)/shard_map/ppermute | solution.py:436
  200.3 25.0 %collective-permute-start.10 = (bf16[128,3072]{1,0:T(8,128)(2,1)}, bf16[128,3072]{1,0:T(8,128)(2,1)}, u32[]{:S(2)}, u32[]{:S(2)}) collective-permute-start(bf16[128,3072]{1,0:T(8,128)(2,1)} %follow.2.refs_5_.refs_1_), channel_id=1, source_target_pairs={{0,12},{1,13},{2,14},{3,15},{4,0},{5,1},{6,2},{7,3},{8,4},{9,5},{1... | collective-permute-start | bytes 2359304 | tf_op jit(solution)/shard_map/ppermute | solution.py:489
  206.6 30.2 %all-to-all-start.1 = ((bf16[8,256,128]{2,1,0:T(8,128)(2,1)}), bf16[8,256,128]{2,1,0:T(8,128)(2,1)}, u32[]{:S(2)}, u32[]{:S(2)}) async-start(bf16[8,256,128]{2,1,0:T(8,128)(2,1)} %copy-done), calls=%async_computation.1 | async-start | bytes 1048576 | tf_op jit(solution)/shard_map/all_to_all | solution.py:456
  229.3 13.2 %collective-permute-start.12 = (bf16[256,128]{1,0:T(8,128)(2,1)S(1)}, bf16[256,128]{1,0:T(8,128)(2,1)S(1)}, u32[]{:S(2)}, u32[]{:S(2)}) collective-permute-start(bf16[256,128]{1,0:T(8,128)(2,1)S(1)} %get-tuple-element.19), channel_id=1, source_target_pairs={{0,14},{1,15},{2,12},{3,13},{4,2},{5,3},{6,0},{7,1},{8,6},{9,7},{1... | collective-permute-start | bytes 196616 | tf_op jit(solution)/shard_map/ppermute | solution.py:448
  229.4 13.1 %collective-permute-start.13 = (bf16[256,128]{1,0:T(8,128)(2,1)S(1)}, bf16[256,128]{1,0:T(8,128)(2,1)S(1)}, u32[]{:S(2)}, u32[]{:S(2)}) collective-permute-start(bf16[256,128]{1,0:T(8,128)(2,1)S(1)} %get-tuple-element.20), channel_id=1, source_target_pairs={{0,6},{1,7},{2,4},{3,5},{4,10},{5,11},{6,8},{7,9},{8,14},{9,15},{1... | collective-permute-start | bytes 196616 | tf_op jit(solution)/shard_map/ppermute | solution.py:448
  231.7 10.8 %collective-permute-start.14 = (bf16[256,128]{1,0:T(8,128)(2,1)S(1)}, bf16[256,128]{1,0:T(8,128)(2,1)S(1)}, u32[]{:S(2)}, u32[]{:S(2)}) collective-permute-start(bf16[256,128]{1,0:T(8,128)(2,1)S(1)} %get-tuple-element.21), channel_id=1, source_target_pairs={{0,8},{1,9},{2,10},{3,11},{4,12},{5,13},{6,14},{7,15},{8,0},{9,1},... | collective-permute-start | bytes 196616 | tf_op jit(solution)/shard_map/ppermute | solution.py:448
  233.2 9.3 %collective-permute-start.15 = (bf16[256,128]{1,0:T(8,128)(2,1)S(1)}, bf16[256,128]{1,0:T(8,128)(2,1)S(1)}, u32[]{:S(2)}, u32[]{:S(2)}) collective-permute-start(bf16[256,128]{1,0:T(8,128)(2,1)S(1)} %get-tuple-element.22), channel_id=1, source_target_pairs={{0,10},{1,11},{2,8},{3,9},{4,14},{5,15},{6,12},{7,13},{8,2},{9,3},... | collective-permute-start | bytes 196616 | tf_op jit(solution)/shard_map/ppermute | solution.py:448
  242.4 1.2 copy-start.2
  242.5 1.2 copy-start.9
  243.6 30.8 %collective-permute-start.16 = (f32[128,3072]{1,0:T(8,128)}, f32[128,3072]{1,0:T(8,128)}, u32[]{:S(2)}, u32[]{:S(2)}) collective-permute-start(f32[128,3072]{1,0:T(8,128)} %follow.3), channel_id=1, source_target_pairs={{0,1},{1,0},{2,3},{3,2},{4,5},{5,4},{6,7},{7,6},{8,9},{9,8},{10,11... | collective-permute-start | bytes 4718600 | tf_op jit(solution)/shard_map/ppermute | solution.py:495
  268.8 5.7 %copy-start.14 = (bf16[128,3072]{1,0:T(8,128)(2,1)S(1)}, bf16[128,3072]{1,0:T(8,128)(2,1)}, u32[]{:S(2)}) copy-start(bf16[128,3072]{1,0:T(8,128)(2,1)} %param.18) | copy-start | bytes 2359300
  268.8 5.7 %copy-start.15 = (bf16[1,128,3072]{2,1,0:T(8,128)(2,1)S(1)}, bf16[1,128,3072]{2,1,0:T(8,128)(2,1)}, u32[]{:S(2)}) copy-start(bf16[1,128,3072]{2,1,0:T(8,128)(2,1)} %param.10) | copy-start | bytes 2359300
  268.8 27.1 %all-to-all-start.2 = ((bf16[16,384,128]{2,1,0:T(8,128)(2,1)}), bf16[16,384,128]{2,1,0:T(8,128)(2,1)}, u32[]{:S(2)}, u32[]{:S(2)}) async-start(bf16[16,384,128]{2,1,0:T(8,128)(2,1)} %attention_backward.1), calls=%async_computation.2 | async-start | bytes 3145728 | tf_op jit(solution)/shard_map/all_to_all | solution.py:452
  277.8 32.4 %collective-permute-start.17 = (bf16[128,3072]{1,0:T(8,128)(2,1)}, bf16[128,3072]{1,0:T(8,128)(2,1)S(1)}, u32[]{:S(2)}, u32[]{:S(2)}) collective-permute-start(bf16[128,3072]{1,0:T(8,128)(2,1)} %fusion.1), channel_id=1, source_target_pairs={{0,16},{16,32},{32,48},{48,64},{64,80},{80,96},{96,112},{112,128},... | collective-permute-start | bytes 2359304 | tf_op jit(solution)/shard_map/ppermute | solution.py:436
  (7 other events, 7.2 us)

commit v2 on v0

v2 whole, which is shorter than its diff:
```python
import functools

import jax
import jax.numpy as jnp
from jax import lax
from jax.experimental import pallas as pl
from jax.experimental.pallas import tpu as pltpu
from jax.sharding import PartitionSpec as P

HD = 128
SCALE = HD ** (-0.5)
EXP2 = SCALE * 1.4426950408889634
LOW = -1e30
QB = 256
KT = 512
SEG_ROWS = 16
F32 = jnp.float32
BF16 = jnp.bfloat16

XN, PER_X = 4, 4
OFFSETS = (0, 3, 1, 2)
CORE = [(i, i ^ 1) for i in range(XN * PER_X)]
YSWAP = [(i, i ^ 2) for i in range(XN * PER_X)]


def along_x(array, offset):
    if offset == 0:
        return array
    count = XN * PER_X
    return lax.ppermute(array, "seq", [(i, (i + PER_X * offset) % count) for i in range(count)])


def x_at(place_ref, offset):
    return (place_ref[0] // PER_X + offset) % XN


def rows_at(place_ref, bits, rows):
    return pl.ds(pl.multiple_of(((place_ref[0] % PER_X) ^ bits) * rows, rows), rows)


def params(mib):
    return pltpu.CompilerParams(vmem_limit_bytes=mib * 1024 * 1024)


def whole(count):
    return [pl.BlockSpec(memory_space=pltpu.VMEM)] * count


def anywhere(arrays):
    return [pl.BlockSpec(memory_space=pl.ANY)] * len(arrays)


def in_hbm(count):
    return [pl.BlockSpec(memory_space=pltpu.HBM)] * count


def cost(microseconds):
    return pl.CostEstimate(
        flops=int(microseconds * 1e9), bytes_accessed=0, transcendentals=0
    )


def dot(a, b, dims):
    return lax.dot_general(a, b, (dims, ((), ())), preferred_element_type=F32)


def pack_kernel(seg_ref, q_ref, k_ref, v_ref, *refs):
    out_ref = refs[-1]
    rows = q_ref.shape[0]
    ids = jnp.broadcast_to(seg_ref[...].astype(F32), (SEG_ROWS, HD)).astype(BF16)
    for h in range(out_ref.shape[0]):
        cols = slice(h * HD, (h + 1) * HD)
        out_ref[h, 0:rows, :] = q_ref[:, cols]
        out_ref[h, rows:2 * rows, :] = k_ref[:, cols]
        out_ref[h, 2 * rows:3 * rows, :] = v_ref[:, cols]
        out_ref[h, 3 * rows:, :] = ids


def pack(queries, keys, values, segments, batch, *later):
    rows, width = queries.shape[2], queries.shape[3]
    heads = width // HD
    height = 3 * rows + SEG_ROWS
    block = pl.BlockSpec((None, None, rows, width), lambda i: (0, batch, 0, 0))
    return pl.pallas_call(
        pack_kernel,
        grid=(1,),
        out_shape=jax.ShapeDtypeStruct((heads, height, HD), BF16),
        in_specs=[pl.BlockSpec((1, rows), lambda i: (0, 0)), block, block, block]
        + anywhere(later),
        out_specs=pl.BlockSpec((heads, height, HD), lambda i: (0, 0, 0)),
        compiler_params=params(16 if later else 60),
        cost_estimate=cost(2),
        name="pack",
    )(segments[0, batch][None], queries, keys, values, *later)


def follow_kernel(array_ref, *refs):
    pass


def follow(array, *later):
    return pl.pallas_call(
        follow_kernel,
        out_shape=jax.ShapeDtypeStruct(array.shape, array.dtype),
        in_specs=anywhere((array,) + later),
        out_specs=pl.BlockSpec(memory_space=pl.ANY),
        input_output_aliases={0: 0},
        compiler_params=params(1),
        cost_estimate=cost(0.01),
        name="follow",
    )(array, *later)


def sample_starts(in_ref, rows):
    ids = in_ref[:, 3 * rows:, :].astype(F32)
    return [
        jnp.sum(jnp.where(ids < s, 1.0, 0.0)).astype(jnp.int32) // SEG_ROWS for s in (1, 2, 3)
    ]


def sample_of(position, starts):
    return sum(jnp.where(position >= b, 1.0, 0.0) for b in starts)


def tile_range(first, last, starts, total):
    low, high = 0, total
    for b in starts:
        low = jnp.maximum(low, jnp.where(b <= first, b, 0))
        high = jnp.minimum(high, jnp.where(b > last, b, total))
    return low // KT, (high + KT - 1) // KT


def block_rows(ref, index, count, start, rows):
    per = count // rows
    return ref[pl.ds(index * per, per), start:start + rows, :].reshape(count, HD)


def fill_samples(seg_s, starts):
    total = seg_s.shape[0]
    for i in range(total // 256):
        position = i * 256 + lax.broadcasted_iota(jnp.int32, (256, HD), 0)
        seg_s[i * 256:(i + 1) * 256, :] = sample_of(position, starts)


def forward_kernel(place_ref, in_ref, *refs):
    outs, (out_s, vt_s, seg_s) = refs[-3 - XN:-3], refs[-3:]
    blocks, rows = in_ref.shape[0], 128
    total = blocks * rows
    starts = sample_starts(in_ref, rows)
    fill_samples(seg_s, starts)
    for i in range(blocks):
        vt_s[:, i * rows:(i + 1) * rows] = in_ref[i, 2 * rows:3 * rows, :].T

    def per_block(i, _):
        q = block_rows(in_ref, i, QB, 0, rows)
        first = i * QB
        seg_q = sample_of(first + lax.broadcasted_iota(jnp.int32, (1, QB), 1), starts)
        begin, end = tile_range(first, first + QB - 1, starts, total)

        def per_tile(t, carry):
            m, l, acc = carry
            k = block_rows(in_ref, t, KT, rows, rows)
            s = dot(k, q, ((1,), (1,)))
            seg_k = seg_s[pl.ds(pl.multiple_of(t * KT, KT), KT), :]
            s = jnp.where(jnp.concatenate([seg_k, seg_k], axis=1) == seg_q, s, LOW)
            m_new = jnp.maximum(m, jnp.max(s, axis=0, keepdims=True))
            p = jnp.exp2((s - m_new) * EXP2)
            alpha = jnp.exp2((m - m_new) * EXP2)
            l = l * alpha + jnp.sum(p, axis=0, keepdims=True)
            vt = vt_s[:, pl.ds(pl.multiple_of(t * KT, KT), KT)]
            acc = acc * alpha + dot(vt, p.astype(BF16), ((1,), (0,)))
            return m_new, l, acc

        m0 = jnp.full((1, QB), LOW, F32)
        l0 = jnp.zeros((1, QB), F32)
        m, l, acc = lax.fori_loop(begin, end, per_tile, (m0, l0, jnp.zeros((HD, QB), F32)))
        out_s[i] = (acc / l).T.astype(BF16)
        return 0

    lax.fori_loop(0, total // QB, per_block, 0)
    per = total // QB // XN
    for offset, ref in zip(OFFSETS, outs):
        ref[...] = out_s[pl.ds(x_at(place_ref, offset) * per, per)].reshape(per * QB, HD)


def attention_forward(place, packed, *later):
    total = packed.shape[0] * 128
    return pl.pallas_call(
        forward_kernel,
        out_shape=(jax.ShapeDtypeStruct((total // XN, HD), BF16),) * XN,
        in_specs=[pl.BlockSpec(memory_space=pltpu.SMEM)] + whole(1) + anywhere(later),
        out_specs=tuple(whole(XN)),
        scratch_shapes=[
            pltpu.VMEM((total // QB, QB, HD), BF16),
            pltpu.VMEM((HD, total), BF16),
            pltpu.VMEM((total, HD), F32),
        ],
        compiler_params=params(24),
        cost_estimate=cost(0.2),
        name="attention_forward",
    )(place, packed, *later)


def backward_kernel(place_ref, in_ref, *refs):
    g_refs = refs[:XN]
    out_ref, g_ref, out_s, kt_s, seg_s, s_s, dp_s, dk_s, dv_s, in_sems, out_sem = refs[-11:]
    blocks, rows = in_ref.shape[0], 128
    arriving = []
    for n, (offset, ref) in enumerate(zip(OFFSETS, g_refs)):
        source = x_at(place_ref, -offset % XN)
        arriving.append(pltpu.make_async_copy(ref, g_ref.at[source], in_sems.at[n]))
        arriving[-1].start()
    total = blocks * rows
    starts = sample_starts(in_ref, rows)
    fill_samples(seg_s, starts)
    for i in range(blocks):
        kt_s[:, i * rows:(i + 1) * rows] = in_ref[i, rows:2 * rows, :].T
    dk_s[...] = jnp.zeros_like(dk_s)
    dv_s[...] = jnp.zeros_like(dv_s)
    for copy in arriving:
        copy.wait()

    def per_block(i, _):
        q = block_rows(in_ref, i, QB, 0, rows)
        share = total // XN // QB
        g = g_ref[i // share, pl.ds(pl.multiple_of(i % share * QB, QB), QB), :]
        first = i * QB
        seg_q = sample_of(first + lax.broadcasted_iota(jnp.int32, (1, QB), 1), starts)
        begin, end = tile_range(first, first + QB - 1, starts, total)

        def scores(t, carry):
            m, l, d = carry
            here = pl.ds(pl.multiple_of(t * KT, KT), KT)
            s = dot(block_rows(in_ref, t, KT, rows, rows), q, ((1,), (1,)))
            dp = dot(block_rows(in_ref, t, KT, 2 * rows, rows), g, ((1,), (1,)))
            seg_k = seg_s[here, :]
            s = jnp.where(jnp.concatenate([seg_k, seg_k], axis=1) == seg_q, s, LOW)
            s_s[here, :] = s
            dp_s[here, :] = dp
            m_new = jnp.maximum(m, jnp.max(s, axis=0, keepdims=True))
            p = jnp.exp2((s - m_new) * EXP2)
            alpha = jnp.exp2((m - m_new) * EXP2)
            l = l * alpha + jnp.sum(p, axis=0, keepdims=True)
            d = d * alpha + jnp.sum(p * dp, axis=0, keepdims=True)
            return m_new, l, d

        zero = jnp.zeros((1, QB), F32)
        m, l, d = lax.fori_loop(begin, end, scores, (jnp.full((1, QB), LOW, F32), zero, zero))
        inverse = 1.0 / l
        delta = d * inverse

        def grads(t, acc):
            here = pl.ds(pl.multiple_of(t * KT, KT), KT)
            p = jnp.exp2((s_s[here, :] - m) * EXP2) * inverse
            ds = (p * (dp_s[here, :] - delta)).astype(BF16)
            dv_s[here, :] += dot(p.astype(BF16), g, ((1,), (0,)))
            dk_s[here, :] += dot(ds, q, ((1,), (0,)))
            return acc + dot(kt_s[:, here], ds, ((1,), (0,)))

        acc = lax.fori_loop(begin, end, grads, jnp.zeros((HD, QB), F32))
        dq = (acc * SCALE).T.astype(BF16)
        per = QB // rows
        out_s[pl.ds(i * per, per), 0:rows, :] = dq.reshape(per, rows, HD)
        return 0

    lax.fori_loop(0, total // QB, per_block, 0)
    for i in range(blocks):
        here = slice(i * rows, (i + 1) * rows)
        out_s[i, rows:2 * rows, :] = (dk_s[here, :] * SCALE).astype(BF16)
        out_s[i, 2 * rows:3 * rows, :] = dv_s[here, :].astype(BF16)
        pltpu.make_async_copy(out_s.at[i], out_ref.at[i], out_sem).start()
    pltpu.make_async_copy(out_s, out_ref, out_sem).wait()


def attention_backward(place, packed, grads, *later):
    blocks = packed.shape[0]
    total = blocks * 128
    return pl.pallas_call(
        backward_kernel,
        out_shape=jax.ShapeDtypeStruct((blocks, 3 * 128, HD), BF16),
        in_specs=[pl.BlockSpec(memory_space=pltpu.SMEM)]
        + whole(1)
        + in_hbm(XN)
        + anywhere(later),
        out_specs=in_hbm(1)[0],
        scratch_shapes=[
            pltpu.VMEM((XN, total // XN, HD), BF16),
            pltpu.VMEM((blocks, 3 * 128, HD), BF16),
            pltpu.VMEM((HD, total), BF16),
            pltpu.VMEM((total, HD), F32),
            pltpu.VMEM((total, QB), F32),
            pltpu.VMEM((total, QB), F32),
            pltpu.VMEM((total, HD), F32),
            pltpu.VMEM((total, HD), F32),
            pltpu.SemaphoreType.DMA((XN,)),
            pltpu.SemaphoreType.DMA,
        ],
        compiler_params=params(60),
        cost_estimate=cost(30),
        name="attention_backward",
    )(place, packed, *grads, *later)


def grad_kernel(place_ref, *refs):
    grads, pieces, outs, g_s = refs[:PER_X], refs[PER_X:PER_X + XN], refs[-1 - XN:-1], refs[-1]
    rows = grads[0].shape[0]
    for bits, ref in enumerate(grads):
        g_s[rows_at(place_ref, bits, rows), :] = ref[...]
    for j in range(0, XN, 2):
        w = jnp.concatenate([pieces[j][...], pieces[j + 1][...]], axis=0)
        r = dot(g_s[...], w, ((1,), (1,))).astype(BF16)
        outs[j][...] = r[:, :HD]
        outs[j + 1][...] = r[:, HD:]


def attention_grad(place, grads, pieces, *later):
    rows, width = grads[0].shape
    return pl.pallas_call(
        grad_kernel,
        out_shape=(jax.ShapeDtypeStruct((PER_X * rows, HD), BF16),) * XN,
        in_specs=[pl.BlockSpec(memory_space=pltpu.SMEM)] + whole(PER_X + XN) + anywhere(later),
        out_specs=tuple(whole(XN)),
        scratch_shapes=[pltpu.VMEM((PER_X * rows, width), BF16)],
        compiler_params=params(24),
        cost_estimate=cost(0.2),
        name="attention_grad",
    )(place, *grads, *pieces, *later)


def project_kernel(place_ref, *refs):
    attns, pieces = refs[:XN], refs[XN:2 * XN]
    own_ref, across_ref, send_ref, a_s = refs[-4:]
    rows, width = own_ref.shape
    for n, bits in enumerate((0, 2, 1, 3)):
        for j in range(XN):
            a_s[n * rows:(n + 1) * rows, j * HD:(j + 1) * HD] = attns[j][
                rows_at(place_ref, bits, rows), :
            ]
    step = 256
    for n in range(0, width, step):
        w = jnp.concatenate([ref[:, n:n + step] for ref in pieces], axis=0)
        acc = dot(a_s[...], w, ((1,), (0,)))
        own_ref[:, n:n + step] = acc[:rows]
        across_ref[:, n:n + step] = acc[rows:2 * rows]
        send_ref[:, n:n + step] = acc[2 * rows:].astype(send_ref.dtype)


def project(place, attns, pieces, *later):
    rows, width = pieces[0].shape
    return pl.pallas_call(
        project_kernel,
        out_shape=(
            jax.ShapeDtypeStruct((rows, width), F32),
            jax.ShapeDtypeStruct((rows, width), F32),
            jax.ShapeDtypeStruct((2 * rows, width), BF16),
        ),
        in_specs=[pl.BlockSpec(memory_space=pltpu.SMEM)] + whole(2 * XN) + anywhere(later),
        out_specs=tuple(whole(3)),
        scratch_shapes=[pltpu.VMEM((PER_X * rows, XN * HD), BF16)],
        compiler_params=params(24),
        cost_estimate=cost(0.2),
        name="project",
    )(place, *attns, *pieces, *later)


def unpack_kernel(in_ref, out_ref):
    rows = out_ref.shape[1]
    for h in range(in_ref.shape[0]):
        for t in range(3):
            out_ref[t, :, h * HD:(h + 1) * HD] = in_ref[h, t * rows:(t + 1) * rows, :]


def unpack(received):
    heads, rows = received.shape[0], received.shape[1] // 3
    return pl.pallas_call(
        unpack_kernel,
        out_shape=jax.ShapeDtypeStruct((3, rows, heads * HD), BF16),
        in_specs=whole(1),
        out_specs=whole(1)[0],
        compiler_params=params(24),
        cost_estimate=cost(2),
        name="unpack",
    )(received)


def choose_kernel(section_ref, first_ref, second_ref, *refs):
    out_ref = refs[-1]
    out_ref[...] = jnp.where(section_ref[0] == section_ref[1], first_ref[...], second_ref[...])


def choose(sections, first, second, *later):
    return pl.pallas_call(
        choose_kernel,
        out_shape=jax.ShapeDtypeStruct(first.shape, first.dtype),
        in_specs=[pl.BlockSpec(memory_space=pltpu.SMEM)] + whole(2) + anywhere(later),
        out_specs=whole(1)[0],
        compiler_params=params(16),
        cost_estimate=cost(2),
        name="choose",
    )(sections, first, second, *later)


def settle_kernel(in_ref, out_ref):
    out_ref[...] = in_ref[...]


def settle(array):
    return pl.pallas_call(
        settle_kernel,
        out_shape=jax.ShapeDtypeStruct(array.shape, array.dtype),
        in_specs=whole(1),
        out_specs=whole(1)[0],
        compiler_params=params(8),
        cost_estimate=cost(0.2),
        name="settle",
    )(array)


def rotated(array, axis, by):
    length = lax.axis_size(axis)
    return lax.ppermute(array, axis, [(i, (i + by) % length) for i in range(length)])


def per_sample(seg, table):
    onehot = (seg[:, None] == jnp.arange(table.shape[0], dtype=jnp.int32)[None, :]).astype(F32)
    return jnp.sum(onehot[:, :, None] * table[None, :, :], axis=1)


def exchange(array):
    return lax.all_to_all(array, "seq", 0, 0, tiled=True)


def body(hidden_in, queries, keys, values, segments, gates, out_weight, upstream, fresh, loss_grad):
    section = lax.axis_index("pipe")
    last_section = lax.axis_size("pipe") - 1
    place = lax.axis_index("seq")[None]

    own = out_weight[0]
    pieces = tuple(along_x(own, -offset % XN) for offset in OFFSETS)

    fwd = exchange(pack(queries, keys, values, segments, 0))
    local_seg = segments[0]
    g_scaled = (per_sample(local_seg[1], gates[0, 1]) * upstream[0].astype(F32)).astype(BF16)
    g_across = lax.ppermute(g_scaled, "seq", YSWAP)
    g_core = lax.ppermute(g_scaled, "seq", CORE)
    g_both = lax.ppermute(g_across, "seq", CORE)
    packed = pack(queries, keys, values, segments, 1, g_across, *pieces[1:])
    bwd = exchange(packed)
    gate_tok = per_sample(local_seg[0], gates[0, 0])

    sections = jnp.stack([section, jnp.zeros_like(section)])
    turned = choose(sections, loss_grad, upstream[0], fwd)
    next_grad = rotated(turned, "pipe", -1)

    attns = attention_forward(place, fwd, packed, turned, gate_tok, g_both)
    attns = tuple(along_x(a, o) for a, o in zip(attns, OFFSETS))
    grads = attention_grad(place, (g_scaled, g_core, g_across, g_both), pieces, attns[0])
    grads = tuple(along_x(g, o) for g, o in zip(grads, OFFSETS))

    attns = (attns[0], attns[2], attns[1], attns[3])
    part, part_across, part_send = project(place, attns, pieces, bwd, next_grad)
    received = lax.ppermute(follow(part_send, *grads), "seq", CORE)
    rows = part.shape[0]
    across = lax.ppermute((part_across + received[rows:].astype(F32)).astype(BF16), "seq", YSWAP)
    proj = part + received[:rows].astype(F32) + across.astype(F32)
    section_out = (hidden_in[0].astype(F32) + gate_tok * proj).astype(BF16)
    section_out = jnp.where(section == last_section, fresh, section_out)

    grads = attention_backward(place, bwd, grads)
    next_act = rotated(section_out, "pipe", 1)

    qkv_grads = unpack(exchange(grads))
    return (next_act[None], settle(next_grad)[None], qkv_grads[None])


def solution(mesh):
    in_specs = (
        P("pipe", "seq", None),
        P("pipe", None, "seq", None),
        P("pipe", None, "seq", None),
        P("pipe", None, "seq", None),
        P("pipe", None, "seq"),
        P("pipe", None, None, None),
        P("pipe", "seq", None),
        P("pipe", "seq", None),
        P("seq", None),
        P("seq", None),
    )
    out_specs = (P("pipe", "seq", None), P("pipe", "seq", None), P("pipe", None, "seq", None))
    return jax.shard_map(body, mesh=mesh, in_specs=in_specs, out_specs=out_specs, check_vma=False)
```

time: 230 us -> 181 us (0.79)
  waiting for transfers between devices: 96.1 us -> 67.7 us
  starting transfers between devices: 54.8 us -> 44.1 us
  local copies, waits for them, and re-layouts: 20.5 us -> 11 us
    ppermute x16 -> x14, waiting for transfers between devices: 68.2 us -> 23.2 us  [the longest x9 19.6 us: along_x(): lax.ppermute(array, 'seq', [(i, (i + PER_X * offset) % count) for i in ra...]
    all_to_all x3, waiting for transfers between devices: 18.1 us -> 30.8 us  [exchange(): return lax.all_to_all(array, 'seq', 0, 0, tiled=True)]
    unnamed x46 -> x45, local copies, waits for them, and re-layouts: 18.3 us -> 9.73 us
    ppermute x16 -> x14, starting transfers between devices: 24 us -> 17.3 us  [the longest x9 12.3 us: along_x(): lax.ppermute(array, 'seq', [(i, (i + PER_X * offset) % count) for i in ra...]
    all_to_all x1 -> x0, starting transfers between devices: 4.37 us -> none  [exchange_same_core(): lax.all_to_all(array, 'seq', 0, 0, tiled=True, axis_index_groups=SAME_CORE)]
    ppermute x2, waiting for transfers between devices: 9.86 us -> 13.8 us  [rotated(): lax.ppermute(array, axis, [(i, (i + by) % length) for i in range(length)])]
    pallas_call x1, Pallas kernels: 5.43 us -> 1.81 us  [project(): pl.pallas_call(project_kernel, out_shape=(jax.ShapeDtypeStruct((rows, wid...]
    pallas_call x1, Pallas kernels: 20.6 us -> 17.6 us  [attention_backward(): pl.pallas_call(backward_kernel, out_shape=jax.ShapeDtypeStruct((blocks, 3...]
  transfers between devices with their start and end apart: 22 -> 19, of which waited for: 7 -> 8; matrix products, arithmetic and copies ran while one was open for 3% -> 4% of each run, Pallas kernels for 23% -> 28%
where the time goes in v2:
time: 181 us; the launch traced here: 180 us
  waiting for transfers between devices  67.7 us (37%)
  Pallas kernels  49.7 us (27%)
  starting transfers between devices  44.1 us (24%)
  local copies, waits for them, and re-layouts  11 us (6%)
  other arithmetic  6.62 us (4%)
    all_to_all x3, waiting for transfers between devices, exchange(): return lax.all_to_all(array, 'seq', 0, 0, tiled=True)  30.8 us
    ppermute x9, waiting for transfers between devices, along_x(): lax.ppermute(array, 'seq', [(i, (i + PER_X * offset) % count) for i in ra...  19.6 us
    pallas_call x1, Pallas kernels, attention_backward(): pl.pallas_call(backward_kernel, out_shape=jax.ShapeDtypeStruct((blocks, 3...  17.6 us
    all_to_all x3, starting transfers between devices, exchange(): return lax.all_to_all(array, 'seq', 0, 0, tiled=True)  16.2 us
    pallas_call x1, Pallas kernels, attention_forward(): pl.pallas_call(forward_kernel, out_shape=(jax.ShapeDtypeStruct((total //...  14.8 us
    ppermute x2, waiting for transfers between devices, rotated(): lax.ppermute(array, axis, [(i, (i + by) % length) for i in range(length)])  13.8 us
    ppermute x9, starting transfers between devices, along_x(): lax.ppermute(array, 'seq', [(i, (i + PER_X * offset) % count) for i in ra...  12.3 us
    ppermute x2, starting transfers between devices, rotated(): lax.ppermute(array, axis, [(i, (i + by) % length) for i in range(length)])  10.6 us
  transfers between devices with their start and end apart: 19, of which 8 were waited for; matrix products, arithmetic and copies ran while one was open for 4% of the time, Pallas kernels for 28%

profile of v2, /device:TPU:1, one launch (start us, length us, event | category | flops | bytes accessed | tf_op | source)
XLA Modules:
  0.0 179.9 jit_solution(7614492704819828322)
XLA Ops:
  0.6 3.7 %collective-permute-start.3 = (bf16[128,3072]{1,0:T(8,128)(2,1)}, bf16[128,3072]{1,0:T(8,128)(2,1)S(1)}, u32[]{:S(2)}, u32[]{:S(2)}) collective-permute-start(bf16[128,3072]{1,0:T(8,128)(2,1)} %bitcast.23), channel_id=1, source_target_pairs={{0,8},{1,9},{2,10},{3,11},{4,12},{5,13},{6,14},{7,15},{8,0},{9,1},... | collective-permute-start | bytes 2359304 | tf_op jit(solution)/shard_map/ppermute | solution.py:30
  5.8 1.3 slice_bitcast_fusion.2
  7.0 2.8 %pack.2 = bf16[16,400,128]{2,1,0:T(8,128)(2,1)} custom-call(s32[1,128]{1,0:T(1,128)} %get-tuple-element.28.seg_ref, bf16[1,2,128,2048]{3,2,1,0:T(8,128)(2,1)} %q_ref.3, bf16[1,2,128,2048]{3,2,1,0:T(8,128)(2,1)} %k_ref.3, bf16[1,2,128,2048]{3,2,1,0:T(8,128)(2,1)} %v_ref.3), custom_call_target="tpu_custom_call" | custom-call | flops 2000000000 | tf_op jit(solution)/shard_map/pack/pallas_call | solution.py:84
  9.9 6.3 %all-to-all-start = ((bf16[16,400,128]{2,1,0:T(8,128)(2,1)}), bf16[16,400,128]{2,1,0:T(8,128)(2,1)}, u32[]{:S(2)}, u32[]{:S(2)}) async-start(bf16[16,400,128]{2,1,0:T(8,128)(2,1)} %pack.2), calls=%async_computation | async-start | bytes 3276800 | tf_op jit(solution)/shard_map/all_to_all | solution.py:430
  17.3 1.1 multiply_convert_fusion.refs_0_
  18.4 1.4 collective-permute-start
  20.9 18.4 %collective-permute-done.2.refs_2_.refs_6_ = bf16[128,3072]{1,0:T(8,128)(2,1)S(1)} collective-permute-done((bf16[128,3072]{1,0:T(8,128)(2,1)}, bf16[128,3072]{1,0:T(8,128)(2,1)S(1)}, u32[]{:S(2)}, u32[]{:S(2)}) %collective-permute-start.2) | collective-permute-done | bytes 786464 | tf_op jit(solution)/shard_map/ppermute | solution.py:30
  39.9 1.4 pack.3.refs_0_
  41.3 16.9 %all-to-all-done.refs_0_.in_ref = bf16[16,400,128]{2,1,0:T(8,128)(2,1)} async-done(((bf16[16,400,128]{2,1,0:T(8,128)(2,1)}), bf16[16,400,128]{2,1,0:T(8,128)(2,1)}, u32[]{:S(2)}, u32[]{:S(2)}) %all-to-all-start) | async-done | bytes 1638432 | tf_op jit(solution)/shard_map/all_to_all | solution.py:430
  58.3 5.0 %all-to-all-start.1 = ((bf16[16,400,128]{2,1,0:T(8,128)(2,1)}), bf16[16,400,128]{2,1,0:T(8,128)(2,1)}, u32[]{:S(2)}, u32[]{:S(2)}) async-start(bf16[16,400,128]{2,1,0:T(8,128)(2,1)} %pack.3.refs_0_), calls=%async_computation.1 | async-start | bytes 3276800 | tf_op jit(solution)/shard_map/all_to_all | solution.py:430
  63.8 1.5 choose.1.refs_1_
  65.3 8.2 %collective-permute-start.8 = (bf16[128,3072]{1,0:T(8,128)(2,1)}, bf16[128,3072]{1,0:T(8,128)(2,1)}, u32[]{:S(2)}, u32[]{:S(2)}) collective-permute-start(bf16[128,3072]{1,0:T(8,128)(2,1)} %choose.1.refs_1_), channel_id=1, source_target_pairs={{0,240},{16,0},{32,16},{48,32},{64,48},{80,64},{96,80},{112,96},{1... | collective-permute-start | bytes 2359304 | tf_op jit(solution)/shard_map/ppermute | solution.py:421
  74.1 14.8 %attention_forward.1 = (bf16[512,128]{1,0:T(8,128)(2,1)S(1)}, bf16[512,128]{1,0:T(8,128)(2,1)S(1)}, bf16[512,128]{1,0:T(8,128)(2,1)S(1)}, bf16[512,128]{1,0:T(8,128)(2,1)S(1)}) custom-call(s32[1]{0:T(128)} %bitcast.3.place_ref, bf16[16,400,128]{2,1,0:T(8,128)(2,1)} %all-to-all-done.refs_0_.in_ref, bf16[16,400,128]{2,1,0:T(8,128)(2,1)} %pack.3.refs_0_, ...), custom_call_target="tpu_custom_call" | custom-call | flops 200000000 | tf_op jit(solution)/shard_map/attention_forward/pallas_call | solution.py:188
  88.9 1.5 collective-permute-start.5
  90.4 1.3 collective-permute-start.6
  91.7 1.7 collective-permute-start.7
  93.4 4.6 %attention_grad.1 = (bf16[512,128]{1,0:T(8,128)(2,1)S(1)}, bf16[512,128]{1,0:T(8,128)(2,1)}, bf16[512,128]{1,0:T(8,128)(2,1)}, bf16[512,128]{1,0:T(8,128)(2,1)}) custom-call(s32[1]{0:T(128)} %bitcast.3.place_ref, bf16[128,3072]{1,0:T(8,128)(2,1)} %multiply_convert_fusion.refs_0_, bf16[128,3072]{1,0:T(8,128)(2,1)} %collective-permute-done.9.refs_1_, ...), custom_call_target="tpu_custom_call" | custom-call | flops 200000000 | tf_op jit(solution)/shard_map/attention_grad/pallas_call | solution.py:318
  100.7 1.3 collective-permute-start.12
  102.7 1.1 copy-done.2
  103.8 1.1 copy-done.4
  107.7 1.8 %project.1 = (f32[128,3072]{1,0:T(8,128)S(1)}, f32[128,3072]{1,0:T(8,128)S(1)}, bf16[256,3072]{1,0:T(8,128)(2,1)S(1)}) custom-call(s32[1]{0:T(128)} %bitcast.3.place_ref, bf16[512,128]{1,0:T(8,128)(2,1)S(1)} %get-tuple-element.14.refs_0_.refs_8_, bf16[512,128]{1,0:T(8,128)(2,1)S(1)} %copy-done.14, bf16[512,128]{1,0:T(8,128)(2,1)S(1)} %copy-done.16, ...), custom_call_target="tpu_custom_call" | custom-call | flops 200000000 | tf_op jit(solution)/shard_map/project/pallas_call | solution.py:350
  110.7 2.2 %collective-permute-start.13 = (bf16[256,3072]{1,0:T(8,128)(2,1)S(1)}, bf16[256,3072]{1,0:T(8,128)(2,1)S(1)}, u32[]{:S(2)}, u32[]{:S(2)}) collective-permute-start(bf16[256,3072]{1,0:T(8,128)(2,1)S(1)} %follow.1), channel_id=1, source_target_pairs={{0,1},{1,0},{2,3},{3,2},{4,5},{5,4},{6,7},{7,6},{8,9},{9,8},{10,11... | collective-permute-start | bytes 4718600 | tf_op jit(solution)/shard_map/ppermute | solution.py:462
  112.8 3.0 %collective-permute-done.13 = bf16[256,3072]{1,0:T(8,128)(2,1)S(1)} collective-permute-done((bf16[256,3072]{1,0:T(8,128)(2,1)S(1)}, bf16[256,3072]{1,0:T(8,128)(2,1)S(1)}, u32[]{:S(2)}, u32[]{:S(2)}) %collective-permute-start.13) | collective-permute-done | bytes 1572896 | tf_op jit(solution)/shard_map/ppermute | solution.py:462
  115.9 1.1 add_convert_fusion
  118.2 17.6 %attention_backward.1 = bf16[16,384,128]{2,1,0:T(8,128)(2,1)} custom-call(s32[1]{0:T(128)} %bitcast.3.place_ref, bf16[16,400,128]{2,1,0:T(8,128)(2,1)} %all-to-all-done.1.refs_8_.in_ref, bf16[512,128]{1,0:T(8,128)(2,1)} %copy-done.11, bf16[512,128]{1,0:T(8,128)(2,1)} %copy-done.12, bf16[512,128]{1,0:T(8,128)(2,1)} %collective-permute-done.11.refs_2_, ...), custom_call_target="tpu_custom_call" | custom-call | flops 30000001024 | tf_op jit(solution)/shard_map/attention_backward/pallas_call | solution.py:278
  135.8 4.9 %all-to-all-start.2 = ((bf16[16,384,128]{2,1,0:T(8,128)(2,1)}), bf16[16,384,128]{2,1,0:T(8,128)(2,1)}, u32[]{:S(2)}, u32[]{:S(2)}) async-start(bf16[16,384,128]{2,1,0:T(8,128)(2,1)} %attention_backward.1), calls=%async_computation.2 | async-start | bytes 3145728 | tf_op jit(solution)/shard_map/all_to_all | solution.py:430
  140.8 3.2 %fusion.1 = bf16[128,3072]{1,0:T(8,128)(2,1)} fusion(bf16[128,3072]{1,0:T(8,128)(2,1)} %param.18, f32[128,3072]{1,0:T(8,128)S(1)} %multiply_reduce_fusion.1.refs_2_, bf16[128,3072]{1,0:T(8,128)(2,1)} %collective-permute-done.14, f32[128,3072]{1,0:T(8,128)S(1)} %copy-done.6, bf16[256,3072]{1,0:T(8,128)(2,1)} %copy-done.20, bf16[1,128,3072]{2,1,0:T(8,128)(2,1)} %param.10, ...), kind=kLoop, calls=%fused_computation.6 | loop fusion | flops 3538944 | bytes 7077889 | tf_op jit(solution)/shard_map/jit(_where)/select_n | solution.py:467
  143.9 2.4 %collective-permute-start.15 = (bf16[128,3072]{1,0:T(8,128)(2,1)}, bf16[128,3072]{1,0:T(8,128)(2,1)S(1)}, u32[]{:S(2)}, u32[]{:S(2)}) collective-permute-start(bf16[128,3072]{1,0:T(8,128)(2,1)} %fusion.1), channel_id=1, source_target_pairs={{0,16},{16,32},{32,48},{48,64},{64,80},{80,96},{96,112},{112,128},... | collective-permute-start | bytes 2359304 | tf_op jit(solution)/shard_map/ppermute | solution.py:421
  146.4 2.1 %settle.1 = bf16[128,3072]{1,0:T(8,128)(2,1)} custom-call(bf16[128,3072]{1,0:T(8,128)(2,1)} %collective-permute-done.8.refs_9_.in_ref), custom_call_target="tpu_custom_call" | custom-call | flops 200000000 | tf_op jit(solution)/shard_map/settle/pallas_call | solution.py:408
  148.4 13.9 %all-to-all-done.2.in_ref = bf16[16,384,128]{2,1,0:T(8,128)(2,1)} async-done(((bf16[16,384,128]{2,1,0:T(8,128)(2,1)}), bf16[16,384,128]{2,1,0:T(8,128)(2,1)}, u32[]{:S(2)}, u32[]{:S(2)}) %all-to-all-start.2) | async-done | bytes 1572896 | tf_op jit(solution)/shard_map/all_to_all | solution.py:430
  162.3 3.0 %unpack.1 = bf16[3,128,2048]{2,1,0:T(8,128)(2,1)} custom-call(bf16[16,384,128]{2,1,0:T(8,128)(2,1)} %all-to-all-done.2.in_ref), custom_call_target="tpu_custom_call" | custom-call | flops 2000000000 | tf_op jit(solution)/shard_map/unpack/pallas_call | solution.py:375
  165.3 13.8 %collective-permute-done.15 = bf16[128,3072]{1,0:T(8,128)(2,1)S(1)} collective-permute-done((bf16[128,3072]{1,0:T(8,128)(2,1)}, bf16[128,3072]{1,0:T(8,128)(2,1)S(1)}, u32[]{:S(2)}, u32[]{:S(2)}) %collective-permute-start.15) | collective-permute-done | bytes 786464 | tf_op jit(solution)/shard_map/ppermute | solution.py:421
  (71 shorter events, 14.8 us)
Async XLA Ops:
  0.6 20.2 %collective-permute-start.3 = (bf16[128,3072]{1,0:T(8,128)(2,1)}, bf16[128,3072]{1,0:T(8,128)(2,1)S(1)}, u32[]{:S(2)}, u32[]{:S(2)}) collective-permute-start(bf16[128,3072]{1,0:T(8,128)(2,1)} %bitcast.23), channel_id=1, source_target_pairs={{0,8},{1,9},{2,10},{3,11},{4,12},{5,13},{6,14},{7,15},{8,0},{9,1},... | collective-permute-start | bytes 2359304 | tf_op jit(solution)/shard_map/ppermute | solution.py:30
  4.3 35.0 %collective-permute-start.2 = (bf16[128,3072]{1,0:T(8,128)(2,1)}, bf16[128,3072]{1,0:T(8,128)(2,1)S(1)}, u32[]{:S(2)}, u32[]{:S(2)}) collective-permute-start(bf16[128,3072]{1,0:T(8,128)(2,1)} %bitcast.24), channel_id=1, source_target_pairs={{0,12},{1,13},{2,14},{3,15},{4,0},{5,1},{6,2},{7,3},{8,4},{9,5},{1... | collective-permute-start | bytes 2359304 | tf_op jit(solution)/shard_map/ppermute | solution.py:30
  5.2 34.2 %collective-permute-start.1 = (bf16[128,3072]{1,0:T(8,128)(2,1)}, bf16[128,3072]{1,0:T(8,128)(2,1)S(1)}, u32[]{:S(2)}, u32[]{:S(2)}) collective-permute-start(bf16[128,3072]{1,0:T(8,128)(2,1)} %bitcast.25), channel_id=1, source_target_pairs={{0,4},{1,5},{2,6},{3,7},{4,8},{5,9},{6,10},{7,11},{8,12},{9,13},{1... | collective-permute-start | bytes 2359304 | tf_op jit(solution)/shard_map/ppermute | solution.py:30
  9.9 6.3 %copy-start.21 = (f32[1,2,4,3072]{3,2,1,0:T(4,128)S(1)}, f32[1,2,4,3072]{3,2,1,0:T(4,128)}, u32[]{:S(2)}) copy-start(f32[1,2,4,3072]{3,2,1,0:T(4,128)} %param.15) | copy-start | bytes 294916
  9.9 48.4 %all-to-all-start = ((bf16[16,400,128]{2,1,0:T(8,128)(2,1)}), bf16[16,400,128]{2,1,0:T(8,128)(2,1)}, u32[]{:S(2)}, u32[]{:S(2)}) async-start(bf16[16,400,128]{2,1,0:T(8,128)(2,1)} %pack.2), calls=%async_computation | async-start | bytes 3276800 | tf_op jit(solution)/shard_map/all_to_all | solution.py:430
  17.3 22.6 %copy-start.7 = (bf16[1,2,128,2048]{3,2,1,0:T(8,128)(2,1)S(1)}, bf16[1,2,128,2048]{3,2,1,0:T(8,128)(2,1)}, u32[]{:S(2)}) copy-start(bf16[1,2,128,2048]{3,2,1,0:T(8,128)(2,1)} %q_ref.3) | copy-start | bytes 3145732
  17.3 22.6 %copy-start.8 = (bf16[1,2,128,2048]{3,2,1,0:T(8,128)(2,1)S(1)}, bf16[1,2,128,2048]{3,2,1,0:T(8,128)(2,1)}, u32[]{:S(2)}) copy-start(bf16[1,2,128,2048]{3,2,1,0:T(8,128)(2,1)} %k_ref.3) | copy-start | bytes 3145732
  17.3 22.6 %copy-start.9 = (bf16[1,2,128,2048]{3,2,1,0:T(8,128)(2,1)S(1)}, bf16[1,2,128,2048]{3,2,1,0:T(8,128)(2,1)}, u32[]{:S(2)}) copy-start(bf16[1,2,128,2048]{3,2,1,0:T(8,128)(2,1)} %v_ref.3) | copy-start | bytes 3145732
  18.4 21.5 %collective-permute-start = (bf16[128,3072]{1,0:T(8,128)(2,1)}, bf16[128,3072]{1,0:T(8,128)(2,1)}, u32[]{:S(2)}, u32[]{:S(2)}) collective-permute-start(bf16[128,3072]{1,0:T(8,128)(2,1)} %multiply_convert_fusion.refs_0_), channel_id=1, source_target_pairs={{0,2},{1,3},{2,0},{3,1},{4,6},{5,7},{6,4},{7,5},{8,10},{9,11},{10,... | collective-permute-start | bytes 2359304 | tf_op jit(solution)/shard_map/ppermute | solution.py:444
  39.4 2.0 %copy-start = (bf16[128,3072]{1,0:T(8,128)(2,1)}, bf16[128,3072]{1,0:T(8,128)(2,1)S(1)}, u32[]{:S(2)}) copy-start(bf16[128,3072]{1,0:T(8,128)(2,1)S(1)} %collective-permute-done.1.refs_1_.refs_5_) | copy-start | bytes 2359300
  58.3 5.6 %copy-start.19 = (bf16[128,3072]{1,0:T(8,128)(2,1)S(1)}, bf16[128,3072]{1,0:T(8,128)(2,1)}, u32[]{:S(2)}) copy-start(bf16[128,3072]{1,0:T(8,128)(2,1)} %first_ref.1) | copy-start | bytes 2359300
  58.3 44.4 %all-to-all-start.1 = ((bf16[16,400,128]{2,1,0:T(8,128)(2,1)}), bf16[16,400,128]{2,1,0:T(8,128)(2,1)}, u32[]{:S(2)}, u32[]{:S(2)}) async-start(bf16[16,400,128]{2,1,0:T(8,128)(2,1)} %pack.3.refs_0_), calls=%async_computation.1 | async-start | bytes 3276800 | tf_op jit(solution)/shard_map/all_to_all | solution.py:430
  63.2 30.1 %collective-permute-start.9 = (bf16[128,3072]{1,0:T(8,128)(2,1)}, bf16[128,3072]{1,0:T(8,128)(2,1)}, u32[]{:S(2)}, u32[]{:S(2)}) collective-permute-start(bf16[128,3072]{1,0:T(8,128)(2,1)} %multiply_convert_fusion.refs_0_), channel_id=1, source_target_pairs={{0,1},{1,0},{2,3},{3,2},{4,5},{5,4},{6,7},{7,6},{8,9},{9,8},{10,11... | collective-permute-start | bytes 2359304 | tf_op jit(solution)/shard_map/ppermute | solution.py:445
  63.5 10.6 %collective-permute-start.4 = (bf16[128,3072]{1,0:T(8,128)(2,1)}, bf16[128,3072]{1,0:T(8,128)(2,1)}, u32[]{:S(2)}, u32[]{:S(2)}) collective-permute-start(bf16[128,3072]{1,0:T(8,128)(2,1)} %collective-permute-done.refs_0_.refs_2_), channel_id=1, source_target_pairs={{0,1},{1,0},{2,3},{3,2},{4,5},{5,4},{6,7},{7,6},{8,9},{9,8},{10,11... | collective-permute-start | bytes 2359304 | tf_op jit(solution)/shard_map/ppermute | solution.py:446
  65.3 37.4 %collective-permute-start.8 = (bf16[128,3072]{1,0:T(8,128)(2,1)}, bf16[128,3072]{1,0:T(8,128)(2,1)}, u32[]{:S(2)}, u32[]{:S(2)}) collective-permute-start(bf16[128,3072]{1,0:T(8,128)(2,1)} %choose.1.refs_1_), channel_id=1, source_target_pairs={{0,240},{16,0},{32,16},{48,32},{64,48},{80,64},{96,80},{112,96},{1... | collective-permute-start | bytes 2359304 | tf_op jit(solution)/shard_map/ppermute | solution.py:421
  74.1 19.2 %copy-start.1 = (bf16[128,3072]{1,0:T(8,128)(2,1)S(1)}, bf16[128,3072]{1,0:T(8,128)(2,1)}, u32[]{:S(2)}) copy-start(bf16[128,3072]{1,0:T(8,128)(2,1)} %copy-done) | copy-start | bytes 2359300
  74.1 19.2 %copy-start.3 = (bf16[1,128,3072]{2,1,0:T(8,128)(2,1)S(1)}, bf16[1,128,3072]{2,1,0:T(8,128)(2,1)}, u32[]{:S(2)}) copy-start(bf16[1,128,3072]{2,1,0:T(8,128)(2,1)} %param.16) | copy-start | bytes 2359300
  88.9 9.9 %collective-permute-start.5 = (bf16[512,128]{1,0:T(8,128)(2,1)S(1)}, bf16[512,128]{1,0:T(8,128)(2,1)S(1)}, u32[]{:S(2)}, u32[]{:S(2)}) collective-permute-start(bf16[512,128]{1,0:T(8,128)(2,1)S(1)} %get-tuple-element.15), channel_id=1, source_target_pairs={{0,4},{1,5},{2,6},{3,7},{4,8},{5,9},{6,10},{7,11},{8,12},{9,13},{1... | collective-permute-start | bytes 393224 | tf_op jit(solution)/shard_map/ppermute | solution.py:30
  90.4 9.7 %collective-permute-start.6 = (bf16[512,128]{1,0:T(8,128)(2,1)S(1)}, bf16[512,128]{1,0:T(8,128)(2,1)S(1)}, u32[]{:S(2)}, u32[]{:S(2)}) collective-permute-start(bf16[512,128]{1,0:T(8,128)(2,1)S(1)} %get-tuple-element.16), channel_id=1, source_target_pairs={{0,12},{1,13},{2,14},{3,15},{4,0},{5,1},{6,2},{7,3},{8,4},{9,5},{1... | collective-permute-start | bytes 393224 | tf_op jit(solution)/shard_map/ppermute | solution.py:30
  91.7 10.3 %collective-permute-start.7 = (bf16[512,128]{1,0:T(8,128)(2,1)S(1)}, bf16[512,128]{1,0:T(8,128)(2,1)S(1)}, u32[]{:S(2)}, u32[]{:S(2)}) collective-permute-start(bf16[512,128]{1,0:T(8,128)(2,1)S(1)} %get-tuple-element.17), channel_id=1, source_target_pairs={{0,8},{1,9},{2,10},{3,11},{4,12},{5,13},{6,14},{7,15},{8,0},{9,1},... | collective-permute-start | bytes 393224 | tf_op jit(solution)/shard_map/ppermute | solution.py:30
  97.9 11.6 %copy-start.11 = (bf16[512,128]{1,0:T(8,128)(2,1)}, bf16[512,128]{1,0:T(8,128)(2,1)S(1)}, u32[]{:S(2)}) copy-start(bf16[512,128]{1,0:T(8,128)(2,1)S(1)} %get-tuple-element.20.refs_0_) | copy-start | bytes 393220
  97.9 11.6 %collective-permute-start.10 = (bf16[512,128]{1,0:T(8,128)(2,1)}, bf16[512,128]{1,0:T(8,128)(2,1)S(1)}, u32[]{:S(2)}, u32[]{:S(2)}) collective-permute-start(bf16[512,128]{1,0:T(8,128)(2,1)} %get-tuple-element.21), channel_id=1, source_target_pairs={{0,12},{1,13},{2,14},{3,15},{4,0},{5,1},{6,2},{7,3},{8,4},{9,5},{1... | collective-permute-start | bytes 393224 | tf_op jit(solution)/shard_map/ppermute | solution.py:30
  99.5 10.0 %collective-permute-start.11 = (bf16[512,128]{1,0:T(8,128)(2,1)}, bf16[512,128]{1,0:T(8,128)(2,1)}, u32[]{:S(2)}, u32[]{:S(2)}) collective-permute-start(bf16[512,128]{1,0:T(8,128)(2,1)} %get-tuple-element.22), channel_id=1, source_target_pairs={{0,4},{1,5},{2,6},{3,7},{4,8},{5,9},{6,10},{7,11},{8,12},{9,13},{1... | collective-permute-start | bytes 393224 | tf_op jit(solution)/shard_map/ppermute | solution.py:30
  100.7 8.8 %collective-permute-start.12 = (bf16[512,128]{1,0:T(8,128)(2,1)}, bf16[512,128]{1,0:T(8,128)(2,1)}, u32[]{:S(2)}, u32[]{:S(2)}) collective-permute-start(bf16[512,128]{1,0:T(8,128)(2,1)} %get-tuple-element.23), channel_id=1, source_target_pairs={{0,8},{1,9},{2,10},{3,11},{4,12},{5,13},{6,14},{7,15},{8,0},{9,1},... | collective-permute-start | bytes 393224 | tf_op jit(solution)/shard_map/ppermute | solution.py:30
  109.5 1.1 copy-start.5
  109.5 1.2 copy-start.12
  110.7 5.2 %collective-permute-start.13 = (bf16[256,3072]{1,0:T(8,128)(2,1)S(1)}, bf16[256,3072]{1,0:T(8,128)(2,1)S(1)}, u32[]{:S(2)}, u32[]{:S(2)}) collective-permute-start(bf16[256,3072]{1,0:T(8,128)(2,1)S(1)} %follow.1), channel_id=1, source_target_pairs={{0,1},{1,0},{2,3},{3,2},{4,5},{5,4},{6,7},{7,6},{8,9},{9,8},{10,11... | collective-permute-start | bytes 4718600 | tf_op jit(solution)/shard_map/ppermute | solution.py:462
  115.9 1.4 copy-start.20
  117.3 23.5 %collective-permute-start.14 = (bf16[128,3072]{1,0:T(8,128)(2,1)}, bf16[128,3072]{1,0:T(8,128)(2,1)}, u32[]{:S(2)}, u32[]{:S(2)}) collective-permute-start(bf16[128,3072]{1,0:T(8,128)(2,1)} %add_convert_fusion), channel_id=1, source_target_pairs={{0,2},{1,3},{2,0},{3,1},{4,6},{5,7},{6,4},{7,5},{8,10},{9,11},{10,... | collective-permute-start | bytes 2359304 | tf_op jit(solution)/shard_map/ppermute | solution.py:464
  135.8 4.9 %copy-start.6 = (f32[128,3072]{1,0:T(8,128)S(1)}, f32[128,3072]{1,0:T(8,128)}, u32[]{:S(2)}) copy-start(f32[128,3072]{1,0:T(8,128)} %copy-done.5) | copy-start | bytes 4718596
  135.8 26.4 %all-to-all-start.2 = ((bf16[16,384,128]{2,1,0:T(8,128)(2,1)}), bf16[16,384,128]{2,1,0:T(8,128)(2,1)}, u32[]{:S(2)}, u32[]{:S(2)}) async-start(bf16[16,384,128]{2,1,0:T(8,128)(2,1)} %attention_backward.1), calls=%async_computation.2 | async-start | bytes 3145728 | tf_op jit(solution)/shard_map/all_to_all | solution.py:430
  143.9 35.1 %collective-permute-start.15 = (bf16[128,3072]{1,0:T(8,128)(2,1)}, bf16[128,3072]{1,0:T(8,128)(2,1)S(1)}, u32[]{:S(2)}, u32[]{:S(2)}) collective-permute-start(bf16[128,3072]{1,0:T(8,128)(2,1)} %fusion.1), channel_id=1, source_target_pairs={{0,16},{16,32},{32,48},{48,64},{64,80},{80,96},{96,112},{112,128},... | collective-permute-start | bytes 2359304 | tf_op jit(solution)/shard_map/ppermute | solution.py:421
  (9 other events, 8.1 us)

commit v3 on v2

--- a/solution.py
+++ b/solution.py
@@ -88,7 +88,7 @@
         in_specs=[pl.BlockSpec((1, rows), lambda i: (0, 0)), block, block, block]
         + anywhere(later),
         out_specs=pl.BlockSpec((heads, height, HD), lambda i: (0, 0, 0)),
-        compiler_params=params(16 if later else 60),
+        compiler_params=params(60),
         cost_estimate=cost(2),
         name="pack",
     )(segments[0, batch][None], queries, keys, values, *later)
@@ -142,8 +142,11 @@
         seg_s[i * 256:(i + 1) * 256, :] = sample_of(position, starts)
 
 
-def forward_kernel(place_ref, in_ref, *refs):
-    outs, (out_s, vt_s, seg_s) = refs[-3 - XN:-3], refs[-3:]
+def forward_kernel(place_ref, in_hbm_ref, *refs):
+    outs, (in_ref, out_s, vt_s, seg_s, in_sem, out_sems) = refs[-6 - XN:-6], refs[-6:]
+    arriving = pltpu.make_async_copy(in_hbm_ref, in_ref, in_sem)
+    arriving.start()
+    arriving.wait()
     blocks, rows = in_ref.shape[0], 128
     total = blocks * rows
     starts = sample_starts(in_ref, rows)
@@ -174,13 +177,20 @@
         m0 = jnp.full((1, QB), LOW, F32)
         l0 = jnp.zeros((1, QB), F32)
         m, l, acc = lax.fori_loop(begin, end, per_tile, (m0, l0, jnp.zeros((HD, QB), F32)))
-        out_s[i] = (acc / l).T.astype(BF16)
+        share = total // XN // QB
+        here = pl.ds(pl.multiple_of(i % share * QB, QB), QB)
+        out_s[i // share, here, :] = (acc / l).T.astype(BF16)
         return 0
 
     lax.fori_loop(0, total // QB, per_block, 0)
-    per = total // QB // XN
-    for offset, ref in zip(OFFSETS, outs):
-        ref[...] = out_s[pl.ds(x_at(place_ref, offset) * per, per)].reshape(per * QB, HD)
+    leaving = [
+        pltpu.make_async_copy(out_s.at[x_at(place_ref, offset)], ref, out_sems.at[n])
+        for n, (offset, ref) in enumerate(zip(OFFSETS, outs))
+    ]
+    for copy in leaving:
+        copy.start()
+    for copy in leaving:
+        copy.wait()
 
 
 def attention_forward(place, packed, *later):
@@ -188,22 +198,27 @@
     return pl.pallas_call(
         forward_kernel,
         out_shape=(jax.ShapeDtypeStruct((total // XN, HD), BF16),) * XN,
-        in_specs=[pl.BlockSpec(memory_space=pltpu.SMEM)] + whole(1) + anywhere(later),
-        out_specs=tuple(whole(XN)),
+        in_specs=[pl.BlockSpec(memory_space=pltpu.SMEM)] + in_hbm(1) + anywhere(later),
+        out_specs=tuple(in_hbm(XN)),
         scratch_shapes=[
-            pltpu.VMEM((total // QB, QB, HD), BF16),
+            pltpu.VMEM(packed.shape, BF16),
+            pltpu.VMEM((XN, total // XN, HD), BF16),
             pltpu.VMEM((HD, total), BF16),
             pltpu.VMEM((total, HD), F32),
+            pltpu.SemaphoreType.DMA,
+            pltpu.SemaphoreType.DMA((XN,)),
         ],
-        compiler_params=params(24),
+        compiler_params=params(60),
         cost_estimate=cost(0.2),
         name="attention_forward",
     )(place, packed, *later)
 
 
-def backward_kernel(place_ref, in_ref, *refs):
+def backward_kernel(place_ref, in_hbm_ref, *refs):
     g_refs = refs[:XN]
-    out_ref, g_ref, out_s, kt_s, seg_s, s_s, dp_s, dk_s, dv_s, in_sems, out_sem = refs[-11:]
+    out_ref, in_ref, g_ref, out_s, kt_s, seg_s, s_s, dp_s, dk_s, dv_s, in_sems, out_sem = refs[-12:]
+    packed = pltpu.make_async_copy(in_hbm_ref, in_ref, in_sems.at[XN])
+    packed.start()
     blocks, rows = in_ref.shape[0], 128
     arriving = []
     for n, (offset, ref) in enumerate(zip(OFFSETS, g_refs)):
@@ -211,6 +226,7 @@
         arriving.append(pltpu.make_async_copy(ref, g_ref.at[source], in_sems.at[n]))
         arriving[-1].start()
     total = blocks * rows
+    packed.wait()
     starts = sample_starts(in_ref, rows)
     fill_samples(seg_s, starts)
     for i in range(blocks):
@@ -279,11 +295,11 @@
         backward_kernel,
         out_shape=jax.ShapeDtypeStruct((blocks, 3 * 128, HD), BF16),
         in_specs=[pl.BlockSpec(memory_space=pltpu.SMEM)]
-        + whole(1)
-        + in_hbm(XN)
+        + in_hbm(1 + XN)
         + anywhere(later),
         out_specs=in_hbm(1)[0],
         scratch_shapes=[
+            pltpu.VMEM(packed.shape, BF16),
             pltpu.VMEM((XN, total // XN, HD), BF16),
             pltpu.VMEM((blocks, 3 * 128, HD), BF16),
             pltpu.VMEM((HD, total), BF16),
@@ -292,7 +308,7 @@
             pltpu.VMEM((total, QB), F32),
             pltpu.VMEM((total, HD), F32),
             pltpu.VMEM((total, HD), F32),
-            pltpu.SemaphoreType.DMA((XN,)),
+            pltpu.SemaphoreType.DMA((XN + 1,)),
             pltpu.SemaphoreType.DMA,
         ],
         compiler_params=params(60),
@@ -302,15 +318,30 @@
 
 
 def grad_kernel(place_ref, *refs):
-    grads, pieces, outs, g_s = refs[:PER_X], refs[PER_X:PER_X + XN], refs[-1 - XN:-1], refs[-1]
+    grads, pieces, outs = refs[:PER_X], refs[PER_X:PER_X + XN], refs[-5 - XN:-5]
+    g_s, w_s, out_s, in_sems, out_sems = refs[-5:]
     rows = grads[0].shape[0]
+    arriving = []
     for bits, ref in enumerate(grads):
-        g_s[rows_at(place_ref, bits, rows), :] = ref[...]
+        target = g_s.at[rows_at(place_ref, bits, rows), :]
+        arriving.append(pltpu.make_async_copy(ref, target, in_sems.at[bits]))
+    for j, ref in enumerate(pieces):
+        target = w_s.at[j * HD:(j + 1) * HD, :]
+        arriving.append(pltpu.make_async_copy(ref, target, in_sems.at[PER_X + j]))
+    for copy in arriving:
+        copy.start()
+    for copy in arriving:
+        copy.wait()
+    leaving = []
     for j in range(0, XN, 2):
-        w = jnp.concatenate([pieces[j][...], pieces[j + 1][...]], axis=0)
-        r = dot(g_s[...], w, ((1,), (1,))).astype(BF16)
-        outs[j][...] = r[:, :HD]
-        outs[j + 1][...] = r[:, HD:]
+        r = dot(g_s[...], w_s[j * HD:(j + 2) * HD, :], ((1,), (1,))).astype(BF16)
+        out_s[j] = r[:, :HD]
+        out_s[j + 1] = r[:, HD:]
+        for n in (j, j + 1):
+            leaving.append(pltpu.make_async_copy(out_s.at[n], outs[n], out_sems.at[n]))
+            leaving[-1].start()
+    for copy in leaving:
+        copy.wait()
 
 
 def attention_grad(place, grads, pieces, *later):
@@ -318,46 +349,68 @@
     return pl.pallas_call(
         grad_kernel,
         out_shape=(jax.ShapeDtypeStruct((PER_X * rows, HD), BF16),) * XN,
-        in_specs=[pl.BlockSpec(memory_space=pltpu.SMEM)] + whole(PER_X + XN) + anywhere(later),
-        out_specs=tuple(whole(XN)),
-        scratch_shapes=[pltpu.VMEM((PER_X * rows, width), BF16)],
-        compiler_params=params(24),
+        in_specs=[pl.BlockSpec(memory_space=pltpu.SMEM)] + in_hbm(PER_X + XN) + anywhere(later),
+        out_specs=tuple(in_hbm(XN)),
+        scratch_shapes=[
+            pltpu.VMEM((PER_X * rows, width), BF16),
+            pltpu.VMEM((XN * HD, width), BF16),
+            pltpu.VMEM((XN, PER_X * rows, HD), BF16),
+            pltpu.SemaphoreType.DMA((PER_X + XN,)),
+            pltpu.SemaphoreType.DMA((XN,)),
+        ],
+        compiler_params=params(60),
         cost_estimate=cost(0.2),
         name="attention_grad",
     )(place, *grads, *pieces, *later)
 
 
 def project_kernel(place_ref, *refs):
-    attns, pieces = refs[:XN], refs[XN:2 * XN]
-    own_ref, across_ref, send_ref, a_s = refs[-4:]
-    rows, width = own_ref.shape
+    attns, pieces, outs = refs[:XN], refs[XN:2 * XN], refs[-11:-8]
+    a_in, w_s, a_s, own_s, across_s, send_s, in_sems, out_sems = refs[-8:]
+    rows, width = outs[0].shape
+    arriving = []
+    for j in range(XN):
+        target = w_s.at[j * HD:(j + 1) * HD, :]
+        arriving.append(pltpu.make_async_copy(attns[j], a_in.at[j], in_sems.at[j]))
+        arriving.append(pltpu.make_async_copy(pieces[j], target, in_sems.at[XN + j]))
+    for copy in arriving:
+        copy.start()
+    for copy in arriving:
+        copy.wait()
     for n, bits in enumerate((0, 2, 1, 3)):
         for j in range(XN):
-            a_s[n * rows:(n + 1) * rows, j * HD:(j + 1) * HD] = attns[j][
-                rows_at(place_ref, bits, rows), :
+            a_s[n * rows:(n + 1) * rows, j * HD:(j + 1) * HD] = a_in[
+                j, rows_at(place_ref, bits, rows), :
             ]
-    step = 256
+    step = 512
     for n in range(0, width, step):
-        w = jnp.concatenate([ref[:, n:n + step] for ref in pieces], axis=0)
-        acc = dot(a_s[...], w, ((1,), (0,)))
-        own_ref[:, n:n + step] = acc[:rows]
-        across_ref[:, n:n + step] = acc[rows:2 * rows]
-        send_ref[:, n:n + step] = acc[2 * rows:].astype(send_ref.dtype)
+        cols = slice(n, n + step)
+        acc = dot(a_s[...], w_s[:, cols], ((1,), (0,)))
+        own_s[:, cols] = acc[:rows]
+        across_s[:, cols] = acc[rows:2 * rows]
+        send_s[:, cols] = acc[2 * rows:].astype(BF16)
+        for k, (result, out) in enumerate(zip((own_s, across_s, send_s), outs)):
+            pltpu.make_async_copy(result.at[:, cols], out.at[:, cols], out_sems.at[k]).start()
+    for k, (result, out) in enumerate(zip((own_s, across_s, send_s), outs)):
+        pltpu.make_async_copy(result, out, out_sems.at[k]).wait()
 
 
 def project(place, attns, pieces, *later):
     rows, width = pieces[0].shape
+    shapes = (((rows, width), F32), ((rows, width), F32), ((2 * rows, width), BF16))
     return pl.pallas_call(
         project_kernel,
-        out_shape=(
-            jax.ShapeDtypeStruct((rows, width), F32),
-            jax.ShapeDtypeStruct((rows, width), F32),
-            jax.ShapeDtypeStruct((2 * rows, width), BF16),
-        ),
-        in_specs=[pl.BlockSpec(memory_space=pltpu.SMEM)] + whole(2 * XN) + anywhere(later),
-        out_specs=tuple(whole(3)),
-        scratch_shapes=[pltpu.VMEM((PER_X * rows, XN * HD), BF16)],
-        compiler_params=params(24),
+        out_shape=tuple(jax.ShapeDtypeStruct(*shape) for shape in shapes),
+        in_specs=[pl.BlockSpec(memory_space=pltpu.SMEM)] + in_hbm(2 * XN) + anywhere(later),
+        out_specs=tuple(in_hbm(3)),
+        scratch_shapes=[
+            pltpu.VMEM((XN, PER_X * rows, HD), BF16),
+            pltpu.VMEM((XN * HD, width), BF16),
+            pltpu.VMEM((PER_X * rows, XN * HD), BF16),
+        ]
+        + [pltpu.VMEM(*shape) for shape in shapes]
+        + [pltpu.SemaphoreType.DMA((2 * XN,)), pltpu.SemaphoreType.DMA((3,))],
+        compiler_params=params(60),
         cost_estimate=cost(0.2),
         name="project",
     )(place, *attns, *pieces, *later)
@@ -400,20 +453,10 @@
     )(sections, first, second, *later)
 
 
-def settle_kernel(in_ref, out_ref):
-    out_ref[...] = in_ref[...]
-
-
-def settle(array):
-    return pl.pallas_call(
-        settle_kernel,
-        out_shape=jax.ShapeDtypeStruct(array.shape, array.dtype),
-        in_specs=whole(1),
-        out_specs=whole(1)[0],
-        compiler_params=params(8),
-        cost_estimate=cost(0.2),
-        name="settle",
-    )(array)
+def shifted(array, axis, by):
+    length = lax.axis_size(axis)
+    pairs = [(i, i + by) for i in range(length) if 0 <= i + by < length]
+    return lax.ppermute(array, axis, pairs)
 
 
 def rotated(array, axis, by):
@@ -437,6 +480,7 @@
 
     own = out_weight[0]
     pieces = tuple(along_x(own, -offset % XN) for offset in OFFSETS)
+    moved = shifted(upstream[0], "pipe", -1)
 
     fwd = exchange(pack(queries, keys, values, segments, 0))
     local_seg = segments[0]
@@ -444,33 +488,32 @@
     g_across = lax.ppermute(g_scaled, "seq", YSWAP)
     g_core = lax.ppermute(g_scaled, "seq", CORE)
     g_both = lax.ppermute(g_across, "seq", CORE)
-    packed = pack(queries, keys, values, segments, 1, g_across, *pieces[1:])
+    packed = pack(queries, keys, values, segments, 1, g_across, moved, *pieces[1:])
     bwd = exchange(packed)
     gate_tok = per_sample(local_seg[0], gates[0, 0])
 
-    sections = jnp.stack([section, jnp.zeros_like(section)])
-    turned = choose(sections, loss_grad, upstream[0], fwd)
-    next_grad = rotated(turned, "pipe", -1)
-
-    attns = attention_forward(place, fwd, packed, turned, gate_tok, g_both)
+    grads = attention_grad(place, (g_scaled, g_core, g_across, g_both), pieces, packed)
+    attns = attention_forward(place, fwd, grads[0], gate_tok)
+    grads = tuple(along_x(g, o) for g, o in zip(grads, OFFSETS))
+    attns = (attns[0], follow(attns[1], *grads[1:])) + attns[2:]
     attns = tuple(along_x(a, o) for a, o in zip(attns, OFFSETS))
-    grads = attention_grad(place, (g_scaled, g_core, g_across, g_both), pieces, attns[0])
-    grads = tuple(along_x(g, o) for g, o in zip(grads, OFFSETS))
 
     attns = (attns[0], attns[2], attns[1], attns[3])
-    part, part_across, part_send = project(place, attns, pieces, bwd, next_grad)
-    received = lax.ppermute(follow(part_send, *grads), "seq", CORE)
+    part, part_across, part_send = project(place, attns, pieces, bwd)
+    received = lax.ppermute(part_send, "seq", CORE)
     rows = part.shape[0]
-    across = lax.ppermute((part_across + received[rows:].astype(F32)).astype(BF16), "seq", YSWAP)
+    across = (part_across + received[rows:].astype(F32)).astype(BF16)
+    grads = attention_backward(place, bwd, grads, across)
+    across = lax.ppermute(across, "seq", YSWAP)
     proj = part + received[:rows].astype(F32) + across.astype(F32)
     section_out = (hidden_in[0].astype(F32) + gate_tok * proj).astype(BF16)
     section_out = jnp.where(section == last_section, fresh, section_out)
-
-    grads = attention_backward(place, bwd, grads)
     next_act = rotated(section_out, "pipe", 1)
 
+    sections = jnp.stack([section, last_section * jnp.ones_like(section)])
+    next_grad = choose(sections, loss_grad, moved)
     qkv_grads = unpack(exchange(grads))
-    return (next_act[None], settle(next_grad)[None], qkv_grads[None])
+    return (next_act[None], next_grad[None], qkv_grads[None])
 
 
 def solution(mesh):

time: 181 us -> 192 us (1.061)
  waiting for transfers between devices: 67.7 us -> 82.8 us
  local copies, waits for them, and re-layouts: 11 us -> 5.63 us
  other arithmetic: 6.62 us -> 9.31 us
  Pallas kernels: 49.7 us -> 47.6 us
    ppermute x1, waiting for transfers between devices: 0.51 us -> 25.2 us  [body(): g_across = lax.ppermute(g_scaled, 'seq', YSWAP)]
    all_to_all x3, waiting for transfers between devices: 30.8 us -> 8.01 us  [exchange(): return lax.all_to_all(array, 'seq', 0, 0, tiled=True)]
    ppermute x2 -> x1, waiting for transfers between devices: 13.8 us -> 20.3 us  [rotated(): lax.ppermute(array, axis, [(i, (i + by) % length) for i in range(length)])]
    unnamed x45, local copies, waits for them, and re-layouts: 9.73 us -> 4.35 us
    ppermute x9, waiting for transfers between devices: 19.6 us -> 22.8 us  [along_x(): lax.ppermute(array, 'seq', [(i, (i + PER_X * offset) % count) for i in ra...]
    pallas_call x1, Pallas kernels: 14.8 us -> 12.1 us  [attention_forward(): pl.pallas_call(forward_kernel, out_shape=(jax.ShapeDtypeStruct((total //...]
    ppermute x2 -> x1, starting transfers between devices: 10.6 us -> 7.95 us  [rotated(): lax.ppermute(array, axis, [(i, (i + by) % length) for i in range(length)])]
    ppermute x2 -> x3, starting transfers between devices: 3.08 us -> 4.26 us  [the longest x1 1.79 us: body(): received = lax.ppermute(part_send, 'seq', CORE)]
  transfers between devices with their start and end apart: 19 -> 19, of which waited for: 8 -> 11; matrix products, arithmetic and copies ran while one was open for 4% -> 4% of each run, Pallas kernels for 28% -> 22%
where the time goes in v3:
time: 192 us; the launch traced here: 191 us
  waiting for transfers between devices  82.8 us (43%)
  Pallas kernels  47.6 us (25%)
  starting transfers between devices  44.6 us (23%)
  other arithmetic  9.31 us (5%)
  local copies, waits for them, and re-layouts  5.63 us (3%)
    ppermute x1, waiting for transfers between devices, body(): g_across = lax.ppermute(g_scaled, 'seq', YSWAP)  25.2 us
    ppermute x9, waiting for transfers between devices, along_x(): lax.ppermute(array, 'seq', [(i, (i + PER_X * offset) % count) for i in ra...  22.8 us
    ppermute x1, waiting for transfers between devices, rotated(): lax.ppermute(array, axis, [(i, (i + by) % length) for i in range(length)])  20.3 us
    all_to_all x3, starting transfers between devices, exchange(): return lax.all_to_all(array, 'seq', 0, 0, tiled=True)  16.5 us
    pallas_call x1, Pallas kernels, attention_backward(): pl.pallas_call(backward_kernel, out_shape=jax.ShapeDtypeStruct((blocks, 3...  16.5 us
    ppermute x9, starting transfers between devices, along_x(): lax.ppermute(array, 'seq', [(i, (i + PER_X * offset) % count) for i in ra...  13.8 us
    pallas_call x1, Pallas kernels, attention_forward(): pl.pallas_call(forward_kernel, out_shape=(jax.ShapeDtypeStruct((total //...  12.1 us
    all_to_all x3, waiting for transfers between devices, exchange(): return lax.all_to_all(array, 'seq', 0, 0, tiled=True)  8.01 us
  transfers between devices with their start and end apart: 19, of which 11 were waited for; matrix products, arithmetic and copies ran while one was open for 4% of the time, Pallas kernels for 22%

profile of v3, /device:TPU:1, one launch (start us, length us, event | category | flops | bytes accessed | tf_op | source)
XLA Modules:
  0.0 190.8 jit_solution(10042850935887057414)
XLA Ops:
  0.6 3.7 %collective-permute-start.5 = (bf16[128,3072]{1,0:T(8,128)(2,1)}, bf16[128,3072]{1,0:T(8,128)(2,1)S(1)}, u32[]{:S(2)}, u32[]{:S(2)}) collective-permute-start(bf16[128,3072]{1,0:T(8,128)(2,1)} %bitcast.23), channel_id=1, source_target_pairs={{0,8},{1,9},{2,10},{3,11},{4,12},{5,13},{6,14},{7,15},{8,0},{9,1},... | collective-permute-start | bytes 2359304 | tf_op jit(solution)/shard_map/ppermute | solution.py:30
  5.8 1.3 collective-permute-start.6
  8.3 2.8 %pack.2 = bf16[16,400,128]{2,1,0:T(8,128)(2,1)} custom-call(s32[1,128]{1,0:T(1,128)} %get-tuple-element.28.seg_ref, bf16[1,2,128,2048]{3,2,1,0:T(8,128)(2,1)} %q_ref.3, bf16[1,2,128,2048]{3,2,1,0:T(8,128)(2,1)} %k_ref.3, bf16[1,2,128,2048]{3,2,1,0:T(8,128)(2,1)} %v_ref.3), custom_call_target="tpu_custom_call" | custom-call | flops 2000000000 | tf_op jit(solution)/shard_map/pack/pallas_call | solution.py:84
  11.2 6.3 %all-to-all-start = ((bf16[16,400,128]{2,1,0:T(8,128)(2,1)}), bf16[16,400,128]{2,1,0:T(8,128)(2,1)}, u32[]{:S(2)}, u32[]{:S(2)}) async-start(bf16[16,400,128]{2,1,0:T(8,128)(2,1)} %pack.2), calls=%async_computation | async-start | bytes 3276800 | tf_op jit(solution)/shard_map/all_to_all | solution.py:473
  18.8 1.5 collective-permute-start.1
  20.9 18.4 %collective-permute-done.4.refs_3_.refs_6_ = bf16[128,3072]{1,0:T(8,128)(2,1)S(1)} collective-permute-done((bf16[128,3072]{1,0:T(8,128)(2,1)}, bf16[128,3072]{1,0:T(8,128)(2,1)S(1)}, u32[]{:S(2)}, u32[]{:S(2)}) %collective-permute-start.4) | collective-permute-done | bytes 786464 | tf_op jit(solution)/shard_map/ppermute | solution.py:30
  39.4 25.2 %collective-permute-done.1.refs_0_.refs_2_ = bf16[128,3072]{1,0:T(8,128)(2,1)} collective-permute-done((bf16[128,3072]{1,0:T(8,128)(2,1)S(1)}, bf16[128,3072]{1,0:T(8,128)(2,1)}, u32[]{:S(2)}, u32[]{:S(2)}) %collective-permute-start.1) | collective-permute-done | bytes 786464 | tf_op jit(solution)/shard_map/ppermute | solution.py:488
  64.6 2.9 %pack.3.refs_8_ = bf16[16,400,128]{2,1,0:T(8,128)(2,1)} custom-call(s32[1,128]{1,0:T(1,128)} %get-tuple-element.27.seg_ref, bf16[1,2,128,2048]{3,2,1,0:T(8,128)(2,1)} %q_ref.3, bf16[1,2,128,2048]{3,2,1,0:T(8,128)(2,1)} %k_ref.3, bf16[1,2,128,2048]{3,2,1,0:T(8,128)(2,1)} %v_ref.3, bf16[128,3072]{1,0:T(8,128)(2,1)} %collective-permute-done.1.refs_0_.refs_2_, ...), custom_call_target="tpu_custom_call" | custom-call | flops 2000000000 | tf_op jit(solution)/shard_map/pack/pallas_call | solution.py:84
  67.5 5.0 %all-to-all-start.1 = ((bf16[16,400,128]{2,1,0:T(8,128)(2,1)}), bf16[16,400,128]{2,1,0:T(8,128)(2,1)S(1)}, u32[]{:S(2)}, u32[]{:S(2)}) async-start(bf16[16,400,128]{2,1,0:T(8,128)(2,1)} %pack.3.refs_8_), calls=%async_computation.1 | async-start | bytes 3276800 | tf_op jit(solution)/shard_map/all_to_all | solution.py:473
  73.1 1.8 collective-permute-done.refs_1_
  75.0 1.4 collective-permute-done.2.refs_3_
  76.4 5.5 %attention_grad.1 = (bf16[512,128]{1,0:T(8,128)(2,1)}, bf16[512,128]{1,0:T(8,128)(2,1)}, bf16[512,128]{1,0:T(8,128)(2,1)}, bf16[512,128]{1,0:T(8,128)(2,1)}) custom-call(s32[1]{0:T(128)} %bitcast.3.place_ref, bf16[128,3072]{1,0:T(8,128)(2,1)} %copy-done.13, bf16[128,3072]{1,0:T(8,128)(2,1)} %copy-done.17, ...), custom_call_target="tpu_custom_call" | custom-call | flops 200000000 | tf_op jit(solution)/shard_map/attention_grad/pallas_call | solution.py:349
  81.8 2.7 %collective-permute-start.8 = (bf16[512,128]{1,0:T(8,128)(2,1)}, bf16[512,128]{1,0:T(8,128)(2,1)S(1)}, u32[]{:S(2)}, u32[]{:S(2)}) collective-permute-start(bf16[512,128]{1,0:T(8,128)(2,1)} %get-tuple-element.18), channel_id=1, source_target_pairs={{0,12},{1,13},{2,14},{3,15},{4,0},{5,1},{6,2},{7,3},{8,4},{9,5},{1... | collective-permute-start | bytes 393224 | tf_op jit(solution)/shard_map/ppermute | solution.py:30
  84.5 1.8 collective-permute-start.10
  86.3 1.7 multiply_reduce_fusion.1.refs_1_
  88.0 12.1 %attention_forward.1 = (bf16[512,128]{1,0:T(8,128)(2,1)}, bf16[512,128]{1,0:T(8,128)(2,1)}, bf16[512,128]{1,0:T(8,128)(2,1)}, bf16[512,128]{1,0:T(8,128)(2,1)}) custom-call(s32[1]{0:T(128)} %bitcast.3.place_ref, bf16[16,400,128]{2,1,0:T(8,128)(2,1)} %all-to-all-done.in_hbm_ref, bf16[512,128]{1,0:T(8,128)(2,1)} %get-tuple-element.14.refs_0_, ...), custom_call_target="tpu_custom_call" | custom-call | flops 200000000 | tf_op jit(solution)/shard_map/attention_forward/pallas_call | solution.py:198
  100.1 1.6 collective-permute-start.7
  104.0 2.1 %collective-permute-start.11 = (bf16[512,128]{1,0:T(8,128)(2,1)}, bf16[512,128]{1,0:T(8,128)(2,1)S(1)}, u32[]{:S(2)}, u32[]{:S(2)}) collective-permute-start(bf16[512,128]{1,0:T(8,128)(2,1)} %copy-done.6), channel_id=1, source_target_pairs={{0,12},{1,13},{2,14},{3,15},{4,0},{5,1},{6,2},{7,3},{8,4},{9,5},{1... | collective-permute-start | bytes 393224 | tf_op jit(solution)/shard_map/ppermute | solution.py:30
  106.1 2.2 %collective-permute-done.12.refs_3_ = bf16[512,128]{1,0:T(8,128)(2,1)S(1)} collective-permute-done((bf16[512,128]{1,0:T(8,128)(2,1)}, bf16[512,128]{1,0:T(8,128)(2,1)S(1)}, u32[]{:S(2)}, u32[]{:S(2)}) %collective-permute-start.12) | collective-permute-done | bytes 131104 | tf_op jit(solution)/shard_map/ppermute | solution.py:30
  108.2 1.5 collective-permute-done.11.refs_2_
  111.0 4.8 %project.1 = (f32[128,3072]{1,0:T(8,128)}, f32[128,3072]{1,0:T(8,128)}, bf16[256,3072]{1,0:T(8,128)(2,1)}) custom-call(s32[1]{0:T(128)} %bitcast.3.place_ref, bf16[512,128]{1,0:T(8,128)(2,1)} %get-tuple-element.15.refs_0_, bf16[512,128]{1,0:T(8,128)(2,1)} %copy-done.18, bf16[512,128]{1,0:T(8,128)(2,1)} %copy-done.20, bf16[512,128]{1,0:T(8,128)(2,1)} %copy-done.19, ...), custom_call_target="tpu_custom_call" | custom-call | flops 200000000 | tf_op jit(solution)/shard_map/project/pallas_call | solution.py:401
  115.8 1.8 collective-permute-start.13
  117.6 3.2 %collective-permute-done.13 = bf16[256,3072]{1,0:T(8,128)(2,1)S(1)} collective-permute-done((bf16[256,3072]{1,0:T(8,128)(2,1)}, bf16[256,3072]{1,0:T(8,128)(2,1)S(1)}, u32[]{:S(2)}, u32[]{:S(2)}) %collective-permute-start.13) | collective-permute-done | bytes 1572896 | tf_op jit(solution)/shard_map/ppermute | solution.py:503
  120.8 3.0 %add_convert_fusion.refs_4_ = bf16[128,3072]{1,0:T(8,128)(2,1)} fusion(f32[128,3072]{1,0:T(8,128)} %get-tuple-element.24, bf16[256,3072]{1,0:T(8,128)(2,1)S(1)} %collective-permute-done.13), kind=kLoop, calls=%fused_computation.4 | loop fusion | flops 1179648 | bytes 3145728 | tf_op jit(solution)/shard_map/convert_element_type | solution.py:505
  125.1 16.5 %attention_backward.1 = bf16[16,384,128]{2,1,0:T(8,128)(2,1)} custom-call(s32[1]{0:T(128)} %bitcast.3.place_ref, bf16[16,400,128]{2,1,0:T(8,128)(2,1)} %copy-done.12, bf16[512,128]{1,0:T(8,128)(2,1)} %get-tuple-element.14.refs_0_, bf16[512,128]{1,0:T(8,128)(2,1)} %copy-done.2, bf16[512,128]{1,0:T(8,128)(2,1)} %copy-done.3, bf16[512,128]{1,0:T(8,128)(2,1)} %copy-done.4, ...), custom_call_target="tpu_custom_call" | custom-call | flops 30000001024 | tf_op jit(solution)/shard_map/attention_backward/pallas_call | solution.py:294
  141.5 5.2 %all-to-all-start.2 = ((bf16[16,384,128]{2,1,0:T(8,128)(2,1)}), bf16[16,384,128]{2,1,0:T(8,128)(2,1)S(1)}, u32[]{:S(2)}, u32[]{:S(2)}) async-start(bf16[16,384,128]{2,1,0:T(8,128)(2,1)} %attention_backward.1), calls=%async_computation.2 | async-start | bytes 3145728 | tf_op jit(solution)/shard_map/all_to_all | solution.py:473
  146.8 3.7 %fusion.1 = bf16[128,3072]{1,0:T(8,128)(2,1)} fusion(bf16[128,3072]{1,0:T(8,128)(2,1)} %param.18, f32[128,3072]{1,0:T(8,128)S(1)} %copy-done.8, bf16[128,3072]{1,0:T(8,128)(2,1)} %collective-permute-done.14, f32[128,3072]{1,0:T(8,128)} %get-tuple-element.22, bf16[256,3072]{1,0:T(8,128)(2,1)} %copy-done.15, bf16[1,128,3072]{2,1,0:T(8,128)(2,1)} %param.10, ...), kind=kLoop, calls=%fused_computation.6 | loop fusion | flops 3538944 | bytes 7077889 | tf_op jit(solution)/shard_map/jit(_where)/select_n | solution.py:510
  150.5 8.0 %collective-permute-start.15 = (bf16[128,3072]{1,0:T(8,128)(2,1)}, bf16[128,3072]{1,0:T(8,128)(2,1)S(1)}, u32[]{:S(2)}, u32[]{:S(2)}) collective-permute-start(bf16[128,3072]{1,0:T(8,128)(2,1)} %fusion.1), channel_id=1, source_target_pairs={{0,16},{16,32},{32,48},{48,64},{64,80},{80,96},{96,112},{112,128},... | collective-permute-start | bytes 2359304 | tf_op jit(solution)/shard_map/ppermute | solution.py:464
  158.6 1.5 choose.1
  160.1 8.0 %all-to-all-done.2.in_ref = bf16[16,384,128]{2,1,0:T(8,128)(2,1)S(1)} async-done(((bf16[16,384,128]{2,1,0:T(8,128)(2,1)}), bf16[16,384,128]{2,1,0:T(8,128)(2,1)S(1)}, u32[]{:S(2)}, u32[]{:S(2)}) %all-to-all-start.2) | async-done | bytes 1572896 | tf_op jit(solution)/shard_map/all_to_all | solution.py:473
  168.1 1.6 unpack.1
  169.7 20.3 %collective-permute-done.15 = bf16[128,3072]{1,0:T(8,128)(2,1)S(1)} collective-permute-done((bf16[128,3072]{1,0:T(8,128)(2,1)}, bf16[128,3072]{1,0:T(8,128)(2,1)S(1)}, u32[]{:S(2)}, u32[]{:S(2)}) %collective-permute-start.15) | collective-permute-done | bytes 786464 | tf_op jit(solution)/shard_map/ppermute | solution.py:464
  (70 shorter events, 11.0 us)
Async XLA Ops:
  0.6 20.2 %collective-permute-start.5 = (bf16[128,3072]{1,0:T(8,128)(2,1)}, bf16[128,3072]{1,0:T(8,128)(2,1)S(1)}, u32[]{:S(2)}, u32[]{:S(2)}) collective-permute-start(bf16[128,3072]{1,0:T(8,128)(2,1)} %bitcast.23), channel_id=1, source_target_pairs={{0,8},{1,9},{2,10},{3,11},{4,12},{5,13},{6,14},{7,15},{8,0},{9,1},... | collective-permute-start | bytes 2359304 | tf_op jit(solution)/shard_map/ppermute | solution.py:30
  4.3 35.0 %collective-permute-start.4 = (bf16[128,3072]{1,0:T(8,128)(2,1)}, bf16[128,3072]{1,0:T(8,128)(2,1)S(1)}, u32[]{:S(2)}, u32[]{:S(2)}) collective-permute-start(bf16[128,3072]{1,0:T(8,128)(2,1)} %bitcast.24), channel_id=1, source_target_pairs={{0,12},{1,13},{2,14},{3,15},{4,0},{5,1},{6,2},{7,3},{8,4},{9,5},{1... | collective-permute-start | bytes 2359304 | tf_op jit(solution)/shard_map/ppermute | solution.py:30
  5.2 34.2 %collective-permute-start.3 = (bf16[128,3072]{1,0:T(8,128)(2,1)}, bf16[128,3072]{1,0:T(8,128)(2,1)S(1)}, u32[]{:S(2)}, u32[]{:S(2)}) collective-permute-start(bf16[128,3072]{1,0:T(8,128)(2,1)} %bitcast.25), channel_id=1, source_target_pairs={{0,4},{1,5},{2,6},{3,7},{4,8},{5,9},{6,10},{7,11},{8,12},{9,13},{1... | collective-permute-start | bytes 2359304 | tf_op jit(solution)/shard_map/ppermute | solution.py:30
  5.8 33.6 %collective-permute-start.6 = (bf16[128,3072]{1,0:T(8,128)(2,1)}, bf16[128,3072]{1,0:T(8,128)(2,1)S(1)}, u32[]{:S(2)}, u32[]{:S(2)}) collective-permute-start(bf16[128,3072]{1,0:T(8,128)(2,1)} %bitcast.29), channel_id=1, source_target_pairs={{16,0},{32,16},{48,32},{64,48},{80,64},{96,80},{112,96},{128,112},... | collective-permute-start | bytes 2359304 | tf_op jit(solution)/shard_map/ppermute | solution.py:459
  11.2 6.3 %copy-start.21 = (f32[1,2,4,3072]{3,2,1,0:T(4,128)S(1)}, f32[1,2,4,3072]{3,2,1,0:T(4,128)}, u32[]{:S(2)}) copy-start(f32[1,2,4,3072]{3,2,1,0:T(4,128)} %param.15) | copy-start | bytes 294916
  11.2 56.3 %all-to-all-start = ((bf16[16,400,128]{2,1,0:T(8,128)(2,1)}), bf16[16,400,128]{2,1,0:T(8,128)(2,1)}, u32[]{:S(2)}, u32[]{:S(2)}) async-start(bf16[16,400,128]{2,1,0:T(8,128)(2,1)} %pack.2), calls=%async_computation | async-start | bytes 3276800 | tf_op jit(solution)/shard_map/all_to_all | solution.py:473
  18.8 20.6 %copy-start.13 = (bf16[128,3072]{1,0:T(8,128)(2,1)}, bf16[128,3072]{1,0:T(8,128)(2,1)S(1)}, u32[]{:S(2)}) copy-start(bf16[128,3072]{1,0:T(8,128)(2,1)S(1)} %multiply_convert_fusion.refs_0_) | copy-start | bytes 2359300
  18.8 45.8 %collective-permute-start.1 = (bf16[128,3072]{1,0:T(8,128)(2,1)S(1)}, bf16[128,3072]{1,0:T(8,128)(2,1)}, u32[]{:S(2)}, u32[]{:S(2)}) collective-permute-start(bf16[128,3072]{1,0:T(8,128)(2,1)S(1)} %multiply_convert_fusion.refs_0_), channel_id=1, source_target_pairs={{0,2},{1,3},{2,0},{3,1},{4,6},{5,7},{6,4},{7,5},{8,10},{9,11},{10,... | collective-permute-start | bytes 2359304 | tf_op jit(solution)/shard_map/ppermute | solution.py:488
  20.9 43.8 %copy-start.9 = (bf16[128,3072]{1,0:T(8,128)(2,1)}, bf16[128,3072]{1,0:T(8,128)(2,1)S(1)}, u32[]{:S(2)}) copy-start(bf16[128,3072]{1,0:T(8,128)(2,1)S(1)} %collective-permute-done.5.refs_4_.refs_7_) | copy-start | bytes 2359300
  39.3 25.4 %copy-start.10 = (bf16[128,3072]{1,0:T(8,128)(2,1)}, bf16[128,3072]{1,0:T(8,128)(2,1)S(1)}, u32[]{:S(2)}) copy-start(bf16[128,3072]{1,0:T(8,128)(2,1)S(1)} %collective-permute-done.4.refs_3_.refs_6_) | copy-start | bytes 2359300
  39.4 25.3 %copy-start.11 = (bf16[128,3072]{1,0:T(8,128)(2,1)}, bf16[128,3072]{1,0:T(8,128)(2,1)S(1)}, u32[]{:S(2)}) copy-start(bf16[128,3072]{1,0:T(8,128)(2,1)S(1)} %collective-permute-done.3.refs_2_.refs_5_) | copy-start | bytes 2359300
  39.4 25.3 %copy-start = (bf16[128,3072]{1,0:T(8,128)(2,1)}, bf16[128,3072]{1,0:T(8,128)(2,1)S(1)}, u32[]{:S(2)}) copy-start(bf16[128,3072]{1,0:T(8,128)(2,1)S(1)} %collective-permute-done.6.refs_1_.second_ref) | copy-start | bytes 2359300
  67.5 5.0 %copy-start.14 = (bf16[128,3072]{1,0:T(8,128)(2,1)S(1)}, bf16[128,3072]{1,0:T(8,128)(2,1)}, u32[]{:S(2)}) copy-start(bf16[128,3072]{1,0:T(8,128)(2,1)} %copy-done.13) | copy-start | bytes 2359300
  67.5 42.2 %all-to-all-start.1 = ((bf16[16,400,128]{2,1,0:T(8,128)(2,1)}), bf16[16,400,128]{2,1,0:T(8,128)(2,1)S(1)}, u32[]{:S(2)}, u32[]{:S(2)}) async-start(bf16[16,400,128]{2,1,0:T(8,128)(2,1)} %pack.3.refs_8_), calls=%async_computation.1 | async-start | bytes 3276800 | tf_op jit(solution)/shard_map/all_to_all | solution.py:473
  72.5 2.4 %collective-permute-start = (bf16[128,3072]{1,0:T(8,128)(2,1)S(1)}, bf16[128,3072]{1,0:T(8,128)(2,1)S(1)}, u32[]{:S(2)}, u32[]{:S(2)}) collective-permute-start(bf16[128,3072]{1,0:T(8,128)(2,1)S(1)} %copy-done.14), channel_id=1, source_target_pairs={{0,1},{1,0},{2,3},{3,2},{4,5},{5,4},{6,7},{7,6},{8,9},{9,8},{10,11... | collective-permute-start | bytes 2359304 | tf_op jit(solution)/shard_map/ppermute | solution.py:489
  72.7 3.6 %collective-permute-start.2 = (bf16[128,3072]{1,0:T(8,128)(2,1)}, bf16[128,3072]{1,0:T(8,128)(2,1)}, u32[]{:S(2)}, u32[]{:S(2)}) collective-permute-start(bf16[128,3072]{1,0:T(8,128)(2,1)} %collective-permute-done.1.refs_0_.refs_2_), channel_id=1, source_target_pairs={{0,1},{1,0},{2,3},{3,2},{4,5},{5,4},{6,7},{7,6},{8,9},{9,8},{10,11... | collective-permute-start | bytes 2359304 | tf_op jit(solution)/shard_map/ppermute | solution.py:490
  81.8 20.4 %collective-permute-start.8 = (bf16[512,128]{1,0:T(8,128)(2,1)}, bf16[512,128]{1,0:T(8,128)(2,1)S(1)}, u32[]{:S(2)}, u32[]{:S(2)}) collective-permute-start(bf16[512,128]{1,0:T(8,128)(2,1)} %get-tuple-element.18), channel_id=1, source_target_pairs={{0,12},{1,13},{2,14},{3,15},{4,0},{5,1},{6,2},{7,3},{8,4},{9,5},{1... | collective-permute-start | bytes 393224 | tf_op jit(solution)/shard_map/ppermute | solution.py:30
  84.5 17.8 %collective-permute-start.9 = (bf16[512,128]{1,0:T(8,128)(2,1)}, bf16[512,128]{1,0:T(8,128)(2,1)S(1)}, u32[]{:S(2)}, u32[]{:S(2)}) collective-permute-start(bf16[512,128]{1,0:T(8,128)(2,1)} %get-tuple-element.19), channel_id=1, source_target_pairs={{0,4},{1,5},{2,6},{3,7},{4,8},{5,9},{6,10},{7,11},{8,12},{9,13},{1... | collective-permute-start | bytes 393224 | tf_op jit(solution)/shard_map/ppermute | solution.py:30
  84.5 17.8 %collective-permute-start.10 = (bf16[512,128]{1,0:T(8,128)(2,1)}, bf16[512,128]{1,0:T(8,128)(2,1)S(1)}, u32[]{:S(2)}, u32[]{:S(2)}) collective-permute-start(bf16[512,128]{1,0:T(8,128)(2,1)} %get-tuple-element.20), channel_id=1, source_target_pairs={{0,8},{1,9},{2,10},{3,11},{4,12},{5,13},{6,14},{7,15},{8,0},{9,1},... | collective-permute-start | bytes 393224 | tf_op jit(solution)/shard_map/ppermute | solution.py:30
  100.1 6.0 %collective-permute-start.7 = (bf16[512,128]{1,0:T(8,128)(2,1)}, bf16[512,128]{1,0:T(8,128)(2,1)S(1)}, u32[]{:S(2)}, u32[]{:S(2)}) collective-permute-start(bf16[512,128]{1,0:T(8,128)(2,1)} %get-tuple-element.16), channel_id=1, source_target_pairs={{0,4},{1,5},{2,6},{3,7},{4,8},{5,9},{6,10},{7,11},{8,12},{9,13},{1... | collective-permute-start | bytes 393224 | tf_op jit(solution)/shard_map/ppermute | solution.py:30
  101.7 6.6 %collective-permute-start.12 = (bf16[512,128]{1,0:T(8,128)(2,1)}, bf16[512,128]{1,0:T(8,128)(2,1)S(1)}, u32[]{:S(2)}, u32[]{:S(2)}) collective-permute-start(bf16[512,128]{1,0:T(8,128)(2,1)} %get-tuple-element.21), channel_id=1, source_target_pairs={{0,8},{1,9},{2,10},{3,11},{4,12},{5,13},{6,14},{7,15},{8,0},{9,1},... | collective-permute-start | bytes 393224 | tf_op jit(solution)/shard_map/ppermute | solution.py:30
  102.3 13.5 %copy-start.2 = (bf16[512,128]{1,0:T(8,128)(2,1)}, bf16[512,128]{1,0:T(8,128)(2,1)S(1)}, u32[]{:S(2)}) copy-start(bf16[512,128]{1,0:T(8,128)(2,1)S(1)} %collective-permute-done.8.refs_0_.refs_1_) | copy-start | bytes 393220
  102.3 13.5 %copy-start.3 = (bf16[512,128]{1,0:T(8,128)(2,1)}, bf16[512,128]{1,0:T(8,128)(2,1)S(1)}, u32[]{:S(2)}) copy-start(bf16[512,128]{1,0:T(8,128)(2,1)S(1)} %collective-permute-done.9.refs_1_.refs_2_) | copy-start | bytes 393220
  102.3 13.5 %copy-start.4 = (bf16[512,128]{1,0:T(8,128)(2,1)}, bf16[512,128]{1,0:T(8,128)(2,1)S(1)}, u32[]{:S(2)}) copy-start(bf16[512,128]{1,0:T(8,128)(2,1)S(1)} %collective-permute-done.10.refs_2_.refs_3_) | copy-start | bytes 393220
  104.0 5.7 %collective-permute-start.11 = (bf16[512,128]{1,0:T(8,128)(2,1)}, bf16[512,128]{1,0:T(8,128)(2,1)S(1)}, u32[]{:S(2)}, u32[]{:S(2)}) collective-permute-start(bf16[512,128]{1,0:T(8,128)(2,1)} %copy-done.6), channel_id=1, source_target_pairs={{0,12},{1,13},{2,14},{3,15},{4,0},{5,1},{6,2},{7,3},{8,4},{9,5},{1... | collective-permute-start | bytes 393224 | tf_op jit(solution)/shard_map/ppermute | solution.py:30
  115.8 5.0 %collective-permute-start.13 = (bf16[256,3072]{1,0:T(8,128)(2,1)}, bf16[256,3072]{1,0:T(8,128)(2,1)S(1)}, u32[]{:S(2)}, u32[]{:S(2)}) collective-permute-start(bf16[256,3072]{1,0:T(8,128)(2,1)} %get-tuple-element.23), channel_id=1, source_target_pairs={{0,1},{1,0},{2,3},{3,2},{4,5},{5,4},{6,7},{7,6},{8,9},{9,8},{10,11... | collective-permute-start | bytes 4718600 | tf_op jit(solution)/shard_map/ppermute | solution.py:503
  123.9 22.9 %collective-permute-start.14 = (bf16[128,3072]{1,0:T(8,128)(2,1)}, bf16[128,3072]{1,0:T(8,128)(2,1)}, u32[]{:S(2)}, u32[]{:S(2)}) collective-permute-start(bf16[128,3072]{1,0:T(8,128)(2,1)} %add_convert_fusion.refs_4_), channel_id=1, source_target_pairs={{0,2},{1,3},{2,0},{3,1},{4,6},{5,7},{6,4},{7,5},{8,10},{9,11},{10,... | collective-permute-start | bytes 2359304 | tf_op jit(solution)/shard_map/ppermute | solution.py:507
  141.5 5.2 %copy-start.8 = (f32[128,3072]{1,0:T(8,128)S(1)}, f32[128,3072]{1,0:T(8,128)}, u32[]{:S(2)}) copy-start(f32[128,3072]{1,0:T(8,128)} %multiply_reduce_fusion.1.refs_1_) | copy-start | bytes 4718596
  141.5 26.5 %all-to-all-start.2 = ((bf16[16,384,128]{2,1,0:T(8,128)(2,1)}), bf16[16,384,128]{2,1,0:T(8,128)(2,1)S(1)}, u32[]{:S(2)}, u32[]{:S(2)}) async-start(bf16[16,384,128]{2,1,0:T(8,128)(2,1)} %attention_backward.1), calls=%async_computation.2 | async-start | bytes 3145728 | tf_op jit(solution)/shard_map/all_to_all | solution.py:473
  146.8 11.8 %copy-start.1 = (bf16[128,3072]{1,0:T(8,128)(2,1)S(1)}, bf16[128,3072]{1,0:T(8,128)(2,1)}, u32[]{:S(2)}) copy-start(bf16[128,3072]{1,0:T(8,128)(2,1)} %copy-done) | copy-start | bytes 2359300
  146.8 11.8 %copy-start.7 = (bf16[128,3072]{1,0:T(8,128)(2,1)S(1)}, bf16[128,3072]{1,0:T(8,128)(2,1)}, u32[]{:S(2)}) copy-start(bf16[128,3072]{1,0:T(8,128)(2,1)} %first_ref.1) | copy-start | bytes 2359300
  150.5 39.4 %collective-permute-start.15 = (bf16[128,3072]{1,0:T(8,128)(2,1)}, bf16[128,3072]{1,0:T(8,128)(2,1)S(1)}, u32[]{:S(2)}, u32[]{:S(2)}) collective-permute-start(bf16[128,3072]{1,0:T(8,128)(2,1)} %fusion.1), channel_id=1, source_target_pairs={{0,16},{16,32},{32,48},{48,64},{64,80},{80,96},{96,112},{112,128},... | collective-permute-start | bytes 2359304 | tf_op jit(solution)/shard_map/ppermute | solution.py:464
  (9 other events, 14.3 us)

commit v4 on v3

--- a/solution.py
+++ b/solution.py
@@ -11,7 +11,7 @@
 SCALE = HD ** (-0.5)
 EXP2 = SCALE * 1.4426950408889634
 LOW = -1e30
-QB = 256
+QB = 512
 KT = 512
 SEG_ROWS = 16
 F32 = jnp.float32
@@ -136,14 +136,18 @@
 
 
 def fill_samples(seg_s, starts):
-    total = seg_s.shape[0]
-    for i in range(total // 256):
+    for i in range(seg_s.shape[0] // 256):
         position = i * 256 + lax.broadcasted_iota(jnp.int32, (256, HD), 0)
         seg_s[i * 256:(i + 1) * 256, :] = sample_of(position, starts)
 
 
+def masked_scores(k, q, seg_k, seg_q):
+    same = jnp.concatenate([seg_k] * (QB // HD), axis=1) == seg_q
+    return jnp.where(same, dot(k, q, ((1,), (0,))), LOW)
+
+
 def forward_kernel(place_ref, in_hbm_ref, *refs):
-    outs, (in_ref, out_s, vt_s, seg_s, in_sem, out_sems) = refs[-6 - XN:-6], refs[-6:]
+    outs, (in_ref, out_s, vt_s, seg_s, qt_s, in_sem, out_sems) = refs[-7 - XN:-7], refs[-7:]
     arriving = pltpu.make_async_copy(in_hbm_ref, in_ref, in_sem)
     arriving.start()
     arriving.wait()
@@ -158,14 +162,15 @@
         q = block_rows(in_ref, i, QB, 0, rows)
         first = i * QB
         seg_q = sample_of(first + lax.broadcasted_iota(jnp.int32, (1, QB), 1), starts)
+        qt_s[...] = q.T
         begin, end = tile_range(first, first + QB - 1, starts, total)
 
         def per_tile(t, carry):
             m, l, acc = carry
-            k = block_rows(in_ref, t, KT, rows, rows)
-            s = dot(k, q, ((1,), (1,)))
-            seg_k = seg_s[pl.ds(pl.multiple_of(t * KT, KT), KT), :]
-            s = jnp.where(jnp.concatenate([seg_k, seg_k], axis=1) == seg_q, s, LOW)
+            here = pl.ds(pl.multiple_of(t * KT, KT), KT)
+            s = masked_scores(
+                block_rows(in_ref, t, KT, rows, rows), qt_s[...], seg_s[here, :], seg_q
+            )
             m_new = jnp.maximum(m, jnp.max(s, axis=0, keepdims=True))
             p = jnp.exp2((s - m_new) * EXP2)
             alpha = jnp.exp2((m - m_new) * EXP2)
@@ -205,6 +210,7 @@
             pltpu.VMEM((XN, total // XN, HD), BF16),
             pltpu.VMEM((HD, total), BF16),
             pltpu.VMEM((total, HD), F32),
+            pltpu.VMEM((HD, QB), BF16),
             pltpu.SemaphoreType.DMA,
             pltpu.SemaphoreType.DMA((XN,)),
         ],
@@ -216,7 +222,8 @@
 
 def backward_kernel(place_ref, in_hbm_ref, *refs):
     g_refs = refs[:XN]
-    out_ref, in_ref, g_ref, out_s, kt_s, seg_s, s_s, dp_s, dk_s, dv_s, in_sems, out_sem = refs[-12:]
+    out_ref, in_ref, g_ref, out_s, kt_s, seg_s, qt_s, gt_s, p_s, dp_s, top_s, dk_s, dv_s, *sems = refs[-15:]
+    in_sems, out_sem = sems
     packed = pltpu.make_async_copy(in_hbm_ref, in_ref, in_sems.at[XN])
     packed.start()
     blocks, rows = in_ref.shape[0], 128
@@ -242,19 +249,22 @@
         g = g_ref[i // share, pl.ds(pl.multiple_of(i % share * QB, QB), QB), :]
         first = i * QB
         seg_q = sample_of(first + lax.broadcasted_iota(jnp.int32, (1, QB), 1), starts)
+        qt_s[...] = q.T
+        gt_s[...] = g.T
         begin, end = tile_range(first, first + QB - 1, starts, total)
 
         def scores(t, carry):
             m, l, d = carry
             here = pl.ds(pl.multiple_of(t * KT, KT), KT)
-            s = dot(block_rows(in_ref, t, KT, rows, rows), q, ((1,), (1,)))
-            dp = dot(block_rows(in_ref, t, KT, 2 * rows, rows), g, ((1,), (1,)))
-            seg_k = seg_s[here, :]
-            s = jnp.where(jnp.concatenate([seg_k, seg_k], axis=1) == seg_q, s, LOW)
-            s_s[here, :] = s
+            s = masked_scores(
+                block_rows(in_ref, t, KT, rows, rows), qt_s[...], seg_s[here, :], seg_q
+            )
+            dp = dot(block_rows(in_ref, t, KT, 2 * rows, rows), gt_s[...], ((1,), (0,)))
             dp_s[here, :] = dp
             m_new = jnp.maximum(m, jnp.max(s, axis=0, keepdims=True))
             p = jnp.exp2((s - m_new) * EXP2)
+            p_s[here, :] = p
+            top_s[t] = m_new
             alpha = jnp.exp2((m - m_new) * EXP2)
             l = l * alpha + jnp.sum(p, axis=0, keepdims=True)
             d = d * alpha + jnp.sum(p * dp, axis=0, keepdims=True)
@@ -267,7 +277,7 @@
 
         def grads(t, acc):
             here = pl.ds(pl.multiple_of(t * KT, KT), KT)
-            p = jnp.exp2((s_s[here, :] - m) * EXP2) * inverse
+            p = p_s[here, :] * (jnp.exp2((top_s[t] - m) * EXP2) * inverse)
             ds = (p * (dp_s[here, :] - delta)).astype(BF16)
             dv_s[here, :] += dot(p.astype(BF16), g, ((1,), (0,)))
             dk_s[here, :] += dot(ds, q, ((1,), (0,)))
@@ -304,8 +314,11 @@
             pltpu.VMEM((blocks, 3 * 128, HD), BF16),
             pltpu.VMEM((HD, total), BF16),
             pltpu.VMEM((total, HD), F32),
+            pltpu.VMEM((HD, QB), BF16),
+            pltpu.VMEM((HD, QB), BF16),
             pltpu.VMEM((total, QB), F32),
             pltpu.VMEM((total, QB), F32),
+            pltpu.VMEM((total // KT, 1, QB), F32),
             pltpu.VMEM((total, HD), F32),
             pltpu.VMEM((total, HD), F32),
             pltpu.SemaphoreType.DMA((XN + 1,)),
@@ -480,7 +493,6 @@
 
     own = out_weight[0]
     pieces = tuple(along_x(own, -offset % XN) for offset in OFFSETS)
-    moved = shifted(upstream[0], "pipe", -1)
 
     fwd = exchange(pack(queries, keys, values, segments, 0))
     local_seg = segments[0]
@@ -488,18 +500,20 @@
     g_across = lax.ppermute(g_scaled, "seq", YSWAP)
     g_core = lax.ppermute(g_scaled, "seq", CORE)
     g_both = lax.ppermute(g_across, "seq", CORE)
-    packed = pack(queries, keys, values, segments, 1, g_across, moved, *pieces[1:])
+    packed = pack(queries, keys, values, segments, 1, g_across, *pieces[1:])
     bwd = exchange(packed)
     gate_tok = per_sample(local_seg[0], gates[0, 0])
 
     grads = attention_grad(place, (g_scaled, g_core, g_across, g_both), pieces, packed)
-    attns = attention_forward(place, fwd, grads[0], gate_tok)
+    turned = follow(upstream[0], grads[0])
+    moved = shifted(turned, "pipe", -1)
+    attns = attention_forward(place, fwd, grads[0], gate_tok, turned)
     grads = tuple(along_x(g, o) for g, o in zip(grads, OFFSETS))
     attns = (attns[0], follow(attns[1], *grads[1:])) + attns[2:]
     attns = tuple(along_x(a, o) for a, o in zip(attns, OFFSETS))
 
     attns = (attns[0], attns[2], attns[1], attns[3])
-    part, part_across, part_send = project(place, attns, pieces, bwd)
+    part, part_across, part_send = project(place, attns, pieces, bwd, moved)
     received = lax.ppermute(part_send, "seq", CORE)
     rows = part.shape[0]
     across = (part_across + received[rows:].astype(F32)).astype(BF16)

time: 192 us -> 191 us (level)
  Pallas kernels: 47.6 us -> 43.8 us
  starting transfers between devices: 44.6 us -> 41.9 us
  local copies, waits for them, and re-layouts: 5.63 us -> 8.09 us
    pallas_call x1, Pallas kernels: 16.5 us -> 13 us  [attention_backward(): pl.pallas_call(backward_kernel, out_shape=jax.ShapeDtypeStruct((blocks, 3...]
    unnamed x45 -> x52, local copies, waits for them, and re-layouts: 4.35 us -> 7.56 us
    ppermute x1, waiting for transfers between devices: 25.2 us -> 28.1 us  [body(): g_across = lax.ppermute(g_scaled, 'seq', YSWAP)]
    ppermute x1, starting transfers between devices: 7.95 us -> 5.21 us  [rotated(): lax.ppermute(array, axis, [(i, (i + by) % length) for i in range(length)])]
    ppermute x1, waiting for transfers between devices: 0.01 us -> 2.65 us  [shifted(): return lax.ppermute(array, axis, pairs)]
    ppermute x1, waiting for transfers between devices: 20.3 us -> 17.8 us  [rotated(): lax.ppermute(array, axis, [(i, (i + by) % length) for i in range(length)])]
  transfers between devices with their start and end apart: 19 -> 19, of which waited for: 11 -> 10; matrix products, arithmetic and copies ran while one was open for 4% -> 4% of each run, Pallas kernels for 22% -> 19%
where the time goes in v4:
time: 191 us; the launch traced here: 189 us
  waiting for transfers between devices  83.5 us (44%)
  Pallas kernels  43.8 us (23%)
  starting transfers between devices  41.9 us (22%)
  other arithmetic  10.7 us (6%)
  local copies, waits for them, and re-layouts  8.09 us (4%)
    ppermute x1, waiting for transfers between devices, body(): g_across = lax.ppermute(g_scaled, 'seq', YSWAP)  28.1 us
    ppermute x9, waiting for transfers between devices, along_x(): lax.ppermute(array, 'seq', [(i, (i + PER_X * offset) % count) for i in ra...  22.4 us
    all_to_all x3, starting transfers between devices, exchange(): return lax.all_to_all(array, 'seq', 0, 0, tiled=True)  18.3 us
    ppermute x1, waiting for transfers between devices, rotated(): lax.ppermute(array, axis, [(i, (i + by) % length) for i in range(length)])  17.8 us
    pallas_call x1, Pallas kernels, attention_backward(): pl.pallas_call(backward_kernel, out_shape=jax.ShapeDtypeStruct((blocks, 3...  13 us
    ppermute x9, starting transfers between devices, along_x(): lax.ppermute(array, 'seq', [(i, (i + PER_X * offset) % count) for i in ra...  12.7 us
    pallas_call x1, Pallas kernels, attention_forward(): pl.pallas_call(forward_kernel, out_shape=(jax.ShapeDtypeStruct((total //...  11.8 us
    all_to_all x3, waiting for transfers between devices, exchange(): return lax.all_to_all(array, 'seq', 0, 0, tiled=True)  9.02 us
  transfers between devices with their start and end apart: 19, of which 10 were waited for; matrix products, arithmetic and copies ran while one was open for 4% of the time, Pallas kernels for 19%

profile of v4, /device:TPU:1, one launch (start us, length us, event | category | flops | bytes accessed | tf_op | source)
XLA Modules:
  0.0 189.0 jit_solution(1629653182513367853)
XLA Ops:
  2.3 2.9 %pack.2 = bf16[16,400,128]{2,1,0:T(8,128)(2,1)} custom-call(s32[1,128]{1,0:T(1,128)} %get-tuple-element.28.seg_ref, bf16[1,2,128,2048]{3,2,1,0:T(8,128)(2,1)} %q_ref.3, bf16[1,2,128,2048]{3,2,1,0:T(8,128)(2,1)} %k_ref.3, bf16[1,2,128,2048]{3,2,1,0:T(8,128)(2,1)} %v_ref.3), custom_call_target="tpu_custom_call" | custom-call | flops 2000000000 | tf_op jit(solution)/shard_map/pack/pallas_call | solution.py:84
  5.2 7.5 %all-to-all-start = ((bf16[16,400,128]{2,1,0:T(8,128)(2,1)}), bf16[16,400,128]{2,1,0:T(8,128)(2,1)}, u32[]{:S(2)}, u32[]{:S(2)}) async-start(bf16[16,400,128]{2,1,0:T(8,128)(2,1)} %pack.2), calls=%async_computation | async-start | bytes 3276800 | tf_op jit(solution)/shard_map/all_to_all | solution.py:486
  14.4 1.4 collective-permute-start.1
  15.8 1.2 collective-permute-start.3
  17.0 1.5 collective-permute-start.4
  18.5 1.5 collective-permute-start.5
  20.0 1.5 collective-permute-start
  21.5 28.1 %collective-permute-done.1.refs_0_.refs_2_ = bf16[128,3072]{1,0:T(8,128)(2,1)} collective-permute-done((bf16[128,3072]{1,0:T(8,128)(2,1)}, bf16[128,3072]{1,0:T(8,128)(2,1)}, u32[]{:S(2)}, u32[]{:S(2)}) %collective-permute-start.1) | collective-permute-done | bytes 786464 | tf_op jit(solution)/shard_map/ppermute | solution.py:500
  50.7 17.6 %collective-permute-done.5.refs_3_.refs_7_ = bf16[128,3072]{1,0:T(8,128)(2,1)S(1)} collective-permute-done((bf16[128,3072]{1,0:T(8,128)(2,1)S(1)}, bf16[128,3072]{1,0:T(8,128)(2,1)S(1)}, u32[]{:S(2)}, u32[]{:S(2)}) %collective-permute-start.5) | collective-permute-done | bytes 786464 | tf_op jit(solution)/shard_map/ppermute | solution.py:30
  69.3 2.8 %pack.3.refs_8_ = bf16[16,400,128]{2,1,0:T(8,128)(2,1)} custom-call(s32[1,128]{1,0:T(1,128)} %get-tuple-element.27.seg_ref, bf16[1,2,128,2048]{3,2,1,0:T(8,128)(2,1)} %q_ref.3, bf16[1,2,128,2048]{3,2,1,0:T(8,128)(2,1)} %k_ref.3, bf16[1,2,128,2048]{3,2,1,0:T(8,128)(2,1)} %v_ref.3, bf16[128,3072]{1,0:T(8,128)(2,1)} %collective-permute-done.1.refs_0_.refs_2_, ...), custom_call_target="tpu_custom_call" | custom-call | flops 2000000000 | tf_op jit(solution)/shard_map/pack/pallas_call | solution.py:84
  72.1 5.3 %all-to-all-start.1 = ((bf16[16,400,128]{2,1,0:T(8,128)(2,1)}), bf16[16,400,128]{2,1,0:T(8,128)(2,1)}, u32[]{:S(2)}, u32[]{:S(2)}) async-start(bf16[16,400,128]{2,1,0:T(8,128)(2,1)} %pack.3.refs_8_), calls=%async_computation.1 | async-start | bytes 3276800 | tf_op jit(solution)/shard_map/all_to_all | solution.py:486
  78.3 5.5 %attention_grad.1 = (bf16[512,128]{1,0:T(8,128)(2,1)}, bf16[512,128]{1,0:T(8,128)(2,1)}, bf16[512,128]{1,0:T(8,128)(2,1)}, bf16[512,128]{1,0:T(8,128)(2,1)}) custom-call(s32[1]{0:T(128)} %bitcast.3.place_ref, bf16[128,3072]{1,0:T(8,128)(2,1)} %multiply_convert_fusion.refs_0_, bf16[128,3072]{1,0:T(8,128)(2,1)} %copy-done.16, ...), custom_call_target="tpu_custom_call" | custom-call | flops 200000000 | tf_op jit(solution)/shard_map/attention_grad/pallas_call | solution.py:362
  84.7 1.4 collective-permute-start.12
  86.2 2.7 %collective-permute-start.7 = (bf16[512,128]{1,0:T(8,128)(2,1)S(1)}, bf16[512,128]{1,0:T(8,128)(2,1)S(1)}, u32[]{:S(2)}, u32[]{:S(2)}) collective-permute-start(bf16[512,128]{1,0:T(8,128)(2,1)S(1)} %copy-done.24), channel_id=1, source_target_pairs={{0,12},{1,13},{2,14},{3,15},{4,0},{5,1},{6,2},{7,3},{8,4},{9,5},{1... | collective-permute-start | bytes 393224 | tf_op jit(solution)/shard_map/ppermute | solution.py:30
  88.9 1.8 collective-permute-start.9
  90.6 1.7 multiply_reduce_fusion.1.refs_1_
  92.4 11.8 %attention_forward.1 = (bf16[512,128]{1,0:T(8,128)(2,1)}, bf16[512,128]{1,0:T(8,128)(2,1)}, bf16[512,128]{1,0:T(8,128)(2,1)}, bf16[512,128]{1,0:T(8,128)(2,1)}) custom-call(s32[1]{0:T(128)} %bitcast.3.place_ref, bf16[16,400,128]{2,1,0:T(8,128)(2,1)} %all-to-all-done.in_hbm_ref, bf16[512,128]{1,0:T(8,128)(2,1)} %get-tuple-element.14.refs_0_, ...), custom_call_target="tpu_custom_call" | custom-call | flops 200000000 | tf_op jit(solution)/shard_map/attention_forward/pallas_call | solution.py:203
  104.2 1.4 collective-permute-start.11
  107.1 2.2 %collective-permute-start.10 = (bf16[512,128]{1,0:T(8,128)(2,1)S(1)}, bf16[512,128]{1,0:T(8,128)(2,1)S(1)}, u32[]{:S(2)}, u32[]{:S(2)}) collective-permute-start(bf16[512,128]{1,0:T(8,128)(2,1)S(1)} %follow.3), channel_id=1, source_target_pairs={{0,12},{1,13},{2,14},{3,15},{4,0},{5,1},{6,2},{7,3},{8,4},{9,5},{1... | collective-permute-start | bytes 393224 | tf_op jit(solution)/shard_map/ppermute | solution.py:30
  110.1 3.6 %collective-permute-done.6.refs_1_ = bf16[512,128]{1,0:T(8,128)(2,1)S(1)} collective-permute-done((bf16[512,128]{1,0:T(8,128)(2,1)}, bf16[512,128]{1,0:T(8,128)(2,1)S(1)}, u32[]{:S(2)}, u32[]{:S(2)}) %collective-permute-start.6) | collective-permute-done | bytes 131104 | tf_op jit(solution)/shard_map/ppermute | solution.py:30
  113.7 2.7 %collective-permute-done.12.refs_9_.second_ref = bf16[128,3072]{1,0:T(8,128)(2,1)S(1)} collective-permute-done((bf16[128,3072]{1,0:T(8,128)(2,1)S(1)}, bf16[128,3072]{1,0:T(8,128)(2,1)S(1)}, u32[]{:S(2)}, u32[]{:S(2)}) %collective-permute-start.12) | collective-permute-done | bytes 786464 | tf_op jit(solution)/shard_map/ppermute | solution.py:472
  117.2 4.8 %project.1 = (f32[128,3072]{1,0:T(8,128)}, f32[128,3072]{1,0:T(8,128)}, bf16[256,3072]{1,0:T(8,128)(2,1)}) custom-call(s32[1]{0:T(128)} %bitcast.3.place_ref, bf16[512,128]{1,0:T(8,128)(2,1)} %get-tuple-element.15.refs_0_, bf16[512,128]{1,0:T(8,128)(2,1)} %copy-done.18, bf16[512,128]{1,0:T(8,128)(2,1)} %copy-done.19, bf16[512,128]{1,0:T(8,128)(2,1)} %copy-done.17, ...), custom_call_target="tpu_custom_call" | custom-call | flops 200000000 | tf_op jit(solution)/shard_map/project/pallas_call | solution.py:414
  122.6 3.2 %collective-permute-done.13 = bf16[256,3072]{1,0:T(8,128)(2,1)S(1)} collective-permute-done((bf16[256,3072]{1,0:T(8,128)(2,1)}, bf16[256,3072]{1,0:T(8,128)(2,1)S(1)}, u32[]{:S(2)}, u32[]{:S(2)}) %collective-permute-start.13) | collective-permute-done | bytes 1572896 | tf_op jit(solution)/shard_map/ppermute | solution.py:517
  125.8 3.0 %add_convert_fusion.refs_4_ = bf16[128,3072]{1,0:T(8,128)(2,1)} fusion(f32[128,3072]{1,0:T(8,128)} %get-tuple-element.24, bf16[256,3072]{1,0:T(8,128)(2,1)S(1)} %collective-permute-done.13), kind=kLoop, calls=%fused_computation.4 | loop fusion | flops 1179648 | bytes 3145728 | tf_op jit(solution)/shard_map/convert_element_type | solution.py:519
  128.9 13.0 %attention_backward.1 = bf16[16,384,128]{2,1,0:T(8,128)(2,1)} custom-call(s32[1]{0:T(128)} %bitcast.3.place_ref, bf16[16,400,128]{2,1,0:T(8,128)(2,1)} %all-to-all-done.1.refs_8_.in_hbm_ref, bf16[512,128]{1,0:T(8,128)(2,1)} %get-tuple-element.14.refs_0_, bf16[512,128]{1,0:T(8,128)(2,1)} %copy-done.4, bf16[512,128]{1,0:T(8,128)(2,1)} %copy-done.5, ...), custom_call_target="tpu_custom_call" | custom-call | flops 30000001024 | tf_op jit(solution)/shard_map/attention_backward/pallas_call | solution.py:304
  141.9 5.5 %all-to-all-start.2 = ((bf16[16,384,128]{2,1,0:T(8,128)(2,1)}), bf16[16,384,128]{2,1,0:T(8,128)(2,1)S(1)}, u32[]{:S(2)}, u32[]{:S(2)}) async-start(bf16[16,384,128]{2,1,0:T(8,128)(2,1)} %attention_backward.1), calls=%async_computation.2 | async-start | bytes 3145728 | tf_op jit(solution)/shard_map/all_to_all | solution.py:486
  148.7 4.2 %fusion.1 = bf16[128,3072]{1,0:T(8,128)(2,1)} fusion(bf16[128,3072]{1,0:T(8,128)(2,1)S(1)} %copy-done.14, f32[128,3072]{1,0:T(8,128)} %multiply_reduce_fusion.1.refs_1_, bf16[128,3072]{1,0:T(8,128)(2,1)} %copy-done.15, f32[128,3072]{1,0:T(8,128)} %get-tuple-element.22, bf16[256,3072]{1,0:T(8,128)(2,1)} %copy-done.13, bf16[1,128,3072]{2,1,0:T(8,128)(2,1)} %param.10, ...), kind=kLoop, calls=%fused_computation.6 | loop fusion | flops 3538944 | bytes 7077889 | tf_op jit(solution)/shard_map/jit(_where)/select_n | solution.py:524
  153.0 5.2 %collective-permute-start.15 = (bf16[128,3072]{1,0:T(8,128)(2,1)}, bf16[128,3072]{1,0:T(8,128)(2,1)S(1)}, u32[]{:S(2)}, u32[]{:S(2)}) collective-permute-start(bf16[128,3072]{1,0:T(8,128)(2,1)} %fusion.1), channel_id=1, source_target_pairs={{0,16},{16,32},{32,48},{48,64},{64,80},{80,96},{96,112},{112,128},... | collective-permute-start | bytes 2359304 | tf_op jit(solution)/shard_map/ppermute | solution.py:477
  158.2 1.5 choose.1
  159.7 9.0 %all-to-all-done.2.in_ref = bf16[16,384,128]{2,1,0:T(8,128)(2,1)S(1)} async-done(((bf16[16,384,128]{2,1,0:T(8,128)(2,1)}), bf16[16,384,128]{2,1,0:T(8,128)(2,1)S(1)}, u32[]{:S(2)}, u32[]{:S(2)}) %all-to-all-start.2) | async-done | bytes 1572896 | tf_op jit(solution)/shard_map/all_to_all | solution.py:486
  168.8 1.6 unpack.1
  170.4 17.8 %collective-permute-done.15 = bf16[128,3072]{1,0:T(8,128)(2,1)S(1)} collective-permute-done((bf16[128,3072]{1,0:T(8,128)(2,1)}, bf16[128,3072]{1,0:T(8,128)(2,1)S(1)}, u32[]{:S(2)}, u32[]{:S(2)}) %collective-permute-start.15) | collective-permute-done | bytes 786464 | tf_op jit(solution)/shard_map/ppermute | solution.py:477
  (78 shorter events, 13.3 us)
Async XLA Ops:
  5.2 7.5 %copy-start.20 = (f32[1,2,4,3072]{3,2,1,0:T(4,128)S(1)}, f32[1,2,4,3072]{3,2,1,0:T(4,128)}, u32[]{:S(2)}) copy-start(f32[1,2,4,3072]{3,2,1,0:T(4,128)} %param.15) | copy-start | bytes 294916
  5.2 67.0 %all-to-all-start = ((bf16[16,400,128]{2,1,0:T(8,128)(2,1)}), bf16[16,400,128]{2,1,0:T(8,128)(2,1)}, u32[]{:S(2)}, u32[]{:S(2)}) async-start(bf16[16,400,128]{2,1,0:T(8,128)(2,1)} %pack.2), calls=%async_computation | async-start | bytes 3276800 | tf_op jit(solution)/shard_map/all_to_all | solution.py:486
  14.4 35.2 %collective-permute-start.1 = (bf16[128,3072]{1,0:T(8,128)(2,1)}, bf16[128,3072]{1,0:T(8,128)(2,1)}, u32[]{:S(2)}, u32[]{:S(2)}) collective-permute-start(bf16[128,3072]{1,0:T(8,128)(2,1)} %multiply_convert_fusion.refs_0_), channel_id=1, source_target_pairs={{0,2},{1,3},{2,0},{3,1},{4,6},{5,7},{6,4},{7,5},{8,10},{9,11},{10,... | collective-permute-start | bytes 2359304 | tf_op jit(solution)/shard_map/ppermute | solution.py:500
  15.8 34.9 %collective-permute-start.3 = (bf16[128,3072]{1,0:T(8,128)(2,1)S(1)}, bf16[128,3072]{1,0:T(8,128)(2,1)S(1)}, u32[]{:S(2)}, u32[]{:S(2)}) collective-permute-start(bf16[128,3072]{1,0:T(8,128)(2,1)S(1)} %bitcast.26), channel_id=1, source_target_pairs={{0,4},{1,5},{2,6},{3,7},{4,8},{5,9},{6,10},{7,11},{8,12},{9,13},{1... | collective-permute-start | bytes 2359304 | tf_op jit(solution)/shard_map/ppermute | solution.py:30
  17.0 33.7 %collective-permute-start.4 = (bf16[128,3072]{1,0:T(8,128)(2,1)S(1)}, bf16[128,3072]{1,0:T(8,128)(2,1)S(1)}, u32[]{:S(2)}, u32[]{:S(2)}) collective-permute-start(bf16[128,3072]{1,0:T(8,128)(2,1)S(1)} %bitcast.27), channel_id=1, source_target_pairs={{0,12},{1,13},{2,14},{3,15},{4,0},{5,1},{6,2},{7,3},{8,4},{9,5},{1... | collective-permute-start | bytes 2359304 | tf_op jit(solution)/shard_map/ppermute | solution.py:30
  18.5 49.9 %collective-permute-start.5 = (bf16[128,3072]{1,0:T(8,128)(2,1)S(1)}, bf16[128,3072]{1,0:T(8,128)(2,1)S(1)}, u32[]{:S(2)}, u32[]{:S(2)}) collective-permute-start(bf16[128,3072]{1,0:T(8,128)(2,1)S(1)} %bitcast.28), channel_id=1, source_target_pairs={{0,8},{1,9},{2,10},{3,11},{4,12},{5,13},{6,14},{7,15},{8,0},{9,1},... | collective-permute-start | bytes 2359304 | tf_op jit(solution)/shard_map/ppermute | solution.py:30
  20.0 57.4 %collective-permute-start = (bf16[128,3072]{1,0:T(8,128)(2,1)}, bf16[128,3072]{1,0:T(8,128)(2,1)S(1)}, u32[]{:S(2)}, u32[]{:S(2)}) collective-permute-start(bf16[128,3072]{1,0:T(8,128)(2,1)} %multiply_convert_fusion.refs_0_), channel_id=1, source_target_pairs={{0,1},{1,0},{2,3},{3,2},{4,5},{5,4},{6,7},{7,6},{8,9},{9,8},{10,11... | collective-permute-start | bytes 2359304 | tf_op jit(solution)/shard_map/ppermute | solution.py:501
  49.6 27.9 %collective-permute-start.2 = (bf16[128,3072]{1,0:T(8,128)(2,1)}, bf16[128,3072]{1,0:T(8,128)(2,1)}, u32[]{:S(2)}, u32[]{:S(2)}) collective-permute-start(bf16[128,3072]{1,0:T(8,128)(2,1)} %collective-permute-done.1.refs_0_.refs_2_), channel_id=1, source_target_pairs={{0,1},{1,0},{2,3},{3,2},{4,5},{5,4},{6,7},{7,6},{8,9},{9,8},{10,11... | collective-permute-start | bytes 2359304 | tf_op jit(solution)/shard_map/ppermute | solution.py:502
  50.7 17.6 %copy-start.9 = (bf16[128,3072]{1,0:T(8,128)(2,1)}, bf16[128,3072]{1,0:T(8,128)(2,1)S(1)}, u32[]{:S(2)}) copy-start(bf16[128,3072]{1,0:T(8,128)(2,1)S(1)} %collective-permute-done.3.refs_1_.refs_5_) | copy-start | bytes 2359300
  50.7 17.6 %copy-start.10 = (bf16[128,3072]{1,0:T(8,128)(2,1)}, bf16[128,3072]{1,0:T(8,128)(2,1)S(1)}, u32[]{:S(2)}) copy-start(bf16[128,3072]{1,0:T(8,128)(2,1)S(1)} %collective-permute-done.4.refs_2_.refs_6_) | copy-start | bytes 2359300
  72.1 41.6 %all-to-all-start.1 = ((bf16[16,400,128]{2,1,0:T(8,128)(2,1)}), bf16[16,400,128]{2,1,0:T(8,128)(2,1)}, u32[]{:S(2)}, u32[]{:S(2)}) async-start(bf16[16,400,128]{2,1,0:T(8,128)(2,1)} %pack.3.refs_8_), calls=%async_computation.1 | async-start | bytes 3276800 | tf_op jit(solution)/shard_map/all_to_all | solution.py:486
  84.7 4.1 %copy-start.23 = (bf16[512,128]{1,0:T(8,128)(2,1)S(1)}, bf16[512,128]{1,0:T(8,128)(2,1)}, u32[]{:S(2)}) copy-start(bf16[512,128]{1,0:T(8,128)(2,1)} %get-tuple-element.19) | copy-start | bytes 393220
  84.7 4.2 %copy-start.22 = (bf16[512,128]{1,0:T(8,128)(2,1)S(1)}, bf16[512,128]{1,0:T(8,128)(2,1)}, u32[]{:S(2)}) copy-start(bf16[512,128]{1,0:T(8,128)(2,1)} %get-tuple-element.20) | copy-start | bytes 393220
  84.7 7.6 %copy-start = (bf16[128,3072]{1,0:T(8,128)(2,1)}, bf16[128,3072]{1,0:T(8,128)(2,1)S(1)}, u32[]{:S(2)}) copy-start(bf16[128,3072]{1,0:T(8,128)(2,1)S(1)} %follow.2.refs_2_) | copy-start | bytes 2359300
  84.7 31.6 %collective-permute-start.12 = (bf16[128,3072]{1,0:T(8,128)(2,1)S(1)}, bf16[128,3072]{1,0:T(8,128)(2,1)S(1)}, u32[]{:S(2)}, u32[]{:S(2)}) collective-permute-start(bf16[128,3072]{1,0:T(8,128)(2,1)S(1)} %follow.2.refs_2_), channel_id=1, source_target_pairs={{16,0},{32,16},{48,32},{64,48},{80,64},{96,80},{112,96},{128,112},... | collective-permute-start | bytes 2359304 | tf_op jit(solution)/shard_map/ppermute | solution.py:472
  86.2 19.4 %collective-permute-start.7 = (bf16[512,128]{1,0:T(8,128)(2,1)S(1)}, bf16[512,128]{1,0:T(8,128)(2,1)S(1)}, u32[]{:S(2)}, u32[]{:S(2)}) collective-permute-start(bf16[512,128]{1,0:T(8,128)(2,1)S(1)} %copy-done.24), channel_id=1, source_target_pairs={{0,12},{1,13},{2,14},{3,15},{4,0},{5,1},{6,2},{7,3},{8,4},{9,5},{1... | collective-permute-start | bytes 393224 | tf_op jit(solution)/shard_map/ppermute | solution.py:30
  88.9 17.2 %collective-permute-start.8 = (bf16[512,128]{1,0:T(8,128)(2,1)S(1)}, bf16[512,128]{1,0:T(8,128)(2,1)S(1)}, u32[]{:S(2)}, u32[]{:S(2)}) collective-permute-start(bf16[512,128]{1,0:T(8,128)(2,1)S(1)} %copy-done.23), channel_id=1, source_target_pairs={{0,4},{1,5},{2,6},{3,7},{4,8},{5,9},{6,10},{7,11},{8,12},{9,13},{1... | collective-permute-start | bytes 393224 | tf_op jit(solution)/shard_map/ppermute | solution.py:30
  88.9 17.2 %collective-permute-start.9 = (bf16[512,128]{1,0:T(8,128)(2,1)S(1)}, bf16[512,128]{1,0:T(8,128)(2,1)S(1)}, u32[]{:S(2)}, u32[]{:S(2)}) collective-permute-start(bf16[512,128]{1,0:T(8,128)(2,1)S(1)} %copy-done.22), channel_id=1, source_target_pairs={{0,8},{1,9},{2,10},{3,11},{4,12},{5,13},{6,14},{7,15},{8,0},{9,1},... | collective-permute-start | bytes 393224 | tf_op jit(solution)/shard_map/ppermute | solution.py:30
  104.2 5.9 %collective-permute-start.11 = (bf16[512,128]{1,0:T(8,128)(2,1)}, bf16[512,128]{1,0:T(8,128)(2,1)S(1)}, u32[]{:S(2)}, u32[]{:S(2)}) collective-permute-start(bf16[512,128]{1,0:T(8,128)(2,1)} %get-tuple-element.21), channel_id=1, source_target_pairs={{0,8},{1,9},{2,10},{3,11},{4,12},{5,13},{6,14},{7,15},{8,0},{9,1},... | collective-permute-start | bytes 393224 | tf_op jit(solution)/shard_map/ppermute | solution.py:30
  105.6 16.5 %copy-start.4 = (bf16[512,128]{1,0:T(8,128)(2,1)}, bf16[512,128]{1,0:T(8,128)(2,1)S(1)}, u32[]{:S(2)}) copy-start(bf16[512,128]{1,0:T(8,128)(2,1)S(1)} %collective-permute-done.7.refs_0_.refs_1_) | copy-start | bytes 393220
  105.6 8.1 %collective-permute-start.6 = (bf16[512,128]{1,0:T(8,128)(2,1)}, bf16[512,128]{1,0:T(8,128)(2,1)S(1)}, u32[]{:S(2)}, u32[]{:S(2)}) collective-permute-start(bf16[512,128]{1,0:T(8,128)(2,1)} %get-tuple-element.16), channel_id=1, source_target_pairs={{0,4},{1,5},{2,6},{3,7},{4,8},{5,9},{6,10},{7,11},{8,12},{9,13},{1... | collective-permute-start | bytes 393224 | tf_op jit(solution)/shard_map/ppermute | solution.py:30
  106.0 16.0 %copy-start.5 = (bf16[512,128]{1,0:T(8,128)(2,1)}, bf16[512,128]{1,0:T(8,128)(2,1)S(1)}, u32[]{:S(2)}) copy-start(bf16[512,128]{1,0:T(8,128)(2,1)S(1)} %collective-permute-done.8.refs_1_.refs_2_) | copy-start | bytes 393220
  106.1 16.0 %copy-start.6 = (bf16[512,128]{1,0:T(8,128)(2,1)}, bf16[512,128]{1,0:T(8,128)(2,1)S(1)}, u32[]{:S(2)}) copy-start(bf16[512,128]{1,0:T(8,128)(2,1)S(1)} %collective-permute-done.9.refs_2_.refs_3_) | copy-start | bytes 393220
  107.1 6.6 %collective-permute-start.10 = (bf16[512,128]{1,0:T(8,128)(2,1)S(1)}, bf16[512,128]{1,0:T(8,128)(2,1)S(1)}, u32[]{:S(2)}, u32[]{:S(2)}) collective-permute-start(bf16[512,128]{1,0:T(8,128)(2,1)S(1)} %follow.3), channel_id=1, source_target_pairs={{0,12},{1,13},{2,14},{3,15},{4,0},{5,1},{6,2},{7,3},{8,4},{9,5},{1... | collective-permute-start | bytes 393224 | tf_op jit(solution)/shard_map/ppermute | solution.py:30
  110.1 6.3 %copy-start.17 = (bf16[512,128]{1,0:T(8,128)(2,1)}, bf16[512,128]{1,0:T(8,128)(2,1)S(1)}, u32[]{:S(2)}) copy-start(bf16[512,128]{1,0:T(8,128)(2,1)S(1)} %collective-permute-done.11.refs_3_) | copy-start | bytes 393220
  122.1 3.8 %collective-permute-start.13 = (bf16[256,3072]{1,0:T(8,128)(2,1)}, bf16[256,3072]{1,0:T(8,128)(2,1)S(1)}, u32[]{:S(2)}, u32[]{:S(2)}) collective-permute-start(bf16[256,3072]{1,0:T(8,128)(2,1)} %get-tuple-element.23), channel_id=1, source_target_pairs={{0,1},{1,0},{2,3},{3,2},{4,5},{5,4},{6,7},{7,6},{8,9},{9,8},{10,11... | collective-permute-start | bytes 4718600 | tf_op jit(solution)/shard_map/ppermute | solution.py:517
  128.9 19.0 %collective-permute-start.14 = (bf16[128,3072]{1,0:T(8,128)(2,1)}, bf16[128,3072]{1,0:T(8,128)(2,1)S(1)}, u32[]{:S(2)}, u32[]{:S(2)}) collective-permute-start(bf16[128,3072]{1,0:T(8,128)(2,1)} %add_convert_fusion.refs_4_), channel_id=1, source_target_pairs={{0,2},{1,3},{2,0},{3,1},{4,6},{5,7},{6,4},{7,5},{8,10},{9,11},{10,... | collective-permute-start | bytes 2359304 | tf_op jit(solution)/shard_map/ppermute | solution.py:521
  141.9 6.8 %copy-start.14 = (bf16[128,3072]{1,0:T(8,128)(2,1)S(1)}, bf16[128,3072]{1,0:T(8,128)(2,1)}, u32[]{:S(2)}) copy-start(bf16[128,3072]{1,0:T(8,128)(2,1)} %param.18) | copy-start | bytes 2359300
  141.9 26.8 %all-to-all-start.2 = ((bf16[16,384,128]{2,1,0:T(8,128)(2,1)}), bf16[16,384,128]{2,1,0:T(8,128)(2,1)S(1)}, u32[]{:S(2)}, u32[]{:S(2)}) async-start(bf16[16,384,128]{2,1,0:T(8,128)(2,1)} %attention_backward.1), calls=%async_computation.2 | async-start | bytes 3145728 | tf_op jit(solution)/shard_map/all_to_all | solution.py:486
  148.7 9.5 %copy-start.2 = (bf16[128,3072]{1,0:T(8,128)(2,1)S(1)}, bf16[128,3072]{1,0:T(8,128)(2,1)}, u32[]{:S(2)}) copy-start(bf16[128,3072]{1,0:T(8,128)(2,1)} %copy-done.1) | copy-start | bytes 2359300
  148.7 9.5 %copy-start.8 = (bf16[128,3072]{1,0:T(8,128)(2,1)S(1)}, bf16[128,3072]{1,0:T(8,128)(2,1)}, u32[]{:S(2)}) copy-start(bf16[128,3072]{1,0:T(8,128)(2,1)} %first_ref.1) | copy-start | bytes 2359300
  153.0 35.1 %collective-permute-start.15 = (bf16[128,3072]{1,0:T(8,128)(2,1)}, bf16[128,3072]{1,0:T(8,128)(2,1)S(1)}, u32[]{:S(2)}, u32[]{:S(2)}) collective-permute-start(bf16[128,3072]{1,0:T(8,128)(2,1)} %fusion.1), channel_id=1, source_target_pairs={{0,16},{16,32},{32,48},{48,64},{64,80},{80,96},{96,112},{112,128},... | collective-permute-start | bytes 2359304 | tf_op jit(solution)/shard_map/ppermute | solution.py:477
  (12 other events, 19.0 us)

commit v5 on v4

--- a/solution.py
+++ b/solution.py
@@ -19,6 +19,7 @@
 
 XN, PER_X = 4, 4
 OFFSETS = (0, 3, 1, 2)
+PIECES = 5
 CORE = [(i, i ^ 1) for i in range(XN * PER_X)]
 YSWAP = [(i, i ^ 2) for i in range(XN * PER_X)]
 
@@ -330,17 +331,24 @@
     )(place, packed, *grads, *later)
 
 
+def weight_copies(pieces, w_s, sems, first_sem):
+    copies, row = [], 0
+    for j, ref in enumerate(pieces):
+        target = w_s.at[row:row + ref.shape[0], :]
+        copies.append(pltpu.make_async_copy(ref, target, sems.at[first_sem + j]))
+        row += ref.shape[0]
+    return copies
+
+
 def grad_kernel(place_ref, *refs):
-    grads, pieces, outs = refs[:PER_X], refs[PER_X:PER_X + XN], refs[-5 - XN:-5]
+    grads, pieces, outs = refs[:PER_X], refs[PER_X:PER_X + PIECES], refs[-5 - XN:-5]
     g_s, w_s, out_s, in_sems, out_sems = refs[-5:]
     rows = grads[0].shape[0]
     arriving = []
     for bits, ref in enumerate(grads):
         target = g_s.at[rows_at(place_ref, bits, rows), :]
         arriving.append(pltpu.make_async_copy(ref, target, in_sems.at[bits]))
-    for j, ref in enumerate(pieces):
-        target = w_s.at[j * HD:(j + 1) * HD, :]
-        arriving.append(pltpu.make_async_copy(ref, target, in_sems.at[PER_X + j]))
+    arriving += weight_copies(pieces, w_s, in_sems, PER_X)
     for copy in arriving:
         copy.start()
     for copy in arriving:
@@ -362,13 +370,13 @@
     return pl.pallas_call(
         grad_kernel,
         out_shape=(jax.ShapeDtypeStruct((PER_X * rows, HD), BF16),) * XN,
-        in_specs=[pl.BlockSpec(memory_space=pltpu.SMEM)] + in_hbm(PER_X + XN) + anywhere(later),
+        in_specs=[pl.BlockSpec(memory_space=pltpu.SMEM)] + in_hbm(PER_X + PIECES) + anywhere(later),
         out_specs=tuple(in_hbm(XN)),
         scratch_shapes=[
             pltpu.VMEM((PER_X * rows, width), BF16),
             pltpu.VMEM((XN * HD, width), BF16),
             pltpu.VMEM((XN, PER_X * rows, HD), BF16),
-            pltpu.SemaphoreType.DMA((PER_X + XN,)),
+            pltpu.SemaphoreType.DMA((PER_X + PIECES,)),
             pltpu.SemaphoreType.DMA((XN,)),
         ],
         compiler_params=params(60),
@@ -378,14 +386,12 @@
 
 
 def project_kernel(place_ref, *refs):
-    attns, pieces, outs = refs[:XN], refs[XN:2 * XN], refs[-11:-8]
+    attns, pieces, outs = refs[:XN], refs[XN:XN + PIECES], refs[-11:-8]
     a_in, w_s, a_s, own_s, across_s, send_s, in_sems, out_sems = refs[-8:]
     rows, width = outs[0].shape
-    arriving = []
+    arriving = weight_copies(pieces, w_s, in_sems, XN)
     for j in range(XN):
-        target = w_s.at[j * HD:(j + 1) * HD, :]
         arriving.append(pltpu.make_async_copy(attns[j], a_in.at[j], in_sems.at[j]))
-        arriving.append(pltpu.make_async_copy(pieces[j], target, in_sems.at[XN + j]))
     for copy in arriving:
         copy.start()
     for copy in arriving:
@@ -414,7 +420,7 @@
     return pl.pallas_call(
         project_kernel,
         out_shape=tuple(jax.ShapeDtypeStruct(*shape) for shape in shapes),
-        in_specs=[pl.BlockSpec(memory_space=pltpu.SMEM)] + in_hbm(2 * XN) + anywhere(later),
+        in_specs=[pl.BlockSpec(memory_space=pltpu.SMEM)] + in_hbm(XN + PIECES) + anywhere(later),
         out_specs=tuple(in_hbm(3)),
         scratch_shapes=[
             pltpu.VMEM((XN, PER_X * rows, HD), BF16),
@@ -422,7 +428,7 @@
             pltpu.VMEM((PER_X * rows, XN * HD), BF16),
         ]
         + [pltpu.VMEM(*shape) for shape in shapes]
-        + [pltpu.SemaphoreType.DMA((2 * XN,)), pltpu.SemaphoreType.DMA((3,))],
+        + [pltpu.SemaphoreType.DMA((XN + PIECES,)), pltpu.SemaphoreType.DMA((3,))],
         compiler_params=params(60),
         cost_estimate=cost(0.2),
         name="project",
@@ -466,10 +472,20 @@
     )(sections, first, second, *later)
 
 
-def shifted(array, axis, by):
-    length = lax.axis_size(axis)
-    pairs = [(i, i + by) for i in range(length) if 0 <= i + by < length]
-    return lax.ppermute(array, axis, pairs)
+def settle_kernel(in_ref, out_ref):
+    out_ref[...] = in_ref[...]
+
+
+def settle(array):
+    return pl.pallas_call(
+        settle_kernel,
+        out_shape=jax.ShapeDtypeStruct(array.shape, array.dtype),
+        in_specs=whole(1),
+        out_specs=whole(1)[0],
+        compiler_params=params(8),
+        cost_estimate=cost(0.2),
+        name="settle",
+    )(array)
 
 
 def rotated(array, axis, by):
@@ -492,7 +508,9 @@
     place = lax.axis_index("seq")[None]
 
     own = out_weight[0]
-    pieces = tuple(along_x(own, -offset % XN) for offset in OFFSETS)
+    left, right = along_x(own, 1), along_x(own, XN - 1)
+    half = own.shape[0] // 2
+    pieces = (own, left, right, along_x(left[:half], 1), along_x(right[half:], XN - 1))
 
     fwd = exchange(pack(queries, keys, values, segments, 0))
     local_seg = segments[0]
@@ -500,13 +518,14 @@
     g_across = lax.ppermute(g_scaled, "seq", YSWAP)
     g_core = lax.ppermute(g_scaled, "seq", CORE)
     g_both = lax.ppermute(g_across, "seq", CORE)
-    packed = pack(queries, keys, values, segments, 1, g_across, *pieces[1:])
+    gate_tok = per_sample(local_seg[0], gates[0, 0])
+    grads = attention_grad(place, (g_scaled, g_core, g_across, g_both), pieces)
+    packed = pack(queries, keys, values, segments, 1, grads[0], gate_tok)
     bwd = exchange(packed)
-    gate_tok = per_sample(local_seg[0], gates[0, 0])
-
-    grads = attention_grad(place, (g_scaled, g_core, g_across, g_both), pieces, packed)
-    turned = follow(upstream[0], grads[0])
-    moved = shifted(turned, "pipe", -1)
+
+    sections = jnp.stack([section, jnp.zeros_like(section)])
+    turned = choose(sections, loss_grad, upstream[0], fwd)
+    moved = rotated(turned, "pipe", -1)
     attns = attention_forward(place, fwd, grads[0], gate_tok, turned)
     grads = tuple(along_x(g, o) for g, o in zip(grads, OFFSETS))
     attns = (attns[0], follow(attns[1], *grads[1:])) + attns[2:]
@@ -524,10 +543,8 @@
     section_out = jnp.where(section == last_section, fresh, section_out)
     next_act = rotated(section_out, "pipe", 1)
 
-    sections = jnp.stack([section, last_section * jnp.ones_like(section)])
-    next_grad = choose(sections, loss_grad, moved)
     qkv_grads = unpack(exchange(grads))
-    return (next_act[None], next_grad[None], qkv_grads[None])
+    return (next_act[None], settle(moved)[None], qkv_grads[None])
 
 
 def solution(mesh):

time: 191 us -> 193 us (1.010)
  starting transfers between devices: 41.9 us -> 61.4 us
  waiting for transfers between devices: 83.5 us -> 70.1 us
  Pallas kernels: 43.8 us -> 41.3 us
    ppermute x1, waiting for transfers between devices: 28.1 us -> 13.3 us  [body(): g_across = lax.ppermute(g_scaled, 'seq', YSWAP)]
    ppermute x1, starting transfers between devices: 0.87 us -> 9.33 us  [body(): g_both = lax.ppermute(g_across, 'seq', CORE)]
    ppermute x1 -> x2, starting transfers between devices: 5.21 us -> 12.2 us  [rotated(): lax.ppermute(array, axis, [(i, (i + by) % length) for i in range(length)])]
    ppermute x9 -> x10, starting transfers between devices: 12.7 us -> 17.2 us  [along_x(): lax.ppermute(array, 'seq', [(i, (i + PER_X * offset) % count) for i in ra...]
    all_to_all x3, waiting for transfers between devices: 9.02 us -> 12.6 us  [exchange(): return lax.all_to_all(array, 'seq', 0, 0, tiled=True)]
    unnamed x52 -> x41, local copies, waits for them, and re-layouts: 7.56 us -> 4.49 us
    ppermute x1 -> x0, waiting for transfers between devices: 2.65 us -> none  [shifted(): return lax.ppermute(array, axis, pairs)]
    pallas_call x1, Pallas kernels: 11.8 us -> 9.17 us  [attention_forward(): pl.pallas_call(forward_kernel, out_shape=(jax.ShapeDtypeStruct((total //...]
  transfers between devices with their start and end apart: 19 -> 20, of which waited for: 10 -> 11; matrix products, arithmetic and copies ran while one was open for 4% -> 3% of each run, Pallas kernels for 19% -> 19%
where the time goes in v5:
time: 193 us; the launch traced here: 192 us
  waiting for transfers between devices  70.1 us (36%)
  starting transfers between devices  61.4 us (32%)
  Pallas kernels  41.3 us (21%)
  other arithmetic  10.2 us (5%)
  local copies, waits for them, and re-layouts  7.81 us (4%)
    ppermute x10, waiting for transfers between devices, along_x(): lax.ppermute(array, 'seq', [(i, (i + PER_X * offset) % count) for i in ra...  21.3 us
    ppermute x2, waiting for transfers between devices, rotated(): lax.ppermute(array, axis, [(i, (i + by) % length) for i in range(length)])  19.6 us
    all_to_all x3, starting transfers between devices, exchange(): return lax.all_to_all(array, 'seq', 0, 0, tiled=True)  17.5 us
    ppermute x10, starting transfers between devices, along_x(): lax.ppermute(array, 'seq', [(i, (i + PER_X * offset) % count) for i in ra...  17.2 us
    ppermute x1, waiting for transfers between devices, body(): g_across = lax.ppermute(g_scaled, 'seq', YSWAP)  13.3 us
    pallas_call x1, Pallas kernels, attention_backward(): pl.pallas_call(backward_kernel, out_shape=jax.ShapeDtypeStruct((blocks, 3...  13 us
    all_to_all x3, waiting for transfers between devices, exchange(): return lax.all_to_all(array, 'seq', 0, 0, tiled=True)  12.6 us
    ppermute x2, starting transfers between devices, rotated(): lax.ppermute(array, axis, [(i, (i + by) % length) for i in range(length)])  12.2 us
  transfers between devices with their start and end apart: 20, of which 11 were waited for; matrix products, arithmetic and copies ran while one was open for 3% of the time, Pallas kernels for 19%

profile of v5, /device:TPU:1, one launch (start us, length us, event | category | flops | bytes accessed | tf_op | source)
XLA Modules:
  0.0 191.8 jit_solution(9697444185052259307)
XLA Ops:
  4.4 2.1 %collective-permute-start.1 = (bf16[128,3072]{1,0:T(8,128)(2,1)}, bf16[128,3072]{1,0:T(8,128)(2,1)}, u32[]{:S(2)}, u32[]{:S(2)}) collective-permute-start(bf16[128,3072]{1,0:T(8,128)(2,1)} %multiply_convert_fusion.refs_0_), channel_id=1, source_target_pairs={{0,2},{1,3},{2,0},{3,1},{4,6},{5,7},{6,4},{7,5},{8,10},{9,11},{10,... | collective-permute-start | bytes 2359304 | tf_op jit(solution)/shard_map/ppermute | solution.py:518
  6.6 2.9 %pack.2 = bf16[16,400,128]{2,1,0:T(8,128)(2,1)} custom-call(s32[1,128]{1,0:T(1,128)} %get-tuple-element.28.seg_ref, bf16[1,2,128,2048]{3,2,1,0:T(8,128)(2,1)} %q_ref.3, bf16[1,2,128,2048]{3,2,1,0:T(8,128)(2,1)} %k_ref.3, bf16[1,2,128,2048]{3,2,1,0:T(8,128)(2,1)} %v_ref.3), custom_call_target="tpu_custom_call" | custom-call | flops 2000000000 | tf_op jit(solution)/shard_map/pack/pallas_call | solution.py:85
  9.4 5.3 %all-to-all-start = ((bf16[16,400,128]{2,1,0:T(8,128)(2,1)}), bf16[16,400,128]{2,1,0:T(8,128)(2,1)S(1)}, u32[]{:S(2)}, u32[]{:S(2)}) async-start(bf16[16,400,128]{2,1,0:T(8,128)(2,1)} %pack.2), calls=%async_computation | async-start | bytes 3276800 | tf_op jit(solution)/shard_map/all_to_all | solution.py:502
  14.7 1.4 collective-permute-start.3
  16.1 1.3 collective-permute-start.4
  18.1 13.3 %collective-permute-done.1.refs_2_ = bf16[128,3072]{1,0:T(8,128)(2,1)} collective-permute-done((bf16[128,3072]{1,0:T(8,128)(2,1)}, bf16[128,3072]{1,0:T(8,128)(2,1)}, u32[]{:S(2)}, u32[]{:S(2)}) %collective-permute-start.1) | collective-permute-done | bytes 786464 | tf_op jit(solution)/shard_map/ppermute | solution.py:518
  31.4 9.3 %collective-permute-start.2 = (bf16[128,3072]{1,0:T(8,128)(2,1)}, bf16[128,3072]{1,0:T(8,128)(2,1)}, u32[]{:S(2)}, u32[]{:S(2)}) collective-permute-start(bf16[128,3072]{1,0:T(8,128)(2,1)} %collective-permute-done.1.refs_2_), channel_id=1, source_target_pairs={{0,1},{1,0},{2,3},{3,2},{4,5},{5,4},{6,7},{7,6},{8,9},{9,8},{10,11... | collective-permute-start | bytes 2359304 | tf_op jit(solution)/shard_map/ppermute | solution.py:520
  40.7 11.9 %collective-permute-done.3.refs_5_ = bf16[128,3072]{1,0:T(8,128)(2,1)S(1)} collective-permute-done((bf16[128,3072]{1,0:T(8,128)(2,1)}, bf16[128,3072]{1,0:T(8,128)(2,1)S(1)}, u32[]{:S(2)}, u32[]{:S(2)}) %collective-permute-start.3) | collective-permute-done | bytes 786464 | tf_op jit(solution)/shard_map/ppermute | solution.py:31
  54.0 2.6 %collective-permute-start.6 = (bf16[64,3072]{1,0:T(8,128)(2,1)S(1)}, bf16[64,3072]{1,0:T(8,128)(2,1)}, u32[]{:S(2)}, u32[]{:S(2)}) collective-permute-start(bf16[64,3072]{1,0:T(8,128)(2,1)S(1)} %slice.37), channel_id=1, source_target_pairs={{0,12},{1,13},{2,14},{3,15},{4,0},{5,1},{6,2},{7,3},{8,4},{9,5},{1... | collective-permute-start | bytes 1179656 | tf_op jit(solution)/shard_map/ppermute | solution.py:31
  56.6 1.7 multiply_reduce_fusion.1.refs_1_
  58.3 5.4 %collective-permute-done.5.refs_7_ = bf16[64,3072]{1,0:T(8,128)(2,1)S(1)} collective-permute-done((bf16[64,3072]{1,0:T(8,128)(2,1)S(1)}, bf16[64,3072]{1,0:T(8,128)(2,1)S(1)}, u32[]{:S(2)}, u32[]{:S(2)}) %collective-permute-start.5) | collective-permute-done | bytes 393248 | tf_op jit(solution)/shard_map/ppermute | solution.py:31
  64.5 5.5 %attention_grad.1 = (bf16[512,128]{1,0:T(8,128)(2,1)}, bf16[512,128]{1,0:T(8,128)(2,1)}, bf16[512,128]{1,0:T(8,128)(2,1)}, bf16[512,128]{1,0:T(8,128)(2,1)}) custom-call(s32[1]{0:T(128)} %bitcast.3.place_ref, bf16[128,3072]{1,0:T(8,128)(2,1)} %multiply_convert_fusion.refs_0_, bf16[128,3072]{1,0:T(8,128)(2,1)} %collective-permute-done.refs_1_, ...), custom_call_target="tpu_custom_call" | custom-call | flops 200000000 | tf_op jit(solution)/shard_map/attention_grad/pallas_call | solution.py:370
  70.0 2.8 %pack.3 = bf16[16,400,128]{2,1,0:T(8,128)(2,1)} custom-call(s32[1,128]{1,0:T(1,128)} %get-tuple-element.27.seg_ref, bf16[1,2,128,2048]{3,2,1,0:T(8,128)(2,1)} %q_ref.3, bf16[1,2,128,2048]{3,2,1,0:T(8,128)(2,1)} %k_ref.3, bf16[1,2,128,2048]{3,2,1,0:T(8,128)(2,1)} %v_ref.3, bf16[512,128]{1,0:T(8,128)(2,1)} %get-tuple-element.14.refs_0_, ...), custom_call_target="tpu_custom_call" | custom-call | flops 2000000000 | tf_op jit(solution)/shard_map/pack/pallas_call | solution.py:85
  72.8 7.4 %all-to-all-start.1 = ((bf16[16,400,128]{2,1,0:T(8,128)(2,1)}), bf16[16,400,128]{2,1,0:T(8,128)(2,1)}, u32[]{:S(2)}, u32[]{:S(2)}) async-start(bf16[16,400,128]{2,1,0:T(8,128)(2,1)} %pack.3), calls=%async_computation.1 | async-start | bytes 3276800 | tf_op jit(solution)/shard_map/all_to_all | solution.py:502
  82.1 8.2 %collective-permute-start.13 = (bf16[128,3072]{1,0:T(8,128)(2,1)S(1)}, bf16[128,3072]{1,0:T(8,128)(2,1)S(1)}, u32[]{:S(2)}, u32[]{:S(2)}) collective-permute-start(bf16[128,3072]{1,0:T(8,128)(2,1)S(1)} %choose.1.refs_2_), channel_id=1, source_target_pairs={{0,240},{16,0},{32,16},{48,32},{64,48},{80,64},{96,80},{112,96},{1... | collective-permute-start | bytes 2359304 | tf_op jit(solution)/shard_map/ppermute | solution.py:493
  90.2 2.9 %collective-permute-start.10 = (bf16[512,128]{1,0:T(8,128)(2,1)S(1)}, bf16[512,128]{1,0:T(8,128)(2,1)S(1)}, u32[]{:S(2)}, u32[]{:S(2)}) collective-permute-start(bf16[512,128]{1,0:T(8,128)(2,1)S(1)} %copy-done.19), channel_id=1, source_target_pairs={{0,8},{1,9},{2,10},{3,11},{4,12},{5,13},{6,14},{7,15},{8,0},{9,1},... | collective-permute-start | bytes 393224 | tf_op jit(solution)/shard_map/ppermute | solution.py:31
  94.6 9.2 %attention_forward.1 = (bf16[512,128]{1,0:T(8,128)(2,1)}, bf16[512,128]{1,0:T(8,128)(2,1)}, bf16[512,128]{1,0:T(8,128)(2,1)}, bf16[512,128]{1,0:T(8,128)(2,1)}) custom-call(s32[1]{0:T(128)} %bitcast.3.place_ref, bf16[16,400,128]{2,1,0:T(8,128)(2,1)} %copy-done, bf16[512,128]{1,0:T(8,128)(2,1)} %get-tuple-element.14.refs_0_, ...), custom_call_target="tpu_custom_call" | custom-call | flops 200000000 | tf_op jit(solution)/shard_map/attention_forward/pallas_call | solution.py:204
  105.8 5.1 %collective-permute-start.7 = (bf16[512,128]{1,0:T(8,128)(2,1)}, bf16[512,128]{1,0:T(8,128)(2,1)S(1)}, u32[]{:S(2)}, u32[]{:S(2)}) collective-permute-start(bf16[512,128]{1,0:T(8,128)(2,1)} %get-tuple-element.16), channel_id=1, source_target_pairs={{0,4},{1,5},{2,6},{3,7},{4,8},{5,9},{6,10},{7,11},{8,12},{9,13},{1... | collective-permute-start | bytes 393224 | tf_op jit(solution)/shard_map/ppermute | solution.py:31
  112.0 1.5 collective-permute-start.11
  114.0 2.1 %collective-permute-done.11.refs_2_ = bf16[512,128]{1,0:T(8,128)(2,1)S(1)} collective-permute-done((bf16[512,128]{1,0:T(8,128)(2,1)S(1)}, bf16[512,128]{1,0:T(8,128)(2,1)S(1)}, u32[]{:S(2)}, u32[]{:S(2)}) %collective-permute-start.11) | collective-permute-done | bytes 131104 | tf_op jit(solution)/shard_map/ppermute | solution.py:31
  116.1 2.5 %collective-permute-done.13.refs_10_.in_ref = bf16[128,3072]{1,0:T(8,128)(2,1)S(1)} collective-permute-done((bf16[128,3072]{1,0:T(8,128)(2,1)S(1)}, bf16[128,3072]{1,0:T(8,128)(2,1)S(1)}, u32[]{:S(2)}, u32[]{:S(2)}) %collective-permute-start.13) | collective-permute-done | bytes 786464 | tf_op jit(solution)/shard_map/ppermute | solution.py:493
  119.5 4.8 %project.1 = (f32[128,3072]{1,0:T(8,128)}, f32[128,3072]{1,0:T(8,128)}, bf16[256,3072]{1,0:T(8,128)(2,1)}) custom-call(s32[1]{0:T(128)} %bitcast.3.place_ref, bf16[512,128]{1,0:T(8,128)(2,1)} %get-tuple-element.15.refs_0_, bf16[512,128]{1,0:T(8,128)(2,1)} %copy-done.15, bf16[512,128]{1,0:T(8,128)(2,1)} %copy-done.16, bf16[512,128]{1,0:T(8,128)(2,1)} %copy-done.14, ...), custom_call_target="tpu_custom_call" | custom-call | flops 200000000 | tf_op jit(solution)/shard_map/project/pallas_call | solution.py:420
  125.1 3.2 %collective-permute-done.14 = bf16[256,3072]{1,0:T(8,128)(2,1)S(1)} collective-permute-done((bf16[256,3072]{1,0:T(8,128)(2,1)}, bf16[256,3072]{1,0:T(8,128)(2,1)S(1)}, u32[]{:S(2)}, u32[]{:S(2)}) %collective-permute-start.14) | collective-permute-done | bytes 1572896 | tf_op jit(solution)/shard_map/ppermute | solution.py:536
  128.3 3.0 %add_convert_fusion.refs_4_ = bf16[128,3072]{1,0:T(8,128)(2,1)} fusion(f32[128,3072]{1,0:T(8,128)} %get-tuple-element.24, bf16[256,3072]{1,0:T(8,128)(2,1)S(1)} %collective-permute-done.14), kind=kLoop, calls=%fused_computation.4 | loop fusion | flops 1179648 | bytes 3145728 | tf_op jit(solution)/shard_map/convert_element_type | solution.py:538
  131.4 1.6 collective-permute-start.15
  133.0 13.0 %attention_backward.1 = bf16[16,384,128]{2,1,0:T(8,128)(2,1)} custom-call(s32[1]{0:T(128)} %bitcast.3.place_ref, bf16[16,400,128]{2,1,0:T(8,128)(2,1)} %all-to-all-done.1.refs_9_.in_hbm_ref, bf16[512,128]{1,0:T(8,128)(2,1)} %get-tuple-element.14.refs_0_, bf16[512,128]{1,0:T(8,128)(2,1)} %copy-done.6, bf16[512,128]{1,0:T(8,128)(2,1)} %copy-done.7, ...), custom_call_target="tpu_custom_call" | custom-call | flops 30000001024 | tf_op jit(solution)/shard_map/attention_backward/pallas_call | solution.py:305
  146.1 4.8 %all-to-all-start.2 = ((bf16[16,384,128]{2,1,0:T(8,128)(2,1)}), bf16[16,384,128]{2,1,0:T(8,128)(2,1)S(1)}, u32[]{:S(2)}, u32[]{:S(2)}) async-start(bf16[16,384,128]{2,1,0:T(8,128)(2,1)} %attention_backward.1), calls=%async_computation.2 | async-start | bytes 3145728 | tf_op jit(solution)/shard_map/all_to_all | solution.py:502
  150.9 3.7 %fusion.1 = bf16[128,3072]{1,0:T(8,128)(2,1)} fusion(bf16[128,3072]{1,0:T(8,128)(2,1)} %param.18, f32[128,3072]{1,0:T(8,128)S(1)} %copy-done.10, bf16[128,3072]{1,0:T(8,128)(2,1)} %collective-permute-done.15, f32[128,3072]{1,0:T(8,128)} %get-tuple-element.22, bf16[256,3072]{1,0:T(8,128)(2,1)} %copy-done.13, bf16[1,128,3072]{2,1,0:T(8,128)(2,1)} %param.10, ...), kind=kLoop, calls=%fused_computation.6 | loop fusion | flops 3538944 | bytes 7077889 | tf_op jit(solution)/shard_map/jit(_where)/select_n | solution.py:543
  154.6 4.0 %collective-permute-start.16 = (bf16[128,3072]{1,0:T(8,128)(2,1)}, bf16[128,3072]{1,0:T(8,128)(2,1)S(1)}, u32[]{:S(2)}, u32[]{:S(2)}) collective-permute-start(bf16[128,3072]{1,0:T(8,128)(2,1)} %fusion.1), channel_id=1, source_target_pairs={{0,16},{16,32},{32,48},{48,64},{64,80},{80,96},{96,112},{112,128},... | collective-permute-start | bytes 2359304 | tf_op jit(solution)/shard_map/ppermute | solution.py:493
  159.6 12.6 %all-to-all-done.2.in_ref = bf16[16,384,128]{2,1,0:T(8,128)(2,1)S(1)} async-done(((bf16[16,384,128]{2,1,0:T(8,128)(2,1)}), bf16[16,384,128]{2,1,0:T(8,128)(2,1)S(1)}, u32[]{:S(2)}, u32[]{:S(2)}) %all-to-all-start.2) | async-done | bytes 1572896 | tf_op jit(solution)/shard_map/all_to_all | solution.py:502
  172.2 1.6 unpack.1
  173.8 17.1 %collective-permute-done.16 = bf16[128,3072]{1,0:T(8,128)(2,1)S(1)} collective-permute-done((bf16[128,3072]{1,0:T(8,128)(2,1)}, bf16[128,3072]{1,0:T(8,128)(2,1)S(1)}, u32[]{:S(2)}, u32[]{:S(2)}) %collective-permute-start.16) | collective-permute-done | bytes 786464 | tf_op jit(solution)/shard_map/ppermute | solution.py:493
  (71 shorter events, 16.9 us)
Async XLA Ops:
  4.4 27.0 %collective-permute-start.1 = (bf16[128,3072]{1,0:T(8,128)(2,1)}, bf16[128,3072]{1,0:T(8,128)(2,1)}, u32[]{:S(2)}, u32[]{:S(2)}) collective-permute-start(bf16[128,3072]{1,0:T(8,128)(2,1)} %multiply_convert_fusion.refs_0_), channel_id=1, source_target_pairs={{0,2},{1,3},{2,0},{3,1},{4,6},{5,7},{6,4},{7,5},{8,10},{9,11},{10,... | collective-permute-start | bytes 2359304 | tf_op jit(solution)/shard_map/ppermute | solution.py:518
  9.4 63.4 %all-to-all-start = ((bf16[16,400,128]{2,1,0:T(8,128)(2,1)}), bf16[16,400,128]{2,1,0:T(8,128)(2,1)S(1)}, u32[]{:S(2)}, u32[]{:S(2)}) async-start(bf16[16,400,128]{2,1,0:T(8,128)(2,1)} %pack.2), calls=%async_computation | async-start | bytes 3276800 | tf_op jit(solution)/shard_map/all_to_all | solution.py:502
  14.7 38.0 %collective-permute-start.3 = (bf16[128,3072]{1,0:T(8,128)(2,1)}, bf16[128,3072]{1,0:T(8,128)(2,1)S(1)}, u32[]{:S(2)}, u32[]{:S(2)}) collective-permute-start(bf16[128,3072]{1,0:T(8,128)(2,1)} %bitcast.24), channel_id=1, source_target_pairs={{0,4},{1,5},{2,6},{3,7},{4,8},{5,9},{6,10},{7,11},{8,12},{9,13},{1... | collective-permute-start | bytes 2359304 | tf_op jit(solution)/shard_map/ppermute | solution.py:31
  16.1 36.7 %collective-permute-start.4 = (bf16[128,3072]{1,0:T(8,128)(2,1)}, bf16[128,3072]{1,0:T(8,128)(2,1)}, u32[]{:S(2)}, u32[]{:S(2)}) collective-permute-start(bf16[128,3072]{1,0:T(8,128)(2,1)} %bitcast.25), channel_id=1, source_target_pairs={{0,12},{1,13},{2,14},{3,15},{4,0},{5,1},{6,2},{7,3},{8,4},{9,5},{1... | collective-permute-start | bytes 2359304 | tf_op jit(solution)/shard_map/ppermute | solution.py:31
  17.4 40.9 %collective-permute-start = (bf16[128,3072]{1,0:T(8,128)(2,1)}, bf16[128,3072]{1,0:T(8,128)(2,1)}, u32[]{:S(2)}, u32[]{:S(2)}) collective-permute-start(bf16[128,3072]{1,0:T(8,128)(2,1)} %multiply_convert_fusion.refs_0_), channel_id=1, source_target_pairs={{0,1},{1,0},{2,3},{3,2},{4,5},{5,4},{6,7},{7,6},{8,9},{9,8},{10,11... | collective-permute-start | bytes 2359304 | tf_op jit(solution)/shard_map/ppermute | solution.py:519
  31.4 32.5 %collective-permute-start.2 = (bf16[128,3072]{1,0:T(8,128)(2,1)}, bf16[128,3072]{1,0:T(8,128)(2,1)}, u32[]{:S(2)}, u32[]{:S(2)}) collective-permute-start(bf16[128,3072]{1,0:T(8,128)(2,1)} %collective-permute-done.1.refs_2_), channel_id=1, source_target_pairs={{0,1},{1,0},{2,3},{3,2},{4,5},{5,4},{6,7},{7,6},{8,9},{9,8},{10,11... | collective-permute-start | bytes 2359304 | tf_op jit(solution)/shard_map/ppermute | solution.py:520
  52.7 5.6 %copy-start.11 = (bf16[128,3072]{1,0:T(8,128)(2,1)}, bf16[128,3072]{1,0:T(8,128)(2,1)S(1)}, u32[]{:S(2)}) copy-start(bf16[128,3072]{1,0:T(8,128)(2,1)S(1)} %collective-permute-done.3.refs_5_) | copy-start | bytes 2359300
  52.7 11.0 %collective-permute-start.5 = (bf16[64,3072]{1,0:T(8,128)(2,1)S(1)}, bf16[64,3072]{1,0:T(8,128)(2,1)S(1)}, u32[]{:S(2)}, u32[]{:S(2)}) collective-permute-start(bf16[64,3072]{1,0:T(8,128)(2,1)S(1)} %slice.36), channel_id=1, source_target_pairs={{0,4},{1,5},{2,6},{3,7},{4,8},{5,9},{6,10},{7,11},{8,12},{9,13},{1... | collective-permute-start | bytes 1179656 | tf_op jit(solution)/shard_map/ppermute | solution.py:31
  54.0 9.9 %collective-permute-start.6 = (bf16[64,3072]{1,0:T(8,128)(2,1)S(1)}, bf16[64,3072]{1,0:T(8,128)(2,1)}, u32[]{:S(2)}, u32[]{:S(2)}) collective-permute-start(bf16[64,3072]{1,0:T(8,128)(2,1)S(1)} %slice.37), channel_id=1, source_target_pairs={{0,12},{1,13},{2,14},{3,15},{4,0},{5,1},{6,2},{7,3},{8,4},{9,5},{1... | collective-permute-start | bytes 1179656 | tf_op jit(solution)/shard_map/ppermute | solution.py:31
  72.8 7.5 %copy-start = (bf16[16,400,128]{2,1,0:T(8,128)(2,1)}, bf16[16,400,128]{2,1,0:T(8,128)(2,1)S(1)}, u32[]{:S(2)}) copy-start(bf16[16,400,128]{2,1,0:T(8,128)(2,1)S(1)} %all-to-all-done.refs_0_.in_hbm_ref) | copy-start | bytes 4915204
  72.8 45.8 %all-to-all-start.1 = ((bf16[16,400,128]{2,1,0:T(8,128)(2,1)}), bf16[16,400,128]{2,1,0:T(8,128)(2,1)}, u32[]{:S(2)}, u32[]{:S(2)}) async-start(bf16[16,400,128]{2,1,0:T(8,128)(2,1)} %pack.3), calls=%async_computation.1 | async-start | bytes 3276800 | tf_op jit(solution)/shard_map/all_to_all | solution.py:502
  81.4 8.8 %copy-start.19 = (bf16[512,128]{1,0:T(8,128)(2,1)S(1)}, bf16[512,128]{1,0:T(8,128)(2,1)}, u32[]{:S(2)}) copy-start(bf16[512,128]{1,0:T(8,128)(2,1)} %get-tuple-element.20) | copy-start | bytes 393220
  81.4 11.7 %copy-start.18 = (bf16[512,128]{1,0:T(8,128)(2,1)S(1)}, bf16[512,128]{1,0:T(8,128)(2,1)}, u32[]{:S(2)}) copy-start(bf16[512,128]{1,0:T(8,128)(2,1)} %get-tuple-element.18) | copy-start | bytes 393220
  81.4 12.6 %copy-start.17 = (bf16[512,128]{1,0:T(8,128)(2,1)S(1)}, bf16[512,128]{1,0:T(8,128)(2,1)}, u32[]{:S(2)}) copy-start(bf16[512,128]{1,0:T(8,128)(2,1)} %get-tuple-element.19) | copy-start | bytes 393220
  82.1 12.6 %copy-start.3 = (bf16[128,3072]{1,0:T(8,128)(2,1)}, bf16[128,3072]{1,0:T(8,128)(2,1)S(1)}, u32[]{:S(2)}) copy-start(bf16[128,3072]{1,0:T(8,128)(2,1)S(1)} %choose.1.refs_2_) | copy-start | bytes 2359300
  82.1 36.6 %collective-permute-start.13 = (bf16[128,3072]{1,0:T(8,128)(2,1)S(1)}, bf16[128,3072]{1,0:T(8,128)(2,1)S(1)}, u32[]{:S(2)}, u32[]{:S(2)}) collective-permute-start(bf16[128,3072]{1,0:T(8,128)(2,1)S(1)} %choose.1.refs_2_), channel_id=1, source_target_pairs={{0,240},{16,0},{32,16},{48,32},{64,48},{80,64},{96,80},{112,96},{1... | collective-permute-start | bytes 2359304 | tf_op jit(solution)/shard_map/ppermute | solution.py:493
  90.2 15.6 %collective-permute-start.10 = (bf16[512,128]{1,0:T(8,128)(2,1)S(1)}, bf16[512,128]{1,0:T(8,128)(2,1)S(1)}, u32[]{:S(2)}, u32[]{:S(2)}) collective-permute-start(bf16[512,128]{1,0:T(8,128)(2,1)S(1)} %copy-done.19), channel_id=1, source_target_pairs={{0,8},{1,9},{2,10},{3,11},{4,12},{5,13},{6,14},{7,15},{8,0},{9,1},... | collective-permute-start | bytes 393224 | tf_op jit(solution)/shard_map/ppermute | solution.py:31
  93.1 17.8 %collective-permute-start.8 = (bf16[512,128]{1,0:T(8,128)(2,1)S(1)}, bf16[512,128]{1,0:T(8,128)(2,1)S(1)}, u32[]{:S(2)}, u32[]{:S(2)}) collective-permute-start(bf16[512,128]{1,0:T(8,128)(2,1)S(1)} %copy-done.18), channel_id=1, source_target_pairs={{0,12},{1,13},{2,14},{3,15},{4,0},{5,1},{6,2},{7,3},{8,4},{9,5},{1... | collective-permute-start | bytes 393224 | tf_op jit(solution)/shard_map/ppermute | solution.py:31
  94.0 16.9 %collective-permute-start.9 = (bf16[512,128]{1,0:T(8,128)(2,1)S(1)}, bf16[512,128]{1,0:T(8,128)(2,1)S(1)}, u32[]{:S(2)}, u32[]{:S(2)}) collective-permute-start(bf16[512,128]{1,0:T(8,128)(2,1)S(1)} %copy-done.17), channel_id=1, source_target_pairs={{0,4},{1,5},{2,6},{3,7},{4,8},{5,9},{6,10},{7,11},{8,12},{9,13},{1... | collective-permute-start | bytes 393224 | tf_op jit(solution)/shard_map/ppermute | solution.py:31
  103.8 9.7 %collective-permute-start.12 = (bf16[512,128]{1,0:T(8,128)(2,1)}, bf16[512,128]{1,0:T(8,128)(2,1)S(1)}, u32[]{:S(2)}, u32[]{:S(2)}) collective-permute-start(bf16[512,128]{1,0:T(8,128)(2,1)} %get-tuple-element.21), channel_id=1, source_target_pairs={{0,8},{1,9},{2,10},{3,11},{4,12},{5,13},{6,14},{7,15},{8,0},{9,1},... | collective-permute-start | bytes 393224 | tf_op jit(solution)/shard_map/ppermute | solution.py:31
  105.8 18.5 %copy-start.5 = (bf16[512,128]{1,0:T(8,128)(2,1)}, bf16[512,128]{1,0:T(8,128)(2,1)S(1)}, u32[]{:S(2)}) copy-start(bf16[512,128]{1,0:T(8,128)(2,1)S(1)} %collective-permute-done.10.refs_2_.refs_3_) | copy-start | bytes 393220
  105.8 8.2 %collective-permute-start.7 = (bf16[512,128]{1,0:T(8,128)(2,1)}, bf16[512,128]{1,0:T(8,128)(2,1)S(1)}, u32[]{:S(2)}, u32[]{:S(2)}) collective-permute-start(bf16[512,128]{1,0:T(8,128)(2,1)} %get-tuple-element.16), channel_id=1, source_target_pairs={{0,4},{1,5},{2,6},{3,7},{4,8},{5,9},{6,10},{7,11},{8,12},{9,13},{1... | collective-permute-start | bytes 393224 | tf_op jit(solution)/shard_map/ppermute | solution.py:31
  111.0 13.4 %copy-start.6 = (bf16[512,128]{1,0:T(8,128)(2,1)}, bf16[512,128]{1,0:T(8,128)(2,1)S(1)}, u32[]{:S(2)}) copy-start(bf16[512,128]{1,0:T(8,128)(2,1)S(1)} %collective-permute-done.8.refs_0_.refs_1_) | copy-start | bytes 393220
  111.0 13.4 %copy-start.7 = (bf16[512,128]{1,0:T(8,128)(2,1)}, bf16[512,128]{1,0:T(8,128)(2,1)S(1)}, u32[]{:S(2)}) copy-start(bf16[512,128]{1,0:T(8,128)(2,1)S(1)} %collective-permute-done.9.refs_1_.refs_2_) | copy-start | bytes 393220
  112.0 4.1 %collective-permute-start.11 = (bf16[512,128]{1,0:T(8,128)(2,1)S(1)}, bf16[512,128]{1,0:T(8,128)(2,1)S(1)}, u32[]{:S(2)}, u32[]{:S(2)}) collective-permute-start(bf16[512,128]{1,0:T(8,128)(2,1)S(1)} %follow.1), channel_id=1, source_target_pairs={{0,12},{1,13},{2,14},{3,15},{4,0},{5,1},{6,2},{7,3},{8,4},{9,5},{1... | collective-permute-start | bytes 393224 | tf_op jit(solution)/shard_map/ppermute | solution.py:31
  113.5 5.2 %copy-start.14 = (bf16[512,128]{1,0:T(8,128)(2,1)}, bf16[512,128]{1,0:T(8,128)(2,1)S(1)}, u32[]{:S(2)}) copy-start(bf16[512,128]{1,0:T(8,128)(2,1)S(1)} %collective-permute-done.12.refs_3_) | copy-start | bytes 393220
  124.4 4.0 %collective-permute-start.14 = (bf16[256,3072]{1,0:T(8,128)(2,1)}, bf16[256,3072]{1,0:T(8,128)(2,1)S(1)}, u32[]{:S(2)}, u32[]{:S(2)}) collective-permute-start(bf16[256,3072]{1,0:T(8,128)(2,1)} %get-tuple-element.23), channel_id=1, source_target_pairs={{0,1},{1,0},{2,3},{3,2},{4,5},{5,4},{6,7},{7,6},{8,9},{9,8},{10,11... | collective-permute-start | bytes 4718600 | tf_op jit(solution)/shard_map/ppermute | solution.py:536
  131.4 19.5 %collective-permute-start.15 = (bf16[128,3072]{1,0:T(8,128)(2,1)}, bf16[128,3072]{1,0:T(8,128)(2,1)}, u32[]{:S(2)}, u32[]{:S(2)}) collective-permute-start(bf16[128,3072]{1,0:T(8,128)(2,1)} %add_convert_fusion.refs_4_), channel_id=1, source_target_pairs={{0,2},{1,3},{2,0},{3,1},{4,6},{5,7},{6,4},{7,5},{8,10},{9,11},{10,... | collective-permute-start | bytes 2359304 | tf_op jit(solution)/shard_map/ppermute | solution.py:540
  146.1 4.8 %copy-start.10 = (f32[128,3072]{1,0:T(8,128)S(1)}, f32[128,3072]{1,0:T(8,128)}, u32[]{:S(2)}) copy-start(f32[128,3072]{1,0:T(8,128)} %multiply_reduce_fusion.1.refs_1_) | copy-start | bytes 4718596
  146.1 26.1 %all-to-all-start.2 = ((bf16[16,384,128]{2,1,0:T(8,128)(2,1)}), bf16[16,384,128]{2,1,0:T(8,128)(2,1)S(1)}, u32[]{:S(2)}, u32[]{:S(2)}) async-start(bf16[16,384,128]{2,1,0:T(8,128)(2,1)} %attention_backward.1), calls=%async_computation.2 | async-start | bytes 3145728 | tf_op jit(solution)/shard_map/all_to_all | solution.py:502
  150.9 7.7 %copy-start.2 = (bf16[128,3072]{1,0:T(8,128)(2,1)S(1)}, bf16[128,3072]{1,0:T(8,128)(2,1)}, u32[]{:S(2)}) copy-start(bf16[128,3072]{1,0:T(8,128)(2,1)} %copy-done.1) | copy-start | bytes 2359300
  154.6 36.3 %collective-permute-start.16 = (bf16[128,3072]{1,0:T(8,128)(2,1)}, bf16[128,3072]{1,0:T(8,128)(2,1)S(1)}, u32[]{:S(2)}, u32[]{:S(2)}) collective-permute-start(bf16[128,3072]{1,0:T(8,128)(2,1)} %fusion.1), channel_id=1, source_target_pairs={{0,16},{16,32},{32,48},{48,64},{64,80},{80,96},{96,112},{112,128},... | collective-permute-start | bytes 2359304 | tf_op jit(solution)/shard_map/ppermute | solution.py:493
  (8 other events, 16.7 us)

commit v6 on v5

--- a/solution.py
+++ b/solution.py
@@ -19,7 +19,7 @@
 
 XN, PER_X = 4, 4
 OFFSETS = (0, 3, 1, 2)
-PIECES = 5
+PIECES = XN
 CORE = [(i, i ^ 1) for i in range(XN * PER_X)]
 YSWAP = [(i, i ^ 2) for i in range(XN * PER_X)]
 
@@ -472,20 +472,27 @@
     )(sections, first, second, *later)
 
 
-def settle_kernel(in_ref, out_ref):
+def settle_kernel(in_ref, *refs):
+    out_ref = refs[-1]
     out_ref[...] = in_ref[...]
 
 
-def settle(array):
+def settle(array, *later):
     return pl.pallas_call(
         settle_kernel,
         out_shape=jax.ShapeDtypeStruct(array.shape, array.dtype),
-        in_specs=whole(1),
+        in_specs=whole(1) + anywhere(later),
         out_specs=whole(1)[0],
         compiler_params=params(8),
         cost_estimate=cost(0.2),
         name="settle",
-    )(array)
+    )(array, *later)
+
+
+def shifted(array, axis, by):
+    length = lax.axis_size(axis)
+    pairs = [(i, i + by) for i in range(length) if 0 <= i + by < length]
+    return lax.ppermute(array, axis, pairs)
 
 
 def rotated(array, axis, by):
@@ -508,9 +515,7 @@
     place = lax.axis_index("seq")[None]
 
     own = out_weight[0]
-    left, right = along_x(own, 1), along_x(own, XN - 1)
-    half = own.shape[0] // 2
-    pieces = (own, left, right, along_x(left[:half], 1), along_x(right[half:], XN - 1))
+    pieces = tuple(along_x(own, -offset % XN) for offset in OFFSETS)
 
     fwd = exchange(pack(queries, keys, values, segments, 0))
     local_seg = segments[0]
@@ -520,19 +525,18 @@
     g_both = lax.ppermute(g_across, "seq", CORE)
     gate_tok = per_sample(local_seg[0], gates[0, 0])
     grads = attention_grad(place, (g_scaled, g_core, g_across, g_both), pieces)
-    packed = pack(queries, keys, values, segments, 1, grads[0], gate_tok)
+    packed = pack(queries, keys, values, segments, 1, g_across, gate_tok, *pieces[1:])
     bwd = exchange(packed)
 
-    sections = jnp.stack([section, jnp.zeros_like(section)])
-    turned = choose(sections, loss_grad, upstream[0], fwd)
-    moved = rotated(turned, "pipe", -1)
+    turned = settle(upstream[0], fwd)
+    moved = shifted(turned, "pipe", -1)
     attns = attention_forward(place, fwd, grads[0], gate_tok, turned)
     grads = tuple(along_x(g, o) for g, o in zip(grads, OFFSETS))
     attns = (attns[0], follow(attns[1], *grads[1:])) + attns[2:]
     attns = tuple(along_x(a, o) for a, o in zip(attns, OFFSETS))
 
-    attns = (attns[0], attns[2], attns[1], attns[3])
-    part, part_across, part_send = project(place, attns, pieces, bwd, moved)
+    attns = (attns[0], attns[2], attns[1], follow(attns[3], bwd, moved))
+    part, part_across, part_send = project(place, attns, pieces)
     received = lax.ppermute(part_send, "seq", CORE)
     rows = part.shape[0]
     across = (part_across + received[rows:].astype(F32)).astype(BF16)
@@ -543,8 +547,10 @@
     section_out = jnp.where(section == last_section, fresh, section_out)
     next_act = rotated(section_out, "pipe", 1)
 
+    sections = jnp.stack([section, last_section * jnp.ones_like(section)])
+    next_grad = choose(sections, loss_grad, moved)
     qkv_grads = unpack(exchange(grads))
-    return (next_act[None], settle(moved)[None], qkv_grads[None])
+    return (next_act[None], next_grad[None], qkv_grads[None])
 
 
 def solution(mesh):

time: 193 us -> 176 us (0.912)
  starting transfers between devices: 61.4 us -> 36.4 us
  Pallas kernels: 41.3 us -> 48.9 us
  waiting for transfers between devices: 70.1 us -> 73.2 us
    all_to_all x3, waiting for transfers between devices: 12.6 us -> 34.3 us  [exchange(): return lax.all_to_all(array, 'seq', 0, 0, tiled=True)]
    ppermute x1, waiting for transfers between devices: 13.3 us -> 0.41 us  [body(): g_across = lax.ppermute(g_scaled, 'seq', YSWAP)]
    ppermute x2 -> x1, starting transfers between devices: 12.2 us -> 0.32 us  [rotated(): lax.ppermute(array, axis, [(i, (i + by) % length) for i in range(length)])]
    ppermute x1, starting transfers between devices: 9.33 us -> 0.32 us  [body(): g_both = lax.ppermute(g_across, 'seq', CORE)]
    ppermute x2 -> x1, waiting for transfers between devices: 19.6 us -> 13.1 us  [rotated(): lax.ppermute(array, axis, [(i, (i + by) % length) for i in range(length)])]
    pallas_call x1, Pallas kernels: 13 us -> 17.2 us  [attention_backward(): pl.pallas_call(backward_kernel, out_shape=jax.ShapeDtypeStruct((blocks, 3...]
    ppermute x10 -> x9, starting transfers between devices: 17.2 us -> 14.6 us  [along_x(): lax.ppermute(array, 'seq', [(i, (i + PER_X * offset) % count) for i in ra...]
    pallas_call x1, Pallas kernels: 9.17 us -> 11.8 us  [attention_forward(): pl.pallas_call(forward_kernel, out_shape=(jax.ShapeDtypeStruct((total //...]
  transfers between devices with their start and end apart: 20 -> 19, of which waited for: 11 -> 11; matrix products, arithmetic and copies ran while one was open for 3% -> 4% of each run, Pallas kernels for 19% -> 25%
where the time goes in v6:
time: 176 us; the launch traced here: 175 us
  waiting for transfers between devices  73.2 us (42%)
  Pallas kernels  48.9 us (28%)
  starting transfers between devices  36.4 us (21%)
  other arithmetic  9.32 us (5%)
  local copies, waits for them, and re-layouts  6.51 us (4%)
    all_to_all x3, waiting for transfers between devices, exchange(): return lax.all_to_all(array, 'seq', 0, 0, tiled=True)  34.3 us
    ppermute x9, waiting for transfers between devices, along_x(): lax.ppermute(array, 'seq', [(i, (i + PER_X * offset) % count) for i in ra...  20.9 us
    pallas_call x1, Pallas kernels, attention_backward(): pl.pallas_call(backward_kernel, out_shape=jax.ShapeDtypeStruct((blocks, 3...  17.2 us
    all_to_all x3, starting transfers between devices, exchange(): return lax.all_to_all(array, 'seq', 0, 0, tiled=True)  16.8 us
    ppermute x9, starting transfers between devices, along_x(): lax.ppermute(array, 'seq', [(i, (i + PER_X * offset) % count) for i in ra...  14.6 us
    ppermute x1, waiting for transfers between devices, rotated(): lax.ppermute(array, axis, [(i, (i + by) % length) for i in range(length)])  13.1 us
    pallas_call x1, Pallas kernels, attention_forward(): pl.pallas_call(forward_kernel, out_shape=(jax.ShapeDtypeStruct((total //...  11.8 us
    pallas_call x2, Pallas kernels, pack(): pl.pallas_call(pack_kernel, grid=(1,), out_shape=jax.ShapeDtypeStruct((he...  5.65 us
  transfers between devices with their start and end apart: 19, of which 11 were waited for; matrix products, arithmetic and copies ran while one was open for 4% of the time, Pallas kernels for 25%

profile of v6, /device:TPU:1, one launch (start us, length us, event | category | flops | bytes accessed | tf_op | source)
XLA Modules:
  0.0 175.3 jit_solution(4122567162853971220)
XLA Ops:
  0.6 3.7 %collective-permute-start.5 = (bf16[128,3072]{1,0:T(8,128)(2,1)}, bf16[128,3072]{1,0:T(8,128)(2,1)S(1)}, u32[]{:S(2)}, u32[]{:S(2)}) collective-permute-start(bf16[128,3072]{1,0:T(8,128)(2,1)} %bitcast.24), channel_id=1, source_target_pairs={{0,8},{1,9},{2,10},{3,11},{4,12},{5,13},{6,14},{7,15},{8,0},{9,1},... | collective-permute-start | bytes 2359304 | tf_op jit(solution)/shard_map/ppermute | solution.py:31
  5.8 1.3 slice_bitcast_fusion.2
  7.0 2.8 %pack.2 = bf16[16,400,128]{2,1,0:T(8,128)(2,1)} custom-call(s32[1,128]{1,0:T(1,128)} %get-tuple-element.28.seg_ref, bf16[1,2,128,2048]{3,2,1,0:T(8,128)(2,1)} %q_ref.3, bf16[1,2,128,2048]{3,2,1,0:T(8,128)(2,1)} %k_ref.3, bf16[1,2,128,2048]{3,2,1,0:T(8,128)(2,1)} %v_ref.3), custom_call_target="tpu_custom_call" | custom-call | flops 2000000000 | tf_op jit(solution)/shard_map/pack/pallas_call | solution.py:85
  9.9 6.3 %all-to-all-start = ((bf16[16,400,128]{2,1,0:T(8,128)(2,1)}), bf16[16,400,128]{2,1,0:T(8,128)(2,1)S(1)}, u32[]{:S(2)}, u32[]{:S(2)}) async-start(bf16[16,400,128]{2,1,0:T(8,128)(2,1)} %pack.2), calls=%async_computation | async-start | bytes 3276800 | tf_op jit(solution)/shard_map/all_to_all | solution.py:509
  17.5 1.5 collective-permute-start.1
  19.0 1.7 multiply_reduce_fusion.1.refs_1_
  20.9 18.4 %collective-permute-done.4.refs_6_.refs_3_ = bf16[128,3072]{1,0:T(8,128)(2,1)S(1)} collective-permute-done((bf16[128,3072]{1,0:T(8,128)(2,1)}, bf16[128,3072]{1,0:T(8,128)(2,1)S(1)}, u32[]{:S(2)}, u32[]{:S(2)}) %collective-permute-start.4) | collective-permute-done | bytes 786464 | tf_op jit(solution)/shard_map/ppermute | solution.py:31
  40.1 2.8 %pack.3 = bf16[16,400,128]{2,1,0:T(8,128)(2,1)} custom-call(s32[1,128]{1,0:T(1,128)} %get-tuple-element.27.seg_ref, bf16[1,2,128,2048]{3,2,1,0:T(8,128)(2,1)} %q_ref.3, bf16[1,2,128,2048]{3,2,1,0:T(8,128)(2,1)} %k_ref.3, bf16[1,2,128,2048]{3,2,1,0:T(8,128)(2,1)} %v_ref.3, bf16[128,3072]{1,0:T(8,128)(2,1)} %collective-permute-done.1.refs_2_.refs_0_, ...), custom_call_target="tpu_custom_call" | custom-call | flops 2000000000 | tf_op jit(solution)/shard_map/pack/pallas_call | solution.py:85
  43.0 15.2 %all-to-all-done.refs_0_.in_hbm_ref = bf16[16,400,128]{2,1,0:T(8,128)(2,1)S(1)} async-done(((bf16[16,400,128]{2,1,0:T(8,128)(2,1)}), bf16[16,400,128]{2,1,0:T(8,128)(2,1)S(1)}, u32[]{:S(2)}, u32[]{:S(2)}) %all-to-all-start) | async-done | bytes 1638432 | tf_op jit(solution)/shard_map/all_to_all | solution.py:509
  58.1 4.8 %all-to-all-start.1 = ((bf16[16,400,128]{2,1,0:T(8,128)(2,1)}), bf16[16,400,128]{2,1,0:T(8,128)(2,1)S(1)}, u32[]{:S(2)}, u32[]{:S(2)}) async-start(bf16[16,400,128]{2,1,0:T(8,128)(2,1)} %pack.3), calls=%async_computation.1 | async-start | bytes 3276800 | tf_op jit(solution)/shard_map/all_to_all | solution.py:509
  63.5 1.1 copy-done.3
  65.6 1.3 collective-permute-start.12
  66.9 5.5 %attention_grad.1 = (bf16[512,128]{1,0:T(8,128)(2,1)}, bf16[512,128]{1,0:T(8,128)(2,1)}, bf16[512,128]{1,0:T(8,128)(2,1)}, bf16[512,128]{1,0:T(8,128)(2,1)}) custom-call(s32[1]{0:T(128)} %bitcast.3.place_ref, bf16[128,3072]{1,0:T(8,128)(2,1)} %copy-done.15, bf16[128,3072]{1,0:T(8,128)(2,1)} %collective-permute-done.refs_1_, ...), custom_call_target="tpu_custom_call" | custom-call | flops 200000000 | tf_op jit(solution)/shard_map/attention_grad/pallas_call | solution.py:370
  72.4 2.7 %collective-permute-start.7 = (bf16[512,128]{1,0:T(8,128)(2,1)}, bf16[512,128]{1,0:T(8,128)(2,1)S(1)}, u32[]{:S(2)}, u32[]{:S(2)}) collective-permute-start(bf16[512,128]{1,0:T(8,128)(2,1)} %get-tuple-element.18), channel_id=1, source_target_pairs={{0,12},{1,13},{2,14},{3,15},{4,0},{5,1},{6,2},{7,3},{8,4},{9,5},{1... | collective-permute-start | bytes 393224 | tf_op jit(solution)/shard_map/ppermute | solution.py:31
  75.1 1.8 collective-permute-start.9
  76.8 11.8 %attention_forward.1 = (bf16[512,128]{1,0:T(8,128)(2,1)}, bf16[512,128]{1,0:T(8,128)(2,1)}, bf16[512,128]{1,0:T(8,128)(2,1)}, bf16[512,128]{1,0:T(8,128)(2,1)}) custom-call(s32[1]{0:T(128)} %bitcast.3.place_ref, bf16[16,400,128]{2,1,0:T(8,128)(2,1)} %copy-done, bf16[512,128]{1,0:T(8,128)(2,1)} %get-tuple-element.14.refs_0_, ...), custom_call_target="tpu_custom_call" | custom-call | flops 200000000 | tf_op jit(solution)/shard_map/attention_forward/pallas_call | solution.py:204
  88.6 1.6 collective-permute-start.6
  90.2 2.5 %collective-permute-start.11 = (bf16[512,128]{1,0:T(8,128)(2,1)}, bf16[512,128]{1,0:T(8,128)(2,1)S(1)}, u32[]{:S(2)}, u32[]{:S(2)}) collective-permute-start(bf16[512,128]{1,0:T(8,128)(2,1)} %get-tuple-element.21), channel_id=1, source_target_pairs={{0,8},{1,9},{2,10},{3,11},{4,12},{5,13},{6,14},{7,15},{8,0},{9,1},... | collective-permute-start | bytes 393224 | tf_op jit(solution)/shard_map/ppermute | solution.py:31
  92.8 1.0 copy-done.10
  94.7 2.1 %collective-permute-done.11.array_ref = bf16[512,128]{1,0:T(8,128)(2,1)S(1)} collective-permute-done((bf16[512,128]{1,0:T(8,128)(2,1)}, bf16[512,128]{1,0:T(8,128)(2,1)S(1)}, u32[]{:S(2)}, u32[]{:S(2)}) %collective-permute-start.11) | collective-permute-done | bytes 131104 | tf_op jit(solution)/shard_map/ppermute | solution.py:31
  96.8 3.5 %all-to-all-done.1.refs_0_.in_hbm_ref = bf16[16,400,128]{2,1,0:T(8,128)(2,1)S(1)} async-done(((bf16[16,400,128]{2,1,0:T(8,128)(2,1)}), bf16[16,400,128]{2,1,0:T(8,128)(2,1)S(1)}, u32[]{:S(2)}, u32[]{:S(2)}) %all-to-all-start.1) | async-done | bytes 1638432 | tf_op jit(solution)/shard_map/all_to_all | solution.py:509
  100.2 1.3 collective-permute-done.12.refs_1_.second_ref
  103.0 4.7 %project.1 = (f32[128,3072]{1,0:T(8,128)}, f32[128,3072]{1,0:T(8,128)}, bf16[256,3072]{1,0:T(8,128)(2,1)}) custom-call(s32[1]{0:T(128)} %bitcast.3.place_ref, bf16[512,128]{1,0:T(8,128)(2,1)} %get-tuple-element.15.refs_0_, bf16[512,128]{1,0:T(8,128)(2,1)} %copy-done.17, bf16[512,128]{1,0:T(8,128)(2,1)} %copy-done.18, bf16[512,128]{1,0:T(8,128)(2,1)} %copy-done.6, ...), custom_call_target="tpu_custom_call" | custom-call | flops 200000000 | tf_op jit(solution)/shard_map/project/pallas_call | solution.py:420
  108.4 3.2 %collective-permute-done.13 = bf16[256,3072]{1,0:T(8,128)(2,1)S(1)} collective-permute-done((bf16[256,3072]{1,0:T(8,128)(2,1)}, bf16[256,3072]{1,0:T(8,128)(2,1)S(1)}, u32[]{:S(2)}, u32[]{:S(2)}) %collective-permute-start.13) | collective-permute-done | bytes 1572896 | tf_op jit(solution)/shard_map/ppermute | solution.py:540
  111.7 3.0 %add_convert_fusion.refs_4_ = bf16[128,3072]{1,0:T(8,128)(2,1)} fusion(f32[128,3072]{1,0:T(8,128)} %get-tuple-element.24, bf16[256,3072]{1,0:T(8,128)(2,1)S(1)} %collective-permute-done.13), kind=kLoop, calls=%fused_computation.4 | loop fusion | flops 1179648 | bytes 3145728 | tf_op jit(solution)/shard_map/convert_element_type | solution.py:542
  115.5 17.2 %attention_backward.1 = bf16[16,384,128]{2,1,0:T(8,128)(2,1)} custom-call(s32[1]{0:T(128)} %bitcast.3.place_ref, bf16[16,400,128]{2,1,0:T(8,128)(2,1)} %copy-done.1, bf16[512,128]{1,0:T(8,128)(2,1)} %get-tuple-element.14.refs_0_, bf16[512,128]{1,0:T(8,128)(2,1)} %copy-done.7, bf16[512,128]{1,0:T(8,128)(2,1)} %copy-done.8, bf16[512,128]{1,0:T(8,128)(2,1)} %copy-done.9, ...), custom_call_target="tpu_custom_call" | custom-call | flops 30000001024 | tf_op jit(solution)/shard_map/attention_backward/pallas_call | solution.py:305
  132.7 5.7 %all-to-all-start.2 = ((bf16[16,384,128]{2,1,0:T(8,128)(2,1)}), bf16[16,384,128]{2,1,0:T(8,128)(2,1)S(1)}, u32[]{:S(2)}, u32[]{:S(2)}) async-start(bf16[16,384,128]{2,1,0:T(8,128)(2,1)} %attention_backward.1), calls=%async_computation.2 | async-start | bytes 3145728 | tf_op jit(solution)/shard_map/all_to_all | solution.py:509
  138.4 3.7 %fusion.1 = bf16[128,3072]{1,0:T(8,128)(2,1)} fusion(bf16[128,3072]{1,0:T(8,128)(2,1)} %param.18, f32[128,3072]{1,0:T(8,128)S(1)} %copy-done.12, bf16[128,3072]{1,0:T(8,128)(2,1)} %collective-permute-done.14, f32[128,3072]{1,0:T(8,128)} %get-tuple-element.22, bf16[256,3072]{1,0:T(8,128)(2,1)} %copy-done.16, bf16[1,128,3072]{2,1,0:T(8,128)(2,1)} %param.10, ...), kind=kLoop, calls=%fused_computation.6 | loop fusion | flops 3538944 | bytes 7077889 | tf_op jit(solution)/shard_map/jit(_where)/select_n | solution.py:547
  142.6 1.5 choose.1
  144.1 15.6 %all-to-all-done.2.in_ref = bf16[16,384,128]{2,1,0:T(8,128)(2,1)S(1)} async-done(((bf16[16,384,128]{2,1,0:T(8,128)(2,1)}), bf16[16,384,128]{2,1,0:T(8,128)(2,1)S(1)}, u32[]{:S(2)}, u32[]{:S(2)}) %all-to-all-start.2) | async-done | bytes 1572896 | tf_op jit(solution)/shard_map/all_to_all | solution.py:509
  159.7 1.6 unpack.1
  161.3 13.1 %collective-permute-done.15 = bf16[128,3072]{1,0:T(8,128)(2,1)S(1)} collective-permute-done((bf16[128,3072]{1,0:T(8,128)(2,1)}, bf16[128,3072]{1,0:T(8,128)(2,1)S(1)}, u32[]{:S(2)}, u32[]{:S(2)}) %collective-permute-start.15) | collective-permute-done | bytes 786464 | tf_op jit(solution)/shard_map/ppermute | solution.py:500
  (68 shorter events, 10.3 us)
Async XLA Ops:
  0.6 20.2 %collective-permute-start.5 = (bf16[128,3072]{1,0:T(8,128)(2,1)}, bf16[128,3072]{1,0:T(8,128)(2,1)S(1)}, u32[]{:S(2)}, u32[]{:S(2)}) collective-permute-start(bf16[128,3072]{1,0:T(8,128)(2,1)} %bitcast.24), channel_id=1, source_target_pairs={{0,8},{1,9},{2,10},{3,11},{4,12},{5,13},{6,14},{7,15},{8,0},{9,1},... | collective-permute-start | bytes 2359304 | tf_op jit(solution)/shard_map/ppermute | solution.py:31
  4.3 35.0 %collective-permute-start.4 = (bf16[128,3072]{1,0:T(8,128)(2,1)}, bf16[128,3072]{1,0:T(8,128)(2,1)S(1)}, u32[]{:S(2)}, u32[]{:S(2)}) collective-permute-start(bf16[128,3072]{1,0:T(8,128)(2,1)} %bitcast.25), channel_id=1, source_target_pairs={{0,12},{1,13},{2,14},{3,15},{4,0},{5,1},{6,2},{7,3},{8,4},{9,5},{1... | collective-permute-start | bytes 2359304 | tf_op jit(solution)/shard_map/ppermute | solution.py:31
  5.2 34.3 %collective-permute-start.3 = (bf16[128,3072]{1,0:T(8,128)(2,1)}, bf16[128,3072]{1,0:T(8,128)(2,1)}, u32[]{:S(2)}, u32[]{:S(2)}) collective-permute-start(bf16[128,3072]{1,0:T(8,128)(2,1)} %bitcast.26), channel_id=1, source_target_pairs={{0,4},{1,5},{2,6},{3,7},{4,8},{5,9},{6,10},{7,11},{8,12},{9,13},{1... | collective-permute-start | bytes 2359304 | tf_op jit(solution)/shard_map/ppermute | solution.py:31
  9.9 6.3 %copy-start.19 = (f32[1,2,4,3072]{3,2,1,0:T(4,128)S(1)}, f32[1,2,4,3072]{3,2,1,0:T(4,128)}, u32[]{:S(2)}) copy-start(f32[1,2,4,3072]{3,2,1,0:T(4,128)} %param.15) | copy-start | bytes 294916
  9.9 48.3 %all-to-all-start = ((bf16[16,400,128]{2,1,0:T(8,128)(2,1)}), bf16[16,400,128]{2,1,0:T(8,128)(2,1)S(1)}, u32[]{:S(2)}, u32[]{:S(2)}) async-start(bf16[16,400,128]{2,1,0:T(8,128)(2,1)} %pack.2), calls=%async_computation | async-start | bytes 3276800 | tf_op jit(solution)/shard_map/all_to_all | solution.py:509
  17.5 21.8 %copy-start.15 = (bf16[128,3072]{1,0:T(8,128)(2,1)}, bf16[128,3072]{1,0:T(8,128)(2,1)S(1)}, u32[]{:S(2)}) copy-start(bf16[128,3072]{1,0:T(8,128)(2,1)S(1)} %multiply_convert_fusion.refs_0_) | copy-start | bytes 2359300
  17.5 22.4 %collective-permute-start.1 = (bf16[128,3072]{1,0:T(8,128)(2,1)S(1)}, bf16[128,3072]{1,0:T(8,128)(2,1)}, u32[]{:S(2)}, u32[]{:S(2)}) collective-permute-start(bf16[128,3072]{1,0:T(8,128)(2,1)S(1)} %multiply_convert_fusion.refs_0_), channel_id=1, source_target_pairs={{0,2},{1,3},{2,0},{3,1},{4,6},{5,7},{6,4},{7,5},{8,10},{9,11},{10,... | collective-permute-start | bytes 2359304 | tf_op jit(solution)/shard_map/ppermute | solution.py:523
  20.9 19.0 %copy-start.13 = (bf16[128,3072]{1,0:T(8,128)(2,1)}, bf16[128,3072]{1,0:T(8,128)(2,1)S(1)}, u32[]{:S(2)}) copy-start(bf16[128,3072]{1,0:T(8,128)(2,1)S(1)} %collective-permute-done.5.refs_7_.refs_4_) | copy-start | bytes 2359300
  58.1 5.3 %copy-start = (bf16[16,400,128]{2,1,0:T(8,128)(2,1)}, bf16[16,400,128]{2,1,0:T(8,128)(2,1)S(1)}, u32[]{:S(2)}) copy-start(bf16[16,400,128]{2,1,0:T(8,128)(2,1)S(1)} %all-to-all-done.refs_0_.in_hbm_ref) | copy-start | bytes 4915204
  58.1 42.1 %all-to-all-start.1 = ((bf16[16,400,128]{2,1,0:T(8,128)(2,1)}), bf16[16,400,128]{2,1,0:T(8,128)(2,1)S(1)}, u32[]{:S(2)}, u32[]{:S(2)}) async-start(bf16[16,400,128]{2,1,0:T(8,128)(2,1)} %pack.3), calls=%async_computation.1 | async-start | bytes 3276800 | tf_op jit(solution)/shard_map/all_to_all | solution.py:509
  63.0 3.9 %collective-permute-start = (bf16[128,3072]{1,0:T(8,128)(2,1)}, bf16[128,3072]{1,0:T(8,128)(2,1)}, u32[]{:S(2)}, u32[]{:S(2)}) collective-permute-start(bf16[128,3072]{1,0:T(8,128)(2,1)} %copy-done.15), channel_id=1, source_target_pairs={{0,1},{1,0},{2,3},{3,2},{4,5},{5,4},{6,7},{7,6},{8,9},{9,8},{10,11... | collective-permute-start | bytes 2359304 | tf_op jit(solution)/shard_map/ppermute | solution.py:524
  63.2 3.7 %collective-permute-start.2 = (bf16[128,3072]{1,0:T(8,128)(2,1)}, bf16[128,3072]{1,0:T(8,128)(2,1)}, u32[]{:S(2)}, u32[]{:S(2)}) collective-permute-start(bf16[128,3072]{1,0:T(8,128)(2,1)} %collective-permute-done.1.refs_2_.refs_0_), channel_id=1, source_target_pairs={{0,1},{1,0},{2,3},{3,2},{4,5},{5,4},{6,7},{7,6},{8,9},{9,8},{10,11... | collective-permute-start | bytes 2359304 | tf_op jit(solution)/shard_map/ppermute | solution.py:525
  65.6 36.0 %collective-permute-start.12 = (bf16[128,3072]{1,0:T(8,128)(2,1)}, bf16[128,3072]{1,0:T(8,128)(2,1)S(1)}, u32[]{:S(2)}, u32[]{:S(2)}) collective-permute-start(bf16[128,3072]{1,0:T(8,128)(2,1)} %settle.1.refs_2_), channel_id=1, source_target_pairs={{16,0},{32,16},{48,32},{64,48},{80,64},{96,80},{112,96},{128,112},... | collective-permute-start | bytes 2359304 | tf_op jit(solution)/shard_map/ppermute | solution.py:495
  72.4 17.8 %collective-permute-start.7 = (bf16[512,128]{1,0:T(8,128)(2,1)}, bf16[512,128]{1,0:T(8,128)(2,1)S(1)}, u32[]{:S(2)}, u32[]{:S(2)}) collective-permute-start(bf16[512,128]{1,0:T(8,128)(2,1)} %get-tuple-element.18), channel_id=1, source_target_pairs={{0,12},{1,13},{2,14},{3,15},{4,0},{5,1},{6,2},{7,3},{8,4},{9,5},{1... | collective-permute-start | bytes 393224 | tf_op jit(solution)/shard_map/ppermute | solution.py:31
  75.1 17.7 %collective-permute-start.8 = (bf16[512,128]{1,0:T(8,128)(2,1)}, bf16[512,128]{1,0:T(8,128)(2,1)S(1)}, u32[]{:S(2)}, u32[]{:S(2)}) collective-permute-start(bf16[512,128]{1,0:T(8,128)(2,1)} %get-tuple-element.19), channel_id=1, source_target_pairs={{0,4},{1,5},{2,6},{3,7},{4,8},{5,9},{6,10},{7,11},{8,12},{9,13},{1... | collective-permute-start | bytes 393224 | tf_op jit(solution)/shard_map/ppermute | solution.py:31
  75.1 17.7 %collective-permute-start.9 = (bf16[512,128]{1,0:T(8,128)(2,1)}, bf16[512,128]{1,0:T(8,128)(2,1)S(1)}, u32[]{:S(2)}, u32[]{:S(2)}) collective-permute-start(bf16[512,128]{1,0:T(8,128)(2,1)} %get-tuple-element.20), channel_id=1, source_target_pairs={{0,8},{1,9},{2,10},{3,11},{4,12},{5,13},{6,14},{7,15},{8,0},{9,1},... | collective-permute-start | bytes 393224 | tf_op jit(solution)/shard_map/ppermute | solution.py:31
  88.6 13.6 %collective-permute-start.6 = (bf16[512,128]{1,0:T(8,128)(2,1)}, bf16[512,128]{1,0:T(8,128)(2,1)S(1)}, u32[]{:S(2)}, u32[]{:S(2)}) collective-permute-start(bf16[512,128]{1,0:T(8,128)(2,1)} %get-tuple-element.16), channel_id=1, source_target_pairs={{0,4},{1,5},{2,6},{3,7},{4,8},{5,9},{6,10},{7,11},{8,12},{9,13},{1... | collective-permute-start | bytes 393224 | tf_op jit(solution)/shard_map/ppermute | solution.py:31
  90.2 11.3 %copy-start.7 = (bf16[512,128]{1,0:T(8,128)(2,1)}, bf16[512,128]{1,0:T(8,128)(2,1)S(1)}, u32[]{:S(2)}) copy-start(bf16[512,128]{1,0:T(8,128)(2,1)S(1)} %collective-permute-done.7.refs_0_.refs_1_) | copy-start | bytes 393220
  90.2 6.5 %collective-permute-start.11 = (bf16[512,128]{1,0:T(8,128)(2,1)}, bf16[512,128]{1,0:T(8,128)(2,1)S(1)}, u32[]{:S(2)}, u32[]{:S(2)}) collective-permute-start(bf16[512,128]{1,0:T(8,128)(2,1)} %get-tuple-element.21), channel_id=1, source_target_pairs={{0,8},{1,9},{2,10},{3,11},{4,12},{5,13},{6,14},{7,15},{8,0},{9,1},... | collective-permute-start | bytes 393224 | tf_op jit(solution)/shard_map/ppermute | solution.py:31
  92.7 8.8 %copy-start.8 = (bf16[512,128]{1,0:T(8,128)(2,1)}, bf16[512,128]{1,0:T(8,128)(2,1)S(1)}, u32[]{:S(2)}) copy-start(bf16[512,128]{1,0:T(8,128)(2,1)S(1)} %collective-permute-done.8.refs_1_.refs_2_) | copy-start | bytes 393220
  92.8 8.8 %copy-start.9 = (bf16[512,128]{1,0:T(8,128)(2,1)}, bf16[512,128]{1,0:T(8,128)(2,1)S(1)}, u32[]{:S(2)}) copy-start(bf16[512,128]{1,0:T(8,128)(2,1)S(1)} %collective-permute-done.9.refs_2_.refs_3_) | copy-start | bytes 393220
  93.8 8.5 %collective-permute-start.10 = (bf16[512,128]{1,0:T(8,128)(2,1)S(1)}, bf16[512,128]{1,0:T(8,128)(2,1)S(1)}, u32[]{:S(2)}, u32[]{:S(2)}) collective-permute-start(bf16[512,128]{1,0:T(8,128)(2,1)S(1)} %follow.2), channel_id=1, source_target_pairs={{0,12},{1,13},{2,14},{3,15},{4,0},{5,1},{6,2},{7,3},{8,4},{9,5},{1... | collective-permute-start | bytes 393224 | tf_op jit(solution)/shard_map/ppermute | solution.py:31
  100.2 7.5 %copy-start.1 = (bf16[16,400,128]{2,1,0:T(8,128)(2,1)}, bf16[16,400,128]{2,1,0:T(8,128)(2,1)S(1)}, u32[]{:S(2)}) copy-start(bf16[16,400,128]{2,1,0:T(8,128)(2,1)S(1)} %all-to-all-done.1.refs_0_.in_hbm_ref) | copy-start | bytes 4915204
  101.5 6.2 %copy-start.4 = (bf16[128,3072]{1,0:T(8,128)(2,1)}, bf16[128,3072]{1,0:T(8,128)(2,1)S(1)}, u32[]{:S(2)}) copy-start(bf16[128,3072]{1,0:T(8,128)(2,1)S(1)} %collective-permute-done.12.refs_1_.second_ref) | copy-start | bytes 2359300
  107.7 3.9 %collective-permute-start.13 = (bf16[256,3072]{1,0:T(8,128)(2,1)}, bf16[256,3072]{1,0:T(8,128)(2,1)S(1)}, u32[]{:S(2)}, u32[]{:S(2)}) collective-permute-start(bf16[256,3072]{1,0:T(8,128)(2,1)} %get-tuple-element.23), channel_id=1, source_target_pairs={{0,1},{1,0},{2,3},{3,2},{4,5},{5,4},{6,7},{7,6},{8,9},{9,8},{10,11... | collective-permute-start | bytes 4718600 | tf_op jit(solution)/shard_map/ppermute | solution.py:540
  111.7 3.0 %copy-start.16 = (bf16[256,3072]{1,0:T(8,128)(2,1)}, bf16[256,3072]{1,0:T(8,128)(2,1)S(1)}, u32[]{:S(2)}) copy-start(bf16[256,3072]{1,0:T(8,128)(2,1)S(1)} %collective-permute-done.13) | copy-start | bytes 4718596
  114.7 23.7 %collective-permute-start.14 = (bf16[128,3072]{1,0:T(8,128)(2,1)}, bf16[128,3072]{1,0:T(8,128)(2,1)}, u32[]{:S(2)}, u32[]{:S(2)}) collective-permute-start(bf16[128,3072]{1,0:T(8,128)(2,1)} %add_convert_fusion.refs_4_), channel_id=1, source_target_pairs={{0,2},{1,3},{2,0},{3,1},{4,6},{5,7},{6,4},{7,5},{8,10},{9,11},{10,... | collective-permute-start | bytes 2359304 | tf_op jit(solution)/shard_map/ppermute | solution.py:544
  132.7 5.7 %copy-start.12 = (f32[128,3072]{1,0:T(8,128)S(1)}, f32[128,3072]{1,0:T(8,128)}, u32[]{:S(2)}) copy-start(f32[128,3072]{1,0:T(8,128)} %multiply_reduce_fusion.1.refs_1_) | copy-start | bytes 4718596
  132.7 27.0 %all-to-all-start.2 = ((bf16[16,384,128]{2,1,0:T(8,128)(2,1)}), bf16[16,384,128]{2,1,0:T(8,128)(2,1)S(1)}, u32[]{:S(2)}, u32[]{:S(2)}) async-start(bf16[16,384,128]{2,1,0:T(8,128)(2,1)} %attention_backward.1), calls=%async_computation.2 | async-start | bytes 3145728 | tf_op jit(solution)/shard_map/all_to_all | solution.py:509
  138.4 4.2 %copy-start.5 = (bf16[128,3072]{1,0:T(8,128)(2,1)S(1)}, bf16[128,3072]{1,0:T(8,128)(2,1)}, u32[]{:S(2)}) copy-start(bf16[128,3072]{1,0:T(8,128)(2,1)} %copy-done.4) | copy-start | bytes 2359300
  138.4 4.2 %copy-start.11 = (bf16[128,3072]{1,0:T(8,128)(2,1)S(1)}, bf16[128,3072]{1,0:T(8,128)(2,1)}, u32[]{:S(2)}) copy-start(bf16[128,3072]{1,0:T(8,128)(2,1)} %first_ref.1) | copy-start | bytes 2359300
  142.2 32.3 %collective-permute-start.15 = (bf16[128,3072]{1,0:T(8,128)(2,1)}, bf16[128,3072]{1,0:T(8,128)(2,1)S(1)}, u32[]{:S(2)}, u32[]{:S(2)}) collective-permute-start(bf16[128,3072]{1,0:T(8,128)(2,1)} %fusion.1), channel_id=1, source_target_pairs={{0,16},{16,32},{32,48},{48,64},{64,80},{80,96},{96,112},{112,128},... | collective-permute-start | bytes 2359304 | tf_op jit(solution)/shard_map/ppermute | solution.py:500
  (7 other events, 6.2 us)

commit v7 on v6

--- a/solution.py
+++ b/solution.py
@@ -522,10 +522,11 @@
     g_scaled = (per_sample(local_seg[1], gates[0, 1]) * upstream[0].astype(F32)).astype(BF16)
     g_across = lax.ppermute(g_scaled, "seq", YSWAP)
     g_core = lax.ppermute(g_scaled, "seq", CORE)
+    g_across = follow(g_across, *pieces[1:])
     g_both = lax.ppermute(g_across, "seq", CORE)
     gate_tok = per_sample(local_seg[0], gates[0, 0])
     grads = attention_grad(place, (g_scaled, g_core, g_across, g_both), pieces)
-    packed = pack(queries, keys, values, segments, 1, g_across, gate_tok, *pieces[1:])
+    packed = pack(queries, keys, values, segments, 1, grads[0], gate_tok)
     bwd = exchange(packed)
 
     turned = settle(upstream[0], fwd)
@@ -535,9 +536,9 @@
     attns = (attns[0], follow(attns[1], *grads[1:])) + attns[2:]
     attns = tuple(along_x(a, o) for a, o in zip(attns, OFFSETS))
 
-    attns = (attns[0], attns[2], attns[1], follow(attns[3], bwd, moved))
+    attns = (attns[0], attns[2], attns[1], follow(attns[3], bwd))
     part, part_across, part_send = project(place, attns, pieces)
-    received = lax.ppermute(part_send, "seq", CORE)
+    received = lax.ppermute(follow(part_send, moved), "seq", CORE)
     rows = part.shape[0]
     across = (part_across + received[rows:].astype(F32)).astype(BF16)
     grads = attention_backward(place, bwd, grads, across)

time: 176 us -> 185 us (1.051)
  starting transfers between devices: 36.4 us -> 49.4 us
  waiting for transfers between devices: 73.2 us -> 65.1 us
  local copies, waits for them, and re-layouts: 6.51 us -> 9.96 us
    all_to_all x3, waiting for transfers between devices: 34.3 us -> 18.7 us  [exchange(): return lax.all_to_all(array, 'seq', 0, 0, tiled=True)]
    ppermute x9, waiting for transfers between devices: 20.9 us -> 28.4 us  [along_x(): lax.ppermute(array, 'seq', [(i, (i + PER_X * offset) % count) for i in ra...]
    ppermute x1, starting transfers between devices: 0.32 us -> 7.22 us  [body(): g_both = lax.ppermute(g_across, 'seq', CORE)]
    all_to_all x3, starting transfers between devices: 16.8 us -> 20.3 us  [exchange(): return lax.all_to_all(array, 'seq', 0, 0, tiled=True)]
    unnamed x41 -> x47, local copies, waits for them, and re-layouts: 5.21 us -> 7.85 us
    ppermute x1, waiting for transfers between devices: 0.41 us -> 2.71 us  [body(): g_across = lax.ppermute(g_scaled, 'seq', YSWAP)]
  transfers between devices with their start and end apart: 19 -> 19, of which waited for: 11 -> 10; matrix products, arithmetic and copies ran while one was open for 4% -> 3% of each run, Pallas kernels for 25% -> 27%
where the time goes in v7:
time: 185 us; the launch traced here: 183 us
  waiting for transfers between devices  65.1 us (35%)
  starting transfers between devices  49.4 us (27%)
  Pallas kernels  49.1 us (27%)
  local copies, waits for them, and re-layouts  9.96 us (5%)
  other arithmetic  8.82 us (5%)
    ppermute x9, waiting for transfers between devices, along_x(): lax.ppermute(array, 'seq', [(i, (i + PER_X * offset) % count) for i in ra...  28.4 us
    all_to_all x3, starting transfers between devices, exchange(): return lax.all_to_all(array, 'seq', 0, 0, tiled=True)  20.3 us
    all_to_all x3, waiting for transfers between devices, exchange(): return lax.all_to_all(array, 'seq', 0, 0, tiled=True)  18.7 us
    pallas_call x1, Pallas kernels, attention_backward(): pl.pallas_call(backward_kernel, out_shape=jax.ShapeDtypeStruct((blocks, 3...  17.2 us
    ppermute x9, starting transfers between devices, along_x(): lax.ppermute(array, 'seq', [(i, (i + PER_X * offset) % count) for i in ra...  14 us
    pallas_call x1, Pallas kernels, attention_forward(): pl.pallas_call(forward_kernel, out_shape=(jax.ShapeDtypeStruct((total //...  11.8 us
    ppermute x1, waiting for transfers between devices, rotated(): lax.ppermute(array, axis, [(i, (i + by) % length) for i in range(length)])  11.5 us
    unnamed x47, local copies, waits for them, and re-layouts  7.85 us
  transfers between devices with their start and end apart: 19, of which 10 were waited for; matrix products, arithmetic and copies ran while one was open for 3% of the time, Pallas kernels for 27%

profile of v7, /device:TPU:1, one launch (start us, length us, event | category | flops | bytes accessed | tf_op | source)
XLA Modules:
  0.0 183.1 jit_solution(3653692192422093970)
XLA Ops:
  4.4 2.1 %collective-permute-start.1 = (bf16[128,3072]{1,0:T(8,128)(2,1)}, bf16[128,3072]{1,0:T(8,128)(2,1)}, u32[]{:S(2)}, u32[]{:S(2)}) collective-permute-start(bf16[128,3072]{1,0:T(8,128)(2,1)} %multiply_convert_fusion.refs_0_), channel_id=1, source_target_pairs={{0,2},{1,3},{2,0},{3,1},{4,6},{5,7},{6,4},{7,5},{8,10},{9,11},{10,... | collective-permute-start | bytes 2359304 | tf_op jit(solution)/shard_map/ppermute | solution.py:523
  7.7 1.5 collective-permute-start.3
  9.2 1.5 collective-permute-start.4
  10.7 2.8 %pack.2 = bf16[16,400,128]{2,1,0:T(8,128)(2,1)} custom-call(s32[1,128]{1,0:T(1,128)} %get-tuple-element.28.seg_ref, bf16[1,2,128,2048]{3,2,1,0:T(8,128)(2,1)} %q_ref.3, bf16[1,2,128,2048]{3,2,1,0:T(8,128)(2,1)} %k_ref.3, bf16[1,2,128,2048]{3,2,1,0:T(8,128)(2,1)} %v_ref.3), custom_call_target="tpu_custom_call" | custom-call | flops 2000000000 | tf_op jit(solution)/shard_map/pack/pallas_call | solution.py:85
  13.5 6.4 %all-to-all-start = ((bf16[16,400,128]{2,1,0:T(8,128)(2,1)}), bf16[16,400,128]{2,1,0:T(8,128)(2,1)S(1)}, u32[]{:S(2)}, u32[]{:S(2)}) async-start(bf16[16,400,128]{2,1,0:T(8,128)(2,1)} %pack.2), calls=%async_computation | async-start | bytes 3276800 | tf_op jit(solution)/shard_map/all_to_all | solution.py:509
  20.1 2.7 %collective-permute-done.1.array_ref = bf16[128,3072]{1,0:T(8,128)(2,1)} collective-permute-done((bf16[128,3072]{1,0:T(8,128)(2,1)}, bf16[128,3072]{1,0:T(8,128)(2,1)}, u32[]{:S(2)}, u32[]{:S(2)}) %collective-permute-start.1) | collective-permute-done | bytes 786464 | tf_op jit(solution)/shard_map/ppermute | solution.py:523
  22.9 3.0 %collective-permute-done.2.refs_0_.refs_5_ = bf16[128,3072]{1,0:T(8,128)(2,1)S(1)} collective-permute-done((bf16[128,3072]{1,0:T(8,128)(2,1)}, bf16[128,3072]{1,0:T(8,128)(2,1)S(1)}, u32[]{:S(2)}, u32[]{:S(2)}) %collective-permute-start.2) | collective-permute-done | bytes 786464 | tf_op jit(solution)/shard_map/ppermute | solution.py:31
  25.9 18.2 %collective-permute-done.4.refs_2_.refs_7_ = bf16[128,3072]{1,0:T(8,128)(2,1)} collective-permute-done((bf16[128,3072]{1,0:T(8,128)(2,1)}, bf16[128,3072]{1,0:T(8,128)(2,1)}, u32[]{:S(2)}, u32[]{:S(2)}) %collective-permute-start.4) | collective-permute-done | bytes 786464 | tf_op jit(solution)/shard_map/ppermute | solution.py:31
  44.0 7.2 %collective-permute-start.5 = (bf16[128,3072]{1,0:T(8,128)(2,1)}, bf16[128,3072]{1,0:T(8,128)(2,1)}, u32[]{:S(2)}, u32[]{:S(2)}) collective-permute-start(bf16[128,3072]{1,0:T(8,128)(2,1)} %follow.4.refs_2_), channel_id=1, source_target_pairs={{0,1},{1,0},{2,3},{3,2},{4,5},{5,4},{6,7},{7,6},{8,9},{9,8},{10,11... | collective-permute-start | bytes 2359304 | tf_op jit(solution)/shard_map/ppermute | solution.py:526
  51.2 1.7 multiply_reduce_fusion.1.refs_1_
  53.5 5.5 %attention_grad.1 = (bf16[512,128]{1,0:T(8,128)(2,1)}, bf16[512,128]{1,0:T(8,128)(2,1)}, bf16[512,128]{1,0:T(8,128)(2,1)}, bf16[512,128]{1,0:T(8,128)(2,1)}) custom-call(s32[1]{0:T(128)} %bitcast.3.place_ref, bf16[128,3072]{1,0:T(8,128)(2,1)} %multiply_convert_fusion.refs_0_, bf16[128,3072]{1,0:T(8,128)(2,1)} %collective-permute-done.refs_1_, ...), custom_call_target="tpu_custom_call" | custom-call | flops 200000000 | tf_op jit(solution)/shard_map/attention_grad/pallas_call | solution.py:370
  59.0 2.8 %pack.3 = bf16[16,400,128]{2,1,0:T(8,128)(2,1)} custom-call(s32[1,128]{1,0:T(1,128)} %get-tuple-element.27.seg_ref, bf16[1,2,128,2048]{3,2,1,0:T(8,128)(2,1)} %q_ref.3, bf16[1,2,128,2048]{3,2,1,0:T(8,128)(2,1)} %k_ref.3, bf16[1,2,128,2048]{3,2,1,0:T(8,128)(2,1)} %v_ref.3, bf16[512,128]{1,0:T(8,128)(2,1)} %get-tuple-element.14.refs_0_, ...), custom_call_target="tpu_custom_call" | custom-call | flops 2000000000 | tf_op jit(solution)/shard_map/pack/pallas_call | solution.py:85
  61.9 8.2 %all-to-all-start.1 = ((bf16[16,400,128]{2,1,0:T(8,128)(2,1)}), bf16[16,400,128]{2,1,0:T(8,128)(2,1)S(1)}, u32[]{:S(2)}, u32[]{:S(2)}) async-start(bf16[16,400,128]{2,1,0:T(8,128)(2,1)} %pack.3), calls=%async_computation.1 | async-start | bytes 3276800 | tf_op jit(solution)/shard_map/all_to_all | solution.py:509
  73.4 2.7 %collective-permute-start.7 = (bf16[512,128]{1,0:T(8,128)(2,1)S(1)}, bf16[512,128]{1,0:T(8,128)(2,1)S(1)}, u32[]{:S(2)}, u32[]{:S(2)}) collective-permute-start(bf16[512,128]{1,0:T(8,128)(2,1)S(1)} %copy-done.22), channel_id=1, source_target_pairs={{0,12},{1,13},{2,14},{3,15},{4,0},{5,1},{6,2},{7,3},{8,4},{9,5},{1... | collective-permute-start | bytes 393224 | tf_op jit(solution)/shard_map/ppermute | solution.py:31
  76.1 1.8 collective-permute-start.9
  77.9 11.8 %attention_forward.1 = (bf16[512,128]{1,0:T(8,128)(2,1)}, bf16[512,128]{1,0:T(8,128)(2,1)}, bf16[512,128]{1,0:T(8,128)(2,1)}, bf16[512,128]{1,0:T(8,128)(2,1)}) custom-call(s32[1]{0:T(128)} %bitcast.3.place_ref, bf16[16,400,128]{2,1,0:T(8,128)(2,1)} %copy-done, bf16[512,128]{1,0:T(8,128)(2,1)} %get-tuple-element.14.refs_0_, ...), custom_call_target="tpu_custom_call" | custom-call | flops 200000000 | tf_op jit(solution)/shard_map/attention_forward/pallas_call | solution.py:204
  89.7 1.4 collective-permute-start.11
  91.1 5.8 %collective-permute-done.7.refs_0_.refs_1_ = bf16[512,128]{1,0:T(8,128)(2,1)S(1)} collective-permute-done((bf16[512,128]{1,0:T(8,128)(2,1)S(1)}, bf16[512,128]{1,0:T(8,128)(2,1)S(1)}, u32[]{:S(2)}, u32[]{:S(2)}) %collective-permute-start.7) | collective-permute-done | bytes 131104 | tf_op jit(solution)/shard_map/ppermute | solution.py:31
  96.9 1.4 collective-permute-done.9.refs_2_.refs_3_
  99.9 3.9 %collective-permute-start.10 = (bf16[512,128]{1,0:T(8,128)(2,1)}, bf16[512,128]{1,0:T(8,128)(2,1)S(1)}, u32[]{:S(2)}, u32[]{:S(2)}) collective-permute-start(bf16[512,128]{1,0:T(8,128)(2,1)} %copy-done.13), channel_id=1, source_target_pairs={{0,12},{1,13},{2,14},{3,15},{4,0},{5,1},{6,2},{7,3},{8,4},{9,5},{1... | collective-permute-start | bytes 393224 | tf_op jit(solution)/shard_map/ppermute | solution.py:31
  103.9 3.2 %all-to-all-done.1.refs_0_.in_hbm_ref = bf16[16,400,128]{2,1,0:T(8,128)(2,1)S(1)} async-done(((bf16[16,400,128]{2,1,0:T(8,128)(2,1)}), bf16[16,400,128]{2,1,0:T(8,128)(2,1)S(1)}, u32[]{:S(2)}, u32[]{:S(2)}) %all-to-all-start.1) | async-done | bytes 1638432 | tf_op jit(solution)/shard_map/all_to_all | solution.py:509
  108.4 4.8 %project.1 = (f32[128,3072]{1,0:T(8,128)}, f32[128,3072]{1,0:T(8,128)}, bf16[256,3072]{1,0:T(8,128)(2,1)}) custom-call(s32[1]{0:T(128)} %bitcast.3.place_ref, bf16[512,128]{1,0:T(8,128)(2,1)} %get-tuple-element.15.refs_0_, bf16[512,128]{1,0:T(8,128)(2,1)} %copy-done.18, bf16[512,128]{1,0:T(8,128)(2,1)} %copy-done.19, bf16[512,128]{1,0:T(8,128)(2,1)} %copy-done.8, ...), custom_call_target="tpu_custom_call" | custom-call | flops 200000000 | tf_op jit(solution)/shard_map/project/pallas_call | solution.py:420
  115.9 2.2 %collective-permute-start.13 = (bf16[256,3072]{1,0:T(8,128)(2,1)}, bf16[256,3072]{1,0:T(8,128)(2,1)S(1)}, u32[]{:S(2)}, u32[]{:S(2)}) collective-permute-start(bf16[256,3072]{1,0:T(8,128)(2,1)} %copy-done.7), channel_id=1, source_target_pairs={{0,1},{1,0},{2,3},{3,2},{4,5},{5,4},{6,7},{7,6},{8,9},{9,8},{10,11... | collective-permute-start | bytes 4718600 | tf_op jit(solution)/shard_map/ppermute | solution.py:541
  118.1 3.2 %collective-permute-done.13 = bf16[256,3072]{1,0:T(8,128)(2,1)S(1)} collective-permute-done((bf16[256,3072]{1,0:T(8,128)(2,1)}, bf16[256,3072]{1,0:T(8,128)(2,1)S(1)}, u32[]{:S(2)}, u32[]{:S(2)}) %collective-permute-start.13) | collective-permute-done | bytes 1572896 | tf_op jit(solution)/shard_map/ppermute | solution.py:541
  122.8 2.1 %collective-permute-start.14 = (bf16[128,3072]{1,0:T(8,128)(2,1)}, bf16[128,3072]{1,0:T(8,128)(2,1)}, u32[]{:S(2)}, u32[]{:S(2)}) collective-permute-start(bf16[128,3072]{1,0:T(8,128)(2,1)} %add_convert_fusion.refs_4_), channel_id=1, source_target_pairs={{0,2},{1,3},{2,0},{3,1},{4,6},{5,7},{6,4},{7,5},{8,10},{9,11},{10,... | collective-permute-start | bytes 2359304 | tf_op jit(solution)/shard_map/ppermute | solution.py:545
  124.9 17.2 %attention_backward.1 = bf16[16,384,128]{2,1,0:T(8,128)(2,1)} custom-call(s32[1]{0:T(128)} %bitcast.3.place_ref, bf16[16,400,128]{2,1,0:T(8,128)(2,1)} %copy-done.3, bf16[512,128]{1,0:T(8,128)(2,1)} %get-tuple-element.14.refs_0_, bf16[512,128]{1,0:T(8,128)(2,1)} %copy-done.9, bf16[512,128]{1,0:T(8,128)(2,1)} %copy-done.10, bf16[512,128]{1,0:T(8,128)(2,1)} %copy-done.11, ...), custom_call_target="tpu_custom_call" | custom-call | flops 30000001024 | tf_op jit(solution)/shard_map/attention_backward/pallas_call | solution.py:305
  142.2 5.6 %all-to-all-start.2 = ((bf16[16,384,128]{2,1,0:T(8,128)(2,1)}), bf16[16,384,128]{2,1,0:T(8,128)(2,1)S(1)}, u32[]{:S(2)}, u32[]{:S(2)}) async-start(bf16[16,384,128]{2,1,0:T(8,128)(2,1)} %attention_backward.1), calls=%async_computation.2 | async-start | bytes 3145728 | tf_op jit(solution)/shard_map/all_to_all | solution.py:509
  147.8 4.2 %fusion.1 = bf16[128,3072]{1,0:T(8,128)(2,1)} fusion(bf16[128,3072]{1,0:T(8,128)(2,1)S(1)} %copy-done.17, f32[128,3072]{1,0:T(8,128)} %multiply_reduce_fusion.1.refs_1_, bf16[128,3072]{1,0:T(8,128)(2,1)} %collective-permute-done.14, f32[128,3072]{1,0:T(8,128)} %get-tuple-element.22, bf16[256,3072]{1,0:T(8,128)(2,1)} %copy-done.15, ...), kind=kLoop, calls=%fused_computation.6 | loop fusion | flops 3538944 | bytes 7077889 | tf_op jit(solution)/shard_map/jit(_where)/select_n | solution.py:548
  152.1 1.5 choose.1
  153.6 15.5 %all-to-all-done.2.in_ref = bf16[16,384,128]{2,1,0:T(8,128)(2,1)S(1)} async-done(((bf16[16,384,128]{2,1,0:T(8,128)(2,1)}), bf16[16,384,128]{2,1,0:T(8,128)(2,1)S(1)}, u32[]{:S(2)}, u32[]{:S(2)}) %all-to-all-start.2) | async-done | bytes 1572896 | tf_op jit(solution)/shard_map/all_to_all | solution.py:509
  169.1 1.6 unpack.1
  170.7 11.5 %collective-permute-done.15 = bf16[128,3072]{1,0:T(8,128)(2,1)S(1)} collective-permute-done((bf16[128,3072]{1,0:T(8,128)(2,1)}, bf16[128,3072]{1,0:T(8,128)(2,1)S(1)}, u32[]{:S(2)}, u32[]{:S(2)}) %collective-permute-start.15) | collective-permute-done | bytes 786464 | tf_op jit(solution)/shard_map/ppermute | solution.py:500
  (76 shorter events, 17.1 us)
Async XLA Ops:
  0.6 2.7 %copy-start.4 = (bf16[1,128,3072]{2,1,0:T(8,128)(2,1)S(1)}, bf16[1,128,3072]{2,1,0:T(8,128)(2,1)}, u32[]{:S(2)}) copy-start(bf16[1,128,3072]{2,1,0:T(8,128)(2,1)} %param.17) | copy-start | bytes 2359300
  4.4 18.5 %collective-permute-start.1 = (bf16[128,3072]{1,0:T(8,128)(2,1)}, bf16[128,3072]{1,0:T(8,128)(2,1)}, u32[]{:S(2)}, u32[]{:S(2)}) collective-permute-start(bf16[128,3072]{1,0:T(8,128)(2,1)} %multiply_convert_fusion.refs_0_), channel_id=1, source_target_pairs={{0,2},{1,3},{2,0},{3,1},{4,6},{5,7},{6,4},{7,5},{8,10},{9,11},{10,... | collective-permute-start | bytes 2359304 | tf_op jit(solution)/shard_map/ppermute | solution.py:523
  6.5 19.3 %collective-permute-start.2 = (bf16[128,3072]{1,0:T(8,128)(2,1)}, bf16[128,3072]{1,0:T(8,128)(2,1)S(1)}, u32[]{:S(2)}, u32[]{:S(2)}) collective-permute-start(bf16[128,3072]{1,0:T(8,128)(2,1)} %bitcast.8.refs_4_), channel_id=1, source_target_pairs={{0,4},{1,5},{2,6},{3,7},{4,8},{5,9},{6,10},{7,11},{8,12},{9,13},{1... | collective-permute-start | bytes 2359304 | tf_op jit(solution)/shard_map/ppermute | solution.py:31
  7.7 18.1 %collective-permute-start.3 = (bf16[128,3072]{1,0:T(8,128)(2,1)}, bf16[128,3072]{1,0:T(8,128)(2,1)S(1)}, u32[]{:S(2)}, u32[]{:S(2)}) collective-permute-start(bf16[128,3072]{1,0:T(8,128)(2,1)} %bitcast.8.refs_4_), channel_id=1, source_target_pairs={{0,12},{1,13},{2,14},{3,15},{4,0},{5,1},{6,2},{7,3},{8,4},{9,5},{1... | collective-permute-start | bytes 2359304 | tf_op jit(solution)/shard_map/ppermute | solution.py:31
  9.2 34.8 %collective-permute-start.4 = (bf16[128,3072]{1,0:T(8,128)(2,1)}, bf16[128,3072]{1,0:T(8,128)(2,1)}, u32[]{:S(2)}, u32[]{:S(2)}) collective-permute-start(bf16[128,3072]{1,0:T(8,128)(2,1)} %bitcast.8.refs_4_), channel_id=1, source_target_pairs={{0,8},{1,9},{2,10},{3,11},{4,12},{5,13},{6,14},{7,15},{8,0},{9,1},... | collective-permute-start | bytes 2359304 | tf_op jit(solution)/shard_map/ppermute | solution.py:31
  13.5 48.3 %all-to-all-start = ((bf16[16,400,128]{2,1,0:T(8,128)(2,1)}), bf16[16,400,128]{2,1,0:T(8,128)(2,1)S(1)}, u32[]{:S(2)}, u32[]{:S(2)}) async-start(bf16[16,400,128]{2,1,0:T(8,128)(2,1)} %pack.2), calls=%async_computation | async-start | bytes 3276800 | tf_op jit(solution)/shard_map/all_to_all | solution.py:509
  20.0 33.0 %collective-permute-start = (bf16[128,3072]{1,0:T(8,128)(2,1)}, bf16[128,3072]{1,0:T(8,128)(2,1)}, u32[]{:S(2)}, u32[]{:S(2)}) collective-permute-start(bf16[128,3072]{1,0:T(8,128)(2,1)} %multiply_convert_fusion.refs_0_), channel_id=1, source_target_pairs={{0,1},{1,0},{2,3},{3,2},{4,5},{5,4},{6,7},{7,6},{8,9},{9,8},{10,11... | collective-permute-start | bytes 2359304 | tf_op jit(solution)/shard_map/ppermute | solution.py:524
  25.8 18.2 %copy-start.1 = (bf16[128,3072]{1,0:T(8,128)(2,1)}, bf16[128,3072]{1,0:T(8,128)(2,1)S(1)}, u32[]{:S(2)}) copy-start(bf16[128,3072]{1,0:T(8,128)(2,1)S(1)} %collective-permute-done.2.refs_0_.refs_5_) | copy-start | bytes 2359300
  25.9 18.2 %copy-start.2 = (bf16[128,3072]{1,0:T(8,128)(2,1)}, bf16[128,3072]{1,0:T(8,128)(2,1)S(1)}, u32[]{:S(2)}) copy-start(bf16[128,3072]{1,0:T(8,128)(2,1)S(1)} %collective-permute-done.3.refs_1_.refs_6_) | copy-start | bytes 2359300
  44.0 9.5 %collective-permute-start.5 = (bf16[128,3072]{1,0:T(8,128)(2,1)}, bf16[128,3072]{1,0:T(8,128)(2,1)}, u32[]{:S(2)}, u32[]{:S(2)}) collective-permute-start(bf16[128,3072]{1,0:T(8,128)(2,1)} %follow.4.refs_2_), channel_id=1, source_target_pairs={{0,1},{1,0},{2,3},{3,2},{4,5},{5,4},{6,7},{7,6},{8,9},{9,8},{10,11... | collective-permute-start | bytes 2359304 | tf_op jit(solution)/shard_map/ppermute | solution.py:526
  61.9 8.2 %copy-start = (bf16[16,400,128]{2,1,0:T(8,128)(2,1)}, bf16[16,400,128]{2,1,0:T(8,128)(2,1)S(1)}, u32[]{:S(2)}) copy-start(bf16[16,400,128]{2,1,0:T(8,128)(2,1)S(1)} %all-to-all-done.refs_0_.in_hbm_ref) | copy-start | bytes 4915204
  61.9 45.1 %all-to-all-start.1 = ((bf16[16,400,128]{2,1,0:T(8,128)(2,1)}), bf16[16,400,128]{2,1,0:T(8,128)(2,1)S(1)}, u32[]{:S(2)}, u32[]{:S(2)}) async-start(bf16[16,400,128]{2,1,0:T(8,128)(2,1)} %pack.3), calls=%async_computation.1 | async-start | bytes 3276800 | tf_op jit(solution)/shard_map/all_to_all | solution.py:509
  71.2 4.9 %copy-start.21 = (bf16[512,128]{1,0:T(8,128)(2,1)S(1)}, bf16[512,128]{1,0:T(8,128)(2,1)}, u32[]{:S(2)}) copy-start(bf16[512,128]{1,0:T(8,128)(2,1)} %get-tuple-element.19) | copy-start | bytes 393220
  71.2 4.9 %copy-start.20 = (bf16[512,128]{1,0:T(8,128)(2,1)S(1)}, bf16[512,128]{1,0:T(8,128)(2,1)}, u32[]{:S(2)}) copy-start(bf16[512,128]{1,0:T(8,128)(2,1)} %get-tuple-element.20) | copy-start | bytes 393220
  72.1 41.1 %collective-permute-start.12 = (bf16[128,3072]{1,0:T(8,128)(2,1)}, bf16[128,3072]{1,0:T(8,128)(2,1)S(1)}, u32[]{:S(2)}, u32[]{:S(2)}) collective-permute-start(bf16[128,3072]{1,0:T(8,128)(2,1)} %settle.1.refs_2_), channel_id=1, source_target_pairs={{16,0},{32,16},{48,32},{64,48},{80,64},{96,80},{112,96},{128,112},... | collective-permute-start | bytes 2359304 | tf_op jit(solution)/shard_map/ppermute | solution.py:495
  73.4 23.4 %collective-permute-start.7 = (bf16[512,128]{1,0:T(8,128)(2,1)S(1)}, bf16[512,128]{1,0:T(8,128)(2,1)S(1)}, u32[]{:S(2)}, u32[]{:S(2)}) collective-permute-start(bf16[512,128]{1,0:T(8,128)(2,1)S(1)} %copy-done.22), channel_id=1, source_target_pairs={{0,12},{1,13},{2,14},{3,15},{4,0},{5,1},{6,2},{7,3},{8,4},{9,5},{1... | collective-permute-start | bytes 393224 | tf_op jit(solution)/shard_map/ppermute | solution.py:31
  76.1 20.8 %collective-permute-start.8 = (bf16[512,128]{1,0:T(8,128)(2,1)S(1)}, bf16[512,128]{1,0:T(8,128)(2,1)S(1)}, u32[]{:S(2)}, u32[]{:S(2)}) collective-permute-start(bf16[512,128]{1,0:T(8,128)(2,1)S(1)} %copy-done.21), channel_id=1, source_target_pairs={{0,4},{1,5},{2,6},{3,7},{4,8},{5,9},{6,10},{7,11},{8,12},{9,13},{1... | collective-permute-start | bytes 393224 | tf_op jit(solution)/shard_map/ppermute | solution.py:31
  76.1 22.2 %collective-permute-start.9 = (bf16[512,128]{1,0:T(8,128)(2,1)S(1)}, bf16[512,128]{1,0:T(8,128)(2,1)S(1)}, u32[]{:S(2)}, u32[]{:S(2)}) collective-permute-start(bf16[512,128]{1,0:T(8,128)(2,1)S(1)} %copy-done.20), channel_id=1, source_target_pairs={{0,8},{1,9},{2,10},{3,11},{4,12},{5,13},{6,14},{7,15},{8,0},{9,1},... | collective-permute-start | bytes 393224 | tf_op jit(solution)/shard_map/ppermute | solution.py:31
  89.7 14.1 %collective-permute-start.11 = (bf16[512,128]{1,0:T(8,128)(2,1)}, bf16[512,128]{1,0:T(8,128)(2,1)S(1)}, u32[]{:S(2)}, u32[]{:S(2)}) collective-permute-start(bf16[512,128]{1,0:T(8,128)(2,1)} %get-tuple-element.21), channel_id=1, source_target_pairs={{0,8},{1,9},{2,10},{3,11},{4,12},{5,13},{6,14},{7,15},{8,0},{9,1},... | collective-permute-start | bytes 393224 | tf_op jit(solution)/shard_map/ppermute | solution.py:31
  96.9 16.3 %copy-start.9 = (bf16[512,128]{1,0:T(8,128)(2,1)}, bf16[512,128]{1,0:T(8,128)(2,1)S(1)}, u32[]{:S(2)}) copy-start(bf16[512,128]{1,0:T(8,128)(2,1)S(1)} %collective-permute-done.7.refs_0_.refs_1_) | copy-start | bytes 393220
  96.9 10.8 %collective-permute-start.6 = (bf16[512,128]{1,0:T(8,128)(2,1)}, bf16[512,128]{1,0:T(8,128)(2,1)S(1)}, u32[]{:S(2)}, u32[]{:S(2)}) collective-permute-start(bf16[512,128]{1,0:T(8,128)(2,1)} %get-tuple-element.16), channel_id=1, source_target_pairs={{0,4},{1,5},{2,6},{3,7},{4,8},{5,9},{6,10},{7,11},{8,12},{9,13},{1... | collective-permute-start | bytes 393224 | tf_op jit(solution)/shard_map/ppermute | solution.py:31
  96.9 16.3 %copy-start.10 = (bf16[512,128]{1,0:T(8,128)(2,1)}, bf16[512,128]{1,0:T(8,128)(2,1)S(1)}, u32[]{:S(2)}) copy-start(bf16[512,128]{1,0:T(8,128)(2,1)S(1)} %collective-permute-done.8.refs_1_.refs_2_) | copy-start | bytes 393220
  98.3 14.9 %copy-start.11 = (bf16[512,128]{1,0:T(8,128)(2,1)}, bf16[512,128]{1,0:T(8,128)(2,1)S(1)}, u32[]{:S(2)}) copy-start(bf16[512,128]{1,0:T(8,128)(2,1)S(1)} %collective-permute-done.9.refs_2_.refs_3_) | copy-start | bytes 393220
  99.9 7.8 %collective-permute-start.10 = (bf16[512,128]{1,0:T(8,128)(2,1)}, bf16[512,128]{1,0:T(8,128)(2,1)S(1)}, u32[]{:S(2)}, u32[]{:S(2)}) collective-permute-start(bf16[512,128]{1,0:T(8,128)(2,1)} %copy-done.13), channel_id=1, source_target_pairs={{0,12},{1,13},{2,14},{3,15},{4,0},{5,1},{6,2},{7,3},{8,4},{9,5},{1... | collective-permute-start | bytes 393224 | tf_op jit(solution)/shard_map/ppermute | solution.py:31
  107.0 6.2 %copy-start.3 = (bf16[16,400,128]{2,1,0:T(8,128)(2,1)}, bf16[16,400,128]{2,1,0:T(8,128)(2,1)S(1)}, u32[]{:S(2)}) copy-start(bf16[16,400,128]{2,1,0:T(8,128)(2,1)S(1)} %all-to-all-done.1.refs_0_.in_hbm_ref) | copy-start | bytes 4915204
  114.7 6.6 %copy-start.16 = (f32[128,3072]{1,0:T(8,128)S(1)}, f32[128,3072]{1,0:T(8,128)}, u32[]{:S(2)}) copy-start(f32[128,3072]{1,0:T(8,128)} %get-tuple-element.24) | copy-start | bytes 4718596
  115.9 5.4 %collective-permute-start.13 = (bf16[256,3072]{1,0:T(8,128)(2,1)}, bf16[256,3072]{1,0:T(8,128)(2,1)S(1)}, u32[]{:S(2)}, u32[]{:S(2)}) collective-permute-start(bf16[256,3072]{1,0:T(8,128)(2,1)} %copy-done.7), channel_id=1, source_target_pairs={{0,1},{1,0},{2,3},{3,2},{4,5},{5,4},{6,7},{7,6},{8,9},{9,8},{10,11... | collective-permute-start | bytes 4718600 | tf_op jit(solution)/shard_map/ppermute | solution.py:541
  122.8 25.0 %collective-permute-start.14 = (bf16[128,3072]{1,0:T(8,128)(2,1)}, bf16[128,3072]{1,0:T(8,128)(2,1)}, u32[]{:S(2)}, u32[]{:S(2)}) collective-permute-start(bf16[128,3072]{1,0:T(8,128)(2,1)} %add_convert_fusion.refs_4_), channel_id=1, source_target_pairs={{0,2},{1,3},{2,0},{3,1},{4,6},{5,7},{6,4},{7,5},{8,10},{9,11},{10,... | collective-permute-start | bytes 2359304 | tf_op jit(solution)/shard_map/ppermute | solution.py:545
  142.1 5.7 %copy-start.17 = (bf16[128,3072]{1,0:T(8,128)(2,1)S(1)}, bf16[128,3072]{1,0:T(8,128)(2,1)}, u32[]{:S(2)}) copy-start(bf16[128,3072]{1,0:T(8,128)(2,1)} %param.18) | copy-start | bytes 2359300
  142.2 27.0 %all-to-all-start.2 = ((bf16[16,384,128]{2,1,0:T(8,128)(2,1)}), bf16[16,384,128]{2,1,0:T(8,128)(2,1)S(1)}, u32[]{:S(2)}, u32[]{:S(2)}) async-start(bf16[16,384,128]{2,1,0:T(8,128)(2,1)} %attention_backward.1), calls=%async_computation.2 | async-start | bytes 3145728 | tf_op jit(solution)/shard_map/all_to_all | solution.py:509
  147.8 4.3 %copy-start.14 = (bf16[128,3072]{1,0:T(8,128)(2,1)S(1)}, bf16[128,3072]{1,0:T(8,128)(2,1)}, u32[]{:S(2)}) copy-start(bf16[128,3072]{1,0:T(8,128)(2,1)} %first_ref.1) | copy-start | bytes 2359300
  152.0 30.3 %collective-permute-start.15 = (bf16[128,3072]{1,0:T(8,128)(2,1)}, bf16[128,3072]{1,0:T(8,128)(2,1)S(1)}, u32[]{:S(2)}, u32[]{:S(2)}) collective-permute-start(bf16[128,3072]{1,0:T(8,128)(2,1)} %fusion.1), channel_id=1, source_target_pairs={{0,16},{16,32},{32,48},{48,64},{64,80},{80,96},{96,112},{112,128},... | collective-permute-start | bytes 2359304 | tf_op jit(solution)/shard_map/ppermute | solution.py:500
  (10 other events, 11.0 us)

commit v8 on v6

--- a/solution.py
+++ b/solution.py
@@ -532,10 +532,9 @@
     moved = shifted(turned, "pipe", -1)
     attns = attention_forward(place, fwd, grads[0], gate_tok, turned)
     grads = tuple(along_x(g, o) for g, o in zip(grads, OFFSETS))
-    attns = (attns[0], follow(attns[1], *grads[1:])) + attns[2:]
     attns = tuple(along_x(a, o) for a, o in zip(attns, OFFSETS))
 
-    attns = (attns[0], attns[2], attns[1], follow(attns[3], bwd, moved))
+    attns = (attns[0], attns[2], attns[1], follow(attns[3], bwd, moved, *grads[1:]))
     part, part_across, part_send = project(place, attns, pieces)
     received = lax.ppermute(part_send, "seq", CORE)
     rows = part.shape[0]

time: 176 us -> 176 us (level); the launches traced: 175 us -> 172 us
  Pallas kernels: 48.9 us -> 44.7 us
  waiting for transfers between devices: 73.2 us -> 75.9 us
    pallas_call x1, Pallas kernels: 17.2 us -> 13 us  [attention_backward(): pl.pallas_call(backward_kernel, out_shape=jax.ShapeDtypeStruct((blocks, 3...]
    unnamed x41 -> x39, local copies, waits for them, and re-layouts: 5.21 us -> 4.22 us
  transfers between devices with their start and end apart: 19 -> 19, of which waited for: 11 -> 11; matrix products, arithmetic and copies ran while one was open for 4% -> 4% of each run, Pallas kernels for 25% -> 23%
where the time goes in v8:
time: 176 us; the launch traced here: 172 us
  waiting for transfers between devices  75.9 us (43%)
  Pallas kernels  44.7 us (25%)
  starting transfers between devices  36 us (20%)
  other arithmetic  9.32 us (5%)
  local copies, waits for them, and re-layouts  5.53 us (3%)
    all_to_all x3, waiting for transfers between devices, exchange(): return lax.all_to_all(array, 'seq', 0, 0, tiled=True)  36 us
    ppermute x9, waiting for transfers between devices, along_x(): lax.ppermute(array, 'seq', [(i, (i + PER_X * offset) % count) for i in ra...  20.6 us
    all_to_all x3, starting transfers between devices, exchange(): return lax.all_to_all(array, 'seq', 0, 0, tiled=True)  16.8 us
    ppermute x1, waiting for transfers between devices, rotated(): lax.ppermute(array, axis, [(i, (i + by) % length) for i in range(length)])  14.3 us
    ppermute x9, starting transfers between devices, along_x(): lax.ppermute(array, 'seq', [(i, (i + PER_X * offset) % count) for i in ra...  13.6 us
    pallas_call x1, Pallas kernels, attention_backward(): pl.pallas_call(backward_kernel, out_shape=jax.ShapeDtypeStruct((blocks, 3...  13 us
    pallas_call x1, Pallas kernels, attention_forward(): pl.pallas_call(forward_kernel, out_shape=(jax.ShapeDtypeStruct((total //...  11.8 us
    pallas_call x2, Pallas kernels, pack(): pl.pallas_call(pack_kernel, grid=(1,), out_shape=jax.ShapeDtypeStruct((he...  5.66 us
  transfers between devices with their start and end apart: 19, of which 11 were waited for; matrix products, arithmetic and copies ran while one was open for 4% of the time, Pallas kernels for 23%

profile of v8, /device:TPU:1, one launch (start us, length us, event | category | flops | bytes accessed | tf_op | source)
XLA Modules:
  0.0 172.3 jit_solution(6046630464923762817)
XLA Ops:
  0.6 3.7 %collective-permute-start.5 = (bf16[128,3072]{1,0:T(8,128)(2,1)}, bf16[128,3072]{1,0:T(8,128)(2,1)S(1)}, u32[]{:S(2)}, u32[]{:S(2)}) collective-permute-start(bf16[128,3072]{1,0:T(8,128)(2,1)} %bitcast.24), channel_id=1, source_target_pairs={{0,8},{1,9},{2,10},{3,11},{4,12},{5,13},{6,14},{7,15},{8,0},{9,1},... | collective-permute-start | bytes 2359304 | tf_op jit(solution)/shard_map/ppermute | solution.py:31
  5.8 1.3 slice_bitcast_fusion.2
  7.1 2.8 %pack.2 = bf16[16,400,128]{2,1,0:T(8,128)(2,1)} custom-call(s32[1,128]{1,0:T(1,128)} %get-tuple-element.28.seg_ref, bf16[1,2,128,2048]{3,2,1,0:T(8,128)(2,1)} %q_ref.3, bf16[1,2,128,2048]{3,2,1,0:T(8,128)(2,1)} %k_ref.3, bf16[1,2,128,2048]{3,2,1,0:T(8,128)(2,1)} %v_ref.3), custom_call_target="tpu_custom_call" | custom-call | flops 2000000000 | tf_op jit(solution)/shard_map/pack/pallas_call | solution.py:85
  9.9 6.3 %all-to-all-start = ((bf16[16,400,128]{2,1,0:T(8,128)(2,1)}), bf16[16,400,128]{2,1,0:T(8,128)(2,1)S(1)}, u32[]{:S(2)}, u32[]{:S(2)}) async-start(bf16[16,400,128]{2,1,0:T(8,128)(2,1)} %pack.2), calls=%async_computation | async-start | bytes 3276800 | tf_op jit(solution)/shard_map/all_to_all | solution.py:509
  17.5 1.5 collective-permute-start.1
  19.0 1.7 %multiply_reduce_fusion.1.refs_1_ = f32[128,3072]{1,0:T(8,128)} fusion(f32[4,3072]{1,0:T(4,128)S(1)} %get-tuple-element.26, f32[128,4]{0,1:T(4,128)S(1)} %fusion.2), kind=kLoop, calls=%fused_computation.1 | loop fusion | flops 2752512 | bytes 1624064 | tf_op jit(solution)/shard_map/reduce_sum | solution.py:505
  20.9 18.4 %collective-permute-done.4.refs_6_.refs_3_ = bf16[128,3072]{1,0:T(8,128)(2,1)S(1)} collective-permute-done((bf16[128,3072]{1,0:T(8,128)(2,1)}, bf16[128,3072]{1,0:T(8,128)(2,1)S(1)}, u32[]{:S(2)}, u32[]{:S(2)}) %collective-permute-start.4) | collective-permute-done | bytes 786464 | tf_op jit(solution)/shard_map/ppermute | solution.py:31
  40.1 2.8 %pack.3 = bf16[16,400,128]{2,1,0:T(8,128)(2,1)} custom-call(s32[1,128]{1,0:T(1,128)} %get-tuple-element.27.seg_ref, bf16[1,2,128,2048]{3,2,1,0:T(8,128)(2,1)} %q_ref.3, bf16[1,2,128,2048]{3,2,1,0:T(8,128)(2,1)} %k_ref.3, bf16[1,2,128,2048]{3,2,1,0:T(8,128)(2,1)} %v_ref.3, bf16[128,3072]{1,0:T(8,128)(2,1)} %collective-permute-done.1.refs_2_.refs_0_, ...), custom_call_target="tpu_custom_call" | custom-call | flops 2000000000 | tf_op jit(solution)/shard_map/pack/pallas_call | solution.py:85
  43.0 15.2 %all-to-all-done.refs_0_.in_hbm_ref = bf16[16,400,128]{2,1,0:T(8,128)(2,1)S(1)} async-done(((bf16[16,400,128]{2,1,0:T(8,128)(2,1)}), bf16[16,400,128]{2,1,0:T(8,128)(2,1)S(1)}, u32[]{:S(2)}, u32[]{:S(2)}) %all-to-all-start) | async-done | bytes 1638432 | tf_op jit(solution)/shard_map/all_to_all | solution.py:509
  58.1 4.8 %all-to-all-start.1 = ((bf16[16,400,128]{2,1,0:T(8,128)(2,1)}), bf16[16,400,128]{2,1,0:T(8,128)(2,1)S(1)}, u32[]{:S(2)}, u32[]{:S(2)}) async-start(bf16[16,400,128]{2,1,0:T(8,128)(2,1)} %pack.3), calls=%async_computation.1 | async-start | bytes 3276800 | tf_op jit(solution)/shard_map/all_to_all | solution.py:509
  63.5 1.1 copy-done.3
  64.6 0.9 settle.1.refs_2_
  65.6 1.3 collective-permute-start.9
  66.9 5.5 %attention_grad.1 = (bf16[512,128]{1,0:T(8,128)(2,1)}, bf16[512,128]{1,0:T(8,128)(2,1)}, bf16[512,128]{1,0:T(8,128)(2,1)}, bf16[512,128]{1,0:T(8,128)(2,1)}) custom-call(s32[1]{0:T(128)} %bitcast.3.place_ref, bf16[128,3072]{1,0:T(8,128)(2,1)} %copy-done.14, bf16[128,3072]{1,0:T(8,128)(2,1)} %collective-permute-done.refs_1_, ...), custom_call_target="tpu_custom_call" | custom-call | flops 200000000 | tf_op jit(solution)/shard_map/attention_grad/pallas_call | solution.py:370
  72.4 2.7 %collective-permute-start.10 = (bf16[512,128]{1,0:T(8,128)(2,1)}, bf16[512,128]{1,0:T(8,128)(2,1)S(1)}, u32[]{:S(2)}, u32[]{:S(2)}) collective-permute-start(bf16[512,128]{1,0:T(8,128)(2,1)} %get-tuple-element.19), channel_id=1, source_target_pairs={{0,12},{1,13},{2,14},{3,15},{4,0},{5,1},{6,2},{7,3},{8,4},{9,5},{1... | collective-permute-start | bytes 393224 | tf_op jit(solution)/shard_map/ppermute | solution.py:31
  75.1 1.8 %collective-permute-start.12 = (bf16[512,128]{1,0:T(8,128)(2,1)}, bf16[512,128]{1,0:T(8,128)(2,1)S(1)}, u32[]{:S(2)}, u32[]{:S(2)}) collective-permute-start(bf16[512,128]{1,0:T(8,128)(2,1)} %get-tuple-element.21), channel_id=1, source_target_pairs={{0,8},{1,9},{2,10},{3,11},{4,12},{5,13},{6,14},{7,15},{8,0},{9,1},... | collective-permute-start | bytes 393224 | tf_op jit(solution)/shard_map/ppermute | solution.py:31
  76.8 11.8 %attention_forward.1 = (bf16[512,128]{1,0:T(8,128)(2,1)}, bf16[512,128]{1,0:T(8,128)(2,1)}, bf16[512,128]{1,0:T(8,128)(2,1)}, bf16[512,128]{1,0:T(8,128)(2,1)}) custom-call(s32[1]{0:T(128)} %bitcast.3.place_ref, bf16[16,400,128]{2,1,0:T(8,128)(2,1)} %copy-done, bf16[512,128]{1,0:T(8,128)(2,1)} %get-tuple-element.14.refs_0_, ...), custom_call_target="tpu_custom_call" | custom-call | flops 200000000 | tf_op jit(solution)/shard_map/attention_forward/pallas_call | solution.py:204
  88.6 1.3 collective-permute-start.8
  90.5 2.2 %collective-permute-start.7 = (bf16[512,128]{1,0:T(8,128)(2,1)}, bf16[512,128]{1,0:T(8,128)(2,1)S(1)}, u32[]{:S(2)}, u32[]{:S(2)}) collective-permute-start(bf16[512,128]{1,0:T(8,128)(2,1)} %get-tuple-element.17), channel_id=1, source_target_pairs={{0,12},{1,13},{2,14},{3,15},{4,0},{5,1},{6,2},{7,3},{8,4},{9,5},{1... | collective-permute-start | bytes 393224 | tf_op jit(solution)/shard_map/ppermute | solution.py:31
  92.7 1.8 %collective-permute-done.8.array_ref = bf16[512,128]{1,0:T(8,128)(2,1)S(1)} collective-permute-done((bf16[512,128]{1,0:T(8,128)(2,1)}, bf16[512,128]{1,0:T(8,128)(2,1)S(1)}, u32[]{:S(2)}, u32[]{:S(2)}) %collective-permute-start.8) | collective-permute-done | bytes 131104 | tf_op jit(solution)/shard_map/ppermute | solution.py:31
  94.6 5.7 %all-to-all-done.1.refs_0_.in_hbm_ref = bf16[16,400,128]{2,1,0:T(8,128)(2,1)S(1)} async-done(((bf16[16,400,128]{2,1,0:T(8,128)(2,1)}), bf16[16,400,128]{2,1,0:T(8,128)(2,1)S(1)}, u32[]{:S(2)}, u32[]{:S(2)}) %all-to-all-start.1) | async-done | bytes 1638432 | tf_op jit(solution)/shard_map/all_to_all | solution.py:509
  100.2 1.3 collective-permute-done.9.refs_1_.second_ref
  103.0 4.7 %project.1 = (f32[128,3072]{1,0:T(8,128)}, f32[128,3072]{1,0:T(8,128)}, bf16[256,3072]{1,0:T(8,128)(2,1)}) custom-call(s32[1]{0:T(128)} %bitcast.3.place_ref, bf16[512,128]{1,0:T(8,128)(2,1)} %get-tuple-element.15.refs_0_, bf16[512,128]{1,0:T(8,128)(2,1)} %copy-done.16, bf16[512,128]{1,0:T(8,128)(2,1)} %copy-done.17, bf16[512,128]{1,0:T(8,128)(2,1)} %copy-done.6, ...), custom_call_target="tpu_custom_call" | custom-call | flops 200000000 | tf_op jit(solution)/shard_map/project/pallas_call | solution.py:420
  108.4 3.2 %collective-permute-done.13 = bf16[256,3072]{1,0:T(8,128)(2,1)S(1)} collective-permute-done((bf16[256,3072]{1,0:T(8,128)(2,1)}, bf16[256,3072]{1,0:T(8,128)(2,1)S(1)}, u32[]{:S(2)}, u32[]{:S(2)}) %collective-permute-start.13) | collective-permute-done | bytes 1572896 | tf_op jit(solution)/shard_map/ppermute | solution.py:539
  111.7 3.0 %add_convert_fusion.refs_4_ = bf16[128,3072]{1,0:T(8,128)(2,1)} fusion(f32[128,3072]{1,0:T(8,128)} %get-tuple-element.24, bf16[256,3072]{1,0:T(8,128)(2,1)S(1)} %collective-permute-done.13), kind=kLoop, calls=%fused_computation.4 | loop fusion | flops 1179648 | bytes 3145728 | tf_op jit(solution)/shard_map/convert_element_type | solution.py:541
  115.5 13.0 %attention_backward.1 = bf16[16,384,128]{2,1,0:T(8,128)(2,1)} custom-call(s32[1]{0:T(128)} %bitcast.3.place_ref, bf16[16,400,128]{2,1,0:T(8,128)(2,1)} %copy-done.1, bf16[512,128]{1,0:T(8,128)(2,1)} %get-tuple-element.14.refs_0_, bf16[512,128]{1,0:T(8,128)(2,1)} %copy-done.7, bf16[512,128]{1,0:T(8,128)(2,1)} %copy-done.8, bf16[512,128]{1,0:T(8,128)(2,1)} %copy-done.9, ...), custom_call_target="tpu_custom_call" | custom-call | flops 30000001024 | tf_op jit(solution)/shard_map/attention_backward/pallas_call | solution.py:305
  128.5 5.7 %all-to-all-start.2 = ((bf16[16,384,128]{2,1,0:T(8,128)(2,1)}), bf16[16,384,128]{2,1,0:T(8,128)(2,1)S(1)}, u32[]{:S(2)}, u32[]{:S(2)}) async-start(bf16[16,384,128]{2,1,0:T(8,128)(2,1)} %attention_backward.1), calls=%async_computation.2 | async-start | bytes 3145728 | tf_op jit(solution)/shard_map/all_to_all | solution.py:509
  134.2 3.7 %fusion.1 = bf16[128,3072]{1,0:T(8,128)(2,1)} fusion(bf16[128,3072]{1,0:T(8,128)(2,1)} %param.18, f32[128,3072]{1,0:T(8,128)S(1)} %copy-done.11, bf16[128,3072]{1,0:T(8,128)(2,1)} %collective-permute-done.14, f32[128,3072]{1,0:T(8,128)} %get-tuple-element.22, bf16[256,3072]{1,0:T(8,128)(2,1)} %copy-done.15, bf16[1,128,3072]{2,1,0:T(8,128)(2,1)} %param.10, ...), kind=kLoop, calls=%fused_computation.6 | loop fusion | flops 3538944 | bytes 7077889 | tf_op jit(solution)/shard_map/jit(_where)/select_n | solution.py:546
  138.8 1.5 choose.1
  140.3 15.2 %all-to-all-done.2.in_ref = bf16[16,384,128]{2,1,0:T(8,128)(2,1)S(1)} async-done(((bf16[16,384,128]{2,1,0:T(8,128)(2,1)}), bf16[16,384,128]{2,1,0:T(8,128)(2,1)S(1)}, u32[]{:S(2)}, u32[]{:S(2)}) %all-to-all-start.2) | async-done | bytes 1572896 | tf_op jit(solution)/shard_map/all_to_all | solution.py:509
  155.5 1.6 unpack.1
  157.1 14.3 %collective-permute-done.15 = bf16[128,3072]{1,0:T(8,128)(2,1)S(1)} collective-permute-done((bf16[128,3072]{1,0:T(8,128)(2,1)}, bf16[128,3072]{1,0:T(8,128)(2,1)S(1)}, u32[]{:S(2)}, u32[]{:S(2)}) %collective-permute-start.15) | collective-permute-done | bytes 786464 | tf_op jit(solution)/shard_map/ppermute | solution.py:500
  (65 shorter events, 9.5 us)
Async XLA Ops:
  0.6 20.2 %collective-permute-start.5 = (bf16[128,3072]{1,0:T(8,128)(2,1)}, bf16[128,3072]{1,0:T(8,128)(2,1)S(1)}, u32[]{:S(2)}, u32[]{:S(2)}) collective-permute-start(bf16[128,3072]{1,0:T(8,128)(2,1)} %bitcast.24), channel_id=1, source_target_pairs={{0,8},{1,9},{2,10},{3,11},{4,12},{5,13},{6,14},{7,15},{8,0},{9,1},... | collective-permute-start | bytes 2359304 | tf_op jit(solution)/shard_map/ppermute | solution.py:31
  4.3 35.0 %collective-permute-start.4 = (bf16[128,3072]{1,0:T(8,128)(2,1)}, bf16[128,3072]{1,0:T(8,128)(2,1)S(1)}, u32[]{:S(2)}, u32[]{:S(2)}) collective-permute-start(bf16[128,3072]{1,0:T(8,128)(2,1)} %bitcast.25), channel_id=1, source_target_pairs={{0,12},{1,13},{2,14},{3,15},{4,0},{5,1},{6,2},{7,3},{8,4},{9,5},{1... | collective-permute-start | bytes 2359304 | tf_op jit(solution)/shard_map/ppermute | solution.py:31
  5.2 34.3 %collective-permute-start.3 = (bf16[128,3072]{1,0:T(8,128)(2,1)}, bf16[128,3072]{1,0:T(8,128)(2,1)}, u32[]{:S(2)}, u32[]{:S(2)}) collective-permute-start(bf16[128,3072]{1,0:T(8,128)(2,1)} %bitcast.26), channel_id=1, source_target_pairs={{0,4},{1,5},{2,6},{3,7},{4,8},{5,9},{6,10},{7,11},{8,12},{9,13},{1... | collective-permute-start | bytes 2359304 | tf_op jit(solution)/shard_map/ppermute | solution.py:31
  9.9 6.3 %copy-start.18 = (f32[1,2,4,3072]{3,2,1,0:T(4,128)S(1)}, f32[1,2,4,3072]{3,2,1,0:T(4,128)}, u32[]{:S(2)}) copy-start(f32[1,2,4,3072]{3,2,1,0:T(4,128)} %param.15) | copy-start | bytes 294916
  9.9 48.3 %all-to-all-start = ((bf16[16,400,128]{2,1,0:T(8,128)(2,1)}), bf16[16,400,128]{2,1,0:T(8,128)(2,1)S(1)}, u32[]{:S(2)}, u32[]{:S(2)}) async-start(bf16[16,400,128]{2,1,0:T(8,128)(2,1)} %pack.2), calls=%async_computation | async-start | bytes 3276800 | tf_op jit(solution)/shard_map/all_to_all | solution.py:509
  17.5 21.8 %copy-start.14 = (bf16[128,3072]{1,0:T(8,128)(2,1)}, bf16[128,3072]{1,0:T(8,128)(2,1)S(1)}, u32[]{:S(2)}) copy-start(bf16[128,3072]{1,0:T(8,128)(2,1)S(1)} %multiply_convert_fusion.refs_0_) | copy-start | bytes 2359300
  17.5 22.4 %collective-permute-start.1 = (bf16[128,3072]{1,0:T(8,128)(2,1)S(1)}, bf16[128,3072]{1,0:T(8,128)(2,1)}, u32[]{:S(2)}, u32[]{:S(2)}) collective-permute-start(bf16[128,3072]{1,0:T(8,128)(2,1)S(1)} %multiply_convert_fusion.refs_0_), channel_id=1, source_target_pairs={{0,2},{1,3},{2,0},{3,1},{4,6},{5,7},{6,4},{7,5},{8,10},{9,11},{10,... | collective-permute-start | bytes 2359304 | tf_op jit(solution)/shard_map/ppermute | solution.py:523
  20.9 19.0 %copy-start.12 = (bf16[128,3072]{1,0:T(8,128)(2,1)}, bf16[128,3072]{1,0:T(8,128)(2,1)S(1)}, u32[]{:S(2)}) copy-start(bf16[128,3072]{1,0:T(8,128)(2,1)S(1)} %collective-permute-done.5.refs_7_.refs_4_) | copy-start | bytes 2359300
  58.1 5.3 %copy-start = (bf16[16,400,128]{2,1,0:T(8,128)(2,1)}, bf16[16,400,128]{2,1,0:T(8,128)(2,1)S(1)}, u32[]{:S(2)}) copy-start(bf16[16,400,128]{2,1,0:T(8,128)(2,1)S(1)} %all-to-all-done.refs_0_.in_hbm_ref) | copy-start | bytes 4915204
  58.1 42.1 %all-to-all-start.1 = ((bf16[16,400,128]{2,1,0:T(8,128)(2,1)}), bf16[16,400,128]{2,1,0:T(8,128)(2,1)S(1)}, u32[]{:S(2)}, u32[]{:S(2)}) async-start(bf16[16,400,128]{2,1,0:T(8,128)(2,1)} %pack.3), calls=%async_computation.1 | async-start | bytes 3276800 | tf_op jit(solution)/shard_map/all_to_all | solution.py:509
  63.0 3.9 %collective-permute-start = (bf16[128,3072]{1,0:T(8,128)(2,1)}, bf16[128,3072]{1,0:T(8,128)(2,1)}, u32[]{:S(2)}, u32[]{:S(2)}) collective-permute-start(bf16[128,3072]{1,0:T(8,128)(2,1)} %copy-done.14), channel_id=1, source_target_pairs={{0,1},{1,0},{2,3},{3,2},{4,5},{5,4},{6,7},{7,6},{8,9},{9,8},{10,11... | collective-permute-start | bytes 2359304 | tf_op jit(solution)/shard_map/ppermute | solution.py:524
  63.2 3.7 %collective-permute-start.2 = (bf16[128,3072]{1,0:T(8,128)(2,1)}, bf16[128,3072]{1,0:T(8,128)(2,1)}, u32[]{:S(2)}, u32[]{:S(2)}) collective-permute-start(bf16[128,3072]{1,0:T(8,128)(2,1)} %collective-permute-done.1.refs_2_.refs_0_), channel_id=1, source_target_pairs={{0,1},{1,0},{2,3},{3,2},{4,5},{5,4},{6,7},{7,6},{8,9},{9,8},{10,11... | collective-permute-start | bytes 2359304 | tf_op jit(solution)/shard_map/ppermute | solution.py:525
  65.6 36.0 %collective-permute-start.9 = (bf16[128,3072]{1,0:T(8,128)(2,1)}, bf16[128,3072]{1,0:T(8,128)(2,1)S(1)}, u32[]{:S(2)}, u32[]{:S(2)}) collective-permute-start(bf16[128,3072]{1,0:T(8,128)(2,1)} %settle.1.refs_2_), channel_id=1, source_target_pairs={{16,0},{32,16},{48,32},{64,48},{80,64},{96,80},{112,96},{128,112},... | collective-permute-start | bytes 2359304 | tf_op jit(solution)/shard_map/ppermute | solution.py:495
  72.4 17.5 %collective-permute-start.10 = (bf16[512,128]{1,0:T(8,128)(2,1)}, bf16[512,128]{1,0:T(8,128)(2,1)S(1)}, u32[]{:S(2)}, u32[]{:S(2)}) collective-permute-start(bf16[512,128]{1,0:T(8,128)(2,1)} %get-tuple-element.19), channel_id=1, source_target_pairs={{0,12},{1,13},{2,14},{3,15},{4,0},{5,1},{6,2},{7,3},{8,4},{9,5},{1... | collective-permute-start | bytes 393224 | tf_op jit(solution)/shard_map/ppermute | solution.py:31
  75.1 15.4 %collective-permute-start.11 = (bf16[512,128]{1,0:T(8,128)(2,1)}, bf16[512,128]{1,0:T(8,128)(2,1)S(1)}, u32[]{:S(2)}, u32[]{:S(2)}) collective-permute-start(bf16[512,128]{1,0:T(8,128)(2,1)} %get-tuple-element.20), channel_id=1, source_target_pairs={{0,4},{1,5},{2,6},{3,7},{4,8},{5,9},{6,10},{7,11},{8,12},{9,13},{1... | collective-permute-start | bytes 393224 | tf_op jit(solution)/shard_map/ppermute | solution.py:31
  75.1 17.6 %collective-permute-start.12 = (bf16[512,128]{1,0:T(8,128)(2,1)}, bf16[512,128]{1,0:T(8,128)(2,1)S(1)}, u32[]{:S(2)}, u32[]{:S(2)}) collective-permute-start(bf16[512,128]{1,0:T(8,128)(2,1)} %get-tuple-element.21), channel_id=1, source_target_pairs={{0,8},{1,9},{2,10},{3,11},{4,12},{5,13},{6,14},{7,15},{8,0},{9,1},... | collective-permute-start | bytes 393224 | tf_op jit(solution)/shard_map/ppermute | solution.py:31
  88.6 5.9 %collective-permute-start.8 = (bf16[512,128]{1,0:T(8,128)(2,1)}, bf16[512,128]{1,0:T(8,128)(2,1)S(1)}, u32[]{:S(2)}, u32[]{:S(2)}) collective-permute-start(bf16[512,128]{1,0:T(8,128)(2,1)} %get-tuple-element.18), channel_id=1, source_target_pairs={{0,8},{1,9},{2,10},{3,11},{4,12},{5,13},{6,14},{7,15},{8,0},{9,1},... | collective-permute-start | bytes 393224 | tf_op jit(solution)/shard_map/ppermute | solution.py:31
  89.9 17.7 %copy-start.7 = (bf16[512,128]{1,0:T(8,128)(2,1)}, bf16[512,128]{1,0:T(8,128)(2,1)S(1)}, u32[]{:S(2)}) copy-start(bf16[512,128]{1,0:T(8,128)(2,1)S(1)} %collective-permute-done.10.refs_2_.refs_1_) | copy-start | bytes 393220
  89.9 12.3 %collective-permute-start.6 = (bf16[512,128]{1,0:T(8,128)(2,1)}, bf16[512,128]{1,0:T(8,128)(2,1)S(1)}, u32[]{:S(2)}, u32[]{:S(2)}) collective-permute-start(bf16[512,128]{1,0:T(8,128)(2,1)} %get-tuple-element.16), channel_id=1, source_target_pairs={{0,4},{1,5},{2,6},{3,7},{4,8},{5,9},{6,10},{7,11},{8,12},{9,13},{1... | collective-permute-start | bytes 393224 | tf_op jit(solution)/shard_map/ppermute | solution.py:31
  90.5 17.2 %copy-start.8 = (bf16[512,128]{1,0:T(8,128)(2,1)}, bf16[512,128]{1,0:T(8,128)(2,1)S(1)}, u32[]{:S(2)}) copy-start(bf16[512,128]{1,0:T(8,128)(2,1)S(1)} %collective-permute-done.11.refs_3_.refs_2_) | copy-start | bytes 393220
  90.5 11.7 %collective-permute-start.7 = (bf16[512,128]{1,0:T(8,128)(2,1)}, bf16[512,128]{1,0:T(8,128)(2,1)S(1)}, u32[]{:S(2)}, u32[]{:S(2)}) collective-permute-start(bf16[512,128]{1,0:T(8,128)(2,1)} %get-tuple-element.17), channel_id=1, source_target_pairs={{0,12},{1,13},{2,14},{3,15},{4,0},{5,1},{6,2},{7,3},{8,4},{9,5},{1... | collective-permute-start | bytes 393224 | tf_op jit(solution)/shard_map/ppermute | solution.py:31
  92.7 14.9 %copy-start.9 = (bf16[512,128]{1,0:T(8,128)(2,1)}, bf16[512,128]{1,0:T(8,128)(2,1)S(1)}, u32[]{:S(2)}) copy-start(bf16[512,128]{1,0:T(8,128)(2,1)S(1)} %collective-permute-done.12.refs_4_.refs_3_) | copy-start | bytes 393220
  100.2 7.5 %copy-start.1 = (bf16[16,400,128]{2,1,0:T(8,128)(2,1)}, bf16[16,400,128]{2,1,0:T(8,128)(2,1)S(1)}, u32[]{:S(2)}) copy-start(bf16[16,400,128]{2,1,0:T(8,128)(2,1)S(1)} %all-to-all-done.1.refs_0_.in_hbm_ref) | copy-start | bytes 4915204
  101.5 6.2 %copy-start.4 = (bf16[128,3072]{1,0:T(8,128)(2,1)}, bf16[128,3072]{1,0:T(8,128)(2,1)S(1)}, u32[]{:S(2)}) copy-start(bf16[128,3072]{1,0:T(8,128)(2,1)S(1)} %collective-permute-done.9.refs_1_.second_ref) | copy-start | bytes 2359300
  107.7 3.9 %collective-permute-start.13 = (bf16[256,3072]{1,0:T(8,128)(2,1)}, bf16[256,3072]{1,0:T(8,128)(2,1)S(1)}, u32[]{:S(2)}, u32[]{:S(2)}) collective-permute-start(bf16[256,3072]{1,0:T(8,128)(2,1)} %get-tuple-element.23), channel_id=1, source_target_pairs={{0,1},{1,0},{2,3},{3,2},{4,5},{5,4},{6,7},{7,6},{8,9},{9,8},{10,11... | collective-permute-start | bytes 4718600 | tf_op jit(solution)/shard_map/ppermute | solution.py:539
  111.7 3.0 %copy-start.15 = (bf16[256,3072]{1,0:T(8,128)(2,1)}, bf16[256,3072]{1,0:T(8,128)(2,1)S(1)}, u32[]{:S(2)}) copy-start(bf16[256,3072]{1,0:T(8,128)(2,1)S(1)} %collective-permute-done.13) | copy-start | bytes 4718596
  114.7 19.5 %collective-permute-start.14 = (bf16[128,3072]{1,0:T(8,128)(2,1)}, bf16[128,3072]{1,0:T(8,128)(2,1)}, u32[]{:S(2)}, u32[]{:S(2)}) collective-permute-start(bf16[128,3072]{1,0:T(8,128)(2,1)} %add_convert_fusion.refs_4_), channel_id=1, source_target_pairs={{0,2},{1,3},{2,0},{3,1},{4,6},{5,7},{6,4},{7,5},{8,10},{9,11},{10,... | collective-permute-start | bytes 2359304 | tf_op jit(solution)/shard_map/ppermute | solution.py:543
  128.5 5.7 %copy-start.11 = (f32[128,3072]{1,0:T(8,128)S(1)}, f32[128,3072]{1,0:T(8,128)}, u32[]{:S(2)}) copy-start(f32[128,3072]{1,0:T(8,128)} %multiply_reduce_fusion.1.refs_1_) | copy-start | bytes 4718596
  128.5 27.0 %all-to-all-start.2 = ((bf16[16,384,128]{2,1,0:T(8,128)(2,1)}), bf16[16,384,128]{2,1,0:T(8,128)(2,1)S(1)}, u32[]{:S(2)}, u32[]{:S(2)}) async-start(bf16[16,384,128]{2,1,0:T(8,128)(2,1)} %attention_backward.1), calls=%async_computation.2 | async-start | bytes 3145728 | tf_op jit(solution)/shard_map/all_to_all | solution.py:509
  134.2 4.6 %copy-start.5 = (bf16[128,3072]{1,0:T(8,128)(2,1)S(1)}, bf16[128,3072]{1,0:T(8,128)(2,1)}, u32[]{:S(2)}) copy-start(bf16[128,3072]{1,0:T(8,128)(2,1)} %copy-done.4) | copy-start | bytes 2359300
  134.2 4.6 %copy-start.10 = (bf16[128,3072]{1,0:T(8,128)(2,1)S(1)}, bf16[128,3072]{1,0:T(8,128)(2,1)}, u32[]{:S(2)}) copy-start(bf16[128,3072]{1,0:T(8,128)(2,1)} %first_ref.1) | copy-start | bytes 2359300
  137.9 33.5 %collective-permute-start.15 = (bf16[128,3072]{1,0:T(8,128)(2,1)}, bf16[128,3072]{1,0:T(8,128)(2,1)S(1)}, u32[]{:S(2)}, u32[]{:S(2)}) collective-permute-start(bf16[128,3072]{1,0:T(8,128)(2,1)} %fusion.1), channel_id=1, source_target_pairs={{0,16},{16,32},{32,48},{48,64},{64,80},{80,96},{96,112},{112,128},... | collective-permute-start | bytes 2359304 | tf_op jit(solution)/shard_map/ppermute | solution.py:500
  (6 other events, 5.2 us)

commit v9 on v8

--- a/solution.py
+++ b/solution.py
@@ -406,7 +406,7 @@
         cols = slice(n, n + step)
         acc = dot(a_s[...], w_s[:, cols], ((1,), (0,)))
         own_s[:, cols] = acc[:rows]
-        across_s[:, cols] = acc[rows:2 * rows]
+        across_s[:, cols] = acc[rows:2 * rows].astype(BF16)
         send_s[:, cols] = acc[2 * rows:].astype(BF16)
         for k, (result, out) in enumerate(zip((own_s, across_s, send_s), outs)):
             pltpu.make_async_copy(result.at[:, cols], out.at[:, cols], out_sems.at[k]).start()
@@ -416,7 +416,7 @@
 
 def project(place, attns, pieces, *later):
     rows, width = pieces[0].shape
-    shapes = (((rows, width), F32), ((rows, width), F32), ((2 * rows, width), BF16))
+    shapes = (((rows, width), F32), ((rows, width), BF16), ((2 * rows, width), BF16))
     return pl.pallas_call(
         project_kernel,
         out_shape=tuple(jax.ShapeDtypeStruct(*shape) for shape in shapes),
@@ -538,7 +538,7 @@
     part, part_across, part_send = project(place, attns, pieces)
     received = lax.ppermute(part_send, "seq", CORE)
     rows = part.shape[0]
-    across = (part_across + received[rows:].astype(F32)).astype(BF16)
+    across = (part_across.astype(F32) + received[rows:].astype(F32)).astype(BF16)
     grads = attention_backward(place, bwd, grads, across)
     across = lax.ppermute(across, "seq", YSWAP)
     proj = part + received[:rows].astype(F32) + across.astype(F32)

time: 176 us -> 175 us (level); the launches traced: 172 us -> 174 us
    pallas_call x1, Pallas kernels: 13 us -> 17.2 us  [attention_backward(): pl.pallas_call(backward_kernel, out_shape=jax.ShapeDtypeStruct((blocks, 3...]
    ppermute x1, waiting for transfers between devices: 14.3 us -> 11.4 us  [rotated(): lax.ppermute(array, axis, [(i, (i + by) % length) for i in range(length)])]
    pallas_call x1, Pallas kernels: 11.8 us -> 9.1 us  [attention_forward(): pl.pallas_call(forward_kernel, out_shape=(jax.ShapeDtypeStruct((total //...]
    ppermute x9, waiting for transfers between devices: 20.6 us -> 22.8 us  [along_x(): lax.ppermute(array, 'seq', [(i, (i + PER_X * offset) % count) for i in ra...]
  transfers between devices with their start and end apart: 19 -> 19, of which waited for: 11 -> 13; matrix products, arithmetic and copies ran while one was open for 4% -> 4% of each run, Pallas kernels for 23% -> 24%
where the time goes in v9:
time: 175 us; the launch traced here: 174 us
  waiting for transfers between devices  76.1 us (43%)
  Pallas kernels  46.2 us (26%)
  starting transfers between devices  35.5 us (20%)
  other arithmetic  8.48 us (5%)
  local copies, waits for them, and re-layouts  6.7 us (4%)
    all_to_all x3, waiting for transfers between devices, exchange(): return lax.all_to_all(array, 'seq', 0, 0, tiled=True)  36.9 us
    ppermute x9, waiting for transfers between devices, along_x(): lax.ppermute(array, 'seq', [(i, (i + PER_X * offset) % count) for i in ra...  22.8 us
    pallas_call x1, Pallas kernels, attention_backward(): pl.pallas_call(backward_kernel, out_shape=jax.ShapeDtypeStruct((blocks, 3...  17.2 us
    all_to_all x3, starting transfers between devices, exchange(): return lax.all_to_all(array, 'seq', 0, 0, tiled=True)  16.8 us
    ppermute x9, starting transfers between devices, along_x(): lax.ppermute(array, 'seq', [(i, (i + PER_X * offset) % count) for i in ra...  14 us
    ppermute x1, waiting for transfers between devices, rotated(): lax.ppermute(array, axis, [(i, (i + by) % length) for i in range(length)])  11.4 us
    pallas_call x1, Pallas kernels, attention_forward(): pl.pallas_call(forward_kernel, out_shape=(jax.ShapeDtypeStruct((total //...  9.1 us
    pallas_call x2, Pallas kernels, pack(): pl.pallas_call(pack_kernel, grid=(1,), out_shape=jax.ShapeDtypeStruct((he...  5.66 us
  transfers between devices with their start and end apart: 19, of which 13 were waited for; matrix products, arithmetic and copies ran while one was open for 4% of the time, Pallas kernels for 24%

profile of v9, /device:TPU:1, one launch (start us, length us, event | category | flops | bytes accessed | tf_op | source)
XLA Modules:
  0.0 173.9 jit_solution(2677783402114351158)
XLA Ops:
  0.6 3.7 %collective-permute-start.5 = (bf16[128,3072]{1,0:T(8,128)(2,1)}, bf16[128,3072]{1,0:T(8,128)(2,1)S(1)}, u32[]{:S(2)}, u32[]{:S(2)}) collective-permute-start(bf16[128,3072]{1,0:T(8,128)(2,1)} %bitcast.24), channel_id=1, source_target_pairs={{0,8},{1,9},{2,10},{3,11},{4,12},{5,13},{6,14},{7,15},{8,0},{9,1},... | collective-permute-start | bytes 2359304 | tf_op jit(solution)/shard_map/ppermute | solution.py:31
  5.8 1.3 slice_bitcast_fusion.2
  7.1 2.8 %pack.2 = bf16[16,400,128]{2,1,0:T(8,128)(2,1)} custom-call(s32[1,128]{1,0:T(1,128)} %get-tuple-element.28.seg_ref, bf16[1,2,128,2048]{3,2,1,0:T(8,128)(2,1)} %q_ref.3, bf16[1,2,128,2048]{3,2,1,0:T(8,128)(2,1)} %k_ref.3, bf16[1,2,128,2048]{3,2,1,0:T(8,128)(2,1)} %v_ref.3), custom_call_target="tpu_custom_call" | custom-call | flops 2000000000 | tf_op jit(solution)/shard_map/pack/pallas_call | solution.py:85
  9.9 6.3 %all-to-all-start = ((bf16[16,400,128]{2,1,0:T(8,128)(2,1)}), bf16[16,400,128]{2,1,0:T(8,128)(2,1)S(1)}, u32[]{:S(2)}, u32[]{:S(2)}) async-start(bf16[16,400,128]{2,1,0:T(8,128)(2,1)} %pack.2), calls=%async_computation | async-start | bytes 3276800 | tf_op jit(solution)/shard_map/all_to_all | solution.py:509
  17.5 1.5 collective-permute-start.1
  19.0 1.7 multiply_reduce_fusion.1.refs_1_
  20.9 18.4 %collective-permute-done.4.refs_6_.refs_3_ = bf16[128,3072]{1,0:T(8,128)(2,1)S(1)} collective-permute-done((bf16[128,3072]{1,0:T(8,128)(2,1)}, bf16[128,3072]{1,0:T(8,128)(2,1)S(1)}, u32[]{:S(2)}, u32[]{:S(2)}) %collective-permute-start.4) | collective-permute-done | bytes 786464 | tf_op jit(solution)/shard_map/ppermute | solution.py:31
  40.1 2.8 %pack.3 = bf16[16,400,128]{2,1,0:T(8,128)(2,1)} custom-call(s32[1,128]{1,0:T(1,128)} %get-tuple-element.27.seg_ref, bf16[1,2,128,2048]{3,2,1,0:T(8,128)(2,1)} %q_ref.3, bf16[1,2,128,2048]{3,2,1,0:T(8,128)(2,1)} %k_ref.3, bf16[1,2,128,2048]{3,2,1,0:T(8,128)(2,1)} %v_ref.3, bf16[128,3072]{1,0:T(8,128)(2,1)} %collective-permute-done.1.refs_2_.refs_0_, ...), custom_call_target="tpu_custom_call" | custom-call | flops 2000000000 | tf_op jit(solution)/shard_map/pack/pallas_call | solution.py:85
  43.0 15.2 %all-to-all-done.refs_0_.in_hbm_ref = bf16[16,400,128]{2,1,0:T(8,128)(2,1)S(1)} async-done(((bf16[16,400,128]{2,1,0:T(8,128)(2,1)}), bf16[16,400,128]{2,1,0:T(8,128)(2,1)S(1)}, u32[]{:S(2)}, u32[]{:S(2)}) %all-to-all-start) | async-done | bytes 1638432 | tf_op jit(solution)/shard_map/all_to_all | solution.py:509
  58.1 4.8 %all-to-all-start.1 = ((bf16[16,400,128]{2,1,0:T(8,128)(2,1)}), bf16[16,400,128]{2,1,0:T(8,128)(2,1)S(1)}, u32[]{:S(2)}, u32[]{:S(2)}) async-start(bf16[16,400,128]{2,1,0:T(8,128)(2,1)} %pack.3), calls=%async_computation.1 | async-start | bytes 3276800 | tf_op jit(solution)/shard_map/all_to_all | solution.py:509
  65.6 1.3 collective-permute-start.9
  66.9 5.5 %attention_grad.1 = (bf16[512,128]{1,0:T(8,128)(2,1)}, bf16[512,128]{1,0:T(8,128)(2,1)}, bf16[512,128]{1,0:T(8,128)(2,1)}, bf16[512,128]{1,0:T(8,128)(2,1)}) custom-call(s32[1]{0:T(128)} %bitcast.3.place_ref, bf16[128,3072]{1,0:T(8,128)(2,1)} %copy-done.14, bf16[128,3072]{1,0:T(8,128)(2,1)} %collective-permute-done.refs_1_, ...), custom_call_target="tpu_custom_call" | custom-call | flops 200000000 | tf_op jit(solution)/shard_map/attention_grad/pallas_call | solution.py:370
  72.4 2.7 %collective-permute-start.10 = (bf16[512,128]{1,0:T(8,128)(2,1)}, bf16[512,128]{1,0:T(8,128)(2,1)S(1)}, u32[]{:S(2)}, u32[]{:S(2)}) collective-permute-start(bf16[512,128]{1,0:T(8,128)(2,1)} %get-tuple-element.19), channel_id=1, source_target_pairs={{0,12},{1,13},{2,14},{3,15},{4,0},{5,1},{6,2},{7,3},{8,4},{9,5},{1... | collective-permute-start | bytes 393224 | tf_op jit(solution)/shard_map/ppermute | solution.py:31
  75.1 1.8 %collective-permute-start.12 = (bf16[512,128]{1,0:T(8,128)(2,1)}, bf16[512,128]{1,0:T(8,128)(2,1)S(1)}, u32[]{:S(2)}, u32[]{:S(2)}) collective-permute-start(bf16[512,128]{1,0:T(8,128)(2,1)} %get-tuple-element.21), channel_id=1, source_target_pairs={{0,8},{1,9},{2,10},{3,11},{4,12},{5,13},{6,14},{7,15},{8,0},{9,1},... | collective-permute-start | bytes 393224 | tf_op jit(solution)/shard_map/ppermute | solution.py:31
  76.9 9.1 %attention_forward.1 = (bf16[512,128]{1,0:T(8,128)(2,1)}, bf16[512,128]{1,0:T(8,128)(2,1)}, bf16[512,128]{1,0:T(8,128)(2,1)}, bf16[512,128]{1,0:T(8,128)(2,1)}) custom-call(s32[1]{0:T(128)} %bitcast.3.place_ref, bf16[16,400,128]{2,1,0:T(8,128)(2,1)} %copy-done, bf16[512,128]{1,0:T(8,128)(2,1)} %get-tuple-element.14.refs_0_, ...), custom_call_target="tpu_custom_call" | custom-call | flops 200000000 | tf_op jit(solution)/shard_map/attention_forward/pallas_call | solution.py:204
  86.0 1.3 collective-permute-start.8
  87.9 1.3 collective-permute-start.6
  89.2 1.8 %collective-permute-start.7 = (bf16[512,128]{1,0:T(8,128)(2,1)}, bf16[512,128]{1,0:T(8,128)(2,1)S(1)}, u32[]{:S(2)}, u32[]{:S(2)}) collective-permute-start(bf16[512,128]{1,0:T(8,128)(2,1)} %get-tuple-element.17), channel_id=1, source_target_pairs={{0,12},{1,13},{2,14},{3,15},{4,0},{5,1},{6,2},{7,3},{8,4},{9,5},{1... | collective-permute-start | bytes 393224 | tf_op jit(solution)/shard_map/ppermute | solution.py:31
  91.6 2.8 %collective-permute-done.8.array_ref = bf16[512,128]{1,0:T(8,128)(2,1)S(1)} collective-permute-done((bf16[512,128]{1,0:T(8,128)(2,1)}, bf16[512,128]{1,0:T(8,128)(2,1)S(1)}, u32[]{:S(2)}, u32[]{:S(2)}) %collective-permute-start.8) | collective-permute-done | bytes 131104 | tf_op jit(solution)/shard_map/ppermute | solution.py:31
  94.4 5.8 %all-to-all-done.1.refs_0_.in_hbm_ref = bf16[16,400,128]{2,1,0:T(8,128)(2,1)S(1)} async-done(((bf16[16,400,128]{2,1,0:T(8,128)(2,1)}), bf16[16,400,128]{2,1,0:T(8,128)(2,1)S(1)}, u32[]{:S(2)}, u32[]{:S(2)}) %all-to-all-start.1) | async-done | bytes 1638432 | tf_op jit(solution)/shard_map/all_to_all | solution.py:509
  100.2 1.3 collective-permute-done.9.refs_1_.second_ref
  102.9 4.7 %project.1 = (f32[128,3072]{1,0:T(8,128)}, bf16[128,3072]{1,0:T(8,128)(2,1)}, bf16[256,3072]{1,0:T(8,128)(2,1)}) custom-call(s32[1]{0:T(128)} %bitcast.3.place_ref, bf16[512,128]{1,0:T(8,128)(2,1)} %get-tuple-element.15.refs_0_, bf16[512,128]{1,0:T(8,128)(2,1)} %copy-done.16, bf16[512,128]{1,0:T(8,128)(2,1)} %copy-done.17, bf16[512,128]{1,0:T(8,128)(2,1)} %copy-done.6, ...), custom_call_target="tpu_custom_call" | custom-call | flops 200000000 | tf_op jit(solution)/shard_map/project/pallas_call | solution.py:420
  108.3 3.2 %collective-permute-done.13 = bf16[256,3072]{1,0:T(8,128)(2,1)S(1)} collective-permute-done((bf16[256,3072]{1,0:T(8,128)(2,1)}, bf16[256,3072]{1,0:T(8,128)(2,1)S(1)}, u32[]{:S(2)}, u32[]{:S(2)}) %collective-permute-start.13) | collective-permute-done | bytes 1572896 | tf_op jit(solution)/shard_map/ppermute | solution.py:539
  111.6 1.2 copy-done.15
  112.8 2.2 %add_convert_fusion.refs_4_ = bf16[128,3072]{1,0:T(8,128)(2,1)} fusion(bf16[128,3072]{1,0:T(8,128)(2,1)} %get-tuple-element.24, bf16[256,3072]{1,0:T(8,128)(2,1)S(1)} %collective-permute-done.13), kind=kLoop, calls=%fused_computation.4 | loop fusion | flops 1572864 | bytes 2359296 | tf_op jit(solution)/shard_map/convert_element_type | solution.py:541
  115.8 17.2 %attention_backward.1 = bf16[16,384,128]{2,1,0:T(8,128)(2,1)} custom-call(s32[1]{0:T(128)} %bitcast.3.place_ref, bf16[16,400,128]{2,1,0:T(8,128)(2,1)} %copy-done.1, bf16[512,128]{1,0:T(8,128)(2,1)} %get-tuple-element.14.refs_0_, bf16[512,128]{1,0:T(8,128)(2,1)} %copy-done.7, bf16[512,128]{1,0:T(8,128)(2,1)} %copy-done.8, bf16[512,128]{1,0:T(8,128)(2,1)} %copy-done.9, ...), custom_call_target="tpu_custom_call" | custom-call | flops 30000001024 | tf_op jit(solution)/shard_map/attention_backward/pallas_call | solution.py:305
  133.0 5.7 %all-to-all-start.2 = ((bf16[16,384,128]{2,1,0:T(8,128)(2,1)}), bf16[16,384,128]{2,1,0:T(8,128)(2,1)S(1)}, u32[]{:S(2)}, u32[]{:S(2)}) async-start(bf16[16,384,128]{2,1,0:T(8,128)(2,1)} %attention_backward.1), calls=%async_computation.2 | async-start | bytes 3145728 | tf_op jit(solution)/shard_map/all_to_all | solution.py:509
  138.7 3.7 %fusion.1 = bf16[128,3072]{1,0:T(8,128)(2,1)} fusion(bf16[128,3072]{1,0:T(8,128)(2,1)} %param.18, f32[128,3072]{1,0:T(8,128)S(1)} %copy-done.11, bf16[128,3072]{1,0:T(8,128)(2,1)} %collective-permute-done.14, f32[128,3072]{1,0:T(8,128)} %get-tuple-element.22, bf16[256,3072]{1,0:T(8,128)(2,1)} %copy-done.15, bf16[1,128,3072]{2,1,0:T(8,128)(2,1)} %param.10, ...), kind=kLoop, calls=%fused_computation.6 | loop fusion | flops 3538944 | bytes 7077889 | tf_op jit(solution)/shard_map/jit(_where)/select_n | solution.py:546
  142.5 1.5 choose.1
  144.0 16.0 %all-to-all-done.2.in_ref = bf16[16,384,128]{2,1,0:T(8,128)(2,1)S(1)} async-done(((bf16[16,384,128]{2,1,0:T(8,128)(2,1)}), bf16[16,384,128]{2,1,0:T(8,128)(2,1)S(1)}, u32[]{:S(2)}, u32[]{:S(2)}) %all-to-all-start.2) | async-done | bytes 1572896 | tf_op jit(solution)/shard_map/all_to_all | solution.py:509
  160.0 1.6 unpack.1
  161.6 11.4 %collective-permute-done.15 = bf16[128,3072]{1,0:T(8,128)(2,1)S(1)} collective-permute-done((bf16[128,3072]{1,0:T(8,128)(2,1)}, bf16[128,3072]{1,0:T(8,128)(2,1)S(1)}, u32[]{:S(2)}, u32[]{:S(2)}) %collective-permute-start.15) | collective-permute-done | bytes 786464 | tf_op jit(solution)/shard_map/ppermute | solution.py:500
  (65 shorter events, 11.4 us)
Async XLA Ops:
  0.6 20.2 %collective-permute-start.5 = (bf16[128,3072]{1,0:T(8,128)(2,1)}, bf16[128,3072]{1,0:T(8,128)(2,1)S(1)}, u32[]{:S(2)}, u32[]{:S(2)}) collective-permute-start(bf16[128,3072]{1,0:T(8,128)(2,1)} %bitcast.24), channel_id=1, source_target_pairs={{0,8},{1,9},{2,10},{3,11},{4,12},{5,13},{6,14},{7,15},{8,0},{9,1},... | collective-permute-start | bytes 2359304 | tf_op jit(solution)/shard_map/ppermute | solution.py:31
  4.3 35.0 %collective-permute-start.4 = (bf16[128,3072]{1,0:T(8,128)(2,1)}, bf16[128,3072]{1,0:T(8,128)(2,1)S(1)}, u32[]{:S(2)}, u32[]{:S(2)}) collective-permute-start(bf16[128,3072]{1,0:T(8,128)(2,1)} %bitcast.25), channel_id=1, source_target_pairs={{0,12},{1,13},{2,14},{3,15},{4,0},{5,1},{6,2},{7,3},{8,4},{9,5},{1... | collective-permute-start | bytes 2359304 | tf_op jit(solution)/shard_map/ppermute | solution.py:31
  5.2 34.3 %collective-permute-start.3 = (bf16[128,3072]{1,0:T(8,128)(2,1)}, bf16[128,3072]{1,0:T(8,128)(2,1)}, u32[]{:S(2)}, u32[]{:S(2)}) collective-permute-start(bf16[128,3072]{1,0:T(8,128)(2,1)} %bitcast.26), channel_id=1, source_target_pairs={{0,4},{1,5},{2,6},{3,7},{4,8},{5,9},{6,10},{7,11},{8,12},{9,13},{1... | collective-permute-start | bytes 2359304 | tf_op jit(solution)/shard_map/ppermute | solution.py:31
  9.9 6.3 %copy-start.18 = (f32[1,2,4,3072]{3,2,1,0:T(4,128)S(1)}, f32[1,2,4,3072]{3,2,1,0:T(4,128)}, u32[]{:S(2)}) copy-start(f32[1,2,4,3072]{3,2,1,0:T(4,128)} %param.15) | copy-start | bytes 294916
  9.9 48.3 %all-to-all-start = ((bf16[16,400,128]{2,1,0:T(8,128)(2,1)}), bf16[16,400,128]{2,1,0:T(8,128)(2,1)S(1)}, u32[]{:S(2)}, u32[]{:S(2)}) async-start(bf16[16,400,128]{2,1,0:T(8,128)(2,1)} %pack.2), calls=%async_computation | async-start | bytes 3276800 | tf_op jit(solution)/shard_map/all_to_all | solution.py:509
  17.5 21.8 %copy-start.14 = (bf16[128,3072]{1,0:T(8,128)(2,1)}, bf16[128,3072]{1,0:T(8,128)(2,1)S(1)}, u32[]{:S(2)}) copy-start(bf16[128,3072]{1,0:T(8,128)(2,1)S(1)} %multiply_convert_fusion.refs_0_) | copy-start | bytes 2359300
  17.5 22.4 %collective-permute-start.1 = (bf16[128,3072]{1,0:T(8,128)(2,1)S(1)}, bf16[128,3072]{1,0:T(8,128)(2,1)}, u32[]{:S(2)}, u32[]{:S(2)}) collective-permute-start(bf16[128,3072]{1,0:T(8,128)(2,1)S(1)} %multiply_convert_fusion.refs_0_), channel_id=1, source_target_pairs={{0,2},{1,3},{2,0},{3,1},{4,6},{5,7},{6,4},{7,5},{8,10},{9,11},{10,... | collective-permute-start | bytes 2359304 | tf_op jit(solution)/shard_map/ppermute | solution.py:523
  20.9 19.0 %copy-start.12 = (bf16[128,3072]{1,0:T(8,128)(2,1)}, bf16[128,3072]{1,0:T(8,128)(2,1)S(1)}, u32[]{:S(2)}) copy-start(bf16[128,3072]{1,0:T(8,128)(2,1)S(1)} %collective-permute-done.5.refs_7_.refs_4_) | copy-start | bytes 2359300
  58.1 5.3 %copy-start = (bf16[16,400,128]{2,1,0:T(8,128)(2,1)}, bf16[16,400,128]{2,1,0:T(8,128)(2,1)S(1)}, u32[]{:S(2)}) copy-start(bf16[16,400,128]{2,1,0:T(8,128)(2,1)S(1)} %all-to-all-done.refs_0_.in_hbm_ref) | copy-start | bytes 4915204
  58.1 42.1 %all-to-all-start.1 = ((bf16[16,400,128]{2,1,0:T(8,128)(2,1)}), bf16[16,400,128]{2,1,0:T(8,128)(2,1)S(1)}, u32[]{:S(2)}, u32[]{:S(2)}) async-start(bf16[16,400,128]{2,1,0:T(8,128)(2,1)} %pack.3), calls=%async_computation.1 | async-start | bytes 3276800 | tf_op jit(solution)/shard_map/all_to_all | solution.py:509
  63.0 3.9 %collective-permute-start = (bf16[128,3072]{1,0:T(8,128)(2,1)}, bf16[128,3072]{1,0:T(8,128)(2,1)}, u32[]{:S(2)}, u32[]{:S(2)}) collective-permute-start(bf16[128,3072]{1,0:T(8,128)(2,1)} %copy-done.14), channel_id=1, source_target_pairs={{0,1},{1,0},{2,3},{3,2},{4,5},{5,4},{6,7},{7,6},{8,9},{9,8},{10,11... | collective-permute-start | bytes 2359304 | tf_op jit(solution)/shard_map/ppermute | solution.py:524
  63.2 3.7 %collective-permute-start.2 = (bf16[128,3072]{1,0:T(8,128)(2,1)}, bf16[128,3072]{1,0:T(8,128)(2,1)}, u32[]{:S(2)}, u32[]{:S(2)}) collective-permute-start(bf16[128,3072]{1,0:T(8,128)(2,1)} %collective-permute-done.1.refs_2_.refs_0_), channel_id=1, source_target_pairs={{0,1},{1,0},{2,3},{3,2},{4,5},{5,4},{6,7},{7,6},{8,9},{9,8},{10,11... | collective-permute-start | bytes 2359304 | tf_op jit(solution)/shard_map/ppermute | solution.py:525
  65.6 36.0 %collective-permute-start.9 = (bf16[128,3072]{1,0:T(8,128)(2,1)}, bf16[128,3072]{1,0:T(8,128)(2,1)S(1)}, u32[]{:S(2)}, u32[]{:S(2)}) collective-permute-start(bf16[128,3072]{1,0:T(8,128)(2,1)} %settle.1.refs_2_), channel_id=1, source_target_pairs={{16,0},{32,16},{48,32},{64,48},{80,64},{96,80},{112,96},{128,112},... | collective-permute-start | bytes 2359304 | tf_op jit(solution)/shard_map/ppermute | solution.py:495
  72.4 15.5 %collective-permute-start.10 = (bf16[512,128]{1,0:T(8,128)(2,1)}, bf16[512,128]{1,0:T(8,128)(2,1)S(1)}, u32[]{:S(2)}, u32[]{:S(2)}) collective-permute-start(bf16[512,128]{1,0:T(8,128)(2,1)} %get-tuple-element.19), channel_id=1, source_target_pairs={{0,12},{1,13},{2,14},{3,15},{4,0},{5,1},{6,2},{7,3},{8,4},{9,5},{1... | collective-permute-start | bytes 393224 | tf_op jit(solution)/shard_map/ppermute | solution.py:31
  75.1 14.1 %collective-permute-start.11 = (bf16[512,128]{1,0:T(8,128)(2,1)}, bf16[512,128]{1,0:T(8,128)(2,1)S(1)}, u32[]{:S(2)}, u32[]{:S(2)}) collective-permute-start(bf16[512,128]{1,0:T(8,128)(2,1)} %get-tuple-element.20), channel_id=1, source_target_pairs={{0,4},{1,5},{2,6},{3,7},{4,8},{5,9},{6,10},{7,11},{8,12},{9,13},{1... | collective-permute-start | bytes 393224 | tf_op jit(solution)/shard_map/ppermute | solution.py:31
  75.1 16.5 %collective-permute-start.12 = (bf16[512,128]{1,0:T(8,128)(2,1)}, bf16[512,128]{1,0:T(8,128)(2,1)S(1)}, u32[]{:S(2)}, u32[]{:S(2)}) collective-permute-start(bf16[512,128]{1,0:T(8,128)(2,1)} %get-tuple-element.21), channel_id=1, source_target_pairs={{0,8},{1,9},{2,10},{3,11},{4,12},{5,13},{6,14},{7,15},{8,0},{9,1},... | collective-permute-start | bytes 393224 | tf_op jit(solution)/shard_map/ppermute | solution.py:31
  86.0 8.5 %collective-permute-start.8 = (bf16[512,128]{1,0:T(8,128)(2,1)}, bf16[512,128]{1,0:T(8,128)(2,1)S(1)}, u32[]{:S(2)}, u32[]{:S(2)}) collective-permute-start(bf16[512,128]{1,0:T(8,128)(2,1)} %get-tuple-element.18), channel_id=1, source_target_pairs={{0,8},{1,9},{2,10},{3,11},{4,12},{5,13},{6,14},{7,15},{8,0},{9,1},... | collective-permute-start | bytes 393224 | tf_op jit(solution)/shard_map/ppermute | solution.py:31
  87.9 19.7 %copy-start.7 = (bf16[512,128]{1,0:T(8,128)(2,1)}, bf16[512,128]{1,0:T(8,128)(2,1)S(1)}, u32[]{:S(2)}) copy-start(bf16[512,128]{1,0:T(8,128)(2,1)S(1)} %collective-permute-done.10.refs_2_.refs_1_) | copy-start | bytes 393220
  87.9 14.3 %collective-permute-start.6 = (bf16[512,128]{1,0:T(8,128)(2,1)}, bf16[512,128]{1,0:T(8,128)(2,1)S(1)}, u32[]{:S(2)}, u32[]{:S(2)}) collective-permute-start(bf16[512,128]{1,0:T(8,128)(2,1)} %get-tuple-element.16), channel_id=1, source_target_pairs={{0,4},{1,5},{2,6},{3,7},{4,8},{5,9},{6,10},{7,11},{8,12},{9,13},{1... | collective-permute-start | bytes 393224 | tf_op jit(solution)/shard_map/ppermute | solution.py:31
  89.2 18.4 %copy-start.8 = (bf16[512,128]{1,0:T(8,128)(2,1)}, bf16[512,128]{1,0:T(8,128)(2,1)S(1)}, u32[]{:S(2)}) copy-start(bf16[512,128]{1,0:T(8,128)(2,1)S(1)} %collective-permute-done.11.refs_3_.refs_2_) | copy-start | bytes 393220
  89.2 13.0 %collective-permute-start.7 = (bf16[512,128]{1,0:T(8,128)(2,1)}, bf16[512,128]{1,0:T(8,128)(2,1)S(1)}, u32[]{:S(2)}, u32[]{:S(2)}) collective-permute-start(bf16[512,128]{1,0:T(8,128)(2,1)} %get-tuple-element.17), channel_id=1, source_target_pairs={{0,12},{1,13},{2,14},{3,15},{4,0},{5,1},{6,2},{7,3},{8,4},{9,5},{1... | collective-permute-start | bytes 393224 | tf_op jit(solution)/shard_map/ppermute | solution.py:31
  91.6 16.0 %copy-start.9 = (bf16[512,128]{1,0:T(8,128)(2,1)}, bf16[512,128]{1,0:T(8,128)(2,1)S(1)}, u32[]{:S(2)}) copy-start(bf16[512,128]{1,0:T(8,128)(2,1)S(1)} %collective-permute-done.12.refs_4_.refs_3_) | copy-start | bytes 393220
  100.2 7.4 %copy-start.1 = (bf16[16,400,128]{2,1,0:T(8,128)(2,1)}, bf16[16,400,128]{2,1,0:T(8,128)(2,1)S(1)}, u32[]{:S(2)}) copy-start(bf16[16,400,128]{2,1,0:T(8,128)(2,1)S(1)} %all-to-all-done.1.refs_0_.in_hbm_ref) | copy-start | bytes 4915204
  101.5 6.1 %copy-start.4 = (bf16[128,3072]{1,0:T(8,128)(2,1)}, bf16[128,3072]{1,0:T(8,128)(2,1)S(1)}, u32[]{:S(2)}) copy-start(bf16[128,3072]{1,0:T(8,128)(2,1)S(1)} %collective-permute-done.9.refs_1_.second_ref) | copy-start | bytes 2359300
  107.6 3.9 %collective-permute-start.13 = (bf16[256,3072]{1,0:T(8,128)(2,1)}, bf16[256,3072]{1,0:T(8,128)(2,1)S(1)}, u32[]{:S(2)}, u32[]{:S(2)}) collective-permute-start(bf16[256,3072]{1,0:T(8,128)(2,1)} %get-tuple-element.23), channel_id=1, source_target_pairs={{0,1},{1,0},{2,3},{3,2},{4,5},{5,4},{6,7},{7,6},{8,9},{9,8},{10,11... | collective-permute-start | bytes 4718600 | tf_op jit(solution)/shard_map/ppermute | solution.py:539
  111.6 1.2 copy-start.15
  115.0 23.7 %collective-permute-start.14 = (bf16[128,3072]{1,0:T(8,128)(2,1)}, bf16[128,3072]{1,0:T(8,128)(2,1)}, u32[]{:S(2)}, u32[]{:S(2)}) collective-permute-start(bf16[128,3072]{1,0:T(8,128)(2,1)} %add_convert_fusion.refs_4_), channel_id=1, source_target_pairs={{0,2},{1,3},{2,0},{3,1},{4,6},{5,7},{6,4},{7,5},{8,10},{9,11},{10,... | collective-permute-start | bytes 2359304 | tf_op jit(solution)/shard_map/ppermute | solution.py:543
  133.0 5.7 %copy-start.11 = (f32[128,3072]{1,0:T(8,128)S(1)}, f32[128,3072]{1,0:T(8,128)}, u32[]{:S(2)}) copy-start(f32[128,3072]{1,0:T(8,128)} %multiply_reduce_fusion.1.refs_1_) | copy-start | bytes 4718596
  133.0 27.0 %all-to-all-start.2 = ((bf16[16,384,128]{2,1,0:T(8,128)(2,1)}), bf16[16,384,128]{2,1,0:T(8,128)(2,1)S(1)}, u32[]{:S(2)}, u32[]{:S(2)}) async-start(bf16[16,384,128]{2,1,0:T(8,128)(2,1)} %attention_backward.1), calls=%async_computation.2 | async-start | bytes 3145728 | tf_op jit(solution)/shard_map/all_to_all | solution.py:509
  138.7 3.8 %copy-start.5 = (bf16[128,3072]{1,0:T(8,128)(2,1)S(1)}, bf16[128,3072]{1,0:T(8,128)(2,1)}, u32[]{:S(2)}) copy-start(bf16[128,3072]{1,0:T(8,128)(2,1)} %copy-done.4) | copy-start | bytes 2359300
  138.7 3.8 %copy-start.10 = (bf16[128,3072]{1,0:T(8,128)(2,1)S(1)}, bf16[128,3072]{1,0:T(8,128)(2,1)}, u32[]{:S(2)}) copy-start(bf16[128,3072]{1,0:T(8,128)(2,1)} %first_ref.1) | copy-start | bytes 2359300
  142.5 30.5 %collective-permute-start.15 = (bf16[128,3072]{1,0:T(8,128)(2,1)}, bf16[128,3072]{1,0:T(8,128)(2,1)S(1)}, u32[]{:S(2)}, u32[]{:S(2)}) collective-permute-start(bf16[128,3072]{1,0:T(8,128)(2,1)} %fusion.1), channel_id=1, source_target_pairs={{0,16},{16,32},{32,48},{48,64},{64,80},{80,96},{96,112},{112,128},... | collective-permute-start | bytes 2359304 | tf_op jit(solution)/shard_map/ppermute | solution.py:500
  (6 other events, 5.2 us)
